TPU v7x, 256 devices: a whole 4x4x8 slice. The times are simulated.
256 devices in a mesh: slab: 8 (over x, core), space: 32 (over y, z).
Axes of the slice: x: 4, y: 4, z: 8, core: 2. Of those that a mesh axis runs over, the one named last changes fastest.
Arguments:
- positions: float32 [8, 1536, 3, 128], P('slab', 'space'), may hold values from -1 to 1
- masses: float32 [8, 1536, 128], P('slab', 'space'), may hold values from 0.0005 to 0.005
- counts: int32 [8, 32, 48], P('slab', 'space'), may hold values from 1 to 128, 4608 in all within a row
- dest_ids: int32 [8, 1536], P('slab', 'space'), may hold values from 0 to 31, as said below
- near_list: int32 [8, 1536, 4], P('slab', 'space'), may hold values from 0 to 143
- cell_list: int32 [8, 1536, 32], P('slab', 'space'), may hold values from 0 to 16383
- cell_centers: float32 [3, 16384], P(None, 'slab'), may hold values from -6 to 6
- cell_mass: float32 [16384], P('slab'), may hold values from 0.5 to 5
Outputs:
- accel: float32 [8, 1536, 3, 128], P('slab', 'space')
Inputs may be any that keep to these rules, and one draw needn't show every extreme that they name: `dest_ids`: of one device's 48 buckets at most 6 name any one destination, and in every slab one destination, drawn from the seed, is named by exactly 6 buckets of every device of that slab.
All inputs are finite; a program needn't handle non-finite values.
Results may differ from a plain program's by a relative error of at most 0.0003.
Values sent between devices are 32-bit elements; how exact they have to be, the bound alone decides.
No kernel may reach another device: no remote copies, remote signals or barrier semaphores. Data moves between devices by JAX's collectives and lax.ppermute only.
A program may use at most 64 MiB of HBM per device.

v0:
```python
import jax
import jax.numpy as jnp
from jax import lax
from jax.sharding import PartitionSpec as P

CAP = 6


soft_near = 0.01
block_rows = 16


def extended(block, sides, width):
    for axis, dim in sides:
        count = lax.axis_size(axis)
        forward = [(i, i + 1) for i in range(count - 1)]
        forward.append((count - 1, 0))
        backward = [(target, source) for source, target in forward]
        low = lax.ppermute(
            lax.slice_in_dim(block, block.shape[dim] - width, None, axis=dim), axis, forward
        )
        high = lax.ppermute(lax.slice_in_dim(block, 0, width, axis=dim), axis, backward)
        block = jnp.concatenate([low, block, high], axis=dim)
    return block


def center_of(packed):
    alive = (packed[:, 3] > 0.0).astype(jnp.float32)
    total = jnp.sum(alive, axis=-1)
    center = jnp.sum(packed[:, :3] * alive[:, None], axis=-1) / jnp.maximum(total, 1.0)[:, None]
    return (center, alive)


def pair_block(targets, sources):
    rel = sources[:, :, :3, None, :] - targets[:, None, :3, :, None]
    dist_sq = jnp.sum(rel * rel, axis=2) + soft_near
    weight = sources[:, :, 3][:, :, None, :] * dist_sq ** (-1.5)
    return jnp.sum(rel * weight[:, :, None], axis=(1, 4))


def cell_terms(center, cell_pos, cell_weight):
    rel = center[:, None, :] - cell_pos
    dist_sq = jnp.sum(rel * rel, axis=0) + 1.0
    inverse_cube = cell_weight * dist_sq ** (-1.5)
    inverse_fifth = 3.0 * cell_weight * dist_sq ** (-2.5)
    field = -jnp.sum(inverse_cube[None] * rel, axis=1)
    terms = []
    for first, second in ((0, 0), (1, 1), (2, 2), (0, 1), (0, 2), (1, 2)):
        value = inverse_fifth * rel[first] * rel[second]
        if first == second:
            value = value - inverse_cube
        terms.append(jnp.sum(value, axis=0))
    return (field, jnp.stack(terms))


def apply_local(field, tidal, offset):
    acc_x = (
        field[0][:, None]
        + tidal[0][:, None] * offset[:, 0]
        + tidal[3][:, None] * offset[:, 1]
        + tidal[4][:, None] * offset[:, 2]
    )
    acc_y = (
        field[1][:, None]
        + tidal[3][:, None] * offset[:, 0]
        + tidal[1][:, None] * offset[:, 1]
        + tidal[5][:, None] * offset[:, 2]
    )
    acc_z = (
        field[2][:, None]
        + tidal[4][:, None] * offset[:, 0]
        + tidal[5][:, None] * offset[:, 1]
        + tidal[2][:, None] * offset[:, 2]
    )
    return jnp.stack([acc_x, acc_y, acc_z], axis=1)


def per_device(positions, masses, counts, dest_ids, near_list, cell_list, cell_centers, cell_mass):
    home_pos = positions[0]
    buckets = home_pos.shape[0]
    places = home_pos.shape[2]
    near_count = near_list.shape[2]
    live_home = (jnp.arange(places, dtype=jnp.int32)[None, :] < counts[0, 0][:, None]).astype(
        jnp.float32
    )
    packed = jnp.concatenate([home_pos, (masses[0] * live_home)[:, None, :]], axis=1)
    window = extended(packed, (("space", 0),), buckets)
    peers = lax.axis_size("space")
    going = dest_ids[0]
    position = jnp.arange(buckets, dtype=jnp.int32)
    earlier = (going[:, None] == going[None, :]) & (position[None, :] < position[:, None])
    rank = jnp.sum(earlier.astype(jnp.int32), axis=1)
    slot = going * CAP + rank
    slot_total = peers * CAP
    listed = jnp.concatenate([near_list[0], cell_list[0]], axis=1)
    send_pack = jnp.zeros((slot_total, 4, places), jnp.float32).at[slot].set(packed)
    send_list = jnp.zeros((slot_total, listed.shape[1]), jnp.int32).at[slot].set(listed)
    recv_pack, recv_list = (
        lax.all_to_all(send_pack, "space", split_axis=0, concat_axis=0, tiled=True),
        lax.all_to_all(send_list, "space", split_axis=0, concat_axis=0, tiled=True),
    )
    center, alive = center_of(recv_pack)
    center_rows = center.T
    cell_ids = recv_list[:, near_count:].T
    cell_block = jnp.concatenate([cell_centers, cell_mass[None, :]], axis=0)
    piece = lax.all_gather(cell_block, "slab", axis=1, tiled=True)
    width = piece.shape[1]
    local = cell_ids - jnp.int32(0)
    inside = (local >= 0) & (local < width)
    local = jnp.clip(local, 0, width - 1)
    fetched = jnp.take(piece, local, axis=1)
    cell_weight = jnp.where(inside, fetched[3], 0.0)
    field, tidal = cell_terms(center_rows, fetched[:3], cell_weight)
    field, tidal = (field, tidal)
    blocks = slot_total // block_rows

    def near_block(inputs):
        targets, leaf_ids = inputs
        return pair_block(targets, window[leaf_ids])

    near = lax.map(
        near_block,
        (
            recv_pack.reshape(blocks, block_rows, 4, places),
            recv_list[:, :near_count].reshape(blocks, block_rows, near_count),
        ),
    )
    near = near.reshape(slot_total, 3, places)
    offset = recv_pack[:, :3] - center[:, :, None]
    results = (near + apply_local(field, tidal, offset)) * alive[:, None, :]
    returned = lax.all_to_all(results, "space", split_axis=0, concat_axis=0, tiled=True)
    home_acc = returned[slot] * live_home[:, None, :]
    return home_acc[None]


def solution(mesh):
    in_specs = (
        P("slab", "space", None, None),
        P("slab", "space", None),
        P("slab", "space", None),
        P("slab", "space"),
        P("slab", "space", None),
        P("slab", "space", None),
        P(None, "slab"),
        P("slab"),
    )
    out_specs = P("slab", "space", None, None)
    return jax.shard_map(
        per_device, mesh=mesh, in_specs=in_specs, out_specs=out_specs, check_vma=False
    )
```

profile of v0, /device:TPU:1, one launch (start us, length us, event | category | flops | bytes accessed | tf_op | source)
XLA Modules:
  0.0 241.3 jit_solution(3876872994363305578)
XLA Ops:
  5.0 6.4 %collective-permute-start.1 = (f32[48,4,128]{2,1,0:T(4,128)}, f32[48,4,128]{2,1,0:T(4,128)}, u32[]{:S(2)}, u32[]{:S(2)}) collective-permute-start(f32[48,4,128]{2,1,0:T(4,128)} %pad_maximum_fusion.1), channel_id=1, source_target_pairs={{1,0},{2,1},{3,2},{4,3},{5,4},{6,5},{7,6},{8,7},{9,8},{10,9},{11,1... | collective-permute-start | bytes 294920 | tf_op jit(solution)/shard_map/ppermute | solution.py:22
  15.3 5.9 %all-to-all-start = ((s32[32,1,216]{2,1,0:T(1,128)}), s32[32,1,216]{2,1,0:T(1,128)S(1)}, u32[]{:S(2)}, u32[]{:S(2)}) async-start(s32[32,1,216]{2,1,0:T(1,128)} %reshape.299), calls=%async_computation | async-start | bytes 65536 | tf_op jit(solution)/shard_map/all_to_all | solution.py:100
  22.3 41.5 %all_gather.3 = f32[4,16384]{0,1:T(8,128)} all-gather(f32[4,2048]{0,1:T(8,128)S(1)} %copy.122), channel_id=1, replica_groups=mesh['slab'=8,'space'=32] {'slab'}, dimensions={1}, use_global_device_ids=true | all-gather | bytes 294912 | tf_op jit(solution)/shard_map/all_gather | solution.py:106
  64.6 5.3 %scatter_fusion = f32[192,4,128]{2,1,0:T(4,128)} fusion(f32[192,4,128]{2,1,0:T(4,128)} %broadcast_in_dim.34, s32[48]{0:T(128)S(1)} %fusion.11, f32[48,4,128]{2,1,0:T(4,128)} %pad_maximum_fusion.1), kind=kCustom, calls=%fused_computation.4 | custom fusion | bytes 295104 | tf_op jit(solution)/shard_map/scatter | solution.py:96
  69.9 9.5 %all-to-all-start.1 = ((f32[192,4,128]{2,1,0:T(4,128)}), f32[192,4,128]{2,1,0:T(4,128)S(1)}, u32[]{:S(2)}, u32[]{:S(2)}) async-start(f32[192,4,128]{2,1,0:T(4,128)} %scatter_fusion), calls=%async_computation.1 | async-start | bytes 786432 | tf_op jit(solution)/shard_map/all_to_all | solution.py:99
  82.0 22.4 %gather_fusion.1 = f32[6144,4]{1,0:T(8,128)S(1)} fusion(f32[4,16384]{0,1:T(8,128)} %all_gather.3, s32[6144]{0:T(1024)} %broadcast_clamp_fusion), kind=kCustom, calls=%fused_computation.1 | custom fusion | bytes 221184 | tf_op jit(solution)/shard_map/jit(_take)/gather | solution.py:111
  104.4 2.5 %copy.124 = f32[32,192,4]{0,1,2:T(8,128)} copy(f32[32,192,4]{2,1,0:T(8,128)S(1)} %bitcast.117) | data formatting | bytes 196608 | tf_op jit(solution)/shard_map/jit(_take)/gather | solution.py:111
  114.3 103.5 %while.10 = (s32[]{:T(128)}, f32[12,16,3,128]{3,1,0,2:T(8,128)S(1)}, s32[12,16,4]{1,2,0:T(4,128)S(1)}, f32[144,4,128]{2,1,0:T(4,128)S(1)}, f32[12,16,4,128]{3,2,1,0:T(4,128)S(1)}, /*index=5*/s32[]{:T(128)}) while((s32[]{:T(128)}, f32[12,16,3,128]{3,1,0,2:T(8,128)S(1)}, s32[12,16,4]{1,2,0:T(4,128)S(1)}, f32[144,4,128]{2,1,0:T(4,128)S(1)}, ...), condition=%wide.region_6.7_spmd, body=%wide.region_3.6_spmd.sunk | while | flops 19918016 | bytes 17537104 | solution.py:121
  115.2 3.5 %fusion.17 = f32[16,4,128,128]{3,2,1,0:T(8,128)S(1)} fusion(f32[16,3,128]{2,1,0:T(4,128)S(1)} %bitcast.112, f32[16,4,3,128]{3,2,1,0:T(4,128)S(1)} %bitcast.109), kind=kLoop, calls=%fused_computation.7.clone.1 | loop fusion | flops 8388608 | bytes 4317184 | tf_op jit(solution)/shard_map/while/body/eval_jaxpr/reduce_sum | solution.py:36
  120.4 2.5 %fusion.18 = f32[16,3,128]{2,1,0:T(4,128)S(1)} fusion(f32[16,4,128,128]{3,2,1,0:T(8,128)S(1)} %power_multiply_fusion.5, f32[16,3,128]{2,1,0:T(4,128)S(1)} %bitcast.113, f32[16,4,3,128]{3,2,1,0:T(4,128)S(1)} %bitcast.111), kind=kLoop, calls=%fused_computation.8.clone.1 | loop fusion | flops 9431040 | bytes 4341760 | tf_op jit(solution)/shard_map/while/body/eval_jaxpr/reduce_sum | solution.py:38
  123.8 3.5 %fusion.17 = f32[16,4,128,128]{3,2,1,0:T(8,128)S(1)} fusion(f32[16,3,128]{2,1,0:T(4,128)S(1)} %bitcast.112, f32[16,4,3,128]{3,2,1,0:T(4,128)S(1)} %bitcast.109), kind=kLoop, calls=%fused_computation.7.clone.1 | loop fusion | flops 8388608 | bytes 4317184 | tf_op jit(solution)/shard_map/while/body/eval_jaxpr/reduce_sum | solution.py:36
  129.0 2.5 %fusion.18 = f32[16,3,128]{2,1,0:T(4,128)S(1)} fusion(f32[16,4,128,128]{3,2,1,0:T(8,128)S(1)} %power_multiply_fusion.5, f32[16,3,128]{2,1,0:T(4,128)S(1)} %bitcast.113, f32[16,4,3,128]{3,2,1,0:T(4,128)S(1)} %bitcast.111), kind=kLoop, calls=%fused_computation.8.clone.1 | loop fusion | flops 9431040 | bytes 4341760 | tf_op jit(solution)/shard_map/while/body/eval_jaxpr/reduce_sum | solution.py:38
  132.5 3.5 %fusion.17 = f32[16,4,128,128]{3,2,1,0:T(8,128)S(1)} fusion(f32[16,3,128]{2,1,0:T(4,128)S(1)} %bitcast.112, f32[16,4,3,128]{3,2,1,0:T(4,128)S(1)} %bitcast.109), kind=kLoop, calls=%fused_computation.7.clone.1 | loop fusion | flops 8388608 | bytes 4317184 | tf_op jit(solution)/shard_map/while/body/eval_jaxpr/reduce_sum | solution.py:36
  141.1 3.5 %fusion.17 = f32[16,4,128,128]{3,2,1,0:T(8,128)S(1)} fusion(f32[16,3,128]{2,1,0:T(4,128)S(1)} %bitcast.112, f32[16,4,3,128]{3,2,1,0:T(4,128)S(1)} %bitcast.109), kind=kLoop, calls=%fused_computation.7.clone.1 | loop fusion | flops 8388608 | bytes 4317184 | tf_op jit(solution)/shard_map/while/body/eval_jaxpr/reduce_sum | solution.py:36
  149.7 3.5 %fusion.17 = f32[16,4,128,128]{3,2,1,0:T(8,128)S(1)} fusion(f32[16,3,128]{2,1,0:T(4,128)S(1)} %bitcast.112, f32[16,4,3,128]{3,2,1,0:T(4,128)S(1)} %bitcast.109), kind=kLoop, calls=%fused_computation.7.clone.1 | loop fusion | flops 8388608 | bytes 4317184 | tf_op jit(solution)/shard_map/while/body/eval_jaxpr/reduce_sum | solution.py:36
  158.3 3.5 %fusion.17 = f32[16,4,128,128]{3,2,1,0:T(8,128)S(1)} fusion(f32[16,3,128]{2,1,0:T(4,128)S(1)} %bitcast.112, f32[16,4,3,128]{3,2,1,0:T(4,128)S(1)} %bitcast.109), kind=kLoop, calls=%fused_computation.7.clone.1 | loop fusion | flops 8388608 | bytes 4317184 | tf_op jit(solution)/shard_map/while/body/eval_jaxpr/reduce_sum | solution.py:36
  167.0 3.5 %fusion.17 = f32[16,4,128,128]{3,2,1,0:T(8,128)S(1)} fusion(f32[16,3,128]{2,1,0:T(4,128)S(1)} %bitcast.112, f32[16,4,3,128]{3,2,1,0:T(4,128)S(1)} %bitcast.109), kind=kLoop, calls=%fused_computation.7.clone.1 | loop fusion | flops 8388608 | bytes 4317184 | tf_op jit(solution)/shard_map/while/body/eval_jaxpr/reduce_sum | solution.py:36
  175.6 3.5 %fusion.17 = f32[16,4,128,128]{3,2,1,0:T(8,128)S(1)} fusion(f32[16,3,128]{2,1,0:T(4,128)S(1)} %bitcast.112, f32[16,4,3,128]{3,2,1,0:T(4,128)S(1)} %bitcast.109), kind=kLoop, calls=%fused_computation.7.clone.1 | loop fusion | flops 8388608 | bytes 4317184 | tf_op jit(solution)/shard_map/while/body/eval_jaxpr/reduce_sum | solution.py:36
  184.2 3.5 %fusion.17 = f32[16,4,128,128]{3,2,1,0:T(8,128)S(1)} fusion(f32[16,3,128]{2,1,0:T(4,128)S(1)} %bitcast.112, f32[16,4,3,128]{3,2,1,0:T(4,128)S(1)} %bitcast.109), kind=kLoop, calls=%fused_computation.7.clone.1 | loop fusion | flops 8388608 | bytes 4317184 | tf_op jit(solution)/shard_map/while/body/eval_jaxpr/reduce_sum | solution.py:36
  192.8 3.5 %fusion.17 = f32[16,4,128,128]{3,2,1,0:T(8,128)S(1)} fusion(f32[16,3,128]{2,1,0:T(4,128)S(1)} %bitcast.112, f32[16,4,3,128]{3,2,1,0:T(4,128)S(1)} %bitcast.109), kind=kLoop, calls=%fused_computation.7.clone.1 | loop fusion | flops 8388608 | bytes 4317184 | tf_op jit(solution)/shard_map/while/body/eval_jaxpr/reduce_sum | solution.py:36
  201.5 3.5 %fusion.17 = f32[16,4,128,128]{3,2,1,0:T(8,128)S(1)} fusion(f32[16,3,128]{2,1,0:T(4,128)S(1)} %bitcast.112, f32[16,4,3,128]{3,2,1,0:T(4,128)S(1)} %bitcast.109), kind=kLoop, calls=%fused_computation.7.clone.1 | loop fusion | flops 8388608 | bytes 4317184 | tf_op jit(solution)/shard_map/while/body/eval_jaxpr/reduce_sum | solution.py:36
  210.1 3.5 %fusion.17 = f32[16,4,128,128]{3,2,1,0:T(8,128)S(1)} fusion(f32[16,3,128]{2,1,0:T(4,128)S(1)} %bitcast.112, f32[16,4,3,128]{3,2,1,0:T(4,128)S(1)} %bitcast.109), kind=kLoop, calls=%fused_computation.7.clone.1 | loop fusion | flops 8388608 | bytes 4317184 | tf_op jit(solution)/shard_map/while/body/eval_jaxpr/reduce_sum | solution.py:36
  219.1 9.2 %all-to-all-start.2 = ((f32[192,3,128]{2,1,0:T(4,128)}), f32[192,3,128]{2,1,0:T(4,128)S(1)}, u32[]{:S(2)}, u32[]{:S(2)}) async-start(f32[192,3,128]{2,1,0:T(4,128)} %copy.131), calls=%async_computation.2 | async-start | bytes 786432 | tf_op jit(solution)/shard_map/all_to_all | solution.py:131
  228.5 11.5 %all-to-all-done.2 = f32[192,3,128]{2,1,0:T(4,128)S(1)} async-done(((f32[192,3,128]{2,1,0:T(4,128)}), f32[192,3,128]{2,1,0:T(4,128)S(1)}, u32[]{:S(2)}, u32[]{:S(2)}) %all-to-all-start.2) | async-done | bytes 294944 | tf_op jit(solution)/shard_map/all_to_all | solution.py:131
  (178 shorter events, 78.7 us)
Async XLA Ops:
  0.9 0.9 copy-start.1
  1.8 0.7 copy-start.3
  2.5 107.6 %collective-permute-start = (f32[48,4,128]{2,1,0:T(4,128)}, f32[48,4,128]{2,1,0:T(4,128)}, u32[]{:S(2)}, u32[]{:S(2)}) collective-permute-start(f32[48,4,128]{2,1,0:T(4,128)} %pad_maximum_fusion.1), channel_id=1, source_target_pairs={{0,1},{1,2},{2,3},{3,4},{4,5},{5,6},{6,7},{7,8},{8,9},{9,10},{10,1... | collective-permute-start | bytes 294920 | tf_op jit(solution)/shard_map/ppermute | solution.py:19
  5.0 105.1 %collective-permute-start.1 = (f32[48,4,128]{2,1,0:T(4,128)}, f32[48,4,128]{2,1,0:T(4,128)}, u32[]{:S(2)}, u32[]{:S(2)}) collective-permute-start(f32[48,4,128]{2,1,0:T(4,128)} %pad_maximum_fusion.1), channel_id=1, source_target_pairs={{1,0},{2,1},{3,2},{4,3},{5,4},{6,5},{7,6},{8,7},{9,8},{10,9},{11,1... | collective-permute-start | bytes 294920 | tf_op jit(solution)/shard_map/ppermute | solution.py:22
  15.3 54.7 %all-to-all-start = ((s32[32,1,216]{2,1,0:T(1,128)}), s32[32,1,216]{2,1,0:T(1,128)S(1)}, u32[]{:S(2)}, u32[]{:S(2)}) async-start(s32[32,1,216]{2,1,0:T(1,128)} %reshape.299), calls=%async_computation | async-start | bytes 65536 | tf_op jit(solution)/shard_map/all_to_all | solution.py:100
  69.9 41.3 %all-to-all-start.1 = ((f32[192,4,128]{2,1,0:T(4,128)}), f32[192,4,128]{2,1,0:T(4,128)S(1)}, u32[]{:S(2)}, u32[]{:S(2)}) async-start(f32[192,4,128]{2,1,0:T(4,128)} %scatter_fusion), calls=%async_computation.1 | async-start | bytes 786432 | tf_op jit(solution)/shard_map/all_to_all | solution.py:99
  80.8 0.6 copy-start
  107.0 7.3 %copy-start.2 = (f32[12,16,3,128]{3,1,0,2:T(8,128)S(1)}, f32[12,16,3,128]{3,1,0,2:T(8,128)}, u32[]{:S(2)}) copy-start(f32[12,16,3,128]{3,1,0,2:T(8,128)} %custom-call.6) | copy-start | bytes 884740
  114.3 114.1 %copy-start.4 = (s32[1,1,48]{2,1,0:T(1,128)S(1)}, s32[1,1,48]{2,1,0:T(1,128)}, u32[]{:S(2)}) copy-start(s32[1,1,48]{2,1,0:T(1,128)} %param.12) | copy-start | bytes 580
  219.1 20.8 %all-to-all-start.2 = ((f32[192,3,128]{2,1,0:T(4,128)}), f32[192,3,128]{2,1,0:T(4,128)S(1)}, u32[]{:S(2)}, u32[]{:S(2)}) async-start(f32[192,3,128]{2,1,0:T(4,128)} %copy.131), calls=%async_computation.2 | async-start | bytes 786432 | tf_op jit(solution)/shard_map/all_to_all | solution.py:131
where the time goes:
time: 245 us; the launch traced here: 241 us
  other arithmetic  105 us (43%)
  local copies, waits for them, and re-layouts  48.9 us (20%)
  blocking collectives  41.5 us (17%)
  starting transfers between devices  33.4 us (14%)
  waiting for transfers between devices  11.5 us (5%)
    reduce_sum x12, other arithmetic, pair_block(): dist_sq = jnp.sum(rel * rel, axis=2) + soft_near  42.1 us
    all_gather x1, blocking collectives, per_device(): piece = lax.all_gather(cell_block, 'slab', axis=1, tiled=True)  41.5 us
    reduce_sum x12, other arithmetic, pair_block(): return jnp.sum(rel * weight[:, :, None], axis=(1, 4))  30.2 us
    gather x2, local copies, waits for them, and re-layouts, per_device(): fetched = jnp.take(piece, local, axis=1)  24.9 us
    mul x12, other arithmetic, pair_block(): weight = sources[:, :, 3][:, :, None, :] * dist_sq ** (-1.5)  19.5 us
    all_to_all x1, waiting for transfers between devices, per_device(): lax.all_to_all(results, 'space', split_axis=0, concat_axis=0, tiled=True)  11.5 us
    all_to_all x1, starting transfers between devices, per_device(): lax.all_to_all(send_pack, 'space', split_axis=0, concat_axis=0, tiled=True)  9.5 us
    all_to_all x1, starting transfers between devices, per_device(): lax.all_to_all(results, 'space', split_axis=0, concat_axis=0, tiled=True)  9.22 us
  transfers between devices with their start and end apart: 5, of which 1 were waited for; matrix products, arithmetic and copies ran while one was open for 18% of the time, Pallas kernels for 0%

commit v1 on v0

v1 whole, which is shorter than its diff:
```python
import jax
import jax.numpy as jnp
from jax import lax
from jax.experimental import pallas as pl
from jax.experimental.pallas import tpu as pltpu
from jax.sharding import PartitionSpec as P

NB = 48
PL = 128
K = 4
LC = 32
NY = 4
NZ = 8
NX = 4
SOFT = 0.01
F32 = jnp.float32
I32 = jnp.int32
BF16 = jnp.bfloat16
VMEM = pltpu.VMEM
SMEM = pltpu.SMEM


def vspec():
    return pl.BlockSpec(memory_space=VMEM)


def sspec():
    return pl.BlockSpec(memory_space=SMEM)


def column_of(row, n):
    square = jnp.broadcast_to(row, (n, n))
    diag = lax.broadcasted_iota(I32, (n, n), 0) == lax.broadcasted_iota(I32, (n, n), 1)
    return jnp.sum(jnp.where(diag, square, 0), axis=1, keepdims=True)


def pack_kernel(pos_ref, mass_ref, cnt_ref, dest_ref, near_ref, src_ref, tgt_ref):
    cnt = column_of(cnt_ref[...], NB)
    dest = column_of(dest_ref[...], NB)
    lane = lax.broadcasted_iota(I32, (NB, PL), 1)
    weight = jnp.where(lane < cnt, mass_ref[...], 0.0)
    near = near_ref[...]
    off = (near >= NB).astype(I32) + (near >= 2 * NB).astype(I32)
    dev = (dest + off - 1) & (NY * NZ - 1)
    code = (dev & (NZ - 1)) * NB + (near - off * NB)
    row = dev >> 3
    info = jnp.zeros((NB, PL), I32)
    for k in range(K):
        info = jnp.where(lane == k, code[:, k : k + 1], info)
        info = jnp.where(lane == 8 + k, row[:, k : k + 1], info)
    info = jnp.where(lane == 4, cnt, info)
    for y in range(NY):
        n = jnp.sum((row == y).astype(I32), axis=1, keepdims=True)
        info = jnp.where(lane == 12 + y, n, info)
    info = info.astype(F32)
    for c in range(3):
        value = pos_ref[:, c, :]
        tgt_ref[:, c, :] = value
        for z in range(NZ):
            src_ref[z, :, c, :] = value
    tgt_ref[:, 3, :] = info
    for z in range(NZ):
        src_ref[z, :, 3, :] = weight


def far_kernel(xc_ref, pos_ref, cnt_ref, list_ref, tab_ref, out_ref, pad):
    xs, cs = xc_ref[0], xc_ref[1]
    lane = lax.broadcasted_iota(I32, (NB, PL), 1)
    cnt = column_of(cnt_ref[...], NB)
    live = lane < cnt
    total = jnp.maximum(cnt, 1).astype(F32)
    pos = [pos_ref[:, c, :] for c in range(3)]
    centre = [jnp.sum(jnp.where(live, v, 0.0), axis=1, keepdims=True) / total for v in pos]
    block = jnp.zeros((NB, PL), F32)
    for c in range(3):
        block = jnp.where(lane == LC + c, centre[c], block)
    pad[...] = jnp.zeros((PL, PL), F32)
    pad[0:NB, :] = block
    pad[0:NB, 0:LC] = list_ref[...].astype(F32)
    turned = pad[...].T
    twice = turned + pltpu.roll(turned, 64, 1)
    half = lax.broadcasted_iota(I32, (1, PL), 1) < 64
    ids = [jnp.where(half, twice[2 * j : 2 * j + 1], twice[2 * j + 1 : 2 * j + 2]) for j in range(LC // 2)]
    ids = jnp.concatenate(ids, axis=0).astype(I32)
    ctr = [twice[LC + c : LC + c + 1] for c in range(3)]
    slab = ids >> 11
    dx = ((slab >> 1) - xs) & (NX - 1)
    order = jnp.where(dx == 3, 1, jnp.where(dx == 0, 0, dx + 1))
    rows = (order * 2 + ((slab & 1) ^ cs)) * 16 + ((ids >> 7) & 15)
    lanes = ids & (PL - 1)
    tables = []
    for c in range(4):
        whole = jnp.concatenate([tab_ref[o, i, c] for o in range(NX) for i in range(2)], axis=0)
        whole = whole.T
        high = whole.astype(BF16)
        low = (whole - high.astype(F32)).astype(BF16)
        tables.append(jnp.concatenate([high, low], axis=1))
    tables = jnp.concatenate(tables, axis=0)
    sub = lax.broadcasted_iota(I32, (PL, 2 * PL), 0)
    got = [[] for _ in range(4)]
    for j in range(0, LC // 2, 2):
        r2 = jnp.concatenate([rows[j : j + 1], rows[j + 1 : j + 2]], axis=1)
        l2 = jnp.concatenate([lanes[j : j + 1], lanes[j + 1 : j + 2]], axis=1)
        hot = jnp.where(sub == r2, 1.0, 0.0).astype(BF16)
        hot = jnp.concatenate([hot, hot], axis=0)
        found = jnp.dot(tables, hot, preferred_element_type=F32)
        pick = sub == l2
        for c in range(4):
            value = jnp.sum(jnp.where(pick, found[c * PL : (c + 1) * PL], 0.0), axis=0, keepdims=True)
            got[c] += [value[:, :PL], value[:, PL:]]
    cells = [jnp.concatenate(v, axis=0) for v in got]
    rel = [ctr[c] - cells[c] for c in range(3)]
    dist = rel[0] * rel[0] + rel[1] * rel[1] + rel[2] * rel[2] + 1.0
    inv = lax.rsqrt(dist)
    cube = cells[3] * (inv * inv * inv)
    fifth = 3.0 * cube * (inv * inv)
    terms = [-(cube * rel[c]) for c in range(3)]
    for a, b in ((0, 0), (1, 1), (2, 2), (0, 1), (0, 2), (1, 2)):
        value = fifth * rel[a] * rel[b]
        if a == b:
            value = value - cube
        terms.append(value)
    terms = [jnp.sum(v, axis=0, keepdims=True) for v in terms]
    pad[...] = jnp.zeros((PL, PL), F32)
    for i, v in enumerate(terms):
        pad[i : i + 1, :] = v + pltpu.roll(v, 64, 1)
    back = pad[...].T
    field = [back[0:NB, i : i + 1] for i in range(3)]
    tide = [back[0:NB, 3 + i : 4 + i] for i in range(6)]
    offset = [pos[c] - centre[c] for c in range(3)]
    for c, (i, j, k) in enumerate(((0, 3, 4), (3, 1, 5), (4, 5, 2))):
        out_ref[:, c, :] = field[c] + tide[i] * offset[0] + tide[j] * offset[1] + tide[k] * offset[2]


def near_kernel(info_ref, y_ref, t0, t1, t2, t3, src_ref, o0, o1, o2, o3, col, res):
    me = y_ref[0]
    lane8 = lax.broadcasted_iota(I32, (8, PL), 1)

    def groups_body(groups, picks, flags):
        srcs = [src_ref[p] for p in picks]
        rows = []
        for s, f in zip(srcs, flags):
            rows.append(
                (
                    jnp.broadcast_to(s[0:1], (8, PL)),
                    jnp.broadcast_to(s[1:2], (8, PL)),
                    jnp.broadcast_to(s[2:3], (8, PL)),
                    jnp.broadcast_to(s[3:4] * f, (8, PL)),
                )
            )
        for g in range(groups):
            part = col[8 * g : 8 * g + 8, :]
            tx, ty, tz = [jnp.broadcast_to(part[:, c : c + 1], (8, PL)) for c in range(3)]
            ax = ay = az = None
            for sx, sy, sz, w in rows:
                dx, dy, dz = sx - tx, sy - ty, sz - tz
                inv = lax.rsqrt(dx * dx + dy * dy + (dz * dz + SOFT))
                f = w * inv * (inv * inv)
                if ax is None:
                    ax, ay, az = f * dx, f * dy, f * dz
                else:
                    ax, ay, az = ax + f * dx, ay + f * dy, az + f * dz
            sums = [jnp.sum(v, axis=1, keepdims=True) for v in (ax, ay, az)]
            res[8 * g : 8 * g + 8, :] = jnp.where(lane8 == 0, sums[0], jnp.where(lane8 == 1, sums[1], sums[2]))

    for which, (t, o) in enumerate(((t0, o0), (t1, o1), (t2, o2), (t3, o3))):
        o[...] = jnp.zeros((NB, 3, PL), F32)

        def bucket(b, _, t=t, o=o, which=which):
            r = which * NB + b

            @pl.when(info_ref[r, 12 + me] > 0)
            def _():
                cnt = info_ref[r, 4]
                picks, flags = [], []
                for k in range(K):
                    picks.append(info_ref[r, k])
                    flags.append((info_ref[r, 8 + k] == me).astype(F32))
                tile = t[b]
                col[:, 0:8] = jnp.concatenate([tile, tile], axis=0).T
                for n in (4, 8, 12, 16):
                    @pl.when((cnt > 8 * (n - 4)) & (cnt <= 8 * n))
                    def _(n=n):
                        groups_body(n, picks, flags)
                o[b] = jnp.where(
                    lax.broadcasted_iota(I32, (3, PL), 1) < cnt, res[...].T[0:3], 0.0
                )

        lax.fori_loop(0, NB, bucket, None)


def ring(n, k):
    return [(i, (i + k) % n) for i in range(n)]


def along_y(k):
    return [(NZ * y + z, NZ * ((y + k) % NY) + z) for y in range(NY) for z in range(NZ)]


def along_x(k):
    return [(2 * x + c, 2 * ((x + k) % NX) + c) for x in range(NX) for c in range(2)]


def per_device(positions, masses, counts, dest_ids, near_list, cell_list, cell_centers, cell_mass):
    pos, cnt = positions[0], counts[0]
    src, tgt = pl.pallas_call(
        pack_kernel,
        out_shape=(
            jax.ShapeDtypeStruct((NZ, NB, 4, PL), F32),
            jax.ShapeDtypeStruct((NB, 4, PL), F32),
        ),
        in_specs=[vspec()] * 5,
        out_specs=[vspec()] * 2,
        name="pack",
    )(pos, masses[0], cnt, dest_ids, near_list[0])
    rows = [[NZ * y + z for z in range(NZ)] for y in range(NY)]
    window = lax.all_to_all(src, "space", 0, 0, axis_index_groups=rows, tiled=True)
    tgts = [tgt] + [lax.ppermute(tgt, "space", along_y(k)) for k in (1, -1, 2)]
    cells = jnp.concatenate([cell_centers, cell_mass[None]], axis=0).reshape(4, 16, PL)
    pair = jnp.stack([cells, lax.ppermute(cells, "slab", [(i, i ^ 1) for i in range(2 * NX)])])
    tab = jnp.stack([pair] + [lax.ppermute(pair, "slab", along_x(k)) for k in (1, -1, 2)])
    slab = lax.axis_index("slab")
    place = jnp.stack([slab >> 1, slab & 1]).astype(I32)
    far = pl.pallas_call(
        far_kernel,
        out_shape=jax.ShapeDtypeStruct((NB, 3, PL), F32),
        in_specs=[sspec()] + [vspec()] * 4,
        out_specs=vspec(),
        scratch_shapes=[pltpu.VMEM((PL, PL), F32)],
        name="far",
    )(place, pos, cnt, cell_list[0], tab)
    info = jnp.concatenate([t[:, 3, :16] for t in tgts], axis=0).astype(I32)
    me = (lax.axis_index("space") // NZ).astype(I32).reshape(1)
    parts = pl.pallas_call(
        near_kernel,
        out_shape=[jax.ShapeDtypeStruct((NB, 3, PL), F32)] * 4,
        in_specs=[sspec(), sspec()] + [vspec()] * 5,
        out_specs=[vspec()] * 4,
        scratch_shapes=[pltpu.VMEM((PL, PL), F32), pltpu.VMEM((PL, PL), F32)],
        name="near",
    )(info, me, *tgts, window.reshape(NZ * NB, 4, PL))
    back = [parts[0]] + [lax.ppermute(parts[1 + i], "space", along_y(-k)) for i, k in enumerate((1, -1, 2))]
    live = lax.broadcasted_iota(I32, (NB, 1, PL), 2) < cnt[0][:, None, None]
    out = jnp.where(live, far + ((back[0] + back[1]) + (back[2] + back[3])), 0.0)
    return out[None]


def solution(mesh):
    in_specs = (
        P("slab", "space", None, None),
        P("slab", "space", None),
        P("slab", "space", None),
        P("slab", "space"),
        P("slab", "space", None),
        P("slab", "space", None),
        P(None, "slab"),
        P("slab"),
    )
    return jax.shard_map(
        per_device,
        mesh=mesh,
        in_specs=in_specs,
        out_specs=P("slab", "space", None, None),
        check_vma=False,
    )
```

time: 245 us -> 140 us (0.57)
  the two profiles are of different devices: /device:TPU:1 before, /device:TPU:66 now
where the time goes in v1:
time: 140 us; the launch traced here: 139 us
  starting transfers between devices  73.2 us (52%)
  Pallas kernels  49.8 us (36%)
  local copies, waits for them, and re-layouts  8.07 us (6%)
  waiting for transfers between devices  4.93 us (4%)
  other arithmetic  3 us (2%)
    ppermute x3, starting transfers between devices, per_device(): lax.ppermute(parts[1 + i], 'space', along_y(-k))  54.2 us
    pallas_call x1, Pallas kernels, per_device(): pl.pallas_call(near_kernel, out_shape=[jax.ShapeDtypeStruct((NB, 3, PL),...  44.1 us
    all_to_all x1, starting transfers between devices, per_device(): lax.all_to_all(src, 'space', 0, 0, axis_index_groups=rows, tiled=True)  8.25 us
    unnamed x20, local copies, waits for them, and re-layouts  6.03 us
    ppermute x3, starting transfers between devices, per_device(): lax.ppermute(pair, 'slab', along_x(k))  5.44 us
    ppermute x3, starting transfers between devices, per_device(): tgts = [tgt] + [lax.ppermute(tgt, 'space', along_y(k)) for k in (1, -1, 2)]  5.3 us
    all_to_all x1, waiting for transfers between devices, per_device(): lax.all_to_all(src, 'space', 0, 0, axis_index_groups=rows, tiled=True)  4.9 us
    pallas_call x1, Pallas kernels, per_device(): pl.pallas_call(far_kernel, out_shape=jax.ShapeDtypeStruct((NB, 3, PL), F3...  3.26 us
  transfers between devices with their start and end apart: 11, of which 1 were waited for; matrix products, arithmetic and copies ran while one was open for 3% of the time, Pallas kernels for 34%

profile of v1, /device:TPU:66, one launch (start us, length us, event | category | flops | bytes accessed | tf_op | source)
XLA Modules:
  0.0 139.1 jit_solution(16876533381605016363)
XLA Ops:
  0.0 1.4 copy.29
  1.4 1.6 %copy.41 = f32[1,48,3,128]{3,2,1,0:T(4,128)} copy(f32[1,48,3,128]{3,1,2,0:T(8,128)} %param.8) | data formatting | bytes 147456 | tf_op args[0]
  2.9 2.5 %pack.1 = (f32[8,48,4,128]{3,2,1,0:T(4,128)}, f32[48,4,128]{2,1,0:T(4,128)}) custom-call(f32[48,3,128]{2,1,0:T(4,128)} %bitcast.38, f32[48,128]{1,0:T(8,128)} %bitcast.51, s32[1,48]{1,0:T(1,128)} %bitcast.52, s32[1,48]{1,0:T(1,128)} %dest_ref.1, s32[48,4]{1,0:T(8,128)} %bitcast.42), custom_call_target="tpu_custom_call" | custom-call | tf_op jit(solution)/shard_map/pack/pallas_call | solution.py:206
  5.5 8.2 %all-to-all-start = ((f32[8,48,4,128]{3,2,1,0:T(4,128)}), f32[8,48,4,128]{3,2,1,0:T(4,128)S(1)}, u32[]{:S(2)}, u32[]{:S(2)}) async-start(f32[8,48,4,128]{3,2,1,0:T(4,128)} %get-tuple-element.12), calls=%async_computation | async-start | bytes 1572864 | tf_op jit(solution)/shard_map/all_to_all | solution.py:217
  13.7 3.1 %collective-permute-start.5 = (f32[48,4,128]{2,0,1:T(8,128)S(1)}, f32[48,4,128]{2,0,1:T(8,128)S(1)}, u32[]{:S(2)}, u32[]{:S(2)}) collective-permute-start(f32[48,4,128]{2,0,1:T(8,128)S(1)} %copy.30), channel_id=1, source_target_pairs={{0,24},{1,25},{2,26},{3,27},{4,28},{5,29},{6,30},{7,31},{8,0},{9,1... | collective-permute-start | bytes 294920 | tf_op jit(solution)/shard_map/ppermute | solution.py:218
  16.8 2.2 %collective-permute-start.6 = (f32[48,4,128]{2,1,0:T(4,128)S(1)}, f32[48,4,128]{2,1,0:T(4,128)S(1)}, u32[]{:S(2)}, u32[]{:S(2)}) collective-permute-start(f32[48,4,128]{2,1,0:T(4,128)S(1)} %copy-done.1), channel_id=1, source_target_pairs={{0,16},{1,17},{2,18},{3,19},{4,20},{5,21},{6,22},{7,23},{8,24},{9,... | collective-permute-start | bytes 294920 | tf_op jit(solution)/shard_map/ppermute | solution.py:218
  19.0 0.7 copy-done.5
  19.7 0.7 copy-done.7
  21.2 0.7 copy.28
  22.5 1.5 %collective-permute-start.1 = (f32[2,4,16,128]{3,2,1,0:T(8,128)S(1)}, f32[2,4,16,128]{3,2,1,0:T(8,128)S(1)}, u32[]{:S(2)}, u32[]{:S(2)}) collective-permute-start(f32[2,4,16,128]{3,2,1,0:T(8,128)S(1)} %get-tuple-element.18), channel_id=1, source_target_pairs={{0,64},{32,96},{64,128},{96,160},{128,192},{160,224},{192,0},{224,... | collective-permute-start | bytes 196616 | tf_op jit(solution)/shard_map/ppermute | solution.py:221
  24.0 3.3 %collective-permute-start.3 = (f32[2,4,16,128]{3,2,1,0:T(8,128)S(1)}, f32[2,4,16,128]{3,2,1,0:T(8,128)S(1)}, u32[]{:S(2)}, u32[]{:S(2)}) collective-permute-start(f32[2,4,16,128]{3,2,1,0:T(8,128)S(1)} %get-tuple-element.18), channel_id=1, source_target_pairs={{0,128},{32,160},{64,192},{96,224},{128,0},{160,32},{192,64},{224,... | collective-permute-start | bytes 196616 | tf_op jit(solution)/shard_map/ppermute | solution.py:221
  27.3 0.7 copy.34.t2
  28.0 0.7 copy.33.t1
  28.8 0.7 maximum_convert_fusion.info_ref
  29.4 4.9 %all-to-all-done = f32[8,48,4,128]{3,2,1,0:T(4,128)S(1)} async-done(((f32[8,48,4,128]{3,2,1,0:T(4,128)}), f32[8,48,4,128]{3,2,1,0:T(4,128)S(1)}, u32[]{:S(2)}, u32[]{:S(2)}) %all-to-all-start) | async-done | bytes 786464 | tf_op jit(solution)/shard_map/all_to_all | solution.py:217
  34.3 0.9 copy-done
  35.2 44.1 %near.1 = (f32[48,3,128]{2,1,0:T(4,128)}, f32[48,3,128]{2,1,0:T(4,128)}, f32[48,3,128]{2,1,0:T(4,128)}, f32[48,3,128]{2,1,0:T(4,128)}) custom-call(s32[192,16]{1,0:T(8,128)} %maximum_convert_fusion.info_ref, s32[1]{0:T(128)} %bitcast.19.y_ref, f32[48,4,128]{2,1,0:T(4,128)} %get-tuple-element.11.t0, f32[48,4,128]{2,1,0:T(4,128)} %copy.33.t1, ...), custom_call_target="tpu_custom_call" | custom-call | tf_op jit(solution)/shard_map/near/pallas_call | solution.py:234
  79.3 19.2 %collective-permute-start.7 = (f32[48,3,128]{2,1,0:T(4,128)}, f32[48,3,128]{2,1,0:T(4,128)S(1)}, u32[]{:S(2)}, u32[]{:S(2)}) collective-permute-start(f32[48,3,128]{2,1,0:T(4,128)} %get-tuple-element.14), channel_id=1, source_target_pairs={{0,24},{1,25},{2,26},{3,27},{4,28},{5,29},{6,30},{7,31},{8,0},{9,1... | collective-permute-start | bytes 221192 | tf_op jit(solution)/shard_map/ppermute | solution.py:242
  98.5 7.4 %collective-permute-start.8 = (f32[48,3,128]{2,1,0:T(4,128)}, f32[48,3,128]{2,1,0:T(4,128)S(1)}, u32[]{:S(2)}, u32[]{:S(2)}) collective-permute-start(f32[48,3,128]{2,1,0:T(4,128)} %get-tuple-element.15), channel_id=1, source_target_pairs={{0,8},{1,9},{2,10},{3,11},{4,12},{5,13},{6,14},{7,15},{8,16},{9,17... | collective-permute-start | bytes 221192 | tf_op jit(solution)/shard_map/ppermute | solution.py:242
  105.9 27.6 %collective-permute-start.9 = (f32[48,3,128]{2,1,0:T(4,128)}, f32[48,3,128]{2,1,0:T(4,128)S(1)}, u32[]{:S(2)}, u32[]{:S(2)}) collective-permute-start(f32[48,3,128]{2,1,0:T(4,128)} %get-tuple-element.16), channel_id=1, source_target_pairs={{0,16},{1,17},{2,18},{3,19},{4,20},{5,21},{6,22},{7,23},{8,24},{9,... | collective-permute-start | bytes 221192 | tf_op jit(solution)/shard_map/ppermute | solution.py:242
  133.5 0.7 pad_maximum_fusion.tab_ref
  134.2 3.3 %far.1 = f32[48,3,128]{2,1,0:T(4,128)} custom-call(s32[2]{0:T(128)} %pad_add_fusion.xc_ref, f32[48,3,128]{2,1,0:T(4,128)} %bitcast.39, s32[1,48]{1,0:T(1,128)} %bitcast.53, s32[48,32]{1,0:T(8,128)} %bitcast.43, f32[4,2,4,16,128]{4,3,2,1,0:T(8,128)} %pad_maximum_fusion.tab_ref), custom_call_target="tpu_custom_call" | custom-call | tf_op jit(solution)/shard_map/far/pallas_call | solution.py:224
  137.5 1.0 select_bitcast_fusion
  138.5 0.6 copy.35
  (36 shorter events, 1.5 us)
Async XLA Ops:
  5.5 8.3 %copy-start.1 = (f32[48,4,128]{2,1,0:T(4,128)S(1)}, f32[48,4,128]{2,1,0:T(4,128)}, u32[]{:S(2)}) copy-start(f32[48,4,128]{2,1,0:T(4,128)} %get-tuple-element.11.t0) | copy-start | bytes 294916
  5.5 28.9 %all-to-all-start = ((f32[8,48,4,128]{3,2,1,0:T(4,128)}), f32[8,48,4,128]{3,2,1,0:T(4,128)S(1)}, u32[]{:S(2)}, u32[]{:S(2)}) async-start(f32[8,48,4,128]{3,2,1,0:T(4,128)} %get-tuple-element.12), calls=%async_computation | async-start | bytes 1572864 | tf_op jit(solution)/shard_map/all_to_all | solution.py:217
  13.7 5.3 %copy-start.4 = (f32[3,2048]{1,0:T(4,128)S(1)}, f32[3,2048]{1,0:T(4,128)}, u32[]{:S(2)}) copy-start(f32[3,2048]{1,0:T(4,128)} %param.14) | copy-start | bytes 73732
  13.7 10.3 %collective-permute-start.5 = (f32[48,4,128]{2,0,1:T(8,128)S(1)}, f32[48,4,128]{2,0,1:T(8,128)S(1)}, u32[]{:S(2)}, u32[]{:S(2)}) collective-permute-start(f32[48,4,128]{2,0,1:T(8,128)S(1)} %copy.30), channel_id=1, source_target_pairs={{0,24},{1,25},{2,26},{3,27},{4,28},{5,29},{6,30},{7,31},{8,0},{9,1... | collective-permute-start | bytes 294920 | tf_op jit(solution)/shard_map/ppermute | solution.py:218
  16.8 11.2 %collective-permute-start.4 = (f32[48,4,128]{2,0,1:T(8,128)S(1)}, f32[48,4,128]{2,0,1:T(8,128)S(1)}, u32[]{:S(2)}, u32[]{:S(2)}) collective-permute-start(f32[48,4,128]{2,0,1:T(8,128)S(1)} %copy.30), channel_id=1, source_target_pairs={{0,8},{1,9},{2,10},{3,11},{4,12},{5,13},{6,14},{7,15},{8,16},{9,17... | collective-permute-start | bytes 294920 | tf_op jit(solution)/shard_map/ppermute | solution.py:218
  16.8 11.9 %collective-permute-start.6 = (f32[48,4,128]{2,1,0:T(4,128)S(1)}, f32[48,4,128]{2,1,0:T(4,128)S(1)}, u32[]{:S(2)}, u32[]{:S(2)}) collective-permute-start(f32[48,4,128]{2,1,0:T(4,128)S(1)} %copy-done.1), channel_id=1, source_target_pairs={{0,16},{1,17},{2,18},{3,19},{4,20},{5,21},{6,22},{7,23},{8,24},{9,... | collective-permute-start | bytes 294920 | tf_op jit(solution)/shard_map/ppermute | solution.py:218
  19.0 0.7 copy-start.5
  19.7 2.2 %collective-permute-start = (f32[4,16,128]{2,1,0:T(8,128)S(1)}, f32[4,16,128]{2,1,0:T(8,128)S(1)}, u32[]{:S(2)}, u32[]{:S(2)}) collective-permute-start(f32[4,16,128]{2,1,0:T(8,128)S(1)} %pad_maximum_fusion.2), channel_id=1, source_target_pairs={{0,32},{32,0},{64,96},{96,64},{128,160},{160,128},{192,224},{224,1... | collective-permute-start | bytes 98312 | tf_op jit(solution)/shard_map/ppermute | solution.py:220
  19.7 0.7 copy-start.7
  20.5 0.7 copy-start.6
  21.9 84.0 %collective-permute-start.2 = (f32[2,4,16,128]{3,2,1,0:T(8,128)S(1)}, f32[2,4,16,128]{3,2,1,0:T(8,128)S(1)}, u32[]{:S(2)}, u32[]{:S(2)}) collective-permute-start(f32[2,4,16,128]{3,2,1,0:T(8,128)S(1)} %get-tuple-element.18), channel_id=1, source_target_pairs={{0,192},{32,224},{64,0},{96,32},{128,64},{160,96},{192,128},{224,1... | collective-permute-start | bytes 196616 | tf_op jit(solution)/shard_map/ppermute | solution.py:221
  22.5 111.0 %collective-permute-start.1 = (f32[2,4,16,128]{3,2,1,0:T(8,128)S(1)}, f32[2,4,16,128]{3,2,1,0:T(8,128)S(1)}, u32[]{:S(2)}, u32[]{:S(2)}) collective-permute-start(f32[2,4,16,128]{3,2,1,0:T(8,128)S(1)} %get-tuple-element.18), channel_id=1, source_target_pairs={{0,64},{32,96},{64,128},{96,160},{128,192},{160,224},{192,0},{224,... | collective-permute-start | bytes 196616 | tf_op jit(solution)/shard_map/ppermute | solution.py:221
  24.0 109.5 %collective-permute-start.3 = (f32[2,4,16,128]{3,2,1,0:T(8,128)S(1)}, f32[2,4,16,128]{3,2,1,0:T(8,128)S(1)}, u32[]{:S(2)}, u32[]{:S(2)}) collective-permute-start(f32[2,4,16,128]{3,2,1,0:T(8,128)S(1)} %get-tuple-element.18), channel_id=1, source_target_pairs={{0,128},{32,160},{64,192},{96,224},{128,0},{160,32},{192,64},{224,... | collective-permute-start | bytes 196616 | tf_op jit(solution)/shard_map/ppermute | solution.py:221
  28.7 0.7 copy-start.2
  34.3 0.9 copy-start
  79.3 58.2 %collective-permute-start.7 = (f32[48,3,128]{2,1,0:T(4,128)}, f32[48,3,128]{2,1,0:T(4,128)S(1)}, u32[]{:S(2)}, u32[]{:S(2)}) collective-permute-start(f32[48,3,128]{2,1,0:T(4,128)} %get-tuple-element.14), channel_id=1, source_target_pairs={{0,24},{1,25},{2,26},{3,27},{4,28},{5,29},{6,30},{7,31},{8,0},{9,1... | collective-permute-start | bytes 221192 | tf_op jit(solution)/shard_map/ppermute | solution.py:242
  98.5 38.9 %collective-permute-start.8 = (f32[48,3,128]{2,1,0:T(4,128)}, f32[48,3,128]{2,1,0:T(4,128)S(1)}, u32[]{:S(2)}, u32[]{:S(2)}) collective-permute-start(f32[48,3,128]{2,1,0:T(4,128)} %get-tuple-element.15), channel_id=1, source_target_pairs={{0,8},{1,9},{2,10},{3,11},{4,12},{5,13},{6,14},{7,15},{8,16},{9,17... | collective-permute-start | bytes 221192 | tf_op jit(solution)/shard_map/ppermute | solution.py:242
  105.9 31.6 %collective-permute-start.9 = (f32[48,3,128]{2,1,0:T(4,128)}, f32[48,3,128]{2,1,0:T(4,128)S(1)}, u32[]{:S(2)}, u32[]{:S(2)}) collective-permute-start(f32[48,3,128]{2,1,0:T(4,128)} %get-tuple-element.16), channel_id=1, source_target_pairs={{0,16},{1,17},{2,18},{3,19},{4,20},{5,21},{6,22},{7,23},{8,24},{9,... | collective-permute-start | bytes 221192 | tf_op jit(solution)/shard_map/ppermute | solution.py:242
  134.2 3.3 %copy-start.3 = (f32[48,3,128]{2,1,0:T(4,128)S(1)}, f32[48,3,128]{2,1,0:T(4,128)}, u32[]{:S(2)}) copy-start(f32[48,3,128]{2,1,0:T(4,128)} %get-tuple-element.13) | copy-start | bytes 221188

commit v2 on v1

--- a/solution.py
+++ b/solution.py
@@ -13,6 +13,8 @@
 NZ = 8
 NX = 4
 SOFT = 0.01
+UNROLL = 4
+LIST = 256
 F32 = jnp.float32
 I32 = jnp.int32
 BF16 = jnp.bfloat16
@@ -132,61 +134,77 @@
         out_ref[:, c, :] = field[c] + tide[i] * offset[0] + tide[j] * offset[1] + tide[k] * offset[2]
 
 
-def near_kernel(info_ref, y_ref, t0, t1, t2, t3, src_ref, o0, o1, o2, o3, col, res):
+def split3(v):
+    high = v.astype(BF16).astype(F32)
+    rest = v - high
+    mid = rest.astype(BF16).astype(F32)
+    return high, mid, rest - mid
+
+
+def prep_kernel(info_ref, y_ref, t0, t1, t2, t3, tall, lst):
     me = y_ref[0]
-    lane8 = lax.broadcasted_iota(I32, (8, PL), 1)
-
-    def groups_body(groups, picks, flags):
-        srcs = [src_ref[p] for p in picks]
-        rows = []
-        for s, f in zip(srcs, flags):
-            rows.append(
-                (
-                    jnp.broadcast_to(s[0:1], (8, PL)),
-                    jnp.broadcast_to(s[1:2], (8, PL)),
-                    jnp.broadcast_to(s[2:3], (8, PL)),
-                    jnp.broadcast_to(s[3:4] * f, (8, PL)),
-                )
-            )
-        for g in range(groups):
-            part = col[8 * g : 8 * g + 8, :]
-            tx, ty, tz = [jnp.broadcast_to(part[:, c : c + 1], (8, PL)) for c in range(3)]
-            ax = ay = az = None
-            for sx, sy, sz, w in rows:
-                dx, dy, dz = sx - tx, sy - ty, sz - tz
-                inv = lax.rsqrt(dx * dx + dy * dy + (dz * dz + SOFT))
-                f = w * inv * (inv * inv)
-                if ax is None:
-                    ax, ay, az = f * dx, f * dy, f * dz
-                else:
-                    ax, ay, az = ax + f * dx, ay + f * dy, az + f * dz
-            sums = [jnp.sum(v, axis=1, keepdims=True) for v in (ax, ay, az)]
-            res[8 * g : 8 * g + 8, :] = jnp.where(lane8 == 0, sums[0], jnp.where(lane8 == 1, sums[1], sums[2]))
-
-    for which, (t, o) in enumerate(((t0, o0), (t1, o1), (t2, o2), (t3, o3))):
-        o[...] = jnp.zeros((NB, 3, PL), F32)
-
-        def bucket(b, _, t=t, o=o, which=which):
-            r = which * NB + b
-
-            @pl.when(info_ref[r, 12 + me] > 0)
-            def _():
-                cnt = info_ref[r, 4]
-                picks, flags = [], []
-                for k in range(K):
-                    picks.append(info_ref[r, k])
-                    flags.append((info_ref[r, 8 + k] == me).astype(F32))
-                tile = t[b]
-                col[:, 0:8] = jnp.concatenate([tile, tile], axis=0).T
-                for n in (4, 8, 12, 16):
-                    @pl.when((cnt > 8 * (n - 4)) & (cnt <= 8 * n))
-                    def _(n=n):
-                        groups_body(n, picks, flags)
-                o[b] = jnp.where(
-                    lax.broadcasted_iota(I32, (3, PL), 1) < cnt, res[...].T[0:3], 0.0
-                )
-
-        lax.fori_loop(0, NB, bucket, None)
+    for i, t in enumerate((t0, t1, t2, t3)):
+        tall[i * NB : (i + 1) * NB] = t[...]
+
+    def scan(r, n):
+        lst[n] = r
+        return n + (info_ref[r, 12 + me] > 0).astype(I32)
+
+    lst[LIST - 1] = lax.fori_loop(0, NY * NB, scan, jnp.int32(0), unroll=8)
+
+
+def near_kernel(info_ref, y_ref, lst, tall, src_ref, o0, o1, o2, o3, oall):
+    me = y_ref[0]
+    n = lst[LIST - 1]
+    oall[...] = jnp.zeros((NY * NB, 4, PL), F32)
+    sub4 = lax.broadcasted_iota(I32, (4, PL), 0)
+    lane4 = lax.broadcasted_iota(I32, (4, PL), 1)
+    spatial = sub4 < 3
+    one = jnp.ones((4, PL), F32)
+    zero4 = jnp.zeros((4, PL), F32)
+    zero8 = jnp.zeros((8, PL), F32)
+
+    def square(v):
+        return jnp.sum(jnp.where(spatial, v * v, 0.0), axis=0, keepdims=True)
+
+    def mix(a, b):
+        return jnp.where(spatial, a, b)
+
+    def stack(*v):
+        return jnp.concatenate(v, axis=0).astype(BF16)
+
+    def job(r):
+        t = tall[r]
+        th, tm, tl = split3(t)
+        qh, qm, ql = split3(square(t))
+        u = stack(mix(th, one), mix(th, one), mix(tm, one), mix(tm, qh), mix(th, qm), mix(tl, ql), zero8)
+        vs, gs = [], []
+        for k in range(K):
+            s = src_ref[info_ref[r, k]]
+            flag = (info_ref[r, 8 + k] == me).astype(F32)
+            sh, sm, sl = split3(-2.0 * s)
+            qh, qm, ql = split3(square(s) + SOFT)
+            vs.append(stack(mix(sh, qh), mix(sm, qm), mix(sh, ql), mix(sm, one), mix(sl, one), mix(sh, one), zero8))
+            w = s[3:4] * flag
+            gs.append(stack(*split3(mix(s * w, w)), zero4))
+        v = jnp.concatenate(vs, axis=1)
+        g = jnp.concatenate(gs, axis=1)
+        dist = lax.dot_general(v, u, (((0,), (0,)), ((), ())), preferred_element_type=F32)
+        inv = lax.rsqrt(dist)
+        f = inv * inv * inv
+        high = f.astype(BF16)
+        low = (f - high.astype(F32)).astype(BF16)
+        o = jnp.dot(g, high, preferred_element_type=F32) + jnp.dot(g, low, preferred_element_type=F32)
+        a = o[0:4] + o[4:8] + o[8:12]
+        oall[r] = jnp.where(lane4 < info_ref[r, 4], a - t * a[3:4], 0.0)
+
+    def step(i, _):
+        for j in range(UNROLL):
+            job(lst[jnp.minimum(UNROLL * i + j, n - 1)])
+
+    lax.fori_loop(0, (n + UNROLL - 1) // UNROLL, step, None)
+    for i, o in enumerate((o0, o1, o2, o3)):
+        o[...] = oall[i * NB : (i + 1) * NB, 0:3, :]
 
 
 def ring(n, k):
@@ -231,14 +249,25 @@
     )(place, pos, cnt, cell_list[0], tab)
     info = jnp.concatenate([t[:, 3, :16] for t in tgts], axis=0).astype(I32)
     me = (lax.axis_index("space") // NZ).astype(I32).reshape(1)
+    tall, lst = pl.pallas_call(
+        prep_kernel,
+        out_shape=(
+            jax.ShapeDtypeStruct((NY * NB, 4, PL), F32),
+            jax.ShapeDtypeStruct((LIST,), I32),
+        ),
+        in_specs=[sspec(), sspec()] + [vspec()] * 4,
+        out_specs=[vspec(), sspec()],
+        name="prep",
+    )(info, me, *tgts)
+    far, tall = lax.optimization_barrier((far, tall))
     parts = pl.pallas_call(
         near_kernel,
         out_shape=[jax.ShapeDtypeStruct((NB, 3, PL), F32)] * 4,
-        in_specs=[sspec(), sspec()] + [vspec()] * 5,
+        in_specs=[sspec()] * 3 + [vspec()] * 2,
         out_specs=[vspec()] * 4,
-        scratch_shapes=[pltpu.VMEM((PL, PL), F32), pltpu.VMEM((PL, PL), F32)],
+        scratch_shapes=[pltpu.VMEM((NY * NB, 4, PL), F32)],
         name="near",
-    )(info, me, *tgts, window.reshape(NZ * NB, 4, PL))
+    )(info, me, lst, tall, window.reshape(NZ * NB, 4, PL))
     back = [parts[0]] + [lax.ppermute(parts[1 + i], "space", along_y(-k)) for i, k in enumerate((1, -1, 2))]
     live = lax.broadcasted_iota(I32, (NB, 1, PL), 2) < cnt[0][:, None, None]
     out = jnp.where(live, far + ((back[0] + back[1]) + (back[2] + back[3])), 0.0)

time: 140 us -> 69.2 us (0.49)
  the two profiles are of different devices: /device:TPU:66 before, /device:TPU:6 now
where the time goes in v2:
time: 69.2 us; the launch traced here: 68.1 us
  Pallas kernels  23.9 us (35%)
  starting transfers between devices  21 us (30%)
  waiting for transfers between devices  10.6 us (15%)
  local copies, waits for them, and re-layouts  9.45 us (14%)
  other arithmetic  3.06 us (4%)
    pallas_call x1, Pallas kernels, per_device(): pl.pallas_call(near_kernel, out_shape=[jax.ShapeDtypeStruct((NB, 3, PL),...  14.3 us
    all_to_all x1, starting transfers between devices, per_device(): lax.all_to_all(src, 'space', 0, 0, axis_index_groups=rows, tiled=True)  8.6 us
    unnamed x16, local copies, waits for them, and re-layouts  5.89 us
    ppermute x3, waiting for transfers between devices, per_device(): lax.ppermute(parts[1 + i], 'space', along_y(-k))  5.83 us
    ppermute x3, starting transfers between devices, per_device(): tgts = [tgt] + [lax.ppermute(tgt, 'space', along_y(k)) for k in (1, -1, 2)]  5.22 us
    ppermute x3, waiting for transfers between devices, per_device(): lax.ppermute(pair, 'slab', along_x(k))  3.96 us
    pallas_call x1, Pallas kernels, per_device(): pl.pallas_call(prep_kernel, out_shape=(jax.ShapeDtypeStruct((NY * NB, 4,...  3.86 us
    ppermute x3, starting transfers between devices, per_device(): lax.ppermute(parts[1 + i], 'space', along_y(-k))  3.71 us
  transfers between devices with their start and end apart: 11, of which 6 were waited for; matrix products, arithmetic and copies ran while one was open for 7% of the time, Pallas kernels for 10%

profile of v2, /device:TPU:6, one launch (start us, length us, event | category | flops | bytes accessed | tf_op | source)
XLA Modules:
  0.0 68.1 jit_solution(1835863754451007090)
XLA Ops:
  0.0 1.4 %copy.31 = s32[1,48,4]{2,1,0:T(8,128)} copy(s32[1,48,4]{1,2,0:T(4,128)} %param.12) | data formatting | bytes 1536 | tf_op args[4]
  1.4 1.6 %copy.45 = f32[1,48,3,128]{3,2,1,0:T(4,128)} copy(f32[1,48,3,128]{3,1,2,0:T(8,128)} %param.8) | data formatting | bytes 147456 | tf_op args[0]
  2.9 2.5 %pack.1 = (f32[8,48,4,128]{3,2,1,0:T(4,128)}, f32[48,4,128]{2,1,0:T(4,128)}) custom-call(f32[48,3,128]{2,1,0:T(4,128)} %bitcast.39, f32[48,128]{1,0:T(8,128)} %bitcast.51, s32[1,48]{1,0:T(1,128)} %bitcast.52, s32[1,48]{1,0:T(1,128)} %dest_ref.1, s32[48,4]{1,0:T(8,128)} %bitcast.42), custom_call_target="tpu_custom_call" | custom-call | tf_op jit(solution)/shard_map/pack/pallas_call | solution.py:224
  5.4 0.9 %copy.32 = f32[48,4,128]{2,0,1:T(8,128)S(1)} copy(f32[48,4,128]{2,1,0:T(4,128)} %get-tuple-element.15.t0) | data formatting | bytes 196608 | tf_op jit(solution)/shard_map/pack/pallas_call | solution.py:224
  6.3 3.2 %collective-permute-start.6 = (f32[48,4,128]{2,0,1:T(8,128)S(1)}, f32[48,4,128]{2,0,1:T(8,128)S(1)}, u32[]{:S(2)}, u32[]{:S(2)}) collective-permute-start(f32[48,4,128]{2,0,1:T(8,128)S(1)} %copy.32), channel_id=1, source_target_pairs={{0,16},{1,17},{2,18},{3,19},{4,20},{5,21},{6,22},{7,23},{8,24},{9,... | collective-permute-start | bytes 294920 | tf_op jit(solution)/shard_map/ppermute | solution.py:236
  9.5 1.1 %collective-permute-start.5 = (f32[48,4,128]{2,0,1:T(8,128)S(1)}, f32[48,4,128]{2,0,1:T(8,128)S(1)}, u32[]{:S(2)}, u32[]{:S(2)}) collective-permute-start(f32[48,4,128]{2,0,1:T(8,128)S(1)} %copy.32), channel_id=1, source_target_pairs={{0,24},{1,25},{2,26},{3,27},{4,28},{5,29},{6,30},{7,31},{8,0},{9,1... | collective-permute-start | bytes 294920 | tf_op jit(solution)/shard_map/ppermute | solution.py:236
  10.6 8.6 %all-to-all-start = ((f32[8,48,4,128]{3,2,1,0:T(4,128)}), f32[8,48,4,128]{3,2,1,0:T(4,128)S(1)}, u32[]{:S(2)}, u32[]{:S(2)}) async-start(f32[8,48,4,128]{3,2,1,0:T(4,128)} %get-tuple-element.20), calls=%async_computation | async-start | bytes 1572864 | tf_op jit(solution)/shard_map/all_to_all | solution.py:235
  21.3 0.9 %collective-permute-start.2 = (f32[2,4,16,128]{3,2,1,0:T(8,128)S(1)}, f32[2,4,16,128]{3,2,1,0:T(8,128)S(1)}, u32[]{:S(2)}, u32[]{:S(2)}) collective-permute-start(f32[2,4,16,128]{3,2,1,0:T(8,128)S(1)} %get-tuple-element.26), channel_id=1, source_target_pairs={{0,192},{32,224},{64,0},{96,32},{128,64},{160,96},{192,128},{224,1... | collective-permute-start | bytes 196616 | tf_op jit(solution)/shard_map/ppermute | solution.py:239
  22.2 2.4 %collective-permute-start.1 = (f32[2,4,16,128]{3,2,1,0:T(8,128)S(1)}, f32[2,4,16,128]{3,2,1,0:T(8,128)S(1)}, u32[]{:S(2)}, u32[]{:S(2)}) collective-permute-start(f32[2,4,16,128]{3,2,1,0:T(8,128)S(1)} %get-tuple-element.26), channel_id=1, source_target_pairs={{0,64},{32,96},{64,128},{96,160},{128,192},{160,224},{192,0},{224,... | collective-permute-start | bytes 196616 | tf_op jit(solution)/shard_map/ppermute | solution.py:239
  25.5 1.6 %collective-permute-done.2 = f32[2,4,16,128]{3,2,1,0:T(8,128)S(1)} collective-permute-done((f32[2,4,16,128]{3,2,1,0:T(8,128)S(1)}, f32[2,4,16,128]{3,2,1,0:T(8,128)S(1)}, u32[]{:S(2)}, u32[]{:S(2)}) %collective-permute-start.2) | collective-permute-done | bytes 65568 | tf_op jit(solution)/shard_map/ppermute | solution.py:239
  27.1 1.0 %collective-permute-start.4 = (f32[48,4,128]{2,0,1:T(8,128)S(1)}, f32[48,4,128]{2,0,1:T(8,128)S(1)}, u32[]{:S(2)}, u32[]{:S(2)}) collective-permute-start(f32[48,4,128]{2,0,1:T(8,128)S(1)} %copy.32), channel_id=1, source_target_pairs={{0,8},{1,9},{2,10},{3,11},{4,12},{5,13},{6,14},{7,15},{8,16},{9,17... | collective-permute-start | bytes 294920 | tf_op jit(solution)/shard_map/ppermute | solution.py:236
  28.1 2.3 %collective-permute-done.3 = f32[2,4,16,128]{3,2,1,0:T(8,128)S(1)} collective-permute-done((f32[2,4,16,128]{3,2,1,0:T(8,128)S(1)}, f32[2,4,16,128]{3,2,1,0:T(8,128)S(1)}, u32[]{:S(2)}, u32[]{:S(2)}) %collective-permute-start.3) | collective-permute-done | bytes 65568 | tf_op jit(solution)/shard_map/ppermute | solution.py:239
  30.4 0.7 %pad_maximum_fusion.tab_ref = f32[4,2,4,16,128]{4,3,2,1,0:T(8,128)} fusion(f32[1,2,4,16,128]{4,3,2,1,0:T(8,128)S(1)} %bitcast.46, f32[1,2,4,16,128]{4,3,2,1,0:T(8,128)S(1)} %bitcast.44, f32[1,2,4,16,128]{4,3,2,1,0:T(8,128)S(1)} %bitcast.45, f32[1,2,4,16,128]{4,3,2,1,0:T(8,128)S(1)} %get-tuple-element.25), kind=kLoop, calls=%fused_computation | loop fusion | flops 196608 | bytes 524288 | tf_op jit(solution)/shard_map/stack | solution.py:239
  31.1 3.2 %far.1 = f32[48,3,128]{2,1,0:T(4,128)} custom-call(s32[2]{0:T(128)} %pad_add_fusion.xc_ref, f32[48,3,128]{2,1,0:T(4,128)} %bitcast.40, s32[1,48]{1,0:T(1,128)} %bitcast.53, s32[48,32]{1,0:T(8,128)} %bitcast.43, f32[4,2,4,16,128]{4,3,2,1,0:T(8,128)} %pad_maximum_fusion.tab_ref), custom_call_target="tpu_custom_call" | custom-call | tf_op jit(solution)/shard_map/far/pallas_call | solution.py:242
  37.0 3.9 %prep.1 = (f32[192,4,128]{2,1,0:T(4,128)}, s32[256]{0:T(256)}) custom-call(s32[192,16]{1,0:T(8,128)} %maximum_convert_fusion.info_ref, s32[1]{0:T(128)} %bitcast.19.y_ref, f32[48,4,128]{2,1,0:T(4,128)} %get-tuple-element.15.t0, f32[48,4,128]{2,1,0:T(4,128)} %copy.36.t1, f32[48,4,128]{2,1,0:T(4,128)} %copy.37.t2, f32[48,4,128]{2,1,0:T(4,128)} %copy.38.t3), custom_call_target="tpu_custom_call" | custom-call | tf_op jit(solution)/shard_map/prep/pallas_call | solution.py:252
  40.9 0.8 %all-to-all-done = f32[8,48,4,128]{3,2,1,0:T(4,128)S(1)} async-done(((f32[8,48,4,128]{3,2,1,0:T(4,128)}), f32[8,48,4,128]{3,2,1,0:T(4,128)S(1)}, u32[]{:S(2)}, u32[]{:S(2)}) %all-to-all-start) | async-done | bytes 786464 | tf_op jit(solution)/shard_map/all_to_all | solution.py:235
  41.7 0.9 %copy-done = f32[8,48,4,128]{3,2,1,0:T(4,128)} copy-done((f32[8,48,4,128]{3,2,1,0:T(4,128)}, f32[8,48,4,128]{3,2,1,0:T(4,128)S(1)}, u32[]{:S(2)}) %copy-start) | copy-done | bytes 786456
  42.6 14.3 %near.1 = (f32[48,3,128]{2,1,0:T(4,128)}, f32[48,3,128]{2,1,0:T(4,128)}, f32[48,3,128]{2,1,0:T(4,128)}, f32[48,3,128]{2,1,0:T(4,128)}) custom-call(s32[192,16]{1,0:T(8,128)} %maximum_convert_fusion.info_ref, s32[1]{0:T(128)} %bitcast.19.y_ref, s32[256]{0:T(256)} %get-tuple-element.18.lst, f32[192,4,128]{2,1,0:T(4,128)} %get-tuple-element.19.tall, ...), custom_call_target="tpu_custom_call" | custom-call | tf_op jit(solution)/shard_map/near/pallas_call | solution.py:263
  56.9 2.0 %collective-permute-start.8 = (f32[48,3,128]{2,1,0:T(4,128)}, f32[48,3,128]{2,1,0:T(4,128)S(1)}, u32[]{:S(2)}, u32[]{:S(2)}) collective-permute-start(f32[48,3,128]{2,1,0:T(4,128)} %get-tuple-element.23), channel_id=1, source_target_pairs={{0,8},{1,9},{2,10},{3,11},{4,12},{5,13},{6,14},{7,15},{8,16},{9,17... | collective-permute-start | bytes 221192 | tf_op jit(solution)/shard_map/ppermute | solution.py:271
  58.9 1.7 %collective-permute-start.9 = (f32[48,3,128]{2,1,0:T(4,128)}, f32[48,3,128]{2,1,0:T(4,128)S(1)}, u32[]{:S(2)}, u32[]{:S(2)}) collective-permute-start(f32[48,3,128]{2,1,0:T(4,128)} %get-tuple-element.24), channel_id=1, source_target_pairs={{0,16},{1,17},{2,18},{3,19},{4,20},{5,21},{6,22},{7,23},{8,24},{9,... | collective-permute-start | bytes 221192 | tf_op jit(solution)/shard_map/ppermute | solution.py:271
  60.7 1.0 %collective-permute-done.7 = f32[48,3,128]{2,1,0:T(4,128)S(1)} collective-permute-done((f32[48,3,128]{2,1,0:T(4,128)}, f32[48,3,128]{2,1,0:T(4,128)S(1)}, u32[]{:S(2)}, u32[]{:S(2)}) %collective-permute-start.7) | collective-permute-done | bytes 73760 | tf_op jit(solution)/shard_map/ppermute | solution.py:271
  61.7 1.6 %collective-permute-done.8 = f32[48,3,128]{2,1,0:T(4,128)S(1)} collective-permute-done((f32[48,3,128]{2,1,0:T(4,128)}, f32[48,3,128]{2,1,0:T(4,128)S(1)}, u32[]{:S(2)}, u32[]{:S(2)}) %collective-permute-start.8) | collective-permute-done | bytes 73760 | tf_op jit(solution)/shard_map/ppermute | solution.py:271
  63.3 3.2 %collective-permute-done.9 = f32[48,3,128]{2,1,0:T(4,128)S(1)} collective-permute-done((f32[48,3,128]{2,1,0:T(4,128)}, f32[48,3,128]{2,1,0:T(4,128)S(1)}, u32[]{:S(2)}, u32[]{:S(2)}) %collective-permute-start.9) | collective-permute-done | bytes 73760 | tf_op jit(solution)/shard_map/ppermute | solution.py:271
  66.5 1.0 %select_bitcast_fusion = f32[1,48,3,128]{3,2,1,0:T(4,128)S(1)} fusion(f32[48,3,128]{2,1,0:T(4,128)S(1)} %copy-done.1, f32[48,3,128]{2,1,0:T(4,128)S(1)} %collective-permute-done.8, f32[48,3,128]{2,1,0:T(4,128)S(1)} %collective-permute-done.9, f32[48,3,128]{2,1,0:T(4,128)} %get-tuple-element.21, f32[48,3,128]{2,1,0:T(4,128)S(1)} %collective-permute-done.7, ...), kind=kLoop, calls=%fused_computation.3 | loop fusion | flops 92160 | bytes 448512 | tf_op jit(solution)/shard_map/broadcast_in_dim | solution.py:274
  (34 shorter events, 6.3 us)
Async XLA Ops:
  6.3 28.0 %collective-permute-start.6 = (f32[48,4,128]{2,0,1:T(8,128)S(1)}, f32[48,4,128]{2,0,1:T(8,128)S(1)}, u32[]{:S(2)}, u32[]{:S(2)}) collective-permute-start(f32[48,4,128]{2,0,1:T(8,128)S(1)} %copy.32), channel_id=1, source_target_pairs={{0,16},{1,17},{2,18},{3,19},{4,20},{5,21},{6,22},{7,23},{8,24},{9,... | collective-permute-start | bytes 294920 | tf_op jit(solution)/shard_map/ppermute | solution.py:236
  9.5 25.5 %collective-permute-start.5 = (f32[48,4,128]{2,0,1:T(8,128)S(1)}, f32[48,4,128]{2,0,1:T(8,128)S(1)}, u32[]{:S(2)}, u32[]{:S(2)}) collective-permute-start(f32[48,4,128]{2,0,1:T(8,128)S(1)} %copy.32), channel_id=1, source_target_pairs={{0,24},{1,25},{2,26},{3,27},{4,28},{5,29},{6,30},{7,31},{8,0},{9,1... | collective-permute-start | bytes 294920 | tf_op jit(solution)/shard_map/ppermute | solution.py:236
  10.6 8.6 %copy-start.2 = (f32[3,2048]{1,0:T(4,128)S(1)}, f32[3,2048]{1,0:T(4,128)}, u32[]{:S(2)}) copy-start(f32[3,2048]{1,0:T(4,128)} %param.14) | copy-start | bytes 73732
  10.6 31.1 %all-to-all-start = ((f32[8,48,4,128]{3,2,1,0:T(4,128)}), f32[8,48,4,128]{3,2,1,0:T(4,128)S(1)}, u32[]{:S(2)}, u32[]{:S(2)}) async-start(f32[8,48,4,128]{3,2,1,0:T(4,128)} %get-tuple-element.20), calls=%async_computation | async-start | bytes 1572864 | tf_op jit(solution)/shard_map/all_to_all | solution.py:235
  19.2 0.7 %copy-start.3 = (f32[2048]{0:T(1024)S(1)}, f32[2048]{0:T(1024)}, u32[]{:S(2)}) copy-start(f32[2048]{0:T(1024)} %param.15) | copy-start | bytes 24580
  19.9 1.4 %collective-permute-start = (f32[4,16,128]{2,1,0:T(8,128)S(1)}, f32[4,16,128]{2,1,0:T(8,128)S(1)}, u32[]{:S(2)}, u32[]{:S(2)}) collective-permute-start(f32[4,16,128]{2,1,0:T(8,128)S(1)} %pad_maximum_fusion.2), channel_id=1, source_target_pairs={{0,32},{32,0},{64,96},{96,64},{128,160},{160,128},{192,224},{224,1... | collective-permute-start | bytes 98312 | tf_op jit(solution)/shard_map/ppermute | solution.py:238
  19.9 0.7 %copy-start.4 = (s32[1,48,32]{1,2,0:T(8,128)S(1)}, s32[1,48,32]{1,2,0:T(8,128)}, u32[]{:S(2)}) copy-start(s32[1,48,32]{1,2,0:T(8,128)} %param.13) | copy-start | bytes 18436
  21.3 5.8 %collective-permute-start.2 = (f32[2,4,16,128]{3,2,1,0:T(8,128)S(1)}, f32[2,4,16,128]{3,2,1,0:T(8,128)S(1)}, u32[]{:S(2)}, u32[]{:S(2)}) collective-permute-start(f32[2,4,16,128]{3,2,1,0:T(8,128)S(1)} %get-tuple-element.26), channel_id=1, source_target_pairs={{0,192},{32,224},{64,0},{96,32},{128,64},{160,96},{192,128},{224,1... | collective-permute-start | bytes 196616 | tf_op jit(solution)/shard_map/ppermute | solution.py:239
  22.2 5.9 %collective-permute-start.1 = (f32[2,4,16,128]{3,2,1,0:T(8,128)S(1)}, f32[2,4,16,128]{3,2,1,0:T(8,128)S(1)}, u32[]{:S(2)}, u32[]{:S(2)}) collective-permute-start(f32[2,4,16,128]{3,2,1,0:T(8,128)S(1)} %get-tuple-element.26), channel_id=1, source_target_pairs={{0,64},{32,96},{64,128},{96,160},{128,192},{160,224},{192,0},{224,... | collective-permute-start | bytes 196616 | tf_op jit(solution)/shard_map/ppermute | solution.py:239
  24.6 5.8 %collective-permute-start.3 = (f32[2,4,16,128]{3,2,1,0:T(8,128)S(1)}, f32[2,4,16,128]{3,2,1,0:T(8,128)S(1)}, u32[]{:S(2)}, u32[]{:S(2)}) collective-permute-start(f32[2,4,16,128]{3,2,1,0:T(8,128)S(1)} %get-tuple-element.26), channel_id=1, source_target_pairs={{0,128},{32,160},{64,192},{96,224},{128,0},{160,32},{192,64},{224,... | collective-permute-start | bytes 196616 | tf_op jit(solution)/shard_map/ppermute | solution.py:239
  27.1 8.6 %collective-permute-start.4 = (f32[48,4,128]{2,0,1:T(8,128)S(1)}, f32[48,4,128]{2,0,1:T(8,128)S(1)}, u32[]{:S(2)}, u32[]{:S(2)}) collective-permute-start(f32[48,4,128]{2,0,1:T(8,128)S(1)} %copy.32), channel_id=1, source_target_pairs={{0,8},{1,9},{2,10},{3,11},{4,12},{5,13},{6,14},{7,15},{8,16},{9,17... | collective-permute-start | bytes 294920 | tf_op jit(solution)/shard_map/ppermute | solution.py:236
  41.7 0.9 %copy-start = (f32[8,48,4,128]{3,2,1,0:T(4,128)}, f32[8,48,4,128]{3,2,1,0:T(4,128)S(1)}, u32[]{:S(2)}) copy-start(f32[8,48,4,128]{3,2,1,0:T(4,128)S(1)} %all-to-all-done) | copy-start | bytes 2359300
  42.6 23.9 %copy-start.1 = (f32[48,3,128]{2,1,0:T(4,128)S(1)}, f32[48,3,128]{2,1,0:T(4,128)}, u32[]{:S(2)}) copy-start(f32[48,3,128]{2,1,0:T(4,128)} %far.1) | copy-start | bytes 221188
  56.9 4.8 %collective-permute-start.7 = (f32[48,3,128]{2,1,0:T(4,128)}, f32[48,3,128]{2,1,0:T(4,128)S(1)}, u32[]{:S(2)}, u32[]{:S(2)}) collective-permute-start(f32[48,3,128]{2,1,0:T(4,128)} %get-tuple-element.22), channel_id=1, source_target_pairs={{0,24},{1,25},{2,26},{3,27},{4,28},{5,29},{6,30},{7,31},{8,0},{9,1... | collective-permute-start | bytes 221192 | tf_op jit(solution)/shard_map/ppermute | solution.py:271
  56.9 6.4 %collective-permute-start.8 = (f32[48,3,128]{2,1,0:T(4,128)}, f32[48,3,128]{2,1,0:T(4,128)S(1)}, u32[]{:S(2)}, u32[]{:S(2)}) collective-permute-start(f32[48,3,128]{2,1,0:T(4,128)} %get-tuple-element.23), channel_id=1, source_target_pairs={{0,8},{1,9},{2,10},{3,11},{4,12},{5,13},{6,14},{7,15},{8,16},{9,17... | collective-permute-start | bytes 221192 | tf_op jit(solution)/shard_map/ppermute | solution.py:271
  58.9 1.7 %copy-start.5 = (s32[1,1,48]{2,1,0:T(1,128)S(1)}, s32[1,1,48]{2,1,0:T(1,128)}, u32[]{:S(2)}) copy-start(s32[1,1,48]{2,1,0:T(1,128)} %param.10) | copy-start | bytes 580
  58.9 7.6 %collective-permute-start.9 = (f32[48,3,128]{2,1,0:T(4,128)}, f32[48,3,128]{2,1,0:T(4,128)S(1)}, u32[]{:S(2)}, u32[]{:S(2)}) collective-permute-start(f32[48,3,128]{2,1,0:T(4,128)} %get-tuple-element.24), channel_id=1, source_target_pairs={{0,16},{1,17},{2,18},{3,19},{4,20},{5,21},{6,22},{7,23},{8,24},{9,... | collective-permute-start | bytes 221192 | tf_op jit(solution)/shard_map/ppermute | solution.py:271

commit v3 on v2

v3 whole, which is shorter than its diff:
```python
import jax
import jax.numpy as jnp
from jax import lax
from jax.experimental import pallas as pl
from jax.experimental.pallas import tpu as pltpu
from jax.sharding import PartitionSpec as P

NB = 48
PL = 128
K = 4
LC = 32
NY = 4
NZ = 8
NX = 4
SOFT = 0.01
UNROLL = 8
FULL_AT = 7
HALF_AT = 8
PADDED = 256
F32 = jnp.float32
I32 = jnp.int32
BF16 = jnp.bfloat16
VMEM = pltpu.VMEM
SMEM = pltpu.SMEM


def vspec():
    return pl.BlockSpec(memory_space=VMEM)


def sspec():
    return pl.BlockSpec(memory_space=SMEM)


def column_of(row, n):
    square = jnp.broadcast_to(row, (n, n))
    diag = lax.broadcasted_iota(I32, (n, n), 0) == lax.broadcasted_iota(I32, (n, n), 1)
    return jnp.sum(jnp.where(diag, square, jnp.zeros_like(square)), axis=1, keepdims=True)


def pack_kernel(pos_ref, mass_ref, cnt_ref, dest_ref, near_ref, ctr_ref, cm_ref, src_ref, tgt_ref, cell_ref):
    cnt = column_of(cnt_ref[...], NB)
    near = near_ref[...]
    off = (near >= NB).astype(I32) + (near >= 2 * NB).astype(I32)
    dev = (dest_ref[...] + off - 1) & (NY * NZ - 1)
    code = (dev & (NZ - 1)) * NB + (near - off * NB)
    row = dev >> 3
    lane = lax.broadcasted_iota(I32, (NB, PL), 1)
    weight = jnp.where(lane < cnt, mass_ref[...], 0.0)
    info = jnp.where(lane == 4, cnt, 0)
    for k in range(K):
        info = jnp.where(lane == k, column_of(code[k : k + 1], NB), info)
        info = jnp.where(lane == 8 + k, column_of(row[k : k + 1], NB), info)
    info = info.astype(F32)
    for c in range(3):
        value = pos_ref[c]
        tgt_ref[:, c, :] = value
        for z in range(NZ):
            src_ref[z, :, c, :] = value
    tgt_ref[:, 3, :] = info
    for z in range(NZ):
        src_ref[z, :, 3, :] = weight
    for j in range(16):
        part = slice(j * PL, (j + 1) * PL)
        for c in range(3):
            cell_ref[c * 16 + j : c * 16 + j + 1, :] = ctr_ref[c : c + 1, part]
        cell_ref[48 + j : 49 + j, :] = cm_ref[0:1, part]
    cell_ref[64:PADDED, :] = jnp.zeros((PADDED - 64, PL), F32)


def far_kernel(pos_ref, cnt_ref, list_ref, cell_hbm, out_ref, pad, tab, sem):
    copies = [
        pltpu.make_async_copy(cell_hbm.at[pl.ds(i * PADDED, 64)], tab.at[i], sem.at[i]) for i in range(2 * NX)
    ]
    for copy in copies:
        copy.start()
    lane = lax.broadcasted_iota(I32, (NB, PL), 1)
    cnt = column_of(cnt_ref[...], NB)
    live = lane < cnt
    total = jnp.maximum(cnt, 1).astype(F32)
    pos = [pos_ref[c] for c in range(3)]
    centre = [jnp.sum(jnp.where(live, v, 0.0), axis=1, keepdims=True) / total for v in pos]
    diag = lax.broadcasted_iota(I32, (NB, PL), 0) == (lane & 63)
    ctr = [jnp.sum(jnp.where(diag, v, 0.0), axis=0, keepdims=True) for v in centre]
    wide = jnp.concatenate([list_ref[...], jnp.zeros((LC, PL - NB), I32)], axis=1)
    twice = wide + pltpu.roll(wide, 64, 1)
    half = lax.broadcasted_iota(I32, (1, PL), 1) < 64
    ids = [jnp.where(half, twice[2 * j : 2 * j + 1], twice[2 * j + 1 : 2 * j + 2]) for j in range(LC // 2)]
    ids = jnp.concatenate(ids, axis=0)
    rows = ids >> 7
    lanes = ids & (PL - 1)
    tables = []
    for copy in copies:
        copy.wait()
    for c in range(4):
        whole = jnp.concatenate([tab[i, 16 * c : 16 * c + 16, :] for i in range(2 * NX)], axis=0)
        whole = whole.T
        high = whole.astype(BF16)
        low = (whole - high.astype(F32)).astype(BF16)
        tables.append(jnp.concatenate([high, low], axis=1))
    tables = jnp.concatenate(tables, axis=0)
    sub = lax.broadcasted_iota(I32, (PL, 2 * PL), 0)
    got = [[] for _ in range(4)]
    for j in range(0, LC // 2, 2):
        r2 = jnp.concatenate([rows[j : j + 1], rows[j + 1 : j + 2]], axis=1)
        l2 = jnp.concatenate([lanes[j : j + 1], lanes[j + 1 : j + 2]], axis=1)
        hot = jnp.where(sub == r2, 1.0, 0.0).astype(BF16)
        hot = jnp.concatenate([hot, hot], axis=0)
        found = jnp.dot(tables, hot, preferred_element_type=F32)
        pick = sub == l2
        for c in range(4):
            value = jnp.sum(jnp.where(pick, found[c * PL : (c + 1) * PL], 0.0), axis=0, keepdims=True)
            got[c] += [value[:, :PL], value[:, PL:]]
    cells = [jnp.concatenate(v, axis=0) for v in got]
    rel = [ctr[c] - cells[c] for c in range(3)]
    dist = rel[0] * rel[0] + rel[1] * rel[1] + rel[2] * rel[2] + 1.0
    inv = lax.rsqrt(dist)
    cube = cells[3] * (inv * inv * inv)
    fifth = 3.0 * cube * (inv * inv)
    terms = [-(cube * rel[c]) for c in range(3)]
    for a, b in ((0, 0), (1, 1), (2, 2), (0, 1), (0, 2), (1, 2)):
        value = fifth * rel[a] * rel[b]
        if a == b:
            value = value - cube
        terms.append(value)
    terms = [jnp.sum(v, axis=0, keepdims=True) for v in terms]
    pad[...] = jnp.zeros((PL, PL), F32)
    for i, v in enumerate(terms):
        pad[i : i + 1, :] = v + pltpu.roll(v, 64, 1)
    back = pad[...].T
    field = [back[0:NB, i : i + 1] for i in range(3)]
    tide = [back[0:NB, 3 + i : 4 + i] for i in range(6)]
    offset = [pos[c] - centre[c] for c in range(3)]
    for c, (i, j, k) in enumerate(((0, 3, 4), (3, 1, 5), (4, 5, 2))):
        out_ref[c] = field[c] + tide[i] * offset[0] + tide[j] * offset[1] + tide[k] * offset[2]


def split3(v):
    high = v.astype(BF16).astype(F32)
    rest = v - high
    mid = rest.astype(BF16).astype(F32)
    return high, mid, rest - mid


def prep_kernel(y_ref, t0, t1, t2, t3, tall, tab, hold, sem):
    me = y_ref[0]
    n_all = NY * NB
    infos = []
    for i, t in enumerate((t0, t1, t2, t3)):
        tall[i * NB : (i + 1) * NB] = t[...]
        infos.append(t[:, 3, :])
    info = jnp.concatenate(infos, axis=0)
    sub = lax.broadcasted_iota(I32, (n_all, PL), 0)
    lane = lax.broadcasted_iota(I32, (n_all, PL), 1)
    here = me.astype(F32)
    flag = [(info[:, 8 + k : 9 + k] == here).astype(F32) for k in range(K)]
    code = [info[:, k : k + 1] for k in range(K)]
    count = (flag[0] + flag[1]) + (flag[2] + flag[3])
    full = (count > 2.5).astype(F32)
    half = ((count > 0.5) & (count < 2.5)).astype(F32)
    marks = jnp.where(lane == 0, full, jnp.where(lane == 1, half, 0.0))
    a = lax.broadcasted_iota(I32, (n_all, n_all), 0)
    b = lax.broadcasted_iota(I32, (n_all, n_all), 1)
    below = jnp.where(b < a, 1.0, 0.0).astype(BF16)
    before = jnp.dot(below, marks.astype(BF16), preferred_element_type=F32)
    n_full = jnp.sum(full, axis=0, keepdims=True)
    n_half = jnp.sum(half, axis=0, keepdims=True)
    place = jnp.where(full > 0.5, before[:, 0:1], jnp.where(half > 0.5, n_full + before[:, 1:2], -1.0))
    moved = jnp.where(b == place.astype(I32), 1.0, 0.0).astype(BF16)
    slot, ins, outs = [], jnp.zeros((n_all, 1), F32), jnp.zeros((n_all, 1), F32)
    for k in range(K):
        slot.append(jnp.where(flag[k] > 0.5, ins, count + outs))
        ins, outs = ins + flag[k], outs + (1.0 - flag[k])
    group = (sub >= NB).astype(I32) + (sub >= 2 * NB).astype(I32) + (sub >= 3 * NB).astype(I32)
    step = jnp.where(group == 2, -1, jnp.where(group == 3, 2, group))
    home = ((me - step) & (NY - 1)) * NB + (sub - group * NB)
    load = jnp.where(lane == 4, info, jnp.where(lane == 5, home.astype(F32), jnp.where(lane == 6, count, 0.0)))
    load = jnp.where(lane == 9, sub.astype(F32), load)
    for j in range(K):
        pick = jnp.zeros((n_all, 1), F32)
        for k in range(K):
            pick = pick + jnp.where(slot[k] == float(j), code[k], 0.0)
        load = jnp.where(lane == j, pick, load)
    high = load.astype(BF16)
    low = (load - high.astype(F32)).astype(BF16)
    dn = (((0,), (0,)), ((), ()))
    out = lax.dot_general(moved, high, dn, preferred_element_type=F32) + lax.dot_general(
        moved, low, dn, preferred_element_type=F32
    )
    out = jnp.where(lane == FULL_AT, n_full, jnp.where(lane == HALF_AT, n_half, out))
    hold[...] = out.astype(I32)
    copy = pltpu.make_async_copy(hold, tab, sem)
    copy.start()
    copy.wait()


def near_kernel(tab, tall, src_ref, out_ref):
    out_ref[...] = jnp.zeros((NY * NB, 3, PL), F32)
    sub4 = lax.broadcasted_iota(I32, (4, PL), 0)
    lane3 = lax.broadcasted_iota(I32, (3, PL), 1)
    spatial = sub4 < 3
    one = jnp.ones((4, PL), F32)
    zero4 = jnp.zeros((4, PL), F32)
    zero8 = jnp.zeros((8, PL), F32)

    def square(v):
        return jnp.sum(jnp.where(spatial, v * v, 0.0), axis=0, keepdims=True)

    def mix(a, b):
        return jnp.where(spatial, a, b)

    def stack(*v):
        return jnp.concatenate(v, axis=0).astype(BF16)

    def job(e, width):
        n = tab[e, 6]
        t = tall[tab[e, 9]]
        th, tm, tl = split3(t)
        qh, qm, ql = split3(square(t))
        u = stack(mix(th, one), mix(th, one), mix(tm, one), mix(tm, qh), mix(th, qm), mix(tl, ql), zero8)
        vs, gs = [], []
        for k in range(width):
            s = src_ref[tab[e, k]]
            flag = (k < n).astype(F32)
            sh, sm, sl = split3(-2.0 * s)
            qh, qm, ql = split3(square(s) + SOFT)
            vs.append(stack(mix(sh, qh), mix(sm, qm), mix(sh, ql), mix(sm, one), mix(sl, one), mix(sh, one), zero8))
            w = s[3:4] * flag
            gs.append(stack(*split3(mix(s * w, w)), zero4))
        v = jnp.concatenate(vs, axis=1)
        g = jnp.concatenate(gs, axis=1)
        dist = lax.dot_general(v, u, (((0,), (0,)), ((), ())), preferred_element_type=F32)
        inv = lax.rsqrt(dist)
        f = inv * inv * inv
        high = f.astype(BF16)
        low = (f - high.astype(F32)).astype(BF16)
        o = jnp.dot(g, high, preferred_element_type=F32) + jnp.dot(g, low, preferred_element_type=F32)
        a = o[0:4] + o[4:8] + o[8:12]
        out_ref[tab[e, 5]] = jnp.where(lane3 < tab[e, 4], a[0:3] - t[0:3] * a[3:4], 0.0)

    n_full = tab[0, FULL_AT]
    n_half = tab[0, HALF_AT]

    def whole(i, _):
        for j in range(UNROLL):
            job(jnp.minimum(UNROLL * i + j, n_full - 1), 4)

    def part(i, _):
        for j in range(UNROLL):
            job(n_full + jnp.minimum(UNROLL * i + j, n_half - 1), 2)

    lax.fori_loop(0, (n_full + UNROLL - 1) // UNROLL, whole, None)
    lax.fori_loop(0, (n_half + UNROLL - 1) // UNROLL, part, None)


def final_kernel(cnt_ref, far_ref, part_ref, out_ref):
    live = lax.broadcasted_iota(I32, (NB, PL), 1) < column_of(cnt_ref[...], NB)
    near = (part_ref[0] + part_ref[1]) + (part_ref[2] + part_ref[3])
    for c in range(3):
        out_ref[c] = jnp.where(live, far_ref[c] + near[:, c, :], 0.0)


def along_y(k):
    return [(NZ * y + z, NZ * ((y + k) % NY) + z) for y in range(NY) for z in range(NZ)]


def per_device(positions, masses, counts, dest_ids, near_list, cell_list, cell_centers, cell_mass):
    pos = jnp.transpose(positions[0], (1, 0, 2))
    cnt = counts[0]
    src, tgt, cells = pl.pallas_call(
        pack_kernel,
        out_shape=(
            jax.ShapeDtypeStruct((NZ, NB, 4, PL), F32),
            jax.ShapeDtypeStruct((NB, 4, PL), F32),
            jax.ShapeDtypeStruct((PADDED, PL), F32),
        ),
        in_specs=[vspec()] * 7,
        out_specs=[vspec()] * 3,
        name="pack",
    )(pos, masses[0], cnt, dest_ids, near_list[0].T, cell_centers, cell_mass[None])
    z_rows = [[NZ * y + z for z in range(NZ)] for y in range(NY)]
    y_rows = [[NZ * y + z for y in range(NY)] for z in range(NZ)]
    window = lax.all_to_all(src, "space", 0, 0, axis_index_groups=z_rows, tiled=True)
    tgts = [tgt] + [lax.ppermute(tgt, "space", along_y(k)) for k in (1, -1, 2)]
    table = lax.all_gather(cells, "slab", axis=0, tiled=True)
    me = (lax.axis_index("space") // NZ).astype(I32).reshape(1)
    tall, tab = pl.pallas_call(
        prep_kernel,
        out_shape=(
            jax.ShapeDtypeStruct((NY * NB, 4, PL), F32),
            jax.ShapeDtypeStruct((NY * NB, PL), I32),
        ),
        in_specs=[sspec()] + [vspec()] * 4,
        out_specs=[vspec(), sspec()],
        scratch_shapes=[pltpu.VMEM((NY * NB, PL), I32), pltpu.SemaphoreType.DMA],
        name="prep",
    )(me, *tgts)
    part = pl.pallas_call(
        near_kernel,
        out_shape=jax.ShapeDtypeStruct((NY * NB, 3, PL), F32),
        in_specs=[sspec()] + [vspec()] * 2,
        out_specs=vspec(),
        name="near",
    )(tab, tall, window.reshape(NZ * NB, 4, PL))
    table, part = lax.optimization_barrier((table, part))
    far = pl.pallas_call(
        far_kernel,
        out_shape=jax.ShapeDtypeStruct((3, NB, PL), F32),
        in_specs=[vspec()] * 3 + [pl.BlockSpec(memory_space=pl.ANY)],
        out_specs=vspec(),
        scratch_shapes=[
            pltpu.VMEM((PL, PL), F32),
            pltpu.VMEM((2 * NX, 64, PL), F32),
            pltpu.SemaphoreType.DMA((2 * NX,)),
        ],
        name="far",
    )(pos, cnt, cell_list[0].T, table)
    back = lax.all_to_all(
        part.reshape(NY, NB, 3, PL), "space", 0, 0, axis_index_groups=y_rows, tiled=True
    )
    out = pl.pallas_call(
        final_kernel,
        out_shape=jax.ShapeDtypeStruct((3, NB, PL), F32),
        in_specs=[vspec()] * 3,
        out_specs=vspec(),
        name="final",
    )(cnt, far, back)
    return jnp.transpose(out, (1, 0, 2))[None]


def solution(mesh):
    in_specs = (
        P("slab", "space", None, None),
        P("slab", "space", None),
        P("slab", "space", None),
        P("slab", "space"),
        P("slab", "space", None),
        P("slab", "space", None),
        P(None, "slab"),
        P("slab"),
    )
    return jax.shard_map(
        per_device,
        mesh=mesh,
        in_specs=in_specs,
        out_specs=P("slab", "space", None, None),
        check_vma=False,
    )
```

time: 69.2 us -> 77.7 us (1.12)
  the two profiles are of different devices: /device:TPU:6 before, /device:TPU:1 now
where the time goes in v3:
time: 77.7 us; the launch traced here: 77.8 us
  Pallas kernels  24.1 us (31%)
  starting transfers between devices  21.5 us (28%)
  waiting for transfers between devices  14.5 us (19%)
  between operations  13.4 us (17%)
  local copies, waits for them, and re-layouts  4.23 us (5%)
    pallas_call x1, Pallas kernels, per_device(): pl.pallas_call(near_kernel, out_shape=jax.ShapeDtypeStruct((NY * NB, 3, P...  9.25 us
    all_to_all x1, starting transfers between devices, per_device(): lax.all_to_all(src, 'space', 0, 0, axis_index_groups=z_rows, tiled=True)  9.16 us
    all_to_all x1, starting transfers between devices, per_device(): lax.all_to_all(part.reshape(NY, NB, 3, PL), 'space', 0, 0, axis_index_gro...  7.93 us
    all_to_all x1, waiting for transfers between devices, per_device(): lax.all_to_all(src, 'space', 0, 0, axis_index_groups=z_rows, tiled=True)  7.48 us
    pallas_call x1, Pallas kernels, per_device(): pl.pallas_call(prep_kernel, out_shape=(jax.ShapeDtypeStruct((NY * NB, 4,...  6.69 us
    ppermute x3, starting transfers between devices, per_device(): tgts = [tgt] + [lax.ppermute(tgt, 'space', along_y(k)) for k in (1, -1, 2)]  4.46 us
    ppermute x3, waiting for transfers between devices, per_device(): tgts = [tgt] + [lax.ppermute(tgt, 'space', along_y(k)) for k in (1, -1, 2)]  4.29 us
    pallas_call x1, Pallas kernels, per_device(): pl.pallas_call(far_kernel, out_shape=jax.ShapeDtypeStruct((3, NB, PL), F3...  3.81 us
  transfers between devices with their start and end apart: 6, of which 5 were waited for; matrix products, arithmetic and copies ran while one was open for 0% of the time, Pallas kernels for 25%

profile of v3, /device:TPU:1, one launch (start us, length us, event | category | flops | bytes accessed | tf_op | source)
XLA Modules:
  0.0 77.8 jit_solution(16234954760568082478)
XLA Ops:
  6.5 0.0 all-gather.2.cloned.1.call-start
  6.5 2.5 %pack.1 = (f32[8,48,4,128]{3,2,1,0:T(4,128)}, f32[48,4,128]{2,1,0:T(4,128)}, f32[256,128]{1,0:T(8,128)}) custom-call(f32[3,48,128]{2,1,0:T(8,128)} %bitcast.20, f32[48,128]{1,0:T(8,128)} %bitcast.22, s32[1,48]{1,0:T(1,128)} %bitcast.25, s32[1,48]{1,0:T(1,128)} %dest_ref.1, s32[4,48]{1,0:T(4,128)} %bitcast.28, f32[3,2048]{1,0:T(4,128)} %ctr_ref.1, ...), custom_call_target="tpu_custom_call" | custom-call | tf_op jit(solution)/shard_map/pack/pallas_call | solution.py:270
  9.1 0.0 all-gather.2.cloned.1.call-update
  9.1 0.0 copy-start.1
  9.1 9.2 %all-to-all-start = ((f32[8,48,4,128]{3,2,1,0:T(4,128)}), f32[8,48,4,128]{3,2,1,0:T(4,128)S(1)}, u32[]{:S(2)}, u32[]{:S(2)}) async-start(f32[8,48,4,128]{3,2,1,0:T(4,128)} %get-tuple-element.16), calls=%async_computation | async-start | bytes 1572864 | tf_op jit(solution)/shard_map/all_to_all | solution.py:283
  18.3 0.0 copy-done.1
  18.3 1.4 %collective-permute-start = (f32[48,4,128]{2,1,0:T(4,128)S(1)}, f32[48,4,128]{2,1,0:T(4,128)S(1)}, u32[]{:S(2)}, u32[]{:S(2)}) collective-permute-start(f32[48,4,128]{2,1,0:T(4,128)S(1)} %copy-done.1), channel_id=1, source_target_pairs={{0,8},{1,9},{2,10},{3,11},{4,12},{5,13},{6,14},{7,15},{8,16},{9,17... | collective-permute-start | bytes 294920 | tf_op jit(solution)/shard_map/ppermute | solution.py:284
  19.7 1.5 %collective-permute-start.1 = (f32[48,4,128]{2,1,0:T(4,128)S(1)}, f32[48,4,128]{2,1,0:T(4,128)S(1)}, u32[]{:S(2)}, u32[]{:S(2)}) collective-permute-start(f32[48,4,128]{2,1,0:T(4,128)S(1)} %copy-done.1), channel_id=1, source_target_pairs={{0,24},{1,25},{2,26},{3,27},{4,28},{5,29},{6,30},{7,31},{8,0},{9,1... | collective-permute-start | bytes 294920 | tf_op jit(solution)/shard_map/ppermute | solution.py:284
  21.2 1.6 %collective-permute-start.2 = (f32[48,4,128]{2,1,0:T(4,128)S(1)}, f32[48,4,128]{2,1,0:T(4,128)S(1)}, u32[]{:S(2)}, u32[]{:S(2)}) collective-permute-start(f32[48,4,128]{2,1,0:T(4,128)S(1)} %copy-done.1), channel_id=1, source_target_pairs={{0,16},{1,17},{2,18},{3,19},{4,20},{5,21},{6,22},{7,23},{8,24},{9,... | collective-permute-start | bytes 294920 | tf_op jit(solution)/shard_map/ppermute | solution.py:284
  22.7 0.4 collective-permute-done.t1
  23.1 0.3 collective-permute-done.1.t2
  23.4 3.6 %collective-permute-done.2.t3 = f32[48,4,128]{2,1,0:T(4,128)S(1)} collective-permute-done((f32[48,4,128]{2,1,0:T(4,128)S(1)}, f32[48,4,128]{2,1,0:T(4,128)S(1)}, u32[]{:S(2)}, u32[]{:S(2)}) %collective-permute-start.2) | collective-permute-done | bytes 98336 | tf_op jit(solution)/shard_map/ppermute | solution.py:284
  27.0 0.0 copy-done.2
  27.1 0.6 copy-done.4
  27.7 6.7 %prep.1 = (f32[192,4,128]{2,1,0:T(4,128)}, s32[192,128]{1,0:T(8,128)}) custom-call(s32[1]{0:T(128)} %bitcast.10.y_ref, f32[48,4,128]{2,1,0:T(4,128)} %get-tuple-element.13.t0, f32[48,4,128]{2,1,0:T(4,128)} %copy-done.2, f32[48,4,128]{2,1,0:T(4,128)} %copy-done.3, f32[48,4,128]{2,1,0:T(4,128)} %copy-done.4), custom_call_target="tpu_custom_call" | custom-call | tf_op jit(solution)/shard_map/prep/pallas_call | solution.py:287
  34.4 7.5 %all-to-all-done = f32[8,48,4,128]{3,2,1,0:T(4,128)S(1)} async-done(((f32[8,48,4,128]{3,2,1,0:T(4,128)}), f32[8,48,4,128]{3,2,1,0:T(4,128)S(1)}, u32[]{:S(2)}, u32[]{:S(2)}) %all-to-all-start) | async-done | bytes 786464 | tf_op jit(solution)/shard_map/all_to_all | solution.py:283
  41.9 0.9 %copy-done = f32[8,48,4,128]{3,2,1,0:T(4,128)} copy-done((f32[8,48,4,128]{3,2,1,0:T(4,128)}, f32[8,48,4,128]{3,2,1,0:T(4,128)S(1)}, u32[]{:S(2)}) %copy-start) | copy-done | bytes 786456
  42.8 9.2 %near.1 = f32[192,3,128]{2,1,0:T(4,128)} custom-call(s32[192,128]{1,0:T(8,128)} %get-tuple-element.14.tab, f32[192,4,128]{2,1,0:T(4,128)} %get-tuple-element.15.tall, f32[384,4,128]{2,1,0:T(4,128)} %bitcast.18), custom_call_target="tpu_custom_call" | custom-call | tf_op jit(solution)/shard_map/near/pallas_call | solution.py:298
  52.0 1.7 %copy.9 = f32[4,48,3,128]{3,1,2,0:T(8,128)} copy(f32[4,48,3,128]{3,2,1,0:T(4,128)} %bitcast.19) | data formatting | bytes 589824 | tf_op jit(solution)/shard_map/reshape | solution.py:319
  53.8 7.9 %all-to-all-start.1 = ((f32[4,48,3,128]{3,1,2,0:T(8,128)}), f32[4,48,3,128]{3,1,2,0:T(8,128)S(1)}, u32[]{:S(2)}, u32[]{:S(2)}) async-start(f32[4,48,3,128]{3,1,2,0:T(8,128)} %copy.9), calls=%async_computation.1 | async-start | bytes 589824 | tf_op jit(solution)/shard_map/all_to_all | solution.py:318
  61.7 3.8 %far.1.far_ref = f32[3,48,128]{2,1,0:T(8,128)} custom-call(f32[3,48,128]{2,1,0:T(8,128)} %bitcast.21, s32[1,48]{1,0:T(1,128)} %bitcast.26, s32[32,48]{1,0:T(8,128)} %bitcast.23, f32[2048,128]{1,0:T(8,128)} %all-gather.2.cloned.1.call-done.cell_hbm), custom_call_target="tpu_custom_call" | custom-call | tf_op jit(solution)/shard_map/far/pallas_call | solution.py:306
  65.5 2.7 %all-to-all-done.1 = f32[4,48,3,128]{3,1,2,0:T(8,128)S(1)} async-done(((f32[4,48,3,128]{3,1,2,0:T(8,128)}), f32[4,48,3,128]{3,1,2,0:T(8,128)S(1)}, u32[]{:S(2)}, u32[]{:S(2)}) %all-to-all-start.1) | async-done | bytes 294944 | tf_op jit(solution)/shard_map/all_to_all | solution.py:318
  68.3 0.9 %copy.10.part_ref = f32[4,48,3,128]{3,2,1,0:T(4,128)} copy(f32[4,48,3,128]{3,1,2,0:T(8,128)S(1)} %all-to-all-done.1) | data formatting | bytes 589824 | tf_op jit(solution)/shard_map/all_to_all | solution.py:318
  69.2 1.8 %final.1 = f32[3,48,128]{2,1,0:T(8,128)} custom-call(s32[1,48]{1,0:T(1,128)} %bitcast.27, f32[3,48,128]{2,1,0:T(8,128)} %far.1.far_ref, f32[4,48,3,128]{3,2,1,0:T(4,128)} %copy.10.part_ref), custom_call_target="tpu_custom_call" | custom-call | tf_op jit(solution)/shard_map/final/pallas_call | solution.py:321
  (6 shorter events, 0.0 us)
Async XLA Ops:
  6.5 45.5 %all-gather.2.cloned.1.call-start = ((), (), s32[]{:S(2)}) async-start(), calls=%async_computation.2 | async-start | bytes 1179648 | tf_op jit(solution)/shard_map/all_gather | solution.py:285
  9.1 9.2 %copy-start.1 = (f32[48,4,128]{2,1,0:T(4,128)S(1)}, f32[48,4,128]{2,1,0:T(4,128)}, u32[]{:S(2)}) copy-start(f32[48,4,128]{2,1,0:T(4,128)} %get-tuple-element.13.t0) | copy-start | bytes 294916
  9.1 32.7 %all-to-all-start = ((f32[8,48,4,128]{3,2,1,0:T(4,128)}), f32[8,48,4,128]{3,2,1,0:T(4,128)S(1)}, u32[]{:S(2)}, u32[]{:S(2)}) async-start(f32[8,48,4,128]{3,2,1,0:T(4,128)} %get-tuple-element.16), calls=%async_computation | async-start | bytes 1572864 | tf_op jit(solution)/shard_map/all_to_all | solution.py:283
  18.3 4.8 %collective-permute-start = (f32[48,4,128]{2,1,0:T(4,128)S(1)}, f32[48,4,128]{2,1,0:T(4,128)S(1)}, u32[]{:S(2)}, u32[]{:S(2)}) collective-permute-start(f32[48,4,128]{2,1,0:T(4,128)S(1)} %copy-done.1), channel_id=1, source_target_pairs={{0,8},{1,9},{2,10},{3,11},{4,12},{5,13},{6,14},{7,15},{8,16},{9,17... | collective-permute-start | bytes 294920 | tf_op jit(solution)/shard_map/ppermute | solution.py:284
  19.7 3.8 %collective-permute-start.1 = (f32[48,4,128]{2,1,0:T(4,128)S(1)}, f32[48,4,128]{2,1,0:T(4,128)S(1)}, u32[]{:S(2)}, u32[]{:S(2)}) collective-permute-start(f32[48,4,128]{2,1,0:T(4,128)S(1)} %copy-done.1), channel_id=1, source_target_pairs={{0,24},{1,25},{2,26},{3,27},{4,28},{5,29},{6,30},{7,31},{8,0},{9,1... | collective-permute-start | bytes 294920 | tf_op jit(solution)/shard_map/ppermute | solution.py:284
  21.2 5.9 %collective-permute-start.2 = (f32[48,4,128]{2,1,0:T(4,128)S(1)}, f32[48,4,128]{2,1,0:T(4,128)S(1)}, u32[]{:S(2)}, u32[]{:S(2)}) collective-permute-start(f32[48,4,128]{2,1,0:T(4,128)S(1)} %copy-done.1), channel_id=1, source_target_pairs={{0,16},{1,17},{2,18},{3,19},{4,20},{5,21},{6,22},{7,23},{8,24},{9,... | collective-permute-start | bytes 294920 | tf_op jit(solution)/shard_map/ppermute | solution.py:284
  23.1 3.9 %copy-start.2 = (f32[48,4,128]{2,1,0:T(4,128)}, f32[48,4,128]{2,1,0:T(4,128)S(1)}, u32[]{:S(2)}) copy-start(f32[48,4,128]{2,1,0:T(4,128)S(1)} %collective-permute-done.t1) | copy-start | bytes 294916
  23.4 3.6 %copy-start.3 = (f32[48,4,128]{2,1,0:T(4,128)}, f32[48,4,128]{2,1,0:T(4,128)S(1)}, u32[]{:S(2)}) copy-start(f32[48,4,128]{2,1,0:T(4,128)S(1)} %collective-permute-done.1.t2) | copy-start | bytes 294916
  27.0 0.6 copy-start.4
  41.9 0.9 %copy-start = (f32[8,48,4,128]{3,2,1,0:T(4,128)}, f32[8,48,4,128]{3,2,1,0:T(4,128)S(1)}, u32[]{:S(2)}) copy-start(f32[8,48,4,128]{3,2,1,0:T(4,128)S(1)} %all-to-all-done) | copy-start | bytes 2359300
  53.8 14.5 %all-to-all-start.1 = ((f32[4,48,3,128]{3,1,2,0:T(8,128)}), f32[4,48,3,128]{3,1,2,0:T(8,128)S(1)}, u32[]{:S(2)}, u32[]{:S(2)}) async-start(f32[4,48,3,128]{3,1,2,0:T(8,128)} %copy.9), calls=%async_computation.1 | async-start | bytes 589824 | tf_op jit(solution)/shard_map/all_to_all | solution.py:318
Sparse Core Ops, SparseCore 0:
  9.2 30.0 all-gather.1

commit v4 on v3

v4 whole, which is shorter than its diff:
```python
import jax
import jax.numpy as jnp
from jax import lax
from jax.experimental import pallas as pl
from jax.experimental.pallas import tpu as pltpu
from jax.sharding import PartitionSpec as P

NB = 48
PL = 128
K = 4
LC = 32
NY = 4
NZ = 8
NX = 4
SOFT = 0.01
UNROLL = 8
MIB = 1 << 20
F32 = jnp.float32
I32 = jnp.int32
BF16 = jnp.bfloat16
VMEM = pltpu.VMEM
SMEM = pltpu.SMEM


def vspec():
    return pl.BlockSpec(memory_space=VMEM)


def sspec():
    return pl.BlockSpec(memory_space=SMEM)


def column_of(row, n):
    square = jnp.broadcast_to(row, (n, n))
    diag = lax.broadcasted_iota(I32, (n, n), 0) == lax.broadcasted_iota(I32, (n, n), 1)
    return jnp.sum(jnp.where(diag, square, jnp.zeros_like(square)), axis=1, keepdims=True)


def pack_kernel(pos_ref, mass_ref, cnt_ref, dest_ref, near_ref, ctr_ref, cm_ref, src_ref, tgt_ref, cell_ref):
    counts = cnt_ref[...]
    cnt = column_of(counts, NB)
    near = near_ref[...]
    off = (near >= NB).astype(I32) + (near >= 2 * NB).astype(I32)
    dev = (dest_ref[...] + off - 1) & (NY * NZ - 1)
    code = (dev >> 3) * 512 + (dev & (NZ - 1)) * NB + (near - off * NB)
    gap = jnp.zeros((4, 64 - NB), I32)
    info = jnp.concatenate([code, gap, jnp.broadcast_to(counts, (4, NB)), gap], axis=1)
    lane = lax.broadcasted_iota(I32, (NB, PL), 1)
    weight = jnp.where(lane < cnt, mass_ref[...], 0.0)
    for c in range(3):
        value = pos_ref[c]
        tgt_ref[0:NB, c, :] = value
        for z in range(NZ):
            src_ref[z, :, c, :] = value
    for z in range(NZ):
        src_ref[z, :, 3, :] = weight
    tgt_ref[0:NB, 3, :] = jnp.zeros((NB, PL), F32)
    tgt_ref[NB] = info.astype(F32)
    for j in range(16):
        part = slice(j * PL, (j + 1) * PL)
        cell_ref[j, 0:3, :] = ctr_ref[:, part]
        cell_ref[j, 3:4, :] = cm_ref[0:1, part]


def far_kernel(place_ref, pos_ref, cnt_ref, list_ref, c0, c1, c2, c3, out_ref, pad):
    xs, cs = place_ref[0] >> 1, place_ref[0] & 1
    lane = lax.broadcasted_iota(I32, (NB, PL), 1)
    cnt = column_of(cnt_ref[...], NB)
    live = lane < cnt
    total = jnp.maximum(cnt, 1).astype(F32)
    pos = [pos_ref[c] for c in range(3)]
    centre = [jnp.sum(jnp.where(live, v, 0.0), axis=1, keepdims=True) / total for v in pos]
    diag = lax.broadcasted_iota(I32, (NB, PL), 0) == (lane & 63)
    ctr = [jnp.sum(jnp.where(diag, v, 0.0), axis=0, keepdims=True) for v in centre]
    wide = jnp.concatenate([list_ref[...], jnp.zeros((LC, PL - NB), I32)], axis=1)
    twice = wide + pltpu.roll(wide, 64, 1)
    half = lax.broadcasted_iota(I32, (1, PL), 1) < 64
    ids = [jnp.where(half, twice[2 * j : 2 * j + 1], twice[2 * j + 1 : 2 * j + 2]) for j in range(LC // 2)]
    ids = jnp.concatenate(ids, axis=0)
    slab = ids >> 11
    dx = ((slab >> 1) - xs) & (NX - 1)
    order = jnp.where(dx == 3, 1, jnp.where(dx == 0, 0, dx + 1))
    rows = (order * 2 + ((slab & 1) ^ cs)) * 16 + ((ids >> 7) & 15)
    lanes = ids & (PL - 1)
    tables = []
    for c in range(4):
        whole = jnp.concatenate([ref[i, :, c, :] for ref in (c0, c1, c2, c3) for i in range(2)], axis=0)
        whole = whole.T
        high = whole.astype(BF16)
        low = (whole - high.astype(F32)).astype(BF16)
        tables.append(jnp.concatenate([high, low], axis=1))
    tables = jnp.concatenate(tables, axis=0)
    sub = lax.broadcasted_iota(I32, (PL, 2 * PL), 0)
    got = [[] for _ in range(4)]
    for j in range(0, LC // 2, 2):
        r2 = jnp.concatenate([rows[j : j + 1], rows[j + 1 : j + 2]], axis=1)
        l2 = jnp.concatenate([lanes[j : j + 1], lanes[j + 1 : j + 2]], axis=1)
        hot = jnp.where(sub == r2, 1.0, 0.0).astype(BF16)
        hot = jnp.concatenate([hot, hot], axis=0)
        found = jnp.dot(tables, hot, preferred_element_type=F32)
        pick = sub == l2
        for c in range(4):
            value = jnp.sum(jnp.where(pick, found[c * PL : (c + 1) * PL], 0.0), axis=0, keepdims=True)
            got[c] += [value[:, :PL], value[:, PL:]]
    cells = [jnp.concatenate(v, axis=0) for v in got]
    rel = [ctr[c] - cells[c] for c in range(3)]
    dist = rel[0] * rel[0] + rel[1] * rel[1] + rel[2] * rel[2] + 1.0
    inv = lax.rsqrt(dist)
    cube = cells[3] * (inv * inv * inv)
    fifth = 3.0 * cube * (inv * inv)
    terms = [-(cube * rel[c]) for c in range(3)]
    for a, b in ((0, 0), (1, 1), (2, 2), (0, 1), (0, 2), (1, 2)):
        value = fifth * rel[a] * rel[b]
        if a == b:
            value = value - cube
        terms.append(value)
    terms = [jnp.sum(v, axis=0, keepdims=True) for v in terms]
    pad[...] = jnp.zeros((PL, PL), F32)
    for i, v in enumerate(terms):
        pad[i : i + 1, :] = v + pltpu.roll(v, 64, 1)
    back = pad[...].T
    field = [back[0:NB, i : i + 1] for i in range(3)]
    tide = [back[0:NB, 3 + i : 4 + i] for i in range(6)]
    offset = [pos[c] - centre[c] for c in range(3)]
    for c, (i, j, k) in enumerate(((0, 3, 4), (3, 1, 5), (4, 5, 2))):
        out_ref[c] = field[c] + tide[i] * offset[0] + tide[j] * offset[1] + tide[k] * offset[2]


def split3(v):
    high = v.astype(BF16).astype(F32)
    rest = v - high
    mid = rest.astype(BF16).astype(F32)
    return high, mid, rest - mid


def prep_kernel(y_ref, t0, t1, t2, t3, tall, tab, hold, sem):
    me = y_ref[0]
    wide = 2 * PL
    tiles = []
    for i, t in enumerate((t0, t1, t2, t3)):
        tall[i * NB : (i + 1) * NB] = t[0:NB]
        tiles.append(t[NB])
    left = lax.broadcasted_iota(I32, (4, PL), 1) < 64
    code, cnt = [], []
    for a, b in ((tiles[0], tiles[1]), (tiles[2], tiles[3])):
        code.append(jnp.where(left, a, pltpu.roll(b, 64, 1)))
        cnt.append(jnp.where(left, pltpu.roll(a, 64, 1), b))
    code = jnp.concatenate(code, axis=1).astype(I32)
    cnt = jnp.concatenate(cnt, axis=1)[0:1]
    lane = lax.broadcasted_iota(I32, (1, wide), 1)
    valid = (lane & 63) < NB
    flag = [jnp.where(((code[k : k + 1] >> 9) == me) & valid, 1.0, 0.0) for k in range(K)]
    local = [(code[k : k + 1] & 511).astype(F32) for k in range(K)]
    count = (flag[0] + flag[1]) + (flag[2] + flag[3])
    full = jnp.where(count > 2.5, 1.0, 0.0)
    half = jnp.where((count > 0.5) & (count < 2.5), 1.0, 0.0)
    marks = jnp.concatenate([full, half, jnp.zeros((14, wide), F32)], axis=0).astype(BF16)
    a = lax.broadcasted_iota(I32, (wide, wide), 0)
    b = lax.broadcasted_iota(I32, (wide, wide), 1)
    before = jnp.dot(marks, jnp.where(a < b, 1.0, 0.0).astype(BF16), preferred_element_type=F32)
    n_full = jnp.sum(full, axis=1, keepdims=True)
    n_half = jnp.sum(half, axis=1, keepdims=True)
    place = jnp.where(full > 0.5, before[0:1], jnp.where(half > 0.5, n_full + before[1:2], -1.0))
    moved = jnp.where(a == place.astype(I32), 1.0, 0.0).astype(BF16)
    group = lane >> 6
    step = jnp.where(group == 2, -1, jnp.where(group == 3, 2, group))
    bucket = lane & 63
    home = ((me - step) & (NY - 1)) * NB + bucket
    slot, ins, outs = [], jnp.zeros((1, wide), F32), jnp.zeros((1, wide), F32)
    for k in range(K):
        slot.append(jnp.where(flag[k] > 0.5, ins, count + outs))
        ins, outs = ins + flag[k], outs + (1.0 - flag[k])
    fields = []
    for j in range(K):
        pick = jnp.zeros((1, wide), F32)
        for k in range(K):
            pick = pick + jnp.where(slot[k] == float(j), local[k], 0.0)
        fields.append(pick)
    fields += [cnt, home.astype(F32), count, (group * NB + bucket).astype(F32)]
    load = jnp.concatenate(fields, axis=0)
    high = load.astype(BF16).astype(F32)
    both = jnp.concatenate([high, load - high], axis=0).astype(BF16)
    out = lax.dot_general(both, moved, (((1,), (1,)), ((), ())), preferred_element_type=F32)
    out = out[0:8] + out[8:16]
    sizes = jnp.where(
        lax.broadcasted_iota(I32, (8, wide), 0) == 0,
        jnp.broadcast_to(n_full, (8, wide)),
        jnp.broadcast_to(n_half, (8, wide)),
    )
    hold[...] = jnp.concatenate([out, sizes], axis=0).astype(I32)
    copy = pltpu.make_async_copy(hold, tab, sem)
    copy.start()
    copy.wait()


def near_kernel(tab, tall, src_ref, out_ref):
    out_ref[...] = jnp.zeros((NY * NB, 4, PL), F32)
    sub4 = lax.broadcasted_iota(I32, (4, PL), 0)
    lane4 = lax.broadcasted_iota(I32, (4, PL), 1)
    spatial = sub4 < 3
    one = jnp.ones((4, PL), F32)
    zero4 = jnp.zeros((4, PL), F32)
    zero8 = jnp.zeros((8, PL), F32)

    def square(v):
        return jnp.sum(jnp.where(spatial, v * v, 0.0), axis=0, keepdims=True)

    def mix(a, b):
        return jnp.where(spatial, a, b)

    def stack(*v):
        return jnp.concatenate(v, axis=0).astype(BF16)

    def job(e, width):
        n = tab[6, e]
        t = tall[tab[7, e]]
        th, tm, tl = split3(t)
        qh, qm, ql = split3(square(t))
        u = stack(mix(th, one), mix(th, one), mix(tm, one), mix(tm, qh), mix(th, qm), mix(tl, ql), zero8)
        vs, gs = [], []
        for k in range(width):
            s = src_ref[tab[k, e]]
            flag = (k < n).astype(F32)
            sh, sm, sl = split3(-2.0 * s)
            qh, qm, ql = split3(square(s) + SOFT)
            vs.append(stack(mix(sh, qh), mix(sm, qm), mix(sh, ql), mix(sm, one), mix(sl, one), mix(sh, one), zero8))
            w = s[3:4] * flag
            gs.append(stack(*split3(mix(s * w, w)), zero4))
        v = jnp.concatenate(vs, axis=1)
        g = jnp.concatenate(gs, axis=1)
        dist = lax.dot_general(v, u, (((0,), (0,)), ((), ())), preferred_element_type=F32)
        inv = lax.rsqrt(dist)
        f = inv * inv * inv
        high = f.astype(BF16)
        low = (f - high.astype(F32)).astype(BF16)
        o = jnp.dot(g, high, preferred_element_type=F32) + jnp.dot(g, low, preferred_element_type=F32)
        a = o[0:4] + o[4:8] + o[8:12]
        out_ref[tab[5, e]] = jnp.where(lane4 < tab[4, e], a - t * a[3:4], 0.0)

    n_full = tab[8, 0]
    n_half = tab[9, 0]

    def whole(i, _):
        for j in range(UNROLL):
            job(jnp.minimum(UNROLL * i + j, n_full - 1), 4)

    def part(i, _):
        for j in range(UNROLL):
            job(n_full + jnp.minimum(UNROLL * i + j, n_half - 1), 2)

    lax.fori_loop(0, (n_full + UNROLL - 1) // UNROLL, whole, None)
    lax.fori_loop(0, (n_half + UNROLL - 1) // UNROLL, part, None)


def final_kernel(cnt_ref, far_ref, part_ref, out_ref):
    live = lax.broadcasted_iota(I32, (NB, PL), 1) < column_of(cnt_ref[...], NB)
    near = (part_ref[0] + part_ref[1]) + (part_ref[2] + part_ref[3])
    for c in range(3):
        out_ref[c] = jnp.where(live, far_ref[c] + near[:, c, :], 0.0)


def along_y(k):
    return [(NZ * y + z, NZ * ((y + k) % NY) + z) for y in range(NY) for z in range(NZ)]


def along_x(k):
    return [(2 * x + c, 2 * ((x + k) % NX) + c) for x in range(NX) for c in range(2)]


def call(kernel, outs, in_specs, out_specs, name, mib, scratch=()):
    return pl.pallas_call(
        kernel,
        out_shape=[jax.ShapeDtypeStruct(shape, dtype) for shape, dtype in outs],
        in_specs=in_specs,
        out_specs=out_specs,
        scratch_shapes=scratch,
        compiler_params=pltpu.CompilerParams(vmem_limit_bytes=mib * MIB),
        name=name,
    )


def per_device(positions, masses, counts, dest_ids, near_list, cell_list, cell_centers, cell_mass):
    pos = jnp.transpose(positions[0], (1, 0, 2))
    cnt = counts[0]
    src, tgt, cells = call(
        pack_kernel,
        (((NZ, NB, 4, PL), F32), ((NB + 1, 4, PL), F32), ((16, 4, PL), F32)),
        [vspec()] * 7,
        [vspec()] * 3,
        "pack",
        8,
    )(pos, masses[0], cnt, dest_ids, near_list[0].T, cell_centers, cell_mass[None])
    z_rows = [[NZ * y + z for z in range(NZ)] for y in range(NY)]
    y_rows = [[NZ * y + z for y in range(NY)] for z in range(NZ)]
    window = lax.all_to_all(src, "space", 0, 0, axis_index_groups=z_rows, tiled=True)
    tgts = [tgt] + [lax.ppermute(tgt, "space", along_y(k)) for k in (1, -1, 2)]
    pair = jnp.stack([cells, lax.ppermute(cells, "slab", [(i, i ^ 1) for i in range(2 * NX)])])
    pairs = [pair] + [lax.ppermute(pair, "slab", along_x(k)) for k in (1, -1, 2)]
    me = (lax.axis_index("space") // NZ).astype(I32).reshape(1)
    place = lax.axis_index("slab").astype(I32).reshape(1)
    tall, tab = call(
        prep_kernel,
        (((NY * NB, 4, PL), F32), ((16, 2 * PL), I32)),
        [sspec()] + [vspec()] * 4,
        [vspec(), sspec()],
        "prep",
        8,
        [pltpu.VMEM((16, 2 * PL), I32), pltpu.SemaphoreType.DMA],
    )(me, *tgts)
    (part,) = call(
        near_kernel,
        (((NY * NB, 4, PL), F32),),
        [sspec()] + [vspec()] * 2,
        [vspec()],
        "near",
        24,
    )(tab, tall, window.reshape(NZ * NB, 4, PL))
    *pairs, part = lax.optimization_barrier((*pairs, part))
    (far,) = call(
        far_kernel,
        (((3, NB, PL), F32),),
        [sspec()] + [vspec()] * 7,
        [vspec()],
        "far",
        16,
        [pltpu.VMEM((PL, PL), F32)],
    )(place, pos, cnt, cell_list[0].T, *pairs)
    back = lax.all_to_all(
        part.reshape(NY, NB, 4, PL), "space", 0, 0, axis_index_groups=y_rows, tiled=True
    )
    (out,) = call(
        final_kernel,
        (((3, NB, PL), F32),),
        [vspec()] * 3,
        [vspec()],
        "final",
        8,
    )(cnt, far, back)
    return jnp.transpose(out, (1, 0, 2))[None]


def solution(mesh):
    in_specs = (
        P("slab", "space", None, None),
        P("slab", "space", None),
        P("slab", "space", None),
        P("slab", "space"),
        P("slab", "space", None),
        P("slab", "space", None),
        P(None, "slab"),
        P("slab"),
    )
    return jax.shard_map(
        per_device,
        mesh=mesh,
        in_specs=in_specs,
        out_specs=P("slab", "space", None, None),
        check_vma=False,
    )
```

time: 77.7 us -> 61.6 us (0.79)
  the two profiles are of different devices: /device:TPU:1 before, /device:TPU:3 now
where the time goes in v4:
time: 61.6 us; the launch traced here: 61.1 us
  starting transfers between devices  23.8 us (39%)
  waiting for transfers between devices  19.7 us (32%)
  Pallas kernels  13.7 us (22%)
  local copies, waits for them, and re-layouts  3.77 us (6%)
    all_to_all x1, waiting for transfers between devices, per_device(): lax.all_to_all(src, 'space', 0, 0, axis_index_groups=z_rows, tiled=True)  11.8 us
    all_to_all x1, starting transfers between devices, per_device(): lax.all_to_all(src, 'space', 0, 0, axis_index_groups=z_rows, tiled=True)  8.19 us
    pallas_call x1, Pallas kernels, per_device(): call(near_kernel, (((NY * NB, 4, PL), F32),), [sspec()] + [vspec()] * 2,...  8.12 us
    all_to_all x1, waiting for transfers between devices, per_device(): lax.all_to_all(part.reshape(NY, NB, 4, PL), 'space', 0, 0, axis_index_gro...  7.01 us
    all_to_all x1, starting transfers between devices, per_device(): lax.all_to_all(part.reshape(NY, NB, 4, PL), 'space', 0, 0, axis_index_gro...  6.91 us
    ppermute x3, starting transfers between devices, per_device(): tgts = [tgt] + [lax.ppermute(tgt, 'space', along_y(k)) for k in (1, -1, 2)]  4.39 us
    unnamed x18, local copies, waits for them, and re-layouts  3.77 us
    ppermute x3, starting transfers between devices, per_device(): lax.ppermute(pair, 'slab', along_x(k))  3.4 us
  transfers between devices with their start and end apart: 9, of which 4 were waited for; matrix products, arithmetic and copies ran while one was open for 0% of the time, Pallas kernels for 19%

profile of v4, /device:TPU:3, one launch (start us, length us, event | category | flops | bytes accessed | tf_op | source)
XLA Modules:
  0.0 61.1 jit_solution(1005076427880012274)
XLA Ops:
  0.0 0.7 %copy-done.5 = f32[2048]{0:T(1024)S(1)} copy-done((f32[2048]{0:T(1024)S(1)}, f32[2048]{0:T(1024)}, u32[]{:S(2)}) %copy-start.5) | copy-done | bytes 8216
  0.7 0.9 %copy-done = f32[1,48,3,128]{3,1,2,0:T(8,128)S(1)} copy-done((f32[1,48,3,128]{3,1,2,0:T(8,128)S(1)}, f32[1,48,3,128]{3,1,2,0:T(8,128)}, u32[]{:S(2)}) %copy-start) | copy-done | bytes 73752
  1.6 0.8 %copy-done.2 = f32[3,2048]{1,0:T(4,128)S(1)} copy-done((f32[3,2048]{1,0:T(4,128)S(1)}, f32[3,2048]{1,0:T(4,128)}, u32[]{:S(2)}) %copy-start.2) | copy-done | bytes 24600
  2.3 0.7 %copy-done.3 = f32[1,48,128]{2,1,0:T(8,128)S(1)} copy-done((f32[1,48,128]{2,1,0:T(8,128)S(1)}, f32[1,48,128]{2,1,0:T(8,128)}, u32[]{:S(2)}) %copy-start.3) | copy-done | bytes 24600
  3.1 0.7 %copy-done.7 = s32[1,48,4]{1,2,0:T(4,128)S(1)} copy-done((s32[1,48,4]{1,2,0:T(4,128)S(1)}, s32[1,48,4]{1,2,0:T(4,128)}, u32[]{:S(2)}) %copy-start.7) | copy-done | bytes 792
  3.8 1.4 %pack.1 = (f32[8,48,4,128]{3,2,1,0:T(4,128)}, f32[49,4,128]{2,1,0:T(4,128)S(1)}, f32[16,4,128]{2,1,0:T(4,128)S(1)}) custom-call(f32[3,48,128]{2,1,0:T(8,128)S(1)} %bitcast.22, f32[48,128]{1,0:T(8,128)S(1)} %bitcast.25, s32[1,48]{1,0:T(1,128)S(1)} %bitcast.28, s32[1,48]{1,0:T(1,128)S(1)} %copy-done.8, s32[4,48]{1,0:T(4,128)S(1)} %bitcast.31, ...), custom_call_target="tpu_custom_call" | custom-call | tf_op jit(solution)/shard_map/pack/pallas_call | solution.py:285
  5.1 8.2 %all-to-all-start = ((f32[8,48,4,128]{3,2,1,0:T(4,128)}), f32[8,48,4,128]{3,2,1,0:T(4,128)S(1)}, u32[]{:S(2)}, u32[]{:S(2)}) async-start(f32[8,48,4,128]{3,2,1,0:T(4,128)} %get-tuple-element.19), calls=%async_computation | async-start | bytes 1572864 | tf_op jit(solution)/shard_map/all_to_all | solution.py:295
  13.3 1.0 %collective-permute-start = (f32[16,4,128]{2,1,0:T(4,128)S(1)}, f32[16,4,128]{2,1,0:T(4,128)S(1)}, u32[]{:S(2)}, u32[]{:S(2)}) collective-permute-start(f32[16,4,128]{2,1,0:T(4,128)S(1)} %get-tuple-element.15), channel_id=1, source_target_pairs={{0,32},{32,0},{64,96},{96,64},{128,160},{160,128},{192,224},{224,1... | collective-permute-start | bytes 98312 | tf_op jit(solution)/shard_map/ppermute | solution.py:297
  14.3 2.9 %collective-permute-start.6 = (f32[49,4,128]{2,1,0:T(4,128)S(1)}, f32[49,4,128]{2,1,0:T(4,128)S(1)}, u32[]{:S(2)}, u32[]{:S(2)}) collective-permute-start(f32[49,4,128]{2,1,0:T(4,128)S(1)} %get-tuple-element.16.t0), channel_id=1, source_target_pairs={{0,16},{1,17},{2,18},{3,19},{4,20},{5,21},{6,22},{7,23},{8,24},{9,... | collective-permute-start | bytes 301064 | tf_op jit(solution)/shard_map/ppermute | solution.py:296
  17.2 0.8 %collective-permute-start.5 = (f32[49,4,128]{2,1,0:T(4,128)S(1)}, f32[49,4,128]{2,1,0:T(4,128)S(1)}, u32[]{:S(2)}, u32[]{:S(2)}) collective-permute-start(f32[49,4,128]{2,1,0:T(4,128)S(1)} %get-tuple-element.16.t0), channel_id=1, source_target_pairs={{0,24},{1,25},{2,26},{3,27},{4,28},{5,29},{6,30},{7,31},{8,0},{9,1... | collective-permute-start | bytes 301064 | tf_op jit(solution)/shard_map/ppermute | solution.py:296
  18.0 0.7 %collective-permute-start.4 = (f32[49,4,128]{2,1,0:T(4,128)S(1)}, f32[49,4,128]{2,1,0:T(4,128)S(1)}, u32[]{:S(2)}, u32[]{:S(2)}) collective-permute-start(f32[49,4,128]{2,1,0:T(4,128)S(1)} %get-tuple-element.16.t0), channel_id=1, source_target_pairs={{0,8},{1,9},{2,10},{3,11},{4,12},{5,13},{6,14},{7,15},{8,16},{9,17... | collective-permute-start | bytes 301064 | tf_op jit(solution)/shard_map/ppermute | solution.py:296
  18.7 1.9 %collective-permute-start.3 = (f32[2,16,4,128]{3,2,1,0:T(4,128)S(1)}, f32[2,16,4,128]{3,2,1,0:T(4,128)S(1)}, u32[]{:S(2)}, u32[]{:S(2)}) collective-permute-start(f32[2,16,4,128]{3,2,1,0:T(4,128)S(1)} %pad_maximum_fusion.c0), channel_id=1, source_target_pairs={{0,128},{32,160},{64,192},{96,224},{128,0},{160,32},{192,64},{224,... | collective-permute-start | bytes 196616 | tf_op jit(solution)/shard_map/ppermute | solution.py:298
  20.6 1.2 %collective-permute-start.2 = (f32[2,16,4,128]{3,2,1,0:T(4,128)S(1)}, f32[2,16,4,128]{3,2,1,0:T(4,128)S(1)}, u32[]{:S(2)}, u32[]{:S(2)}) collective-permute-start(f32[2,16,4,128]{3,2,1,0:T(4,128)S(1)} %pad_maximum_fusion.c0), channel_id=1, source_target_pairs={{0,192},{32,224},{64,0},{96,32},{128,64},{160,96},{192,128},{224,1... | collective-permute-start | bytes 196616 | tf_op jit(solution)/shard_map/ppermute | solution.py:298
  21.8 0.3 collective-permute-start.1
  22.1 0.6 collective-permute-done.5.t2
  22.7 0.3 collective-permute-done.4.t1
  23.0 2.1 %prep.1 = (f32[192,4,128]{2,1,0:T(4,128)S(1)}, s32[16,256]{1,0:T(8,128)S(1)}) custom-call(s32[1]{0:T(128)} %bitcast.13.y_ref, f32[49,4,128]{2,1,0:T(4,128)S(1)} %get-tuple-element.16.t0, f32[49,4,128]{2,1,0:T(4,128)S(1)} %collective-permute-done.4.t1, f32[49,4,128]{2,1,0:T(4,128)S(1)} %collective-permute-done.5.t2, f32[49,4,128]{2,1,0:T(4,128)S(1)} %collective-permute-done.6.t3), custom_call_target="tpu_custom_call" | custom-call | tf_op jit(solution)/shard_map/prep/pallas_call | solution.py:301
  25.0 11.8 %all-to-all-done = f32[8,48,4,128]{3,2,1,0:T(4,128)S(1)} async-done(((f32[8,48,4,128]{3,2,1,0:T(4,128)}), f32[8,48,4,128]{3,2,1,0:T(4,128)S(1)}, u32[]{:S(2)}, u32[]{:S(2)}) %all-to-all-start) | async-done | bytes 786464 | tf_op jit(solution)/shard_map/all_to_all | solution.py:295
  36.9 8.1 %near.1 = f32[192,4,128]{2,1,0:T(4,128)} custom-call(s32[16,256]{1,0:T(8,128)S(1)} %get-tuple-element.17.tab, f32[192,4,128]{2,1,0:T(4,128)S(1)} %get-tuple-element.18.tall, f32[384,4,128]{2,1,0:T(4,128)S(1)} %bitcast.21), custom_call_target="tpu_custom_call" | custom-call | tf_op jit(solution)/shard_map/near/pallas_call | solution.py:310
  45.0 0.0 copy-start.1
  45.0 6.9 %all-to-all-start.1 = ((f32[4,48,4,128]{3,2,1,0:T(4,128)}), f32[4,48,4,128]{3,2,1,0:T(4,128)S(1)}, u32[]{:S(2)}, u32[]{:S(2)}) async-start(f32[4,48,4,128]{3,2,1,0:T(4,128)} %bitcast.15), calls=%async_computation.1 | async-start | bytes 786432 | tf_op jit(solution)/shard_map/all_to_all | solution.py:328
  52.0 1.4 %far.1.far_ref = f32[3,48,128]{2,1,0:T(8,128)S(1)} custom-call(s32[1]{0:T(128)} %bitcast.1.place_ref, f32[3,48,128]{2,1,0:T(8,128)S(1)} %bitcast.23, s32[1,48]{1,0:T(1,128)S(1)} %bitcast.29, s32[32,48]{1,0:T(8,128)S(1)} %bitcast.26, f32[2,16,4,128]{3,2,1,0:T(4,128)S(1)} %pad_maximum_fusion.c0, f32[2,16,4,128]{3,2,1,0:T(4,128)S(1)} %collective-permute-done.1.c1, ...), custom_call_target="tpu_custom_call" | custom-call | tf_op jit(solution)/shard_map/far/pallas_call | solution.py:319
  53.4 7.0 %all-to-all-done.1.part_ref = f32[4,48,4,128]{3,2,1,0:T(4,128)S(1)} async-done(((f32[4,48,4,128]{3,2,1,0:T(4,128)}), f32[4,48,4,128]{3,2,1,0:T(4,128)S(1)}, u32[]{:S(2)}, u32[]{:S(2)}) %all-to-all-start.1) | async-done | bytes 393248 | tf_op jit(solution)/shard_map/all_to_all | solution.py:328
  60.4 0.7 %final.1 = f32[3,48,128]{2,1,0:T(8,128)} custom-call(s32[1,48]{1,0:T(1,128)S(1)} %bitcast.30, f32[3,48,128]{2,1,0:T(8,128)S(1)} %far.1.far_ref, f32[4,48,4,128]{3,2,1,0:T(4,128)S(1)} %all-to-all-done.1.part_ref), custom_call_target="tpu_custom_call" | custom-call | tf_op jit(solution)/shard_map/final/pallas_call | solution.py:331
  (18 shorter events, 0.1 us)
Async XLA Ops:
  0.0 0.7 %copy-start.5 = (f32[2048]{0:T(1024)S(1)}, f32[2048]{0:T(1024)}, u32[]{:S(2)}) copy-start(f32[2048]{0:T(1024)} %param.15) | copy-start | bytes 24580
  0.0 0.7 %copy-start.6 = (s32[1,1,48]{2,1,0:T(1,128)S(1)}, s32[1,1,48]{2,1,0:T(1,128)}, u32[]{:S(2)}) copy-start(s32[1,1,48]{2,1,0:T(1,128)} %param.10) | copy-start | bytes 580
  0.0 0.7 %copy-start.8 = (s32[1,48]{1,0:T(1,128)S(1)}, s32[1,48]{1,0:T(1,128)}, u32[]{:S(2)}) copy-start(s32[1,48]{1,0:T(1,128)} %dest_ref.1) | copy-start | bytes 580
  0.7 0.9 %copy-start = (f32[1,48,3,128]{3,1,2,0:T(8,128)S(1)}, f32[1,48,3,128]{3,1,2,0:T(8,128)}, u32[]{:S(2)}) copy-start(f32[1,48,3,128]{3,1,2,0:T(8,128)} %param.8) | copy-start | bytes 221188
  1.6 0.8 %copy-start.2 = (f32[3,2048]{1,0:T(4,128)S(1)}, f32[3,2048]{1,0:T(4,128)}, u32[]{:S(2)}) copy-start(f32[3,2048]{1,0:T(4,128)} %ctr_ref.1) | copy-start | bytes 73732
  2.3 0.7 %copy-start.3 = (f32[1,48,128]{2,1,0:T(8,128)S(1)}, f32[1,48,128]{2,1,0:T(8,128)}, u32[]{:S(2)}) copy-start(f32[1,48,128]{2,1,0:T(8,128)} %param.9) | copy-start | bytes 73732
  3.1 0.7 %copy-start.7 = (s32[1,48,4]{1,2,0:T(4,128)S(1)}, s32[1,48,4]{1,2,0:T(4,128)}, u32[]{:S(2)}) copy-start(s32[1,48,4]{1,2,0:T(4,128)} %param.12) | copy-start | bytes 2308
  5.1 31.8 %all-to-all-start = ((f32[8,48,4,128]{3,2,1,0:T(4,128)}), f32[8,48,4,128]{3,2,1,0:T(4,128)S(1)}, u32[]{:S(2)}, u32[]{:S(2)}) async-start(f32[8,48,4,128]{3,2,1,0:T(4,128)} %get-tuple-element.19), calls=%async_computation | async-start | bytes 1572864 | tf_op jit(solution)/shard_map/all_to_all | solution.py:295
  13.3 5.4 %collective-permute-start = (f32[16,4,128]{2,1,0:T(4,128)S(1)}, f32[16,4,128]{2,1,0:T(4,128)S(1)}, u32[]{:S(2)}, u32[]{:S(2)}) collective-permute-start(f32[16,4,128]{2,1,0:T(4,128)S(1)} %get-tuple-element.15), channel_id=1, source_target_pairs={{0,32},{32,0},{64,96},{96,64},{128,160},{160,128},{192,224},{224,1... | collective-permute-start | bytes 98312 | tf_op jit(solution)/shard_map/ppermute | solution.py:297
  14.3 7.5 %collective-permute-start.6 = (f32[49,4,128]{2,1,0:T(4,128)S(1)}, f32[49,4,128]{2,1,0:T(4,128)S(1)}, u32[]{:S(2)}, u32[]{:S(2)}) collective-permute-start(f32[49,4,128]{2,1,0:T(4,128)S(1)} %get-tuple-element.16.t0), channel_id=1, source_target_pairs={{0,16},{1,17},{2,18},{3,19},{4,20},{5,21},{6,22},{7,23},{8,24},{9,... | collective-permute-start | bytes 301064 | tf_op jit(solution)/shard_map/ppermute | solution.py:296
  17.2 5.5 %collective-permute-start.5 = (f32[49,4,128]{2,1,0:T(4,128)S(1)}, f32[49,4,128]{2,1,0:T(4,128)S(1)}, u32[]{:S(2)}, u32[]{:S(2)}) collective-permute-start(f32[49,4,128]{2,1,0:T(4,128)S(1)} %get-tuple-element.16.t0), channel_id=1, source_target_pairs={{0,24},{1,25},{2,26},{3,27},{4,28},{5,29},{6,30},{7,31},{8,0},{9,1... | collective-permute-start | bytes 301064 | tf_op jit(solution)/shard_map/ppermute | solution.py:296
  18.0 5.0 %collective-permute-start.4 = (f32[49,4,128]{2,1,0:T(4,128)S(1)}, f32[49,4,128]{2,1,0:T(4,128)S(1)}, u32[]{:S(2)}, u32[]{:S(2)}) collective-permute-start(f32[49,4,128]{2,1,0:T(4,128)S(1)} %get-tuple-element.16.t0), channel_id=1, source_target_pairs={{0,8},{1,9},{2,10},{3,11},{4,12},{5,13},{6,14},{7,15},{8,16},{9,17... | collective-permute-start | bytes 301064 | tf_op jit(solution)/shard_map/ppermute | solution.py:296
  18.7 26.3 %collective-permute-start.3 = (f32[2,16,4,128]{3,2,1,0:T(4,128)S(1)}, f32[2,16,4,128]{3,2,1,0:T(4,128)S(1)}, u32[]{:S(2)}, u32[]{:S(2)}) collective-permute-start(f32[2,16,4,128]{3,2,1,0:T(4,128)S(1)} %pad_maximum_fusion.c0), channel_id=1, source_target_pairs={{0,128},{32,160},{64,192},{96,224},{128,0},{160,32},{192,64},{224,... | collective-permute-start | bytes 196616 | tf_op jit(solution)/shard_map/ppermute | solution.py:298
  20.6 24.4 %collective-permute-start.2 = (f32[2,16,4,128]{3,2,1,0:T(4,128)S(1)}, f32[2,16,4,128]{3,2,1,0:T(4,128)S(1)}, u32[]{:S(2)}, u32[]{:S(2)}) collective-permute-start(f32[2,16,4,128]{3,2,1,0:T(4,128)S(1)} %pad_maximum_fusion.c0), channel_id=1, source_target_pairs={{0,192},{32,224},{64,0},{96,32},{128,64},{160,96},{192,128},{224,1... | collective-permute-start | bytes 196616 | tf_op jit(solution)/shard_map/ppermute | solution.py:298
  21.8 23.2 %collective-permute-start.1 = (f32[2,16,4,128]{3,2,1,0:T(4,128)S(1)}, f32[2,16,4,128]{3,2,1,0:T(4,128)S(1)}, u32[]{:S(2)}, u32[]{:S(2)}) collective-permute-start(f32[2,16,4,128]{3,2,1,0:T(4,128)S(1)} %pad_maximum_fusion.c0), channel_id=1, source_target_pairs={{0,64},{32,96},{64,128},{96,160},{128,192},{160,224},{192,0},{224,... | collective-permute-start | bytes 196616 | tf_op jit(solution)/shard_map/ppermute | solution.py:298
  45.0 6.9 %copy-start.1 = (f32[1,48,3,128]{3,1,2,0:T(8,128)S(1)}, f32[1,48,3,128]{3,1,2,0:T(8,128)}, u32[]{:S(2)}) copy-start(f32[1,48,3,128]{3,1,2,0:T(8,128)} %param.8) | copy-start | bytes 221188
  45.0 6.9 %copy-start.4 = (s32[1,48,32]{1,2,0:T(8,128)S(1)}, s32[1,48,32]{1,2,0:T(8,128)}, u32[]{:S(2)}) copy-start(s32[1,48,32]{1,2,0:T(8,128)} %param.13) | copy-start | bytes 18436
  45.0 15.3 %all-to-all-start.1 = ((f32[4,48,4,128]{3,2,1,0:T(4,128)}), f32[4,48,4,128]{3,2,1,0:T(4,128)S(1)}, u32[]{:S(2)}, u32[]{:S(2)}) async-start(f32[4,48,4,128]{3,2,1,0:T(4,128)} %bitcast.15), calls=%async_computation.1 | async-start | bytes 786432 | tf_op jit(solution)/shard_map/all_to_all | solution.py:328

commit v5 on v4

--- a/solution.py
+++ b/solution.py
@@ -1,3 +1,5 @@
+import functools
+
 import jax
 import jax.numpy as jnp
 from jax import lax
@@ -36,7 +38,14 @@
     return jnp.sum(jnp.where(diag, square, jnp.zeros_like(square)), axis=1, keepdims=True)
 
 
-def pack_kernel(pos_ref, mass_ref, cnt_ref, dest_ref, near_ref, ctr_ref, cm_ref, src_ref, tgt_ref, cell_ref):
+def pack_kernel(*refs):
+    ins, (src_ref, tgt_ref, cell_ref), holds, sem = refs[:7], refs[7:10], refs[10:17], refs[17]
+    copies = [pltpu.make_async_copy(ins[i], holds[i], sem.at[i]) for i in range(7)]
+    for copy in copies:
+        copy.start()
+    for copy in copies:
+        copy.wait()
+    pos_ref, mass_ref, cnt_ref, dest_ref, near_ref, ctr_ref, cm_ref = holds
     counts = cnt_ref[...]
     cnt = column_of(counts, NB)
     near = near_ref[...]
@@ -154,18 +163,21 @@
     count = (flag[0] + flag[1]) + (flag[2] + flag[3])
     full = jnp.where(count > 2.5, 1.0, 0.0)
     half = jnp.where((count > 0.5) & (count < 2.5), 1.0, 0.0)
-    marks = jnp.concatenate([full, half, jnp.zeros((14, wide), F32)], axis=0).astype(BF16)
+    group = lane >> 6
+    mine = group == 0
+    lists = [jnp.where(mine, 0.0, v) for v in (full, half)] + [jnp.where(mine, v, 0.0) for v in (full, half)]
+    marks = jnp.concatenate(lists + [jnp.zeros((12, wide), F32)], axis=0).astype(BF16)
     a = lax.broadcasted_iota(I32, (wide, wide), 0)
     b = lax.broadcasted_iota(I32, (wide, wide), 1)
     before = jnp.dot(marks, jnp.where(a < b, 1.0, 0.0).astype(BF16), preferred_element_type=F32)
-    n_full = jnp.sum(full, axis=1, keepdims=True)
-    n_half = jnp.sum(half, axis=1, keepdims=True)
-    place = jnp.where(full > 0.5, before[0:1], jnp.where(half > 0.5, n_full + before[1:2], -1.0))
+    sizes = [jnp.sum(v, axis=1, keepdims=True) for v in lists]
+    place, begin = jnp.full((1, wide), -1.0, F32), jnp.zeros((1, 1), F32)
+    for i, v in enumerate(lists):
+        place = jnp.where(v > 0.5, begin + before[i : i + 1], place)
+        begin = begin + sizes[i]
     moved = jnp.where(a == place.astype(I32), 1.0, 0.0).astype(BF16)
-    group = lane >> 6
-    step = jnp.where(group == 2, -1, jnp.where(group == 3, 2, group))
     bucket = lane & 63
-    home = ((me - step) & (NY - 1)) * NB + bucket
+    home = jnp.where(mine, bucket, (group - 1) * NB + bucket)
     slot, ins, outs = [], jnp.zeros((1, wide), F32), jnp.zeros((1, wide), F32)
     for k in range(K):
         slot.append(jnp.where(flag[k] > 0.5, ins, count + outs))
@@ -182,19 +194,16 @@
     both = jnp.concatenate([high, load - high], axis=0).astype(BF16)
     out = lax.dot_general(both, moved, (((1,), (1,)), ((), ())), preferred_element_type=F32)
     out = out[0:8] + out[8:16]
-    sizes = jnp.where(
-        lax.broadcasted_iota(I32, (8, wide), 0) == 0,
-        jnp.broadcast_to(n_full, (8, wide)),
-        jnp.broadcast_to(n_half, (8, wide)),
-    )
+    sizes = jnp.concatenate([jnp.broadcast_to(v, (1, wide)) for v in sizes + [begin] * 4], axis=0)
     hold[...] = jnp.concatenate([out, sizes], axis=0).astype(I32)
     copy = pltpu.make_async_copy(hold, tab, sem)
     copy.start()
     copy.wait()
 
 
-def near_kernel(tab, tall, src_ref, out_ref):
-    out_ref[...] = jnp.zeros((NY * NB, 4, PL), F32)
+def near_kernel(first, tab, tall, src_ref, *refs):
+    outs, out_ref = refs[:-1], refs[-1]
+    out_ref[...] = jnp.zeros(out_ref.shape, F32)
     sub4 = lax.broadcasted_iota(I32, (4, PL), 0)
     lane4 = lax.broadcasted_iota(I32, (4, PL), 1)
     spatial = sub4 < 3
@@ -233,30 +242,33 @@
         f = inv * inv * inv
         high = f.astype(BF16)
         low = (f - high.astype(F32)).astype(BF16)
-        o = jnp.dot(g, high, preferred_element_type=F32) + jnp.dot(g, low, preferred_element_type=F32)
+        o = jnp.dot(g, jnp.concatenate([high, low], axis=1), preferred_element_type=F32)
+        o = o[:, :PL] + o[:, PL:]
         a = o[0:4] + o[4:8] + o[8:12]
         out_ref[tab[5, e]] = jnp.where(lane4 < tab[4, e], a - t * a[3:4], 0.0)
 
-    n_full = tab[8, 0]
-    n_half = tab[9, 0]
-
-    def whole(i, _):
-        for j in range(UNROLL):
-            job(jnp.minimum(UNROLL * i + j, n_full - 1), 4)
-
-    def part(i, _):
-        for j in range(UNROLL):
-            job(n_full + jnp.minimum(UNROLL * i + j, n_half - 1), 2)
-
-    lax.fori_loop(0, (n_full + UNROLL - 1) // UNROLL, whole, None)
-    lax.fori_loop(0, (n_half + UNROLL - 1) // UNROLL, part, None)
-
-
-def final_kernel(cnt_ref, far_ref, part_ref, out_ref):
+    sizes = [tab[8 + i, 0] for i in range(4)]
+
+    def run(begin, size, width, step):
+        def body(i, _):
+            for j in range(step):
+                job(begin + jnp.minimum(step * i + j, size - 1), width)
+
+        lax.fori_loop(0, (size + step - 1) // step, body, None)
+
+    begin = jnp.int32(0) if first else sizes[0] + sizes[1]
+    n_full, n_half = (sizes[0], sizes[1]) if first else (sizes[2], sizes[3])
+    run(begin, n_full, 4, UNROLL)
+    run(begin + n_full, n_half, 2, UNROLL // 2)
+    for i, o in enumerate(outs):
+        o[...] = out_ref[i * NB : (i + 1) * NB]
+
+
+def final_kernel(cnt_ref, far_ref, p0, p1, p2, p3, out_ref):
     live = lax.broadcasted_iota(I32, (NB, PL), 1) < column_of(cnt_ref[...], NB)
-    near = (part_ref[0] + part_ref[1]) + (part_ref[2] + part_ref[3])
     for c in range(3):
-        out_ref[c] = jnp.where(live, far_ref[c] + near[:, c, :], 0.0)
+        near = (p0[:, c, :] + p1[:, c, :]) + (p2[:, c, :] + p3[:, c, :])
+        out_ref[c] = jnp.where(live, far_ref[c] + near, 0.0)
 
 
 def along_y(k):
@@ -285,13 +297,22 @@
     src, tgt, cells = call(
         pack_kernel,
         (((NZ, NB, 4, PL), F32), ((NB + 1, 4, PL), F32), ((16, 4, PL), F32)),
-        [vspec()] * 7,
+        [pl.BlockSpec(memory_space=pltpu.HBM)] * 7,
         [vspec()] * 3,
         "pack",
-        8,
+        60,
+        [
+            pltpu.VMEM((3, NB, PL), F32),
+            pltpu.VMEM((NB, PL), F32),
+            pltpu.VMEM((1, NB), I32),
+            pltpu.VMEM((1, NB), I32),
+            pltpu.VMEM((K, NB), I32),
+            pltpu.VMEM((3, 2048), F32),
+            pltpu.VMEM((1, 2048), F32),
+            pltpu.SemaphoreType.DMA((7,)),
+        ],
     )(pos, masses[0], cnt, dest_ids, near_list[0].T, cell_centers, cell_mass[None])
     z_rows = [[NZ * y + z for z in range(NZ)] for y in range(NY)]
-    y_rows = [[NZ * y + z for y in range(NY)] for z in range(NZ)]
     window = lax.all_to_all(src, "space", 0, 0, axis_index_groups=z_rows, tiled=True)
     tgts = [tgt] + [lax.ppermute(tgt, "space", along_y(k)) for k in (1, -1, 2)]
     pair = jnp.stack([cells, lax.ppermute(cells, "slab", [(i, i ^ 1) for i in range(2 * NX)])])
@@ -307,15 +328,25 @@
         8,
         [pltpu.VMEM((16, 2 * PL), I32), pltpu.SemaphoreType.DMA],
     )(me, *tgts)
-    (part,) = call(
-        near_kernel,
-        (((NY * NB, 4, PL), F32),),
-        [sspec()] + [vspec()] * 2,
-        [vspec()],
-        "near",
-        24,
-    )(tab, tall, window.reshape(NZ * NB, 4, PL))
-    *pairs, part = lax.optimization_barrier((*pairs, part))
+    window = window.reshape(NZ * NB, 4, PL)
+
+    def near(first, tab):
+        count = NY - 1 if first else 1
+        return call(
+            functools.partial(near_kernel, first),
+            (((NB, 4, PL), F32),) * count,
+            [sspec()] + [vspec()] * 2,
+            [vspec()] * count,
+            "near",
+            24,
+            [pltpu.VMEM((count * NB, 4, PL), F32)],
+        )(tab, tall, window)
+
+    sent = near(True, tab)
+    back = [lax.ppermute(v, "space", along_y(-k)) for v, k in zip(sent, (1, -1, 2))]
+    tab, sent = lax.optimization_barrier((tab, sent))
+    (own,) = near(False, tab)
+    *pairs, own = lax.optimization_barrier((*pairs, own))
     (far,) = call(
         far_kernel,
         (((3, NB, PL), F32),),
@@ -325,17 +356,14 @@
         16,
         [pltpu.VMEM((PL, PL), F32)],
     )(place, pos, cnt, cell_list[0].T, *pairs)
-    back = lax.all_to_all(
-        part.reshape(NY, NB, 4, PL), "space", 0, 0, axis_index_groups=y_rows, tiled=True
-    )
     (out,) = call(
         final_kernel,
         (((3, NB, PL), F32),),
-        [vspec()] * 3,
+        [vspec()] * 6,
         [vspec()],
         "final",
         8,
-    )(cnt, far, back)
+    )(cnt, far, own, *back)
     return jnp.transpose(out, (1, 0, 2))[None]
 
 

time: 61.6 us -> 57.2 us (0.929)
  the two profiles are of different devices: /device:TPU:3 before, /device:TPU:1 now
where the time goes in v5:
time: 57.2 us; the launch traced here: 56.8 us
  starting transfers between devices  26.3 us (46%)
  waiting for transfers between devices  15.3 us (27%)
  Pallas kernels  14.3 us (25%)
  local copies, waits for them, and re-layouts  0.67 us (1%)
    all_to_all x1, waiting for transfers between devices, per_device(): lax.all_to_all(src, 'space', 0, 0, axis_index_groups=z_rows, tiled=True)  11.7 us
    all_to_all x1, starting transfers between devices, per_device(): lax.all_to_all(src, 'space', 0, 0, axis_index_groups=z_rows, tiled=True)  9.16 us
    pallas_call x2, Pallas kernels, near(): call(functools.partial(near_kernel, first), (((NB, 4, PL), F32),) * count...  7.77 us
    ppermute x3, starting transfers between devices, per_device(): lax.ppermute(pair, 'slab', along_x(k))  6.23 us
    ppermute x3, starting transfers between devices, per_device(): lax.ppermute(v, 'space', along_y(-k))  5.5 us
    ppermute x3, starting transfers between devices, per_device(): tgts = [tgt] + [lax.ppermute(tgt, 'space', along_y(k)) for k in (1, -1, 2)]  4.41 us
    pallas_call x1, Pallas kernels, per_device(): call(pack_kernel, (((NZ, NB, 4, PL), F32), ((NB + 1, 4, PL), F32), ((16,...  2.33 us
    ppermute x3, waiting for transfers between devices, per_device(): lax.ppermute(pair, 'slab', along_x(k))  2.06 us
  transfers between devices with their start and end apart: 11, of which 4 were waited for; matrix products, arithmetic and copies ran while one was open for 0% of the time, Pallas kernels for 20%

profile of v5, /device:TPU:1, one launch (start us, length us, event | category | flops | bytes accessed | tf_op | source)
XLA Modules:
  0.0 56.8 jit_solution(1212990355175618205)
XLA Ops:
  0.0 2.3 %pack.1 = (f32[8,48,4,128]{3,2,1,0:T(4,128)}, f32[49,4,128]{2,1,0:T(4,128)}, f32[16,4,128]{2,1,0:T(4,128)}) custom-call(f32[3,48,128]{2,1,0:T(8,128)} %bitcast.22, f32[48,128]{1,0:T(8,128)} %bitcast.30, s32[1,48]{1,0:T(1,128)} %bitcast.25, s32[1,48]{1,0:T(1,128)} %refs_3_.1, s32[4,48]{1,0:T(4,128)} %bitcast.32, f32[3,2048]{1,0:T(4,128)} %refs_5_.1, ...), custom_call_target="tpu_custom_call" | custom-call | tf_op jit(solution)/shard_map/pack/pallas_call | solution.py:297
  2.3 0.0 copy-start.4
  2.4 9.2 %all-to-all-start = ((f32[8,48,4,128]{3,2,1,0:T(4,128)}), f32[8,48,4,128]{3,2,1,0:T(4,128)S(1)}, u32[]{:S(2)}, u32[]{:S(2)}) async-start(f32[8,48,4,128]{3,2,1,0:T(4,128)} %get-tuple-element.23), calls=%async_computation | async-start | bytes 1572864 | tf_op jit(solution)/shard_map/all_to_all | solution.py:316
  11.5 1.0 %collective-permute-start = (f32[16,4,128]{2,1,0:T(4,128)S(1)}, f32[16,4,128]{2,1,0:T(4,128)S(1)}, u32[]{:S(2)}, u32[]{:S(2)}) collective-permute-start(f32[16,4,128]{2,1,0:T(4,128)S(1)} %copy-done.4), channel_id=1, source_target_pairs={{0,32},{32,0},{64,96},{96,64},{128,160},{160,128},{192,224},{224,1... | collective-permute-start | bytes 98312 | tf_op jit(solution)/shard_map/ppermute | solution.py:318
  12.6 2.9 %collective-permute-start.6 = (f32[49,4,128]{2,1,0:T(4,128)S(1)}, f32[49,4,128]{2,1,0:T(4,128)S(1)}, u32[]{:S(2)}, u32[]{:S(2)}) collective-permute-start(f32[49,4,128]{2,1,0:T(4,128)S(1)} %copy-done.1), channel_id=1, source_target_pairs={{0,16},{1,17},{2,18},{3,19},{4,20},{5,21},{6,22},{7,23},{8,24},{9,... | collective-permute-start | bytes 301064 | tf_op jit(solution)/shard_map/ppermute | solution.py:317
  15.5 0.8 %collective-permute-start.5 = (f32[49,4,128]{2,1,0:T(4,128)S(1)}, f32[49,4,128]{2,1,0:T(4,128)S(1)}, u32[]{:S(2)}, u32[]{:S(2)}) collective-permute-start(f32[49,4,128]{2,1,0:T(4,128)S(1)} %copy-done.1), channel_id=1, source_target_pairs={{0,24},{1,25},{2,26},{3,27},{4,28},{5,29},{6,30},{7,31},{8,0},{9,1... | collective-permute-start | bytes 301064 | tf_op jit(solution)/shard_map/ppermute | solution.py:317
  16.3 0.7 %collective-permute-start.4 = (f32[49,4,128]{2,1,0:T(4,128)S(1)}, f32[49,4,128]{2,1,0:T(4,128)S(1)}, u32[]{:S(2)}, u32[]{:S(2)}) collective-permute-start(f32[49,4,128]{2,1,0:T(4,128)S(1)} %copy-done.1), channel_id=1, source_target_pairs={{0,8},{1,9},{2,10},{3,11},{4,12},{5,13},{6,14},{7,15},{8,16},{9,17... | collective-permute-start | bytes 301064 | tf_op jit(solution)/shard_map/ppermute | solution.py:317
  17.0 2.8 %collective-permute-start.3 = (f32[2,16,4,128]{3,2,1,0:T(4,128)S(1)}, f32[2,16,4,128]{3,2,1,0:T(4,128)S(1)}, u32[]{:S(2)}, u32[]{:S(2)}) collective-permute-start(f32[2,16,4,128]{3,2,1,0:T(4,128)S(1)} %pad_maximum_fusion.c0), channel_id=1, source_target_pairs={{0,128},{32,160},{64,192},{96,224},{128,0},{160,32},{192,64},{224,... | collective-permute-start | bytes 196616 | tf_op jit(solution)/shard_map/ppermute | solution.py:319
  19.8 0.0 collective-permute-done.6.t3
  19.8 1.1 %collective-permute-done.5.t2 = f32[49,4,128]{2,1,0:T(4,128)S(1)} collective-permute-done((f32[49,4,128]{2,1,0:T(4,128)S(1)}, f32[49,4,128]{2,1,0:T(4,128)S(1)}, u32[]{:S(2)}, u32[]{:S(2)}) %collective-permute-start.5) | collective-permute-done | bytes 100384 | tf_op jit(solution)/shard_map/ppermute | solution.py:317
  21.0 0.3 collective-permute-done.4.t1
  21.3 2.1 %prep.1 = (f32[192,4,128]{2,1,0:T(4,128)S(1)}, s32[16,256]{1,0:T(8,128)S(1)}) custom-call(s32[1]{0:T(128)} %bitcast.13.y_ref, f32[49,4,128]{2,1,0:T(4,128)S(1)} %copy-done.1, f32[49,4,128]{2,1,0:T(4,128)S(1)} %collective-permute-done.4.t1, f32[49,4,128]{2,1,0:T(4,128)S(1)} %collective-permute-done.5.t2, f32[49,4,128]{2,1,0:T(4,128)S(1)} %collective-permute-done.6.t3), custom_call_target="tpu_custom_call" | custom-call | tf_op jit(solution)/shard_map/prep/pallas_call | solution.py:322
  23.3 11.7 %all-to-all-done = f32[8,48,4,128]{3,2,1,0:T(4,128)S(1)} async-done(((f32[8,48,4,128]{3,2,1,0:T(4,128)}), f32[8,48,4,128]{3,2,1,0:T(4,128)S(1)}, u32[]{:S(2)}, u32[]{:S(2)}) %all-to-all-start) | async-done | bytes 786464 | tf_op jit(solution)/shard_map/all_to_all | solution.py:316
  35.1 5.5 %near.2 = (f32[48,4,128]{2,1,0:T(4,128)S(1)}, f32[48,4,128]{2,1,0:T(4,128)S(1)}, f32[48,4,128]{2,1,0:T(4,128)S(1)}) custom-call(s32[16,256]{1,0:T(8,128)S(1)} %get-tuple-element.27.tab, f32[192,4,128]{2,1,0:T(4,128)S(1)} %get-tuple-element.22.tall, f32[384,4,128]{2,1,0:T(4,128)S(1)} %bitcast.20), custom_call_target="tpu_custom_call" | custom-call | tf_op jit(solution)/shard_map/near/pallas_call | solution.py:335
  40.6 2.8 %collective-permute-start.7 = (f32[48,4,128]{2,1,0:T(4,128)S(1)}, f32[48,4,128]{2,1,0:T(4,128)S(1)}, u32[]{:S(2)}, u32[]{:S(2)}) collective-permute-start(f32[48,4,128]{2,1,0:T(4,128)S(1)} %get-tuple-element.24), channel_id=1, source_target_pairs={{0,24},{1,25},{2,26},{3,27},{4,28},{5,29},{6,30},{7,31},{8,0},{9,1... | collective-permute-start | bytes 294920 | tf_op jit(solution)/shard_map/ppermute | solution.py:346
  43.4 1.0 %collective-permute-start.8 = (f32[48,4,128]{2,1,0:T(4,128)S(1)}, f32[48,4,128]{2,1,0:T(4,128)S(1)}, u32[]{:S(2)}, u32[]{:S(2)}) collective-permute-start(f32[48,4,128]{2,1,0:T(4,128)S(1)} %get-tuple-element.25), channel_id=1, source_target_pairs={{0,8},{1,9},{2,10},{3,11},{4,12},{5,13},{6,14},{7,15},{8,16},{9,17... | collective-permute-start | bytes 294920 | tf_op jit(solution)/shard_map/ppermute | solution.py:346
  44.4 1.7 %collective-permute-start.9 = (f32[48,4,128]{2,1,0:T(4,128)S(1)}, f32[48,4,128]{2,1,0:T(4,128)S(1)}, u32[]{:S(2)}, u32[]{:S(2)}) collective-permute-start(f32[48,4,128]{2,1,0:T(4,128)S(1)} %get-tuple-element.26), channel_id=1, source_target_pairs={{0,16},{1,17},{2,18},{3,19},{4,20},{5,21},{6,22},{7,23},{8,24},{9,... | collective-permute-start | bytes 294920 | tf_op jit(solution)/shard_map/ppermute | solution.py:346
  46.1 3.4 %collective-permute-start.2 = (f32[2,16,4,128]{3,2,1,0:T(4,128)S(1)}, f32[2,16,4,128]{3,2,1,0:T(4,128)S(1)}, u32[]{:S(2)}, u32[]{:S(2)}) collective-permute-start(f32[2,16,4,128]{3,2,1,0:T(4,128)S(1)} %pad_maximum_fusion.c0), channel_id=1, source_target_pairs={{0,192},{32,224},{64,0},{96,32},{128,64},{160,96},{192,128},{224,1... | collective-permute-start | bytes 196616 | tf_op jit(solution)/shard_map/ppermute | solution.py:319
  49.6 0.0 copy-start.2
  49.6 2.2 %near.3.p0 = f32[48,4,128]{2,1,0:T(4,128)S(1)} custom-call(s32[16,256]{1,0:T(8,128)S(1)} %get-tuple-element.27.tab, f32[192,4,128]{2,1,0:T(4,128)S(1)} %get-tuple-element.22.tall, f32[384,4,128]{2,1,0:T(4,128)S(1)} %bitcast.21), custom_call_target="tpu_custom_call" | custom-call | tf_op jit(solution)/shard_map/near/pallas_call | solution.py:335
  51.8 2.1 %collective-permute-done.1.c1 = f32[2,16,4,128]{3,2,1,0:T(4,128)S(1)} collective-permute-done((f32[2,16,4,128]{3,2,1,0:T(4,128)S(1)}, f32[2,16,4,128]{3,2,1,0:T(4,128)S(1)}, u32[]{:S(2)}, u32[]{:S(2)}) %collective-permute-start.1) | collective-permute-done | bytes 65568 | tf_op jit(solution)/shard_map/ppermute | solution.py:319
  53.9 0.6 %copy-done.3 = s32[1,1,48]{2,1,0:T(1,128)S(1)} copy-done((s32[1,1,48]{2,1,0:T(1,128)S(1)}, s32[1,1,48]{2,1,0:T(1,128)}, u32[]{:S(2)}) %copy-start.3) | copy-done | bytes 216
  54.5 1.4 %far.1.far_ref = f32[3,48,128]{2,1,0:T(8,128)S(1)} custom-call(s32[1]{0:T(128)} %bitcast.1.place_ref, f32[3,48,128]{2,1,0:T(8,128)S(1)} %bitcast.23, s32[1,48]{1,0:T(1,128)S(1)} %bitcast.26, s32[32,48]{1,0:T(8,128)S(1)} %bitcast.24, f32[2,16,4,128]{3,2,1,0:T(4,128)S(1)} %pad_maximum_fusion.c0, f32[2,16,4,128]{3,2,1,0:T(4,128)S(1)} %collective-permute-done.1.c1, ...), custom_call_target="tpu_custom_call" | custom-call | tf_op jit(solution)/shard_map/far/pallas_call | solution.py:350
  56.0 0.8 %final.1 = f32[3,48,128]{2,1,0:T(8,128)} custom-call(s32[1,48]{1,0:T(1,128)S(1)} %bitcast.27, f32[3,48,128]{2,1,0:T(8,128)S(1)} %far.1.far_ref, f32[48,4,128]{2,1,0:T(4,128)S(1)} %near.3.p0, f32[48,4,128]{2,1,0:T(4,128)S(1)} %collective-permute-done.7.p1, f32[48,4,128]{2,1,0:T(4,128)S(1)} %collective-permute-done.8.p2, ...), custom_call_target="tpu_custom_call" | custom-call | tf_op jit(solution)/shard_map/final/pallas_call | solution.py:359
  (15 shorter events, 0.0 us)
Async XLA Ops:
  2.3 9.2 %copy-start.4 = (f32[16,4,128]{2,1,0:T(4,128)S(1)}, f32[16,4,128]{2,1,0:T(4,128)}, u32[]{:S(2)}) copy-start(f32[16,4,128]{2,1,0:T(4,128)} %get-tuple-element.19) | copy-start | bytes 98308
  2.3 10.2 %copy-start.1 = (f32[49,4,128]{2,1,0:T(4,128)S(1)}, f32[49,4,128]{2,1,0:T(4,128)}, u32[]{:S(2)}) copy-start(f32[49,4,128]{2,1,0:T(4,128)} %get-tuple-element.20.t0) | copy-start | bytes 301060
  2.4 32.7 %all-to-all-start = ((f32[8,48,4,128]{3,2,1,0:T(4,128)}), f32[8,48,4,128]{3,2,1,0:T(4,128)S(1)}, u32[]{:S(2)}, u32[]{:S(2)}) async-start(f32[8,48,4,128]{3,2,1,0:T(4,128)} %get-tuple-element.23), calls=%async_computation | async-start | bytes 1572864 | tf_op jit(solution)/shard_map/all_to_all | solution.py:316
  11.5 5.5 %collective-permute-start = (f32[16,4,128]{2,1,0:T(4,128)S(1)}, f32[16,4,128]{2,1,0:T(4,128)S(1)}, u32[]{:S(2)}, u32[]{:S(2)}) collective-permute-start(f32[16,4,128]{2,1,0:T(4,128)S(1)} %copy-done.4), channel_id=1, source_target_pairs={{0,32},{32,0},{64,96},{96,64},{128,160},{160,128},{192,224},{224,1... | collective-permute-start | bytes 98312 | tf_op jit(solution)/shard_map/ppermute | solution.py:318
  12.6 7.3 %collective-permute-start.6 = (f32[49,4,128]{2,1,0:T(4,128)S(1)}, f32[49,4,128]{2,1,0:T(4,128)S(1)}, u32[]{:S(2)}, u32[]{:S(2)}) collective-permute-start(f32[49,4,128]{2,1,0:T(4,128)S(1)} %copy-done.1), channel_id=1, source_target_pairs={{0,16},{1,17},{2,18},{3,19},{4,20},{5,21},{6,22},{7,23},{8,24},{9,... | collective-permute-start | bytes 301064 | tf_op jit(solution)/shard_map/ppermute | solution.py:317
  15.5 5.5 %collective-permute-start.5 = (f32[49,4,128]{2,1,0:T(4,128)S(1)}, f32[49,4,128]{2,1,0:T(4,128)S(1)}, u32[]{:S(2)}, u32[]{:S(2)}) collective-permute-start(f32[49,4,128]{2,1,0:T(4,128)S(1)} %copy-done.1), channel_id=1, source_target_pairs={{0,24},{1,25},{2,26},{3,27},{4,28},{5,29},{6,30},{7,31},{8,0},{9,1... | collective-permute-start | bytes 301064 | tf_op jit(solution)/shard_map/ppermute | solution.py:317
  16.3 5.0 %collective-permute-start.4 = (f32[49,4,128]{2,1,0:T(4,128)S(1)}, f32[49,4,128]{2,1,0:T(4,128)S(1)}, u32[]{:S(2)}, u32[]{:S(2)}) collective-permute-start(f32[49,4,128]{2,1,0:T(4,128)S(1)} %copy-done.1), channel_id=1, source_target_pairs={{0,8},{1,9},{2,10},{3,11},{4,12},{5,13},{6,14},{7,15},{8,16},{9,17... | collective-permute-start | bytes 301064 | tf_op jit(solution)/shard_map/ppermute | solution.py:317
  17.0 32.5 %collective-permute-start.3 = (f32[2,16,4,128]{3,2,1,0:T(4,128)S(1)}, f32[2,16,4,128]{3,2,1,0:T(4,128)S(1)}, u32[]{:S(2)}, u32[]{:S(2)}) collective-permute-start(f32[2,16,4,128]{3,2,1,0:T(4,128)S(1)} %pad_maximum_fusion.c0), channel_id=1, source_target_pairs={{0,128},{32,160},{64,192},{96,224},{128,0},{160,32},{192,64},{224,... | collective-permute-start | bytes 196616 | tf_op jit(solution)/shard_map/ppermute | solution.py:319
  40.6 15.3 %collective-permute-start.7 = (f32[48,4,128]{2,1,0:T(4,128)S(1)}, f32[48,4,128]{2,1,0:T(4,128)S(1)}, u32[]{:S(2)}, u32[]{:S(2)}) collective-permute-start(f32[48,4,128]{2,1,0:T(4,128)S(1)} %get-tuple-element.24), channel_id=1, source_target_pairs={{0,24},{1,25},{2,26},{3,27},{4,28},{5,29},{6,30},{7,31},{8,0},{9,1... | collective-permute-start | bytes 294920 | tf_op jit(solution)/shard_map/ppermute | solution.py:346
  43.4 12.5 %collective-permute-start.8 = (f32[48,4,128]{2,1,0:T(4,128)S(1)}, f32[48,4,128]{2,1,0:T(4,128)S(1)}, u32[]{:S(2)}, u32[]{:S(2)}) collective-permute-start(f32[48,4,128]{2,1,0:T(4,128)S(1)} %get-tuple-element.25), channel_id=1, source_target_pairs={{0,8},{1,9},{2,10},{3,11},{4,12},{5,13},{6,14},{7,15},{8,16},{9,17... | collective-permute-start | bytes 294920 | tf_op jit(solution)/shard_map/ppermute | solution.py:346
  44.4 11.5 %collective-permute-start.9 = (f32[48,4,128]{2,1,0:T(4,128)S(1)}, f32[48,4,128]{2,1,0:T(4,128)S(1)}, u32[]{:S(2)}, u32[]{:S(2)}) collective-permute-start(f32[48,4,128]{2,1,0:T(4,128)S(1)} %get-tuple-element.26), channel_id=1, source_target_pairs={{0,16},{1,17},{2,18},{3,19},{4,20},{5,21},{6,22},{7,23},{8,24},{9,... | collective-permute-start | bytes 294920 | tf_op jit(solution)/shard_map/ppermute | solution.py:346
  46.1 5.7 %collective-permute-start.2 = (f32[2,16,4,128]{3,2,1,0:T(4,128)S(1)}, f32[2,16,4,128]{3,2,1,0:T(4,128)S(1)}, u32[]{:S(2)}, u32[]{:S(2)}) collective-permute-start(f32[2,16,4,128]{3,2,1,0:T(4,128)S(1)} %pad_maximum_fusion.c0), channel_id=1, source_target_pairs={{0,192},{32,224},{64,0},{96,32},{128,64},{160,96},{192,128},{224,1... | collective-permute-start | bytes 196616 | tf_op jit(solution)/shard_map/ppermute | solution.py:319
  49.5 4.3 %collective-permute-start.1 = (f32[2,16,4,128]{3,2,1,0:T(4,128)S(1)}, f32[2,16,4,128]{3,2,1,0:T(4,128)S(1)}, u32[]{:S(2)}, u32[]{:S(2)}) collective-permute-start(f32[2,16,4,128]{3,2,1,0:T(4,128)S(1)} %pad_maximum_fusion.c0), channel_id=1, source_target_pairs={{0,64},{32,96},{64,128},{96,160},{128,192},{160,224},{192,0},{224,... | collective-permute-start | bytes 196616 | tf_op jit(solution)/shard_map/ppermute | solution.py:319
  49.5 4.3 %copy-start = (f32[1,48,3,128]{3,1,2,0:T(8,128)S(1)}, f32[1,48,3,128]{3,1,2,0:T(8,128)}, u32[]{:S(2)}) copy-start(f32[1,48,3,128]{3,1,2,0:T(8,128)} %param.8) | copy-start | bytes 221188
  49.6 4.3 %copy-start.2 = (s32[1,48,32]{1,2,0:T(8,128)S(1)}, s32[1,48,32]{1,2,0:T(8,128)}, u32[]{:S(2)}) copy-start(s32[1,48,32]{1,2,0:T(8,128)} %param.13) | copy-start | bytes 18436
  53.9 0.7 %copy-start.3 = (s32[1,1,48]{2,1,0:T(1,128)S(1)}, s32[1,1,48]{2,1,0:T(1,128)}, u32[]{:S(2)}) copy-start(s32[1,1,48]{2,1,0:T(1,128)} %param.10) | copy-start | bytes 580

commit v6 on v5

--- a/solution.py
+++ b/solution.py
@@ -328,6 +328,16 @@
         8,
         [pltpu.VMEM((16, 2 * PL), I32), pltpu.SemaphoreType.DMA],
     )(me, *tgts)
+    (far,) = call(
+        far_kernel,
+        (((3, NB, PL), F32),),
+        [sspec()] + [vspec()] * 7,
+        [vspec()],
+        "far",
+        16,
+        [pltpu.VMEM((PL, PL), F32)],
+    )(place, pos, cnt, cell_list[0].T, *pairs)
+    tall, tab, far = lax.optimization_barrier((tall, tab, far))
     window = window.reshape(NZ * NB, 4, PL)
 
     def near(first, tab):
@@ -346,16 +356,6 @@
     back = [lax.ppermute(v, "space", along_y(-k)) for v, k in zip(sent, (1, -1, 2))]
     tab, sent = lax.optimization_barrier((tab, sent))
     (own,) = near(False, tab)
-    *pairs, own = lax.optimization_barrier((*pairs, own))
-    (far,) = call(
-        far_kernel,
-        (((3, NB, PL), F32),),
-        [sspec()] + [vspec()] * 7,
-        [vspec()],
-        "far",
-        16,
-        [pltpu.VMEM((PL, PL), F32)],
-    )(place, pos, cnt, cell_list[0].T, *pairs)
     (out,) = call(
         final_kernel,
         (((3, NB, PL), F32),),

time: 57.2 us -> 53.6 us (0.937)
  waiting for transfers between devices: 15.3 us -> 11.7 us
  starting transfers between devices: 26.3 us -> 26.9 us
    all_to_all x1, waiting for transfers between devices: 11.7 us -> 4.74 us  [per_device(): lax.all_to_all(src, 'space', 0, 0, axis_index_groups=z_rows, tiled=True)]
    ppermute x3, starting transfers between devices: 5.5 us -> 8.2 us  [per_device(): lax.ppermute(v, 'space', along_y(-k))]
    ppermute x3, waiting for transfers between devices: 0.01 us -> 2.11 us  [per_device(): lax.ppermute(v, 'space', along_y(-k))]
    ppermute x3, waiting for transfers between devices: 2.06 us -> 4.02 us  [per_device(): lax.ppermute(pair, 'slab', along_x(k))]
    ppermute x3, starting transfers between devices: 6.23 us -> 4.3 us  [per_device(): lax.ppermute(pair, 'slab', along_x(k))]
    ppermute x3, waiting for transfers between devices: 1.45 us -> 0.01 us  [per_device(): tgts = [tgt] + [lax.ppermute(tgt, 'space', along_y(k)) for k in (1, -1, 2)]]
    ppermute x1, waiting for transfers between devices: 0.01 us -> 0.86 us  [per_device(): lax.ppermute(cells, 'slab', [(i, i ^ 1) for i in range(2 * NX)])]
  transfers between devices with their start and end apart: 11 -> 11, of which waited for: 4 -> 5; matrix products, arithmetic and copies ran while one was open for 0% -> 0% of each run, Pallas kernels for 20% -> 12%
where the time goes in v6:
time: 53.6 us; the launch traced here: 53.4 us
  starting transfers between devices  26.9 us (50%)
  Pallas kernels  13.9 us (26%)
  waiting for transfers between devices  11.7 us (22%)
  local copies, waits for them, and re-layouts  0.67 us (1%)
    all_to_all x1, starting transfers between devices, per_device(): lax.all_to_all(src, 'space', 0, 0, axis_index_groups=z_rows, tiled=True)  9.03 us
    ppermute x3, starting transfers between devices, per_device(): lax.ppermute(v, 'space', along_y(-k))  8.2 us
    pallas_call x2, Pallas kernels, near(): call(functools.partial(near_kernel, first), (((NB, 4, PL), F32),) * count...  7.3 us
    all_to_all x1, waiting for transfers between devices, per_device(): lax.all_to_all(src, 'space', 0, 0, axis_index_groups=z_rows, tiled=True)  4.74 us
    ppermute x3, starting transfers between devices, per_device(): tgts = [tgt] + [lax.ppermute(tgt, 'space', along_y(k)) for k in (1, -1, 2)]  4.38 us
    ppermute x3, starting transfers between devices, per_device(): lax.ppermute(pair, 'slab', along_x(k))  4.3 us
    ppermute x3, waiting for transfers between devices, per_device(): lax.ppermute(pair, 'slab', along_x(k))  4.02 us
    pallas_call x1, Pallas kernels, per_device(): call(pack_kernel, (((NZ, NB, 4, PL), F32), ((NB + 1, 4, PL), F32), ((16,...  2.33 us
  transfers between devices with their start and end apart: 11, of which 5 were waited for; matrix products, arithmetic and copies ran while one was open for 0% of the time, Pallas kernels for 12%

profile of v6, /device:TPU:1, one launch (start us, length us, event | category | flops | bytes accessed | tf_op | source)
XLA Modules:
  0.0 53.4 jit_solution(9123419935915642893)
XLA Ops:
  0.0 2.3 %pack.1 = (f32[8,48,4,128]{3,2,1,0:T(4,128)}, f32[49,4,128]{2,1,0:T(4,128)}, f32[16,4,128]{2,1,0:T(4,128)}) custom-call(f32[3,48,128]{2,1,0:T(8,128)} %bitcast.22, f32[48,128]{1,0:T(8,128)} %bitcast.30, s32[1,48]{1,0:T(1,128)} %bitcast.25, s32[1,48]{1,0:T(1,128)} %refs_3_.1, s32[4,48]{1,0:T(4,128)} %bitcast.32, f32[3,2048]{1,0:T(4,128)} %refs_5_.1, ...), custom_call_target="tpu_custom_call" | custom-call | tf_op jit(solution)/shard_map/pack/pallas_call | solution.py:297
  2.3 0.0 copy-start.4
  2.3 0.0 copy-start.2
  2.4 9.0 %all-to-all-start = ((f32[8,48,4,128]{3,2,1,0:T(4,128)}), f32[8,48,4,128]{3,2,1,0:T(4,128)S(1)}, u32[]{:S(2)}, u32[]{:S(2)}) async-start(f32[8,48,4,128]{3,2,1,0:T(4,128)} %get-tuple-element.24), calls=%async_computation | async-start | bytes 1572864 | tf_op jit(solution)/shard_map/all_to_all | solution.py:316
  11.4 1.0 %collective-permute-start.3 = (f32[16,4,128]{2,1,0:T(4,128)S(1)}, f32[16,4,128]{2,1,0:T(4,128)S(1)}, u32[]{:S(2)}, u32[]{:S(2)}) collective-permute-start(f32[16,4,128]{2,1,0:T(4,128)S(1)} %copy-done.4), channel_id=1, source_target_pairs={{0,32},{32,0},{64,96},{96,64},{128,160},{160,128},{192,224},{224,1... | collective-permute-start | bytes 98312 | tf_op jit(solution)/shard_map/ppermute | solution.py:318
  12.4 0.9 %collective-permute-done.3 = f32[16,4,128]{2,1,0:T(4,128)S(1)} collective-permute-done((f32[16,4,128]{2,1,0:T(4,128)S(1)}, f32[16,4,128]{2,1,0:T(4,128)S(1)}, u32[]{:S(2)}, u32[]{:S(2)}) %collective-permute-start.3) | collective-permute-done | bytes 32800 | tf_op jit(solution)/shard_map/ppermute | solution.py:318
  13.3 2.8 %collective-permute-start.6 = (f32[2,16,4,128]{3,2,1,0:T(4,128)S(1)}, f32[2,16,4,128]{3,2,1,0:T(4,128)S(1)}, u32[]{:S(2)}, u32[]{:S(2)}) collective-permute-start(f32[2,16,4,128]{3,2,1,0:T(4,128)S(1)} %pad_maximum_fusion.c0), channel_id=1, source_target_pairs={{0,128},{32,160},{64,192},{96,224},{128,0},{160,32},{192,64},{224,... | collective-permute-start | bytes 196616 | tf_op jit(solution)/shard_map/ppermute | solution.py:319
  16.2 2.9 %collective-permute-start.2 = (f32[49,4,128]{2,1,0:T(4,128)S(1)}, f32[49,4,128]{2,1,0:T(4,128)S(1)}, u32[]{:S(2)}, u32[]{:S(2)}) collective-permute-start(f32[49,4,128]{2,1,0:T(4,128)S(1)} %copy-done.1), channel_id=1, source_target_pairs={{0,16},{1,17},{2,18},{3,19},{4,20},{5,21},{6,22},{7,23},{8,24},{9,... | collective-permute-start | bytes 301064 | tf_op jit(solution)/shard_map/ppermute | solution.py:317
  19.1 0.8 %collective-permute-start.1 = (f32[49,4,128]{2,1,0:T(4,128)S(1)}, f32[49,4,128]{2,1,0:T(4,128)S(1)}, u32[]{:S(2)}, u32[]{:S(2)}) collective-permute-start(f32[49,4,128]{2,1,0:T(4,128)S(1)} %copy-done.1), channel_id=1, source_target_pairs={{0,24},{1,25},{2,26},{3,27},{4,28},{5,29},{6,30},{7,31},{8,0},{9,1... | collective-permute-start | bytes 301064 | tf_op jit(solution)/shard_map/ppermute | solution.py:317
  19.9 0.7 %collective-permute-start = (f32[49,4,128]{2,1,0:T(4,128)S(1)}, f32[49,4,128]{2,1,0:T(4,128)S(1)}, u32[]{:S(2)}, u32[]{:S(2)}) collective-permute-start(f32[49,4,128]{2,1,0:T(4,128)S(1)} %copy-done.1), channel_id=1, source_target_pairs={{0,8},{1,9},{2,10},{3,11},{4,12},{5,13},{6,14},{7,15},{8,16},{9,17... | collective-permute-start | bytes 301064 | tf_op jit(solution)/shard_map/ppermute | solution.py:317
  20.5 0.9 %collective-permute-start.5 = (f32[2,16,4,128]{3,2,1,0:T(4,128)S(1)}, f32[2,16,4,128]{3,2,1,0:T(4,128)S(1)}, u32[]{:S(2)}, u32[]{:S(2)}) collective-permute-start(f32[2,16,4,128]{3,2,1,0:T(4,128)S(1)} %pad_maximum_fusion.c0), channel_id=1, source_target_pairs={{0,192},{32,224},{64,0},{96,32},{128,64},{160,96},{192,128},{224,1... | collective-permute-start | bytes 196616 | tf_op jit(solution)/shard_map/ppermute | solution.py:319
  21.4 0.6 %collective-permute-start.4 = (f32[2,16,4,128]{3,2,1,0:T(4,128)S(1)}, f32[2,16,4,128]{3,2,1,0:T(4,128)S(1)}, u32[]{:S(2)}, u32[]{:S(2)}) collective-permute-start(f32[2,16,4,128]{3,2,1,0:T(4,128)S(1)} %pad_maximum_fusion.c0), channel_id=1, source_target_pairs={{0,64},{32,96},{64,128},{96,160},{128,192},{160,224},{192,0},{224,... | collective-permute-start | bytes 196616 | tf_op jit(solution)/shard_map/ppermute | solution.py:319
  22.0 1.9 %collective-permute-done.5.c2 = f32[2,16,4,128]{3,2,1,0:T(4,128)S(1)} collective-permute-done((f32[2,16,4,128]{3,2,1,0:T(4,128)S(1)}, f32[2,16,4,128]{3,2,1,0:T(4,128)S(1)}, u32[]{:S(2)}, u32[]{:S(2)}) %collective-permute-start.5) | collective-permute-done | bytes 65568 | tf_op jit(solution)/shard_map/ppermute | solution.py:319
  24.0 2.1 %collective-permute-done.4.c1 = f32[2,16,4,128]{3,2,1,0:T(4,128)S(1)} collective-permute-done((f32[2,16,4,128]{3,2,1,0:T(4,128)S(1)}, f32[2,16,4,128]{3,2,1,0:T(4,128)S(1)}, u32[]{:S(2)}, u32[]{:S(2)}) %collective-permute-start.4) | collective-permute-done | bytes 65568 | tf_op jit(solution)/shard_map/ppermute | solution.py:319
  26.0 0.6 %copy-done.3 = s32[1,1,48]{2,1,0:T(1,128)S(1)} copy-done((s32[1,1,48]{2,1,0:T(1,128)S(1)}, s32[1,1,48]{2,1,0:T(1,128)}, u32[]{:S(2)}) %copy-start.3) | copy-done | bytes 216
  26.7 1.4 %far.1.far_ref = f32[3,48,128]{2,1,0:T(8,128)S(1)} custom-call(s32[1]{0:T(128)} %bitcast.8.place_ref, f32[3,48,128]{2,1,0:T(8,128)S(1)} %bitcast.23, s32[1,48]{1,0:T(1,128)S(1)} %bitcast.26, s32[32,48]{1,0:T(8,128)S(1)} %bitcast.24, f32[2,16,4,128]{3,2,1,0:T(4,128)S(1)} %pad_maximum_fusion.c0, f32[2,16,4,128]{3,2,1,0:T(4,128)S(1)} %collective-permute-done.4.c1, ...), custom_call_target="tpu_custom_call" | custom-call | tf_op jit(solution)/shard_map/far/pallas_call | solution.py:331
  28.1 2.1 %prep.1 = (f32[192,4,128]{2,1,0:T(4,128)S(1)}, s32[16,256]{1,0:T(8,128)S(1)}) custom-call(s32[1]{0:T(128)} %bitcast.1.y_ref, f32[49,4,128]{2,1,0:T(4,128)S(1)} %copy-done.1, f32[49,4,128]{2,1,0:T(4,128)S(1)} %collective-permute-done.t1, f32[49,4,128]{2,1,0:T(4,128)S(1)} %collective-permute-done.1.t2, f32[49,4,128]{2,1,0:T(4,128)S(1)} %collective-permute-done.2.t3), custom_call_target="tpu_custom_call" | custom-call | tf_op jit(solution)/shard_map/prep/pallas_call | solution.py:322
  30.2 4.7 %all-to-all-done = f32[8,48,4,128]{3,2,1,0:T(4,128)S(1)} async-done(((f32[8,48,4,128]{3,2,1,0:T(4,128)}), f32[8,48,4,128]{3,2,1,0:T(4,128)S(1)}, u32[]{:S(2)}, u32[]{:S(2)}) %all-to-all-start) | async-done | bytes 786464 | tf_op jit(solution)/shard_map/all_to_all | solution.py:316
  35.0 4.6 %near.2 = (f32[48,4,128]{2,1,0:T(4,128)S(1)}, f32[48,4,128]{2,1,0:T(4,128)S(1)}, f32[48,4,128]{2,1,0:T(4,128)S(1)}) custom-call(s32[16,256]{1,0:T(8,128)S(1)} %get-tuple-element.28.tab, f32[192,4,128]{2,1,0:T(4,128)S(1)} %get-tuple-element.23.tall, f32[384,4,128]{2,1,0:T(4,128)S(1)} %bitcast.20), custom_call_target="tpu_custom_call" | custom-call | tf_op jit(solution)/shard_map/near/pallas_call | solution.py:345
  39.6 5.6 %collective-permute-start.7 = (f32[48,4,128]{2,1,0:T(4,128)S(1)}, f32[48,4,128]{2,1,0:T(4,128)S(1)}, u32[]{:S(2)}, u32[]{:S(2)}) collective-permute-start(f32[48,4,128]{2,1,0:T(4,128)S(1)} %get-tuple-element.25), channel_id=1, source_target_pairs={{0,24},{1,25},{2,26},{3,27},{4,28},{5,29},{6,30},{7,31},{8,0},{9,1... | collective-permute-start | bytes 294920 | tf_op jit(solution)/shard_map/ppermute | solution.py:356
  45.2 2.6 %collective-permute-start.9 = (f32[48,4,128]{2,1,0:T(4,128)S(1)}, f32[48,4,128]{2,1,0:T(4,128)S(1)}, u32[]{:S(2)}, u32[]{:S(2)}) collective-permute-start(f32[48,4,128]{2,1,0:T(4,128)S(1)} %get-tuple-element.27), channel_id=1, source_target_pairs={{0,16},{1,17},{2,18},{3,19},{4,20},{5,21},{6,22},{7,23},{8,24},{9,... | collective-permute-start | bytes 294920 | tf_op jit(solution)/shard_map/ppermute | solution.py:356
  47.8 2.7 %near.3.p0 = f32[48,4,128]{2,1,0:T(4,128)S(1)} custom-call(s32[16,256]{1,0:T(8,128)S(1)} %get-tuple-element.28.tab, f32[192,4,128]{2,1,0:T(4,128)S(1)} %get-tuple-element.23.tall, f32[384,4,128]{2,1,0:T(4,128)S(1)} %bitcast.21), custom_call_target="tpu_custom_call" | custom-call | tf_op jit(solution)/shard_map/near/pallas_call | solution.py:345
  50.5 2.1 %collective-permute-done.8.p2 = f32[48,4,128]{2,1,0:T(4,128)S(1)} collective-permute-done((f32[48,4,128]{2,1,0:T(4,128)S(1)}, f32[48,4,128]{2,1,0:T(4,128)S(1)}, u32[]{:S(2)}, u32[]{:S(2)}) %collective-permute-start.8) | collective-permute-done | bytes 98336 | tf_op jit(solution)/shard_map/ppermute | solution.py:356
  52.6 0.8 %final.1 = f32[3,48,128]{2,1,0:T(8,128)} custom-call(s32[1,48]{1,0:T(1,128)S(1)} %bitcast.27, f32[3,48,128]{2,1,0:T(8,128)S(1)} %far.1.far_ref, f32[48,4,128]{2,1,0:T(4,128)S(1)} %near.3.p0, f32[48,4,128]{2,1,0:T(4,128)S(1)} %collective-permute-done.7.p1, f32[48,4,128]{2,1,0:T(4,128)S(1)} %collective-permute-done.8.p2, ...), custom_call_target="tpu_custom_call" | custom-call | tf_op jit(solution)/shard_map/final/pallas_call | solution.py:359
  (15 shorter events, 0.0 us)
Async XLA Ops:
  2.3 9.1 %copy-start.4 = (f32[16,4,128]{2,1,0:T(4,128)S(1)}, f32[16,4,128]{2,1,0:T(4,128)}, u32[]{:S(2)}) copy-start(f32[16,4,128]{2,1,0:T(4,128)} %get-tuple-element.20) | copy-start | bytes 98308
  2.3 23.7 %copy-start.2 = (s32[1,48,32]{1,2,0:T(8,128)S(1)}, s32[1,48,32]{1,2,0:T(8,128)}, u32[]{:S(2)}) copy-start(s32[1,48,32]{1,2,0:T(8,128)} %param.13) | copy-start | bytes 18436
  2.4 32.6 %all-to-all-start = ((f32[8,48,4,128]{3,2,1,0:T(4,128)}), f32[8,48,4,128]{3,2,1,0:T(4,128)S(1)}, u32[]{:S(2)}, u32[]{:S(2)}) async-start(f32[8,48,4,128]{3,2,1,0:T(4,128)} %get-tuple-element.24), calls=%async_computation | async-start | bytes 1572864 | tf_op jit(solution)/shard_map/all_to_all | solution.py:316
  11.4 4.8 %copy-start.1 = (f32[49,4,128]{2,1,0:T(4,128)S(1)}, f32[49,4,128]{2,1,0:T(4,128)}, u32[]{:S(2)}) copy-start(f32[49,4,128]{2,1,0:T(4,128)} %get-tuple-element.17.t0) | copy-start | bytes 301060
  11.4 1.9 %collective-permute-start.3 = (f32[16,4,128]{2,1,0:T(4,128)S(1)}, f32[16,4,128]{2,1,0:T(4,128)S(1)}, u32[]{:S(2)}, u32[]{:S(2)}) collective-permute-start(f32[16,4,128]{2,1,0:T(4,128)S(1)} %copy-done.4), channel_id=1, source_target_pairs={{0,32},{32,0},{64,96},{96,64},{128,160},{160,128},{192,224},{224,1... | collective-permute-start | bytes 98312 | tf_op jit(solution)/shard_map/ppermute | solution.py:318
  13.3 12.7 %copy-start = (f32[1,48,3,128]{3,1,2,0:T(8,128)S(1)}, f32[1,48,3,128]{3,1,2,0:T(8,128)}, u32[]{:S(2)}) copy-start(f32[1,48,3,128]{3,1,2,0:T(8,128)} %param.8) | copy-start | bytes 221188
  13.3 8.1 %collective-permute-start.6 = (f32[2,16,4,128]{3,2,1,0:T(4,128)S(1)}, f32[2,16,4,128]{3,2,1,0:T(4,128)S(1)}, u32[]{:S(2)}, u32[]{:S(2)}) collective-permute-start(f32[2,16,4,128]{3,2,1,0:T(4,128)S(1)} %pad_maximum_fusion.c0), channel_id=1, source_target_pairs={{0,128},{32,160},{64,192},{96,224},{128,0},{160,32},{192,64},{224,... | collective-permute-start | bytes 196616 | tf_op jit(solution)/shard_map/ppermute | solution.py:319
  16.2 12.0 %collective-permute-start.2 = (f32[49,4,128]{2,1,0:T(4,128)S(1)}, f32[49,4,128]{2,1,0:T(4,128)S(1)}, u32[]{:S(2)}, u32[]{:S(2)}) collective-permute-start(f32[49,4,128]{2,1,0:T(4,128)S(1)} %copy-done.1), channel_id=1, source_target_pairs={{0,16},{1,17},{2,18},{3,19},{4,20},{5,21},{6,22},{7,23},{8,24},{9,... | collective-permute-start | bytes 301064 | tf_op jit(solution)/shard_map/ppermute | solution.py:317
  19.1 9.1 %collective-permute-start.1 = (f32[49,4,128]{2,1,0:T(4,128)S(1)}, f32[49,4,128]{2,1,0:T(4,128)S(1)}, u32[]{:S(2)}, u32[]{:S(2)}) collective-permute-start(f32[49,4,128]{2,1,0:T(4,128)S(1)} %copy-done.1), channel_id=1, source_target_pairs={{0,24},{1,25},{2,26},{3,27},{4,28},{5,29},{6,30},{7,31},{8,0},{9,1... | collective-permute-start | bytes 301064 | tf_op jit(solution)/shard_map/ppermute | solution.py:317
  19.9 8.3 %collective-permute-start = (f32[49,4,128]{2,1,0:T(4,128)S(1)}, f32[49,4,128]{2,1,0:T(4,128)S(1)}, u32[]{:S(2)}, u32[]{:S(2)}) collective-permute-start(f32[49,4,128]{2,1,0:T(4,128)S(1)} %copy-done.1), channel_id=1, source_target_pairs={{0,8},{1,9},{2,10},{3,11},{4,12},{5,13},{6,14},{7,15},{8,16},{9,17... | collective-permute-start | bytes 301064 | tf_op jit(solution)/shard_map/ppermute | solution.py:317
  20.5 3.4 %collective-permute-start.5 = (f32[2,16,4,128]{3,2,1,0:T(4,128)S(1)}, f32[2,16,4,128]{3,2,1,0:T(4,128)S(1)}, u32[]{:S(2)}, u32[]{:S(2)}) collective-permute-start(f32[2,16,4,128]{3,2,1,0:T(4,128)S(1)} %pad_maximum_fusion.c0), channel_id=1, source_target_pairs={{0,192},{32,224},{64,0},{96,32},{128,64},{160,96},{192,128},{224,1... | collective-permute-start | bytes 196616 | tf_op jit(solution)/shard_map/ppermute | solution.py:319
  21.4 4.6 %collective-permute-start.4 = (f32[2,16,4,128]{3,2,1,0:T(4,128)S(1)}, f32[2,16,4,128]{3,2,1,0:T(4,128)S(1)}, u32[]{:S(2)}, u32[]{:S(2)}) collective-permute-start(f32[2,16,4,128]{3,2,1,0:T(4,128)S(1)} %pad_maximum_fusion.c0), channel_id=1, source_target_pairs={{0,64},{32,96},{64,128},{96,160},{128,192},{160,224},{192,0},{224,... | collective-permute-start | bytes 196616 | tf_op jit(solution)/shard_map/ppermute | solution.py:319
  26.0 0.7 %copy-start.3 = (s32[1,1,48]{2,1,0:T(1,128)S(1)}, s32[1,1,48]{2,1,0:T(1,128)}, u32[]{:S(2)}) copy-start(s32[1,1,48]{2,1,0:T(1,128)} %param.10) | copy-start | bytes 580
  39.6 10.9 %collective-permute-start.7 = (f32[48,4,128]{2,1,0:T(4,128)S(1)}, f32[48,4,128]{2,1,0:T(4,128)S(1)}, u32[]{:S(2)}, u32[]{:S(2)}) collective-permute-start(f32[48,4,128]{2,1,0:T(4,128)S(1)} %get-tuple-element.25), channel_id=1, source_target_pairs={{0,24},{1,25},{2,26},{3,27},{4,28},{5,29},{6,30},{7,31},{8,0},{9,1... | collective-permute-start | bytes 294920 | tf_op jit(solution)/shard_map/ppermute | solution.py:356
  45.2 7.4 %collective-permute-start.8 = (f32[48,4,128]{2,1,0:T(4,128)S(1)}, f32[48,4,128]{2,1,0:T(4,128)S(1)}, u32[]{:S(2)}, u32[]{:S(2)}) collective-permute-start(f32[48,4,128]{2,1,0:T(4,128)S(1)} %get-tuple-element.26), channel_id=1, source_target_pairs={{0,8},{1,9},{2,10},{3,11},{4,12},{5,13},{6,14},{7,15},{8,16},{9,17... | collective-permute-start | bytes 294920 | tf_op jit(solution)/shard_map/ppermute | solution.py:356
  45.2 7.4 %collective-permute-start.9 = (f32[48,4,128]{2,1,0:T(4,128)S(1)}, f32[48,4,128]{2,1,0:T(4,128)S(1)}, u32[]{:S(2)}, u32[]{:S(2)}) collective-permute-start(f32[48,4,128]{2,1,0:T(4,128)S(1)} %get-tuple-element.27), channel_id=1, source_target_pairs={{0,16},{1,17},{2,18},{3,19},{4,20},{5,21},{6,22},{7,23},{8,24},{9,... | collective-permute-start | bytes 294920 | tf_op jit(solution)/shard_map/ppermute | solution.py:356

commit v7 on v6

--- a/solution.py
+++ b/solution.py
@@ -17,6 +17,7 @@
 SOFT = 0.01
 UNROLL = 8
 MIB = 1 << 20
+TILES = 36
 F32 = jnp.float32
 I32 = jnp.int32
 BF16 = jnp.bfloat16
@@ -39,19 +40,21 @@
 
 
 def pack_kernel(*refs):
-    ins, (src_ref, tgt_ref, cell_ref), holds, sem = refs[:7], refs[7:10], refs[10:17], refs[17]
+    ins, (src_ref, tgt_ref, cell_ref), holds = refs[:7], refs[7:10], refs[10:18]
+    full, sem = refs[18:]
     copies = [pltpu.make_async_copy(ins[i], holds[i], sem.at[i]) for i in range(7)]
+    copies.append(pltpu.make_async_copy(ins[2], holds[7], sem.at[7]))
     for copy in copies:
         copy.start()
     for copy in copies:
         copy.wait()
-    pos_ref, mass_ref, cnt_ref, dest_ref, near_ref, ctr_ref, cm_ref = holds
+    pos_ref, mass_ref, cnt_ref, dest_ref, near_ref, ctr_ref, cm_ref, cnt_smem = holds
     counts = cnt_ref[...]
     cnt = column_of(counts, NB)
     near = near_ref[...]
     off = (near >= NB).astype(I32) + (near >= 2 * NB).astype(I32)
     dev = (dest_ref[...] + off - 1) & (NY * NZ - 1)
-    code = (dev >> 3) * 512 + (dev & (NZ - 1)) * NB + (near - off * NB)
+    code = (dev >> 3) * 512 + (dev & (NZ - 1)) * 64 + (near - off * NB)
     gap = jnp.zeros((4, 64 - NB), I32)
     info = jnp.concatenate([code, gap, jnp.broadcast_to(counts, (4, NB)), gap], axis=1)
     lane = lax.broadcasted_iota(I32, (NB, PL), 1)
@@ -59,10 +62,24 @@
     for c in range(3):
         value = pos_ref[c]
         tgt_ref[0:NB, c, :] = value
-        for z in range(NZ):
-            src_ref[z, :, c, :] = value
-    for z in range(NZ):
-        src_ref[z, :, 3, :] = weight
+        full[:, c, :] = value
+    full[:, 3, :] = weight
+    lane4 = lax.broadcasted_iota(I32, (4, PL), 1)
+    carry, begin = jnp.zeros((4, PL), F32), jnp.int32(0)
+    for b in range(NB):
+        shift, tile = begin & (PL - 1), begin >> 7
+        turned = pltpu.roll(full[b], shift, 1)[0:4]
+        merged = jnp.where(lane4 >= shift, turned, carry)
+        src_ref[0, tile] = merged
+        begin = begin + cnt_smem[0, b]
+        carry = jnp.where((begin >> 7) != tile, turned, merged)
+    square = (NB, NB)
+    earlier = lax.broadcasted_iota(I32, square, 0) < lax.broadcasted_iota(I32, square, 1)
+    starts = jnp.sum(jnp.where(earlier, cnt, 0), axis=0, keepdims=True)
+    places = jnp.concatenate([starts, gap[0:1], counts, gap[0:1]], axis=1)
+    src_ref[0, TILES] = jnp.broadcast_to(places, (4, PL)).astype(F32)
+    for z in range(1, NZ):
+        src_ref[z] = src_ref[0]
     tgt_ref[0:NB, 3, :] = jnp.zeros((NB, PL), F32)
     tgt_ref[NB] = info.astype(F32)
     for j in range(16):
@@ -202,8 +219,14 @@
 
 
 def near_kernel(first, tab, tall, src_ref, *refs):
-    outs, out_ref = refs[:-1], refs[-1]
+    outs, (out_ref, hold, spots, sem) = refs[:-4], refs[-4:]
+    for z in range(NZ):
+        hold[z : z + 1, :] = src_ref[z * (TILES + 1) + TILES][0:1].astype(I32)
+    copy = pltpu.make_async_copy(hold, spots, sem)
+    copy.start()
     out_ref[...] = jnp.zeros(out_ref.shape, F32)
+    copy.wait()
+    lane1 = lax.broadcasted_iota(I32, (1, PL), 1)
     sub4 = lax.broadcasted_iota(I32, (4, PL), 0)
     lane4 = lax.broadcasted_iota(I32, (4, PL), 1)
     spatial = sub4 < 3
@@ -228,12 +251,18 @@
         u = stack(mix(th, one), mix(th, one), mix(tm, one), mix(tm, qh), mix(th, qm), mix(tl, ql), zero8)
         vs, gs = [], []
         for k in range(width):
-            s = src_ref[tab[k, e]]
-            flag = (k < n).astype(F32)
+            z, bucket = tab[k, e] >> 6, tab[k, e] & 63
+            begin = spots[z, bucket]
+            shift = begin & (PL - 1)
+            tile = z * (TILES + 1) + (begin >> 7)
+            s = jnp.concatenate([src_ref[tile], src_ref[tile + 1]], axis=0)
+            s = pltpu.roll(s, (PL - shift) & (PL - 1), 1)
+            s = jnp.where(lane4 < PL - shift, s[0:4], s[4:8])
+            live = jnp.where(k < n, spots[z, 64 + bucket], 0)
             sh, sm, sl = split3(-2.0 * s)
             qh, qm, ql = split3(square(s) + SOFT)
             vs.append(stack(mix(sh, qh), mix(sm, qm), mix(sh, ql), mix(sm, one), mix(sl, one), mix(sh, one), zero8))
-            w = s[3:4] * flag
+            w = jnp.where(lane1 < live, s[3:4], 0.0)
             gs.append(stack(*split3(mix(s * w, w)), zero4))
         v = jnp.concatenate(vs, axis=1)
         g = jnp.concatenate(gs, axis=1)
@@ -261,13 +290,14 @@
     run(begin, n_full, 4, UNROLL)
     run(begin + n_full, n_half, 2, UNROLL // 2)
     for i, o in enumerate(outs):
-        o[...] = out_ref[i * NB : (i + 1) * NB]
+        for c in range(3):
+            o[c] = out_ref[i * NB : (i + 1) * NB, c, :]
 
 
 def final_kernel(cnt_ref, far_ref, p0, p1, p2, p3, out_ref):
     live = lax.broadcasted_iota(I32, (NB, PL), 1) < column_of(cnt_ref[...], NB)
     for c in range(3):
-        near = (p0[:, c, :] + p1[:, c, :]) + (p2[:, c, :] + p3[:, c, :])
+        near = (p0[c] + p1[c]) + (p2[c] + p3[c])
         out_ref[c] = jnp.where(live, far_ref[c] + near, 0.0)
 
 
@@ -296,7 +326,7 @@
     cnt = counts[0]
     src, tgt, cells = call(
         pack_kernel,
-        (((NZ, NB, 4, PL), F32), ((NB + 1, 4, PL), F32), ((16, 4, PL), F32)),
+        (((NZ, TILES + 1, 4, PL), F32), ((NB + 1, 4, PL), F32), ((16, 4, PL), F32)),
         [pl.BlockSpec(memory_space=pltpu.HBM)] * 7,
         [vspec()] * 3,
         "pack",
@@ -309,7 +339,9 @@
             pltpu.VMEM((K, NB), I32),
             pltpu.VMEM((3, 2048), F32),
             pltpu.VMEM((1, 2048), F32),
-            pltpu.SemaphoreType.DMA((7,)),
+            pltpu.SMEM((1, NB), I32),
+            pltpu.VMEM((NB, 8, PL), F32),
+            pltpu.SemaphoreType.DMA((8,)),
         ],
     )(pos, masses[0], cnt, dest_ids, near_list[0].T, cell_centers, cell_mass[None])
     z_rows = [[NZ * y + z for z in range(NZ)] for y in range(NY)]
@@ -338,18 +370,23 @@
         [pltpu.VMEM((PL, PL), F32)],
     )(place, pos, cnt, cell_list[0].T, *pairs)
     tall, tab, far = lax.optimization_barrier((tall, tab, far))
-    window = window.reshape(NZ * NB, 4, PL)
+    window = window.reshape(NZ * (TILES + 1), 4, PL)
 
     def near(first, tab):
         count = NY - 1 if first else 1
         return call(
             functools.partial(near_kernel, first),
-            (((NB, 4, PL), F32),) * count,
+            (((3, NB, PL), F32),) * count,
             [sspec()] + [vspec()] * 2,
             [vspec()] * count,
             "near",
             24,
-            [pltpu.VMEM((count * NB, 4, PL), F32)],
+            [
+                pltpu.VMEM((count * NB, 4, PL), F32),
+                pltpu.VMEM((NZ, PL), I32),
+                pltpu.SMEM((NZ, PL), I32),
+                pltpu.SemaphoreType.DMA,
+            ],
         )(tab, tall, window)
 
     sent = near(True, tab)

time: 53.6 us -> 51.1 us (0.953)
  Pallas kernels: 13.9 us -> 19.1 us
  waiting for transfers between devices: 11.7 us -> 6.63 us
  starting transfers between devices: 26.9 us -> 24.5 us
    pallas_call x3, Pallas kernels: 9.63 us -> 14.8 us  [the longest x2 12.7 us: near(): call(functools.partial(near_kernel, first), (((3, NB, PL), F32),) * count...]
    all_to_all x1, waiting for transfers between devices: 4.74 us -> 0.88 us  [per_device(): lax.all_to_all(src, 'space', 0, 0, axis_index_groups=z_rows, tiled=True)]
    ppermute x3, starting transfers between devices: 8.2 us -> 5.78 us  [per_device(): lax.ppermute(v, 'space', along_y(-k))]
    ppermute x3, waiting for transfers between devices: 2.11 us -> 0.87 us  [per_device(): lax.ppermute(v, 'space', along_y(-k))]
  transfers between devices with their start and end apart: 11 -> 11, of which waited for: 5 -> 5; matrix products, arithmetic and copies ran while one was open for 0% -> 0% of each run, Pallas kernels for 12% -> 15%
where the time goes in v7:
time: 51.1 us; the launch traced here: 51 us
  starting transfers between devices  24.5 us (48%)
  Pallas kernels  19.1 us (37%)
  waiting for transfers between devices  6.63 us (13%)
  local copies, waits for them, and re-layouts  0.67 us (1%)
    pallas_call x2, Pallas kernels, near(): call(functools.partial(near_kernel, first), (((3, NB, PL), F32),) * count...  12.7 us
    all_to_all x1, starting transfers between devices, per_device(): lax.all_to_all(src, 'space', 0, 0, axis_index_groups=z_rows, tiled=True)  9.03 us
    ppermute x3, starting transfers between devices, per_device(): lax.ppermute(v, 'space', along_y(-k))  5.78 us
    ppermute x3, starting transfers between devices, per_device(): tgts = [tgt] + [lax.ppermute(tgt, 'space', along_y(k)) for k in (1, -1, 2)]  4.38 us
    ppermute x3, starting transfers between devices, per_device(): lax.ppermute(pair, 'slab', along_x(k))  4.3 us
    ppermute x3, waiting for transfers between devices, per_device(): lax.ppermute(pair, 'slab', along_x(k))  4.02 us
    pallas_call x1, Pallas kernels, per_device(): call(pack_kernel, (((NZ, TILES + 1, 4, PL), F32), ((NB + 1, 4, PL), F32),...  2.13 us
    pallas_call x1, Pallas kernels, per_device(): call(prep_kernel, (((NY * NB, 4, PL), F32), ((16, 2 * PL), I32)), [sspec(...  2.06 us
  transfers between devices with their start and end apart: 11, of which 5 were waited for; matrix products, arithmetic and copies ran while one was open for 0% of the time, Pallas kernels for 15%

profile of v7, /device:TPU:1, one launch (start us, length us, event | category | flops | bytes accessed | tf_op | source)
XLA Modules:
  0.0 51.0 jit_solution(11859206891238706802)
XLA Ops:
  0.0 2.1 %pack.1 = (f32[8,37,4,128]{3,2,1,0:T(4,128)}, f32[49,4,128]{2,1,0:T(4,128)}, f32[16,4,128]{2,1,0:T(4,128)}) custom-call(f32[3,48,128]{2,1,0:T(8,128)} %bitcast.22, f32[48,128]{1,0:T(8,128)} %bitcast.30, s32[1,48]{1,0:T(1,128)} %bitcast.25, s32[1,48]{1,0:T(1,128)} %refs_3_.1, s32[4,48]{1,0:T(4,128)} %bitcast.32, f32[3,2048]{1,0:T(4,128)} %refs_5_.1, ...), custom_call_target="tpu_custom_call" | custom-call | tf_op jit(solution)/shard_map/pack/pallas_call | solution.py:327
  2.1 0.0 copy-start.4
  2.2 0.0 copy-start.2
  2.2 9.0 %all-to-all-start = ((f32[8,37,4,128]{3,2,1,0:T(4,128)}), f32[8,37,4,128]{3,2,1,0:T(4,128)S(1)}, u32[]{:S(2)}, u32[]{:S(2)}) async-start(f32[8,37,4,128]{3,2,1,0:T(4,128)} %get-tuple-element.24), calls=%async_computation | async-start | bytes 1212416 | tf_op jit(solution)/shard_map/all_to_all | solution.py:348
  11.2 1.0 %collective-permute-start.3 = (f32[16,4,128]{2,1,0:T(4,128)S(1)}, f32[16,4,128]{2,1,0:T(4,128)S(1)}, u32[]{:S(2)}, u32[]{:S(2)}) collective-permute-start(f32[16,4,128]{2,1,0:T(4,128)S(1)} %copy-done.4), channel_id=1, source_target_pairs={{0,32},{32,0},{64,96},{96,64},{128,160},{160,128},{192,224},{224,1... | collective-permute-start | bytes 98312 | tf_op jit(solution)/shard_map/ppermute | solution.py:350
  12.2 0.9 %collective-permute-done.3 = f32[16,4,128]{2,1,0:T(4,128)S(1)} collective-permute-done((f32[16,4,128]{2,1,0:T(4,128)S(1)}, f32[16,4,128]{2,1,0:T(4,128)S(1)}, u32[]{:S(2)}, u32[]{:S(2)}) %collective-permute-start.3) | collective-permute-done | bytes 32800 | tf_op jit(solution)/shard_map/ppermute | solution.py:350
  13.1 2.8 %collective-permute-start.6 = (f32[2,16,4,128]{3,2,1,0:T(4,128)S(1)}, f32[2,16,4,128]{3,2,1,0:T(4,128)S(1)}, u32[]{:S(2)}, u32[]{:S(2)}) collective-permute-start(f32[2,16,4,128]{3,2,1,0:T(4,128)S(1)} %pad_maximum_fusion.c0), channel_id=1, source_target_pairs={{0,128},{32,160},{64,192},{96,224},{128,0},{160,32},{192,64},{224,... | collective-permute-start | bytes 196616 | tf_op jit(solution)/shard_map/ppermute | solution.py:351
  16.0 2.9 %collective-permute-start.2 = (f32[49,4,128]{2,1,0:T(4,128)S(1)}, f32[49,4,128]{2,1,0:T(4,128)S(1)}, u32[]{:S(2)}, u32[]{:S(2)}) collective-permute-start(f32[49,4,128]{2,1,0:T(4,128)S(1)} %copy-done.1), channel_id=1, source_target_pairs={{0,16},{1,17},{2,18},{3,19},{4,20},{5,21},{6,22},{7,23},{8,24},{9,... | collective-permute-start | bytes 301064 | tf_op jit(solution)/shard_map/ppermute | solution.py:349
  18.9 0.8 %collective-permute-start.1 = (f32[49,4,128]{2,1,0:T(4,128)S(1)}, f32[49,4,128]{2,1,0:T(4,128)S(1)}, u32[]{:S(2)}, u32[]{:S(2)}) collective-permute-start(f32[49,4,128]{2,1,0:T(4,128)S(1)} %copy-done.1), channel_id=1, source_target_pairs={{0,24},{1,25},{2,26},{3,27},{4,28},{5,29},{6,30},{7,31},{8,0},{9,1... | collective-permute-start | bytes 301064 | tf_op jit(solution)/shard_map/ppermute | solution.py:349
  19.7 0.7 %collective-permute-start = (f32[49,4,128]{2,1,0:T(4,128)S(1)}, f32[49,4,128]{2,1,0:T(4,128)S(1)}, u32[]{:S(2)}, u32[]{:S(2)}) collective-permute-start(f32[49,4,128]{2,1,0:T(4,128)S(1)} %copy-done.1), channel_id=1, source_target_pairs={{0,8},{1,9},{2,10},{3,11},{4,12},{5,13},{6,14},{7,15},{8,16},{9,17... | collective-permute-start | bytes 301064 | tf_op jit(solution)/shard_map/ppermute | solution.py:349
  20.3 0.9 %collective-permute-start.5 = (f32[2,16,4,128]{3,2,1,0:T(4,128)S(1)}, f32[2,16,4,128]{3,2,1,0:T(4,128)S(1)}, u32[]{:S(2)}, u32[]{:S(2)}) collective-permute-start(f32[2,16,4,128]{3,2,1,0:T(4,128)S(1)} %pad_maximum_fusion.c0), channel_id=1, source_target_pairs={{0,192},{32,224},{64,0},{96,32},{128,64},{160,96},{192,128},{224,1... | collective-permute-start | bytes 196616 | tf_op jit(solution)/shard_map/ppermute | solution.py:351
  21.2 0.6 %collective-permute-start.4 = (f32[2,16,4,128]{3,2,1,0:T(4,128)S(1)}, f32[2,16,4,128]{3,2,1,0:T(4,128)S(1)}, u32[]{:S(2)}, u32[]{:S(2)}) collective-permute-start(f32[2,16,4,128]{3,2,1,0:T(4,128)S(1)} %pad_maximum_fusion.c0), channel_id=1, source_target_pairs={{0,64},{32,96},{64,128},{96,160},{128,192},{160,224},{192,0},{224,... | collective-permute-start | bytes 196616 | tf_op jit(solution)/shard_map/ppermute | solution.py:351
  21.8 1.9 %collective-permute-done.5.c2 = f32[2,16,4,128]{3,2,1,0:T(4,128)S(1)} collective-permute-done((f32[2,16,4,128]{3,2,1,0:T(4,128)S(1)}, f32[2,16,4,128]{3,2,1,0:T(4,128)S(1)}, u32[]{:S(2)}, u32[]{:S(2)}) %collective-permute-start.5) | collective-permute-done | bytes 65568 | tf_op jit(solution)/shard_map/ppermute | solution.py:351
  23.8 2.1 %collective-permute-done.4.c1 = f32[2,16,4,128]{3,2,1,0:T(4,128)S(1)} collective-permute-done((f32[2,16,4,128]{3,2,1,0:T(4,128)S(1)}, f32[2,16,4,128]{3,2,1,0:T(4,128)S(1)}, u32[]{:S(2)}, u32[]{:S(2)}) %collective-permute-start.4) | collective-permute-done | bytes 65568 | tf_op jit(solution)/shard_map/ppermute | solution.py:351
  25.8 0.6 %copy-done.3 = s32[1,1,48]{2,1,0:T(1,128)S(1)} copy-done((s32[1,1,48]{2,1,0:T(1,128)S(1)}, s32[1,1,48]{2,1,0:T(1,128)}, u32[]{:S(2)}) %copy-start.3) | copy-done | bytes 216
  26.5 1.4 %far.1.far_ref = f32[3,48,128]{2,1,0:T(8,128)S(1)} custom-call(s32[1]{0:T(128)} %bitcast.8.place_ref, f32[3,48,128]{2,1,0:T(8,128)S(1)} %bitcast.23, s32[1,48]{1,0:T(1,128)S(1)} %bitcast.26, s32[32,48]{1,0:T(8,128)S(1)} %bitcast.24, f32[2,16,4,128]{3,2,1,0:T(4,128)S(1)} %pad_maximum_fusion.c0, f32[2,16,4,128]{3,2,1,0:T(4,128)S(1)} %collective-permute-done.4.c1, ...), custom_call_target="tpu_custom_call" | custom-call | tf_op jit(solution)/shard_map/far/pallas_call | solution.py:363
  28.0 2.1 %prep.1 = (f32[192,4,128]{2,1,0:T(4,128)S(1)}, s32[16,256]{1,0:T(8,128)S(1)}) custom-call(s32[1]{0:T(128)} %bitcast.1.y_ref, f32[49,4,128]{2,1,0:T(4,128)S(1)} %copy-done.1, f32[49,4,128]{2,1,0:T(4,128)S(1)} %collective-permute-done.t1, f32[49,4,128]{2,1,0:T(4,128)S(1)} %collective-permute-done.1.t2, f32[49,4,128]{2,1,0:T(4,128)S(1)} %collective-permute-done.2.t3), custom_call_target="tpu_custom_call" | custom-call | tf_op jit(solution)/shard_map/prep/pallas_call | solution.py:354
  30.0 0.9 %all-to-all-done = f32[8,37,4,128]{3,2,1,0:T(4,128)S(1)} async-done(((f32[8,37,4,128]{3,2,1,0:T(4,128)}), f32[8,37,4,128]{3,2,1,0:T(4,128)S(1)}, u32[]{:S(2)}, u32[]{:S(2)}) %all-to-all-start) | async-done | bytes 606240 | tf_op jit(solution)/shard_map/all_to_all | solution.py:348
  30.9 8.4 %near.2 = (f32[3,48,128]{2,1,0:T(8,128)S(1)}, f32[3,48,128]{2,1,0:T(8,128)S(1)}, f32[3,48,128]{2,1,0:T(8,128)S(1)}) custom-call(s32[16,256]{1,0:T(8,128)S(1)} %get-tuple-element.28.tab, f32[192,4,128]{2,1,0:T(4,128)S(1)} %get-tuple-element.23.tall, f32[296,4,128]{2,1,0:T(4,128)S(1)} %bitcast.20), custom_call_target="tpu_custom_call" | custom-call | tf_op jit(solution)/shard_map/near/pallas_call | solution.py:377
  39.3 4.5 %collective-permute-start.7 = (f32[3,48,128]{2,1,0:T(8,128)S(1)}, f32[3,48,128]{2,1,0:T(8,128)S(1)}, u32[]{:S(2)}, u32[]{:S(2)}) collective-permute-start(f32[3,48,128]{2,1,0:T(8,128)S(1)} %get-tuple-element.25), channel_id=1, source_target_pairs={{0,24},{1,25},{2,26},{3,27},{4,28},{5,29},{6,30},{7,31},{8,0},{9,1... | collective-permute-start | bytes 221192 | tf_op jit(solution)/shard_map/ppermute | solution.py:393
  43.8 1.3 %collective-permute-start.9 = (f32[3,48,128]{2,1,0:T(8,128)S(1)}, f32[3,48,128]{2,1,0:T(8,128)S(1)}, u32[]{:S(2)}, u32[]{:S(2)}) collective-permute-start(f32[3,48,128]{2,1,0:T(8,128)S(1)} %get-tuple-element.27), channel_id=1, source_target_pairs={{0,16},{1,17},{2,18},{3,19},{4,20},{5,21},{6,22},{7,23},{8,24},{9,... | collective-permute-start | bytes 221192 | tf_op jit(solution)/shard_map/ppermute | solution.py:393
  45.1 4.3 %near.3.p0 = f32[3,48,128]{2,1,0:T(8,128)S(1)} custom-call(s32[16,256]{1,0:T(8,128)S(1)} %get-tuple-element.28.tab, f32[192,4,128]{2,1,0:T(4,128)S(1)} %get-tuple-element.23.tall, f32[296,4,128]{2,1,0:T(4,128)S(1)} %bitcast.21), custom_call_target="tpu_custom_call" | custom-call | tf_op jit(solution)/shard_map/near/pallas_call | solution.py:377
  49.4 0.9 %collective-permute-done.8.p2 = f32[3,48,128]{2,1,0:T(8,128)S(1)} collective-permute-done((f32[3,48,128]{2,1,0:T(8,128)S(1)}, f32[3,48,128]{2,1,0:T(8,128)S(1)}, u32[]{:S(2)}, u32[]{:S(2)}) %collective-permute-start.8) | collective-permute-done | bytes 73760 | tf_op jit(solution)/shard_map/ppermute | solution.py:393
  50.3 0.7 %final.1 = f32[3,48,128]{2,1,0:T(8,128)} custom-call(s32[1,48]{1,0:T(1,128)S(1)} %bitcast.27, f32[3,48,128]{2,1,0:T(8,128)S(1)} %far.1.far_ref, f32[3,48,128]{2,1,0:T(8,128)S(1)} %near.3.p0, f32[3,48,128]{2,1,0:T(8,128)S(1)} %collective-permute-done.7.p1, f32[3,48,128]{2,1,0:T(8,128)S(1)} %collective-permute-done.8.p2, ...), custom_call_target="tpu_custom_call" | custom-call | tf_op jit(solution)/shard_map/final/pallas_call | solution.py:396
  (15 shorter events, 0.0 us)
Async XLA Ops:
  2.1 9.1 %copy-start.4 = (f32[16,4,128]{2,1,0:T(4,128)S(1)}, f32[16,4,128]{2,1,0:T(4,128)}, u32[]{:S(2)}) copy-start(f32[16,4,128]{2,1,0:T(4,128)} %get-tuple-element.20) | copy-start | bytes 98308
  2.2 23.7 %copy-start.2 = (s32[1,48,32]{1,2,0:T(8,128)S(1)}, s32[1,48,32]{1,2,0:T(8,128)}, u32[]{:S(2)}) copy-start(s32[1,48,32]{1,2,0:T(8,128)} %param.13) | copy-start | bytes 18436
  2.2 28.7 %all-to-all-start = ((f32[8,37,4,128]{3,2,1,0:T(4,128)}), f32[8,37,4,128]{3,2,1,0:T(4,128)S(1)}, u32[]{:S(2)}, u32[]{:S(2)}) async-start(f32[8,37,4,128]{3,2,1,0:T(4,128)} %get-tuple-element.24), calls=%async_computation | async-start | bytes 1212416 | tf_op jit(solution)/shard_map/all_to_all | solution.py:348
  11.2 4.8 %copy-start.1 = (f32[49,4,128]{2,1,0:T(4,128)S(1)}, f32[49,4,128]{2,1,0:T(4,128)}, u32[]{:S(2)}) copy-start(f32[49,4,128]{2,1,0:T(4,128)} %get-tuple-element.17.t0) | copy-start | bytes 301060
  11.2 1.9 %collective-permute-start.3 = (f32[16,4,128]{2,1,0:T(4,128)S(1)}, f32[16,4,128]{2,1,0:T(4,128)S(1)}, u32[]{:S(2)}, u32[]{:S(2)}) collective-permute-start(f32[16,4,128]{2,1,0:T(4,128)S(1)} %copy-done.4), channel_id=1, source_target_pairs={{0,32},{32,0},{64,96},{96,64},{128,160},{160,128},{192,224},{224,1... | collective-permute-start | bytes 98312 | tf_op jit(solution)/shard_map/ppermute | solution.py:350
  13.1 12.7 %copy-start = (f32[1,48,3,128]{3,1,2,0:T(8,128)S(1)}, f32[1,48,3,128]{3,1,2,0:T(8,128)}, u32[]{:S(2)}) copy-start(f32[1,48,3,128]{3,1,2,0:T(8,128)} %param.8) | copy-start | bytes 221188
  13.1 8.1 %collective-permute-start.6 = (f32[2,16,4,128]{3,2,1,0:T(4,128)S(1)}, f32[2,16,4,128]{3,2,1,0:T(4,128)S(1)}, u32[]{:S(2)}, u32[]{:S(2)}) collective-permute-start(f32[2,16,4,128]{3,2,1,0:T(4,128)S(1)} %pad_maximum_fusion.c0), channel_id=1, source_target_pairs={{0,128},{32,160},{64,192},{96,224},{128,0},{160,32},{192,64},{224,... | collective-permute-start | bytes 196616 | tf_op jit(solution)/shard_map/ppermute | solution.py:351
  16.0 12.0 %collective-permute-start.2 = (f32[49,4,128]{2,1,0:T(4,128)S(1)}, f32[49,4,128]{2,1,0:T(4,128)S(1)}, u32[]{:S(2)}, u32[]{:S(2)}) collective-permute-start(f32[49,4,128]{2,1,0:T(4,128)S(1)} %copy-done.1), channel_id=1, source_target_pairs={{0,16},{1,17},{2,18},{3,19},{4,20},{5,21},{6,22},{7,23},{8,24},{9,... | collective-permute-start | bytes 301064 | tf_op jit(solution)/shard_map/ppermute | solution.py:349
  18.9 9.1 %collective-permute-start.1 = (f32[49,4,128]{2,1,0:T(4,128)S(1)}, f32[49,4,128]{2,1,0:T(4,128)S(1)}, u32[]{:S(2)}, u32[]{:S(2)}) collective-permute-start(f32[49,4,128]{2,1,0:T(4,128)S(1)} %copy-done.1), channel_id=1, source_target_pairs={{0,24},{1,25},{2,26},{3,27},{4,28},{5,29},{6,30},{7,31},{8,0},{9,1... | collective-permute-start | bytes 301064 | tf_op jit(solution)/shard_map/ppermute | solution.py:349
  19.7 8.3 %collective-permute-start = (f32[49,4,128]{2,1,0:T(4,128)S(1)}, f32[49,4,128]{2,1,0:T(4,128)S(1)}, u32[]{:S(2)}, u32[]{:S(2)}) collective-permute-start(f32[49,4,128]{2,1,0:T(4,128)S(1)} %copy-done.1), channel_id=1, source_target_pairs={{0,8},{1,9},{2,10},{3,11},{4,12},{5,13},{6,14},{7,15},{8,16},{9,17... | collective-permute-start | bytes 301064 | tf_op jit(solution)/shard_map/ppermute | solution.py:349
  20.3 3.4 %collective-permute-start.5 = (f32[2,16,4,128]{3,2,1,0:T(4,128)S(1)}, f32[2,16,4,128]{3,2,1,0:T(4,128)S(1)}, u32[]{:S(2)}, u32[]{:S(2)}) collective-permute-start(f32[2,16,4,128]{3,2,1,0:T(4,128)S(1)} %pad_maximum_fusion.c0), channel_id=1, source_target_pairs={{0,192},{32,224},{64,0},{96,32},{128,64},{160,96},{192,128},{224,1... | collective-permute-start | bytes 196616 | tf_op jit(solution)/shard_map/ppermute | solution.py:351
  21.2 4.6 %collective-permute-start.4 = (f32[2,16,4,128]{3,2,1,0:T(4,128)S(1)}, f32[2,16,4,128]{3,2,1,0:T(4,128)S(1)}, u32[]{:S(2)}, u32[]{:S(2)}) collective-permute-start(f32[2,16,4,128]{3,2,1,0:T(4,128)S(1)} %pad_maximum_fusion.c0), channel_id=1, source_target_pairs={{0,64},{32,96},{64,128},{96,160},{128,192},{160,224},{192,0},{224,... | collective-permute-start | bytes 196616 | tf_op jit(solution)/shard_map/ppermute | solution.py:351
  25.8 0.7 %copy-start.3 = (s32[1,1,48]{2,1,0:T(1,128)S(1)}, s32[1,1,48]{2,1,0:T(1,128)}, u32[]{:S(2)}) copy-start(s32[1,1,48]{2,1,0:T(1,128)} %param.10) | copy-start | bytes 580
  39.3 10.1 %collective-permute-start.7 = (f32[3,48,128]{2,1,0:T(8,128)S(1)}, f32[3,48,128]{2,1,0:T(8,128)S(1)}, u32[]{:S(2)}, u32[]{:S(2)}) collective-permute-start(f32[3,48,128]{2,1,0:T(8,128)S(1)} %get-tuple-element.25), channel_id=1, source_target_pairs={{0,24},{1,25},{2,26},{3,27},{4,28},{5,29},{6,30},{7,31},{8,0},{9,1... | collective-permute-start | bytes 221192 | tf_op jit(solution)/shard_map/ppermute | solution.py:393
  43.8 6.5 %collective-permute-start.8 = (f32[3,48,128]{2,1,0:T(8,128)S(1)}, f32[3,48,128]{2,1,0:T(8,128)S(1)}, u32[]{:S(2)}, u32[]{:S(2)}) collective-permute-start(f32[3,48,128]{2,1,0:T(8,128)S(1)} %get-tuple-element.26), channel_id=1, source_target_pairs={{0,8},{1,9},{2,10},{3,11},{4,12},{5,13},{6,14},{7,15},{8,16},{9,17... | collective-permute-start | bytes 221192 | tf_op jit(solution)/shard_map/ppermute | solution.py:393
  43.8 6.5 %collective-permute-start.9 = (f32[3,48,128]{2,1,0:T(8,128)S(1)}, f32[3,48,128]{2,1,0:T(8,128)S(1)}, u32[]{:S(2)}, u32[]{:S(2)}) collective-permute-start(f32[3,48,128]{2,1,0:T(8,128)S(1)} %get-tuple-element.27), channel_id=1, source_target_pairs={{0,16},{1,17},{2,18},{3,19},{4,20},{5,21},{6,22},{7,23},{8,24},{9,... | collective-permute-start | bytes 221192 | tf_op jit(solution)/shard_map/ppermute | solution.py:393

commit v8 on v7

--- a/solution.py
+++ b/solution.py
@@ -15,7 +15,8 @@
 NZ = 8
 NX = 4
 SOFT = 0.01
-UNROLL = 8
+UNROLL = (14, 12)
+UNROLL_OWN = (14, 4)
 MIB = 1 << 20
 TILES = 36
 F32 = jnp.float32
@@ -159,7 +160,7 @@
     return high, mid, rest - mid
 
 
-def prep_kernel(y_ref, t0, t1, t2, t3, tall, tab, hold, sem):
+def prep_kernel(y_ref, t0, t1, t2, t3, tall, tab):
     me = y_ref[0]
     wide = 2 * PL
     tiles = []
@@ -212,20 +213,19 @@
     out = lax.dot_general(both, moved, (((1,), (1,)), ((), ())), preferred_element_type=F32)
     out = out[0:8] + out[8:16]
     sizes = jnp.concatenate([jnp.broadcast_to(v, (1, wide)) for v in sizes + [begin] * 4], axis=0)
-    hold[...] = jnp.concatenate([out, sizes], axis=0).astype(I32)
-    copy = pltpu.make_async_copy(hold, tab, sem)
-    copy.start()
-    copy.wait()
-
-
-def near_kernel(first, tab, tall, src_ref, *refs):
-    outs, (out_ref, hold, spots, sem) = refs[:-4], refs[-4:]
+    tab[...] = jnp.concatenate([out, sizes], axis=0).astype(I32)
+
+
+def near_kernel(first, table, tall, src_ref, *refs):
+    outs, (out_ref, hold, spots, tab, sem) = refs[:-5], refs[-5:]
+    copies = [pltpu.make_async_copy(table, tab, sem.at[0]), pltpu.make_async_copy(hold, spots, sem.at[1])]
+    copies[0].start()
     for z in range(NZ):
         hold[z : z + 1, :] = src_ref[z * (TILES + 1) + TILES][0:1].astype(I32)
-    copy = pltpu.make_async_copy(hold, spots, sem)
-    copy.start()
+    copies[1].start()
     out_ref[...] = jnp.zeros(out_ref.shape, F32)
-    copy.wait()
+    for copy in copies:
+        copy.wait()
     lane1 = lax.broadcasted_iota(I32, (1, PL), 1)
     sub4 = lax.broadcasted_iota(I32, (4, PL), 0)
     lane4 = lax.broadcasted_iota(I32, (4, PL), 1)
@@ -287,8 +287,9 @@
 
     begin = jnp.int32(0) if first else sizes[0] + sizes[1]
     n_full, n_half = (sizes[0], sizes[1]) if first else (sizes[2], sizes[3])
-    run(begin, n_full, 4, UNROLL)
-    run(begin + n_full, n_half, 2, UNROLL // 2)
+    steps = UNROLL if first else UNROLL_OWN
+    run(begin, n_full, 4, steps[0])
+    run(begin + n_full, n_half, 2, steps[1])
     for i, o in enumerate(outs):
         for c in range(3):
             o[c] = out_ref[i * NB : (i + 1) * NB, c, :]
@@ -355,10 +356,9 @@
         prep_kernel,
         (((NY * NB, 4, PL), F32), ((16, 2 * PL), I32)),
         [sspec()] + [vspec()] * 4,
-        [vspec(), sspec()],
+        [vspec(), vspec()],
         "prep",
         8,
-        [pltpu.VMEM((16, 2 * PL), I32), pltpu.SemaphoreType.DMA],
     )(me, *tgts)
     (far,) = call(
         far_kernel,
@@ -377,7 +377,7 @@
         return call(
             functools.partial(near_kernel, first),
             (((3, NB, PL), F32),) * count,
-            [sspec()] + [vspec()] * 2,
+            [vspec()] * 3,
             [vspec()] * count,
             "near",
             24,
@@ -385,7 +385,8 @@
                 pltpu.VMEM((count * NB, 4, PL), F32),
                 pltpu.VMEM((NZ, PL), I32),
                 pltpu.SMEM((NZ, PL), I32),
-                pltpu.SemaphoreType.DMA,
+                pltpu.SMEM((16, 2 * PL), I32),
+                pltpu.SemaphoreType.DMA((2,)),
             ],
         )(tab, tall, window)
 

time: 51.1 us -> 48.8 us (0.955)
  the two profiles are of different devices: /device:TPU:1 before, /device:TPU:4 now
where the time goes in v8:
time: 48.8 us; the launch traced here: 48.4 us
  starting transfers between devices  21.8 us (45%)
  Pallas kernels  17.1 us (35%)
  waiting for transfers between devices  8.66 us (18%)
  local copies, waits for them, and re-layouts  0.67 us (1%)
    pallas_call x2, Pallas kernels, near(): call(functools.partial(near_kernel, first), (((3, NB, PL), F32),) * count...  12.4 us
    all_to_all x1, starting transfers between devices, per_device(): lax.all_to_all(src, 'space', 0, 0, axis_index_groups=z_rows, tiled=True)  8.48 us
    ppermute x3, starting transfers between devices, per_device(): lax.ppermute(v, 'space', along_y(-k))  5.29 us
    ppermute x3, starting transfers between devices, per_device(): tgts = [tgt] + [lax.ppermute(tgt, 'space', along_y(k)) for k in (1, -1, 2)]  5.22 us
    ppermute x3, waiting for transfers between devices, per_device(): lax.ppermute(pair, 'slab', along_x(k))  4.27 us
    all_to_all x1, waiting for transfers between devices, per_device(): lax.all_to_all(src, 'space', 0, 0, axis_index_groups=z_rows, tiled=True)  3.18 us
    ppermute x3, starting transfers between devices, per_device(): lax.ppermute(pair, 'slab', along_x(k))  2.75 us
    pallas_call x1, Pallas kernels, per_device(): call(pack_kernel, (((NZ, TILES + 1, 4, PL), F32), ((NB + 1, 4, PL), F32),...  2.13 us
  transfers between devices with their start and end apart: 11, of which 4 were waited for; matrix products, arithmetic and copies ran while one was open for 0% of the time, Pallas kernels for 15%

profile of v8, /device:TPU:4, one launch (start us, length us, event | category | flops | bytes accessed | tf_op | source)
XLA Modules:
  0.0 48.4 jit_solution(11499745249641807448)
XLA Ops:
  0.0 2.1 %pack.1 = (f32[8,37,4,128]{3,2,1,0:T(4,128)}, f32[49,4,128]{2,1,0:T(4,128)}, f32[16,4,128]{2,1,0:T(4,128)}) custom-call(f32[3,48,128]{2,1,0:T(8,128)} %bitcast.22, f32[48,128]{1,0:T(8,128)} %bitcast.30, s32[1,48]{1,0:T(1,128)} %bitcast.25, s32[1,48]{1,0:T(1,128)} %refs_3_.1, s32[4,48]{1,0:T(4,128)} %bitcast.32, f32[3,2048]{1,0:T(4,128)} %refs_5_.1, ...), custom_call_target="tpu_custom_call" | custom-call | tf_op jit(solution)/shard_map/pack/pallas_call | solution.py:328
  2.1 0.0 copy-start.4
  2.2 0.0 copy-start.2
  2.2 8.5 %all-to-all-start = ((f32[8,37,4,128]{3,2,1,0:T(4,128)}), f32[8,37,4,128]{3,2,1,0:T(4,128)S(1)}, u32[]{:S(2)}, u32[]{:S(2)}) async-start(f32[8,37,4,128]{3,2,1,0:T(4,128)} %get-tuple-element.24), calls=%async_computation | async-start | bytes 1212416 | tf_op jit(solution)/shard_map/all_to_all | solution.py:349
  10.7 0.1 collective-permute-start.3
  10.8 1.2 %collective-permute-done.3 = f32[16,4,128]{2,1,0:T(4,128)S(1)} collective-permute-done((f32[16,4,128]{2,1,0:T(4,128)S(1)}, f32[16,4,128]{2,1,0:T(4,128)S(1)}, u32[]{:S(2)}, u32[]{:S(2)}) %collective-permute-start.3) | collective-permute-done | bytes 32800 | tf_op jit(solution)/shard_map/ppermute | solution.py:351
  12.0 0.6 %collective-permute-start.6 = (f32[2,16,4,128]{3,2,1,0:T(4,128)S(1)}, f32[2,16,4,128]{3,2,1,0:T(4,128)S(1)}, u32[]{:S(2)}, u32[]{:S(2)}) collective-permute-start(f32[2,16,4,128]{3,2,1,0:T(4,128)S(1)} %pad_maximum_fusion.c0), channel_id=1, source_target_pairs={{0,128},{32,160},{64,192},{96,224},{128,0},{160,32},{192,64},{224,... | collective-permute-start | bytes 196616 | tf_op jit(solution)/shard_map/ppermute | solution.py:352
  12.6 3.2 %collective-permute-start.2 = (f32[49,4,128]{2,1,0:T(4,128)S(1)}, f32[49,4,128]{2,1,0:T(4,128)S(1)}, u32[]{:S(2)}, u32[]{:S(2)}) collective-permute-start(f32[49,4,128]{2,1,0:T(4,128)S(1)} %copy-done.1), channel_id=1, source_target_pairs={{0,16},{1,17},{2,18},{3,19},{4,20},{5,21},{6,22},{7,23},{8,24},{9,... | collective-permute-start | bytes 301064 | tf_op jit(solution)/shard_map/ppermute | solution.py:350
  15.8 1.1 %collective-permute-start.1 = (f32[49,4,128]{2,1,0:T(4,128)S(1)}, f32[49,4,128]{2,1,0:T(4,128)S(1)}, u32[]{:S(2)}, u32[]{:S(2)}) collective-permute-start(f32[49,4,128]{2,1,0:T(4,128)S(1)} %copy-done.1), channel_id=1, source_target_pairs={{0,24},{1,25},{2,26},{3,27},{4,28},{5,29},{6,30},{7,31},{8,0},{9,1... | collective-permute-start | bytes 301064 | tf_op jit(solution)/shard_map/ppermute | solution.py:350
  16.8 1.0 %collective-permute-start = (f32[49,4,128]{2,1,0:T(4,128)S(1)}, f32[49,4,128]{2,1,0:T(4,128)S(1)}, u32[]{:S(2)}, u32[]{:S(2)}) collective-permute-start(f32[49,4,128]{2,1,0:T(4,128)S(1)} %copy-done.1), channel_id=1, source_target_pairs={{0,8},{1,9},{2,10},{3,11},{4,12},{5,13},{6,14},{7,15},{8,16},{9,17... | collective-permute-start | bytes 301064 | tf_op jit(solution)/shard_map/ppermute | solution.py:350
  17.8 2.2 %collective-permute-start.5 = (f32[2,16,4,128]{3,2,1,0:T(4,128)S(1)}, f32[2,16,4,128]{3,2,1,0:T(4,128)S(1)}, u32[]{:S(2)}, u32[]{:S(2)}) collective-permute-start(f32[2,16,4,128]{3,2,1,0:T(4,128)S(1)} %pad_maximum_fusion.c0), channel_id=1, source_target_pairs={{0,192},{32,224},{64,0},{96,32},{128,64},{160,96},{192,128},{224,1... | collective-permute-start | bytes 196616 | tf_op jit(solution)/shard_map/ppermute | solution.py:352
  19.9 0.0 collective-permute-done.6.c3
  20.0 2.2 %collective-permute-done.5.c2 = f32[2,16,4,128]{3,2,1,0:T(4,128)S(1)} collective-permute-done((f32[2,16,4,128]{3,2,1,0:T(4,128)S(1)}, f32[2,16,4,128]{3,2,1,0:T(4,128)S(1)}, u32[]{:S(2)}, u32[]{:S(2)}) %collective-permute-start.5) | collective-permute-done | bytes 65568 | tf_op jit(solution)/shard_map/ppermute | solution.py:352
  22.1 2.1 %collective-permute-done.4.c1 = f32[2,16,4,128]{3,2,1,0:T(4,128)S(1)} collective-permute-done((f32[2,16,4,128]{3,2,1,0:T(4,128)S(1)}, f32[2,16,4,128]{3,2,1,0:T(4,128)S(1)}, u32[]{:S(2)}, u32[]{:S(2)}) %collective-permute-start.4) | collective-permute-done | bytes 65568 | tf_op jit(solution)/shard_map/ppermute | solution.py:352
  24.2 0.6 %copy-done.3 = s32[1,1,48]{2,1,0:T(1,128)S(1)} copy-done((s32[1,1,48]{2,1,0:T(1,128)S(1)}, s32[1,1,48]{2,1,0:T(1,128)}, u32[]{:S(2)}) %copy-start.3) | copy-done | bytes 216
  24.9 1.4 %far.1.far_ref = f32[3,48,128]{2,1,0:T(8,128)S(1)} custom-call(s32[1]{0:T(128)} %bitcast.8.place_ref, f32[3,48,128]{2,1,0:T(8,128)S(1)} %bitcast.23, s32[1,48]{1,0:T(1,128)S(1)} %bitcast.26, s32[32,48]{1,0:T(8,128)S(1)} %bitcast.24, f32[2,16,4,128]{3,2,1,0:T(4,128)S(1)} %pad_maximum_fusion.c0, f32[2,16,4,128]{3,2,1,0:T(4,128)S(1)} %collective-permute-done.4.c1, ...), custom_call_target="tpu_custom_call" | custom-call | tf_op jit(solution)/shard_map/far/pallas_call | solution.py:363
  26.3 0.4 prep.1
  26.7 3.2 %all-to-all-done = f32[8,37,4,128]{3,2,1,0:T(4,128)S(1)} async-done(((f32[8,37,4,128]{3,2,1,0:T(4,128)}), f32[8,37,4,128]{3,2,1,0:T(4,128)S(1)}, u32[]{:S(2)}, u32[]{:S(2)}) %all-to-all-start) | async-done | bytes 606240 | tf_op jit(solution)/shard_map/all_to_all | solution.py:349
  29.9 7.0 %near.2 = (f32[3,48,128]{2,1,0:T(8,128)S(1)}, f32[3,48,128]{2,1,0:T(8,128)S(1)}, f32[3,48,128]{2,1,0:T(8,128)S(1)}) custom-call(s32[16,256]{1,0:T(8,128)S(1)} %get-tuple-element.28.table, f32[192,4,128]{2,1,0:T(4,128)S(1)} %get-tuple-element.23.tall, f32[296,4,128]{2,1,0:T(4,128)S(1)} %bitcast.20), custom_call_target="tpu_custom_call" | custom-call | tf_op jit(solution)/shard_map/near/pallas_call | solution.py:377
  36.9 1.4 %collective-permute-start.7 = (f32[3,48,128]{2,1,0:T(8,128)S(1)}, f32[3,48,128]{2,1,0:T(8,128)S(1)}, u32[]{:S(2)}, u32[]{:S(2)}) collective-permute-start(f32[3,48,128]{2,1,0:T(8,128)S(1)} %get-tuple-element.25), channel_id=1, source_target_pairs={{0,24},{1,25},{2,26},{3,27},{4,28},{5,29},{6,30},{7,31},{8,0},{9,1... | collective-permute-start | bytes 221192 | tf_op jit(solution)/shard_map/ppermute | solution.py:394
  38.3 0.7 %collective-permute-start.8 = (f32[3,48,128]{2,1,0:T(8,128)S(1)}, f32[3,48,128]{2,1,0:T(8,128)S(1)}, u32[]{:S(2)}, u32[]{:S(2)}) collective-permute-start(f32[3,48,128]{2,1,0:T(8,128)S(1)} %get-tuple-element.26), channel_id=1, source_target_pairs={{0,8},{1,9},{2,10},{3,11},{4,12},{5,13},{6,14},{7,15},{8,16},{9,17... | collective-permute-start | bytes 221192 | tf_op jit(solution)/shard_map/ppermute | solution.py:394
  39.0 3.2 %collective-permute-start.9 = (f32[3,48,128]{2,1,0:T(8,128)S(1)}, f32[3,48,128]{2,1,0:T(8,128)S(1)}, u32[]{:S(2)}, u32[]{:S(2)}) collective-permute-start(f32[3,48,128]{2,1,0:T(8,128)S(1)} %get-tuple-element.27), channel_id=1, source_target_pairs={{0,16},{1,17},{2,18},{3,19},{4,20},{5,21},{6,22},{7,23},{8,24},{9,... | collective-permute-start | bytes 221192 | tf_op jit(solution)/shard_map/ppermute | solution.py:394
  42.2 5.4 %near.3.p0 = f32[3,48,128]{2,1,0:T(8,128)S(1)} custom-call(s32[16,256]{1,0:T(8,128)S(1)} %get-tuple-element.28.table, f32[192,4,128]{2,1,0:T(4,128)S(1)} %get-tuple-element.23.tall, f32[296,4,128]{2,1,0:T(4,128)S(1)} %bitcast.21), custom_call_target="tpu_custom_call" | custom-call | tf_op jit(solution)/shard_map/near/pallas_call | solution.py:377
  47.6 0.7 %final.1 = f32[3,48,128]{2,1,0:T(8,128)} custom-call(s32[1,48]{1,0:T(1,128)S(1)} %bitcast.27, f32[3,48,128]{2,1,0:T(8,128)S(1)} %far.1.far_ref, f32[3,48,128]{2,1,0:T(8,128)S(1)} %near.3.p0, f32[3,48,128]{2,1,0:T(8,128)S(1)} %collective-permute-done.7.p1, f32[3,48,128]{2,1,0:T(8,128)S(1)} %collective-permute-done.8.p2, ...), custom_call_target="tpu_custom_call" | custom-call | tf_op jit(solution)/shard_map/final/pallas_call | solution.py:397
  (15 shorter events, 0.0 us)
Async XLA Ops:
  2.1 8.5 %copy-start.4 = (f32[16,4,128]{2,1,0:T(4,128)S(1)}, f32[16,4,128]{2,1,0:T(4,128)}, u32[]{:S(2)}) copy-start(f32[16,4,128]{2,1,0:T(4,128)} %get-tuple-element.20) | copy-start | bytes 98308
  2.2 22.1 %copy-start.2 = (s32[1,48,32]{1,2,0:T(8,128)S(1)}, s32[1,48,32]{1,2,0:T(8,128)}, u32[]{:S(2)}) copy-start(s32[1,48,32]{1,2,0:T(8,128)} %param.13) | copy-start | bytes 18436
  2.2 27.7 %all-to-all-start = ((f32[8,37,4,128]{3,2,1,0:T(4,128)}), f32[8,37,4,128]{3,2,1,0:T(4,128)S(1)}, u32[]{:S(2)}, u32[]{:S(2)}) async-start(f32[8,37,4,128]{3,2,1,0:T(4,128)} %get-tuple-element.24), calls=%async_computation | async-start | bytes 1212416 | tf_op jit(solution)/shard_map/all_to_all | solution.py:349
  10.6 1.9 %copy-start.1 = (f32[49,4,128]{2,1,0:T(4,128)S(1)}, f32[49,4,128]{2,1,0:T(4,128)}, u32[]{:S(2)}) copy-start(f32[49,4,128]{2,1,0:T(4,128)} %get-tuple-element.17.t0) | copy-start | bytes 301060
  10.7 1.3 %collective-permute-start.3 = (f32[16,4,128]{2,1,0:T(4,128)S(1)}, f32[16,4,128]{2,1,0:T(4,128)S(1)}, u32[]{:S(2)}, u32[]{:S(2)}) collective-permute-start(f32[16,4,128]{2,1,0:T(4,128)S(1)} %copy-done.4), channel_id=1, source_target_pairs={{0,32},{32,0},{64,96},{96,64},{128,160},{160,128},{192,224},{224,1... | collective-permute-start | bytes 98312 | tf_op jit(solution)/shard_map/ppermute | solution.py:351
  12.0 12.3 %copy-start = (f32[1,48,3,128]{3,1,2,0:T(8,128)S(1)}, f32[1,48,3,128]{3,1,2,0:T(8,128)}, u32[]{:S(2)}) copy-start(f32[1,48,3,128]{3,1,2,0:T(8,128)} %param.8) | copy-start | bytes 221188
  12.0 8.0 %collective-permute-start.6 = (f32[2,16,4,128]{3,2,1,0:T(4,128)S(1)}, f32[2,16,4,128]{3,2,1,0:T(4,128)S(1)}, u32[]{:S(2)}, u32[]{:S(2)}) collective-permute-start(f32[2,16,4,128]{3,2,1,0:T(4,128)S(1)} %pad_maximum_fusion.c0), channel_id=1, source_target_pairs={{0,128},{32,160},{64,192},{96,224},{128,0},{160,32},{192,64},{224,... | collective-permute-start | bytes 196616 | tf_op jit(solution)/shard_map/ppermute | solution.py:352
  12.6 13.7 %collective-permute-start.2 = (f32[49,4,128]{2,1,0:T(4,128)S(1)}, f32[49,4,128]{2,1,0:T(4,128)S(1)}, u32[]{:S(2)}, u32[]{:S(2)}) collective-permute-start(f32[49,4,128]{2,1,0:T(4,128)S(1)} %copy-done.1), channel_id=1, source_target_pairs={{0,16},{1,17},{2,18},{3,19},{4,20},{5,21},{6,22},{7,23},{8,24},{9,... | collective-permute-start | bytes 301064 | tf_op jit(solution)/shard_map/ppermute | solution.py:350
  15.8 10.6 %collective-permute-start.1 = (f32[49,4,128]{2,1,0:T(4,128)S(1)}, f32[49,4,128]{2,1,0:T(4,128)S(1)}, u32[]{:S(2)}, u32[]{:S(2)}) collective-permute-start(f32[49,4,128]{2,1,0:T(4,128)S(1)} %copy-done.1), channel_id=1, source_target_pairs={{0,24},{1,25},{2,26},{3,27},{4,28},{5,29},{6,30},{7,31},{8,0},{9,1... | collective-permute-start | bytes 301064 | tf_op jit(solution)/shard_map/ppermute | solution.py:350
  16.8 9.5 %collective-permute-start = (f32[49,4,128]{2,1,0:T(4,128)S(1)}, f32[49,4,128]{2,1,0:T(4,128)S(1)}, u32[]{:S(2)}, u32[]{:S(2)}) collective-permute-start(f32[49,4,128]{2,1,0:T(4,128)S(1)} %copy-done.1), channel_id=1, source_target_pairs={{0,8},{1,9},{2,10},{3,11},{4,12},{5,13},{6,14},{7,15},{8,16},{9,17... | collective-permute-start | bytes 301064 | tf_op jit(solution)/shard_map/ppermute | solution.py:350
  17.8 4.3 %collective-permute-start.5 = (f32[2,16,4,128]{3,2,1,0:T(4,128)S(1)}, f32[2,16,4,128]{3,2,1,0:T(4,128)S(1)}, u32[]{:S(2)}, u32[]{:S(2)}) collective-permute-start(f32[2,16,4,128]{3,2,1,0:T(4,128)S(1)} %pad_maximum_fusion.c0), channel_id=1, source_target_pairs={{0,192},{32,224},{64,0},{96,32},{128,64},{160,96},{192,128},{224,1... | collective-permute-start | bytes 196616 | tf_op jit(solution)/shard_map/ppermute | solution.py:352
  19.9 4.3 %collective-permute-start.4 = (f32[2,16,4,128]{3,2,1,0:T(4,128)S(1)}, f32[2,16,4,128]{3,2,1,0:T(4,128)S(1)}, u32[]{:S(2)}, u32[]{:S(2)}) collective-permute-start(f32[2,16,4,128]{3,2,1,0:T(4,128)S(1)} %pad_maximum_fusion.c0), channel_id=1, source_target_pairs={{0,64},{32,96},{64,128},{96,160},{128,192},{160,224},{192,0},{224,... | collective-permute-start | bytes 196616 | tf_op jit(solution)/shard_map/ppermute | solution.py:352
  24.2 0.7 %copy-start.3 = (s32[1,1,48]{2,1,0:T(1,128)S(1)}, s32[1,1,48]{2,1,0:T(1,128)}, u32[]{:S(2)}) copy-start(s32[1,1,48]{2,1,0:T(1,128)} %param.10) | copy-start | bytes 580
  36.9 10.7 %collective-permute-start.7 = (f32[3,48,128]{2,1,0:T(8,128)S(1)}, f32[3,48,128]{2,1,0:T(8,128)S(1)}, u32[]{:S(2)}, u32[]{:S(2)}) collective-permute-start(f32[3,48,128]{2,1,0:T(8,128)S(1)} %get-tuple-element.25), channel_id=1, source_target_pairs={{0,24},{1,25},{2,26},{3,27},{4,28},{5,29},{6,30},{7,31},{8,0},{9,1... | collective-permute-start | bytes 221192 | tf_op jit(solution)/shard_map/ppermute | solution.py:394
  38.3 9.3 %collective-permute-start.8 = (f32[3,48,128]{2,1,0:T(8,128)S(1)}, f32[3,48,128]{2,1,0:T(8,128)S(1)}, u32[]{:S(2)}, u32[]{:S(2)}) collective-permute-start(f32[3,48,128]{2,1,0:T(8,128)S(1)} %get-tuple-element.26), channel_id=1, source_target_pairs={{0,8},{1,9},{2,10},{3,11},{4,12},{5,13},{6,14},{7,15},{8,16},{9,17... | collective-permute-start | bytes 221192 | tf_op jit(solution)/shard_map/ppermute | solution.py:394
  39.0 8.6 %collective-permute-start.9 = (f32[3,48,128]{2,1,0:T(8,128)S(1)}, f32[3,48,128]{2,1,0:T(8,128)S(1)}, u32[]{:S(2)}, u32[]{:S(2)}) collective-permute-start(f32[3,48,128]{2,1,0:T(8,128)S(1)} %get-tuple-element.27), channel_id=1, source_target_pairs={{0,16},{1,17},{2,18},{3,19},{4,20},{5,21},{6,22},{7,23},{8,24},{9,... | collective-permute-start | bytes 221192 | tf_op jit(solution)/shard_map/ppermute | solution.py:394

commit v9 on v8

--- a/solution.py
+++ b/solution.py
@@ -15,8 +15,8 @@
 NZ = 8
 NX = 4
 SOFT = 0.01
-UNROLL = (14, 12)
-UNROLL_OWN = (14, 4)
+UNROLL = (18, 16)
+UNROLL_OWN = (18, 6)
 MIB = 1 << 20
 TILES = 36
 F32 = jnp.float32
@@ -331,7 +331,7 @@
         [pl.BlockSpec(memory_space=pltpu.HBM)] * 7,
         [vspec()] * 3,
         "pack",
-        60,
+        8,
         [
             pltpu.VMEM((3, NB, PL), F32),
             pltpu.VMEM((NB, PL), F32),
@@ -344,7 +344,12 @@
             pltpu.VMEM((NB, 8, PL), F32),
             pltpu.SemaphoreType.DMA((8,)),
         ],
-    )(pos, masses[0], cnt, dest_ids, near_list[0].T, cell_centers, cell_mass[None])
+    )(
+        *[
+            pltpu.with_memory_space_constraint(v, pltpu.HBM)
+            for v in (pos, masses[0], cnt, dest_ids, near_list[0].T, cell_centers, cell_mass[None])
+        ]
+    )
     z_rows = [[NZ * y + z for z in range(NZ)] for y in range(NY)]
     window = lax.all_to_all(src, "space", 0, 0, axis_index_groups=z_rows, tiled=True)
     tgts = [tgt] + [lax.ppermute(tgt, "space", along_y(k)) for k in (1, -1, 2)]

time: 48.8 us -> 48.9 us (level)
  the two profiles are of different devices: /device:TPU:4 before, /device:TPU:8 now
where the time goes in v9:
time: 48.9 us; the launch traced here: 48.4 us
  starting transfers between devices  23.5 us (48%)
  Pallas kernels  16.7 us (34%)
  waiting for transfers between devices  7.29 us (15%)
  local copies, waits for them, and re-layouts  0.66 us (1%)
    pallas_call x2, Pallas kernels, near(): call(functools.partial(near_kernel, first), (((3, NB, PL), F32),) * count...  12.1 us
    all_to_all x1, starting transfers between devices, per_device(): lax.all_to_all(src, 'space', 0, 0, axis_index_groups=z_rows, tiled=True)  8.48 us
    ppermute x3, starting transfers between devices, per_device(): lax.ppermute(v, 'space', along_y(-k))  5.6 us
    ppermute x3, starting transfers between devices, per_device(): lax.ppermute(pair, 'slab', along_x(k))  5.14 us
    ppermute x3, waiting for transfers between devices, per_device(): lax.ppermute(pair, 'slab', along_x(k))  4.59 us
    ppermute x3, starting transfers between devices, per_device(): tgts = [tgt] + [lax.ppermute(tgt, 'space', along_y(k)) for k in (1, -1, 2)]  4.32 us
    pallas_call x1, Pallas kernels, per_device(): call(pack_kernel, (((NZ, TILES + 1, 4, PL), F32), ((NB + 1, 4, PL), F32),...  2.12 us
    all_to_all x1, waiting for transfers between devices, per_device(): lax.all_to_all(src, 'space', 0, 0, axis_index_groups=z_rows, tiled=True)  1.48 us
  transfers between devices with their start and end apart: 11, of which 4 were waited for; matrix products, arithmetic and copies ran while one was open for 0% of the time, Pallas kernels for 12%

profile of v9, /device:TPU:8, one launch (start us, length us, event | category | flops | bytes accessed | tf_op | source)
XLA Modules:
  0.0 48.4 jit_solution(4278067820023721920)
XLA Ops:
  0.0 2.1 %pack.1 = (f32[8,37,4,128]{3,2,1,0:T(4,128)}, f32[49,4,128]{2,1,0:T(4,128)S(1)}, f32[16,4,128]{2,1,0:T(4,128)S(1)}) custom-call(f32[3,48,128]{2,1,0:T(8,128)} %bitcast.22, f32[48,128]{1,0:T(8,128)} %bitcast.30, s32[1,48]{1,0:T(1,128)} %bitcast.26, s32[1,48]{1,0:T(1,128)} %refs_3_.1, s32[4,48]{1,0:T(4,128)} %bitcast.32, f32[3,2048]{1,0:T(4,128)} %refs_5_.1, ...), custom_call_target="tpu_custom_call" | custom-call | tf_op jit(solution)/shard_map/pack/pallas_call | solution.py:328
  2.1 8.5 %all-to-all-start = ((f32[8,37,4,128]{3,2,1,0:T(4,128)}), f32[8,37,4,128]{3,2,1,0:T(4,128)S(1)}, u32[]{:S(2)}, u32[]{:S(2)}) async-start(f32[8,37,4,128]{3,2,1,0:T(4,128)} %get-tuple-element.24), calls=%async_computation | async-start | bytes 1212416 | tf_op jit(solution)/shard_map/all_to_all | solution.py:354
  10.6 0.0 collective-permute-start.3
  10.6 1.2 %collective-permute-done.3 = f32[16,4,128]{2,1,0:T(4,128)S(1)} collective-permute-done((f32[16,4,128]{2,1,0:T(4,128)S(1)}, f32[16,4,128]{2,1,0:T(4,128)S(1)}, u32[]{:S(2)}, u32[]{:S(2)}) %collective-permute-start.3) | collective-permute-done | bytes 32800 | tf_op jit(solution)/shard_map/ppermute | solution.py:356
  11.8 3.1 %collective-permute-start.6 = (f32[2,16,4,128]{3,2,1,0:T(4,128)S(1)}, f32[2,16,4,128]{3,2,1,0:T(4,128)S(1)}, u32[]{:S(2)}, u32[]{:S(2)}) collective-permute-start(f32[2,16,4,128]{3,2,1,0:T(4,128)S(1)} %pad_maximum_fusion.c0), channel_id=1, source_target_pairs={{0,128},{32,160},{64,192},{96,224},{128,0},{160,32},{192,64},{224,... | collective-permute-start | bytes 196616 | tf_op jit(solution)/shard_map/ppermute | solution.py:357
  14.9 2.3 %collective-permute-start.2 = (f32[49,4,128]{2,1,0:T(4,128)S(1)}, f32[49,4,128]{2,1,0:T(4,128)S(1)}, u32[]{:S(2)}, u32[]{:S(2)}) collective-permute-start(f32[49,4,128]{2,1,0:T(4,128)S(1)} %get-tuple-element.17.t0), channel_id=1, source_target_pairs={{0,16},{1,17},{2,18},{3,19},{4,20},{5,21},{6,22},{7,23},{8,24},{9,... | collective-permute-start | bytes 301064 | tf_op jit(solution)/shard_map/ppermute | solution.py:355
  17.2 1.3 %collective-permute-start.1 = (f32[49,4,128]{2,1,0:T(4,128)S(1)}, f32[49,4,128]{2,1,0:T(4,128)S(1)}, u32[]{:S(2)}, u32[]{:S(2)}) collective-permute-start(f32[49,4,128]{2,1,0:T(4,128)S(1)} %get-tuple-element.17.t0), channel_id=1, source_target_pairs={{0,24},{1,25},{2,26},{3,27},{4,28},{5,29},{6,30},{7,31},{8,0},{9,1... | collective-permute-start | bytes 301064 | tf_op jit(solution)/shard_map/ppermute | solution.py:355
  18.6 0.7 %collective-permute-start = (f32[49,4,128]{2,1,0:T(4,128)S(1)}, f32[49,4,128]{2,1,0:T(4,128)S(1)}, u32[]{:S(2)}, u32[]{:S(2)}) collective-permute-start(f32[49,4,128]{2,1,0:T(4,128)S(1)} %get-tuple-element.17.t0), channel_id=1, source_target_pairs={{0,8},{1,9},{2,10},{3,11},{4,12},{5,13},{6,14},{7,15},{8,16},{9,17... | collective-permute-start | bytes 301064 | tf_op jit(solution)/shard_map/ppermute | solution.py:355
  19.3 1.1 %collective-permute-start.5 = (f32[2,16,4,128]{3,2,1,0:T(4,128)S(1)}, f32[2,16,4,128]{3,2,1,0:T(4,128)S(1)}, u32[]{:S(2)}, u32[]{:S(2)}) collective-permute-start(f32[2,16,4,128]{3,2,1,0:T(4,128)S(1)} %pad_maximum_fusion.c0), channel_id=1, source_target_pairs={{0,192},{32,224},{64,0},{96,32},{128,64},{160,96},{192,128},{224,1... | collective-permute-start | bytes 196616 | tf_op jit(solution)/shard_map/ppermute | solution.py:357
  20.4 0.0 collective-permute-done.6.c3
  20.4 0.9 %collective-permute-start.4 = (f32[2,16,4,128]{3,2,1,0:T(4,128)S(1)}, f32[2,16,4,128]{3,2,1,0:T(4,128)S(1)}, u32[]{:S(2)}, u32[]{:S(2)}) collective-permute-start(f32[2,16,4,128]{3,2,1,0:T(4,128)S(1)} %pad_maximum_fusion.c0), channel_id=1, source_target_pairs={{0,64},{32,96},{64,128},{96,160},{128,192},{160,224},{192,0},{224,... | collective-permute-start | bytes 196616 | tf_op jit(solution)/shard_map/ppermute | solution.py:357
  21.3 2.2 %collective-permute-done.5.c2 = f32[2,16,4,128]{3,2,1,0:T(4,128)S(1)} collective-permute-done((f32[2,16,4,128]{3,2,1,0:T(4,128)S(1)}, f32[2,16,4,128]{3,2,1,0:T(4,128)S(1)}, u32[]{:S(2)}, u32[]{:S(2)}) %collective-permute-start.5) | collective-permute-done | bytes 65568 | tf_op jit(solution)/shard_map/ppermute | solution.py:357
  23.5 2.4 %collective-permute-done.4.c1 = f32[2,16,4,128]{3,2,1,0:T(4,128)S(1)} collective-permute-done((f32[2,16,4,128]{3,2,1,0:T(4,128)S(1)}, f32[2,16,4,128]{3,2,1,0:T(4,128)S(1)}, u32[]{:S(2)}, u32[]{:S(2)}) %collective-permute-start.4) | collective-permute-done | bytes 65568 | tf_op jit(solution)/shard_map/ppermute | solution.py:357
  25.9 0.6 %copy-done.2 = s32[1,1,48]{2,1,0:T(1,128)S(1)} copy-done((s32[1,1,48]{2,1,0:T(1,128)S(1)}, s32[1,1,48]{2,1,0:T(1,128)}, u32[]{:S(2)}) %copy-start.2) | copy-done | bytes 216
  26.6 1.4 %far.1.far_ref = f32[3,48,128]{2,1,0:T(8,128)S(1)} custom-call(s32[1]{0:T(128)} %bitcast.8.place_ref, f32[3,48,128]{2,1,0:T(8,128)S(1)} %bitcast.23, s32[1,48]{1,0:T(1,128)S(1)} %bitcast.27, s32[32,48]{1,0:T(8,128)S(1)} %bitcast.25, f32[2,16,4,128]{3,2,1,0:T(4,128)S(1)} %pad_maximum_fusion.c0, f32[2,16,4,128]{3,2,1,0:T(4,128)S(1)} %collective-permute-done.4.c1, ...), custom_call_target="tpu_custom_call" | custom-call | tf_op jit(solution)/shard_map/far/pallas_call | solution.py:368
  28.0 0.0 collective-permute-done.2.t3
  28.0 0.4 prep.1
  28.4 1.5 %all-to-all-done = f32[8,37,4,128]{3,2,1,0:T(4,128)S(1)} async-done(((f32[8,37,4,128]{3,2,1,0:T(4,128)}), f32[8,37,4,128]{3,2,1,0:T(4,128)S(1)}, u32[]{:S(2)}, u32[]{:S(2)}) %all-to-all-start) | async-done | bytes 606240 | tf_op jit(solution)/shard_map/all_to_all | solution.py:354
  29.9 8.3 %near.2 = (f32[3,48,128]{2,1,0:T(8,128)S(1)}, f32[3,48,128]{2,1,0:T(8,128)S(1)}, f32[3,48,128]{2,1,0:T(8,128)S(1)}) custom-call(s32[16,256]{1,0:T(8,128)S(1)} %get-tuple-element.28.table, f32[192,4,128]{2,1,0:T(4,128)S(1)} %get-tuple-element.23.tall, f32[296,4,128]{2,1,0:T(4,128)S(1)} %bitcast.20), custom_call_target="tpu_custom_call" | custom-call | tf_op jit(solution)/shard_map/near/pallas_call | solution.py:382
  38.1 0.1 collective-permute-start.7
  38.2 2.0 %collective-permute-start.8 = (f32[3,48,128]{2,1,0:T(8,128)S(1)}, f32[3,48,128]{2,1,0:T(8,128)S(1)}, u32[]{:S(2)}, u32[]{:S(2)}) collective-permute-start(f32[3,48,128]{2,1,0:T(8,128)S(1)} %get-tuple-element.26), channel_id=1, source_target_pairs={{0,8},{1,9},{2,10},{3,11},{4,12},{5,13},{6,14},{7,15},{8,16},{9,17... | collective-permute-start | bytes 221192 | tf_op jit(solution)/shard_map/ppermute | solution.py:399
  40.2 3.5 %collective-permute-start.9 = (f32[3,48,128]{2,1,0:T(8,128)S(1)}, f32[3,48,128]{2,1,0:T(8,128)S(1)}, u32[]{:S(2)}, u32[]{:S(2)}) collective-permute-start(f32[3,48,128]{2,1,0:T(8,128)S(1)} %get-tuple-element.27), channel_id=1, source_target_pairs={{0,16},{1,17},{2,18},{3,19},{4,20},{5,21},{6,22},{7,23},{8,24},{9,... | collective-permute-start | bytes 221192 | tf_op jit(solution)/shard_map/ppermute | solution.py:399
  43.7 3.8 %near.3.p0 = f32[3,48,128]{2,1,0:T(8,128)S(1)} custom-call(s32[16,256]{1,0:T(8,128)S(1)} %get-tuple-element.28.table, f32[192,4,128]{2,1,0:T(4,128)S(1)} %get-tuple-element.23.tall, f32[296,4,128]{2,1,0:T(4,128)S(1)} %bitcast.21), custom_call_target="tpu_custom_call" | custom-call | tf_op jit(solution)/shard_map/near/pallas_call | solution.py:382
  47.6 0.7 %final.1 = f32[3,48,128]{2,1,0:T(8,128)} custom-call(s32[1,48]{1,0:T(1,128)S(1)} %bitcast.28, f32[3,48,128]{2,1,0:T(8,128)S(1)} %far.1.far_ref, f32[3,48,128]{2,1,0:T(8,128)S(1)} %near.3.p0, f32[3,48,128]{2,1,0:T(8,128)S(1)} %collective-permute-done.7.p1, f32[3,48,128]{2,1,0:T(8,128)S(1)} %collective-permute-done.8.p2, ...), custom_call_target="tpu_custom_call" | custom-call | tf_op jit(solution)/shard_map/final/pallas_call | solution.py:402
  (11 shorter events, 0.0 us)
Async XLA Ops:
  2.1 27.7 %all-to-all-start = ((f32[8,37,4,128]{3,2,1,0:T(4,128)}), f32[8,37,4,128]{3,2,1,0:T(4,128)S(1)}, u32[]{:S(2)}, u32[]{:S(2)}) async-start(f32[8,37,4,128]{3,2,1,0:T(4,128)} %get-tuple-element.24), calls=%async_computation | async-start | bytes 1212416 | tf_op jit(solution)/shard_map/all_to_all | solution.py:354
  10.6 1.2 %collective-permute-start.3 = (f32[16,4,128]{2,1,0:T(4,128)S(1)}, f32[16,4,128]{2,1,0:T(4,128)S(1)}, u32[]{:S(2)}, u32[]{:S(2)}) collective-permute-start(f32[16,4,128]{2,1,0:T(4,128)S(1)} %get-tuple-element.20), channel_id=1, source_target_pairs={{0,32},{32,0},{64,96},{96,64},{128,160},{160,128},{192,224},{224,1... | collective-permute-start | bytes 98312 | tf_op jit(solution)/shard_map/ppermute | solution.py:356
  11.8 14.1 %copy-start = (f32[1,48,3,128]{3,1,2,0:T(8,128)S(1)}, f32[1,48,3,128]{3,1,2,0:T(8,128)}, u32[]{:S(2)}) copy-start(f32[1,48,3,128]{3,1,2,0:T(8,128)} %param.8) | copy-start | bytes 221188
  11.8 8.6 %collective-permute-start.6 = (f32[2,16,4,128]{3,2,1,0:T(4,128)S(1)}, f32[2,16,4,128]{3,2,1,0:T(4,128)S(1)}, u32[]{:S(2)}, u32[]{:S(2)}) collective-permute-start(f32[2,16,4,128]{3,2,1,0:T(4,128)S(1)} %pad_maximum_fusion.c0), channel_id=1, source_target_pairs={{0,128},{32,160},{64,192},{96,224},{128,0},{160,32},{192,64},{224,... | collective-permute-start | bytes 196616 | tf_op jit(solution)/shard_map/ppermute | solution.py:357
  14.9 13.0 %collective-permute-start.2 = (f32[49,4,128]{2,1,0:T(4,128)S(1)}, f32[49,4,128]{2,1,0:T(4,128)S(1)}, u32[]{:S(2)}, u32[]{:S(2)}) collective-permute-start(f32[49,4,128]{2,1,0:T(4,128)S(1)} %get-tuple-element.17.t0), channel_id=1, source_target_pairs={{0,16},{1,17},{2,18},{3,19},{4,20},{5,21},{6,22},{7,23},{8,24},{9,... | collective-permute-start | bytes 301064 | tf_op jit(solution)/shard_map/ppermute | solution.py:355
  17.2 10.7 %collective-permute-start.1 = (f32[49,4,128]{2,1,0:T(4,128)S(1)}, f32[49,4,128]{2,1,0:T(4,128)S(1)}, u32[]{:S(2)}, u32[]{:S(2)}) collective-permute-start(f32[49,4,128]{2,1,0:T(4,128)S(1)} %get-tuple-element.17.t0), channel_id=1, source_target_pairs={{0,24},{1,25},{2,26},{3,27},{4,28},{5,29},{6,30},{7,31},{8,0},{9,1... | collective-permute-start | bytes 301064 | tf_op jit(solution)/shard_map/ppermute | solution.py:355
  18.6 9.4 %collective-permute-start = (f32[49,4,128]{2,1,0:T(4,128)S(1)}, f32[49,4,128]{2,1,0:T(4,128)S(1)}, u32[]{:S(2)}, u32[]{:S(2)}) collective-permute-start(f32[49,4,128]{2,1,0:T(4,128)S(1)} %get-tuple-element.17.t0), channel_id=1, source_target_pairs={{0,8},{1,9},{2,10},{3,11},{4,12},{5,13},{6,14},{7,15},{8,16},{9,17... | collective-permute-start | bytes 301064 | tf_op jit(solution)/shard_map/ppermute | solution.py:355
  19.3 4.3 %collective-permute-start.5 = (f32[2,16,4,128]{3,2,1,0:T(4,128)S(1)}, f32[2,16,4,128]{3,2,1,0:T(4,128)S(1)}, u32[]{:S(2)}, u32[]{:S(2)}) collective-permute-start(f32[2,16,4,128]{3,2,1,0:T(4,128)S(1)} %pad_maximum_fusion.c0), channel_id=1, source_target_pairs={{0,192},{32,224},{64,0},{96,32},{128,64},{160,96},{192,128},{224,1... | collective-permute-start | bytes 196616 | tf_op jit(solution)/shard_map/ppermute | solution.py:357
  20.4 5.5 %collective-permute-start.4 = (f32[2,16,4,128]{3,2,1,0:T(4,128)S(1)}, f32[2,16,4,128]{3,2,1,0:T(4,128)S(1)}, u32[]{:S(2)}, u32[]{:S(2)}) collective-permute-start(f32[2,16,4,128]{3,2,1,0:T(4,128)S(1)} %pad_maximum_fusion.c0), channel_id=1, source_target_pairs={{0,64},{32,96},{64,128},{96,160},{128,192},{160,224},{192,0},{224,... | collective-permute-start | bytes 196616 | tf_op jit(solution)/shard_map/ppermute | solution.py:357
  21.3 4.6 %copy-start.1 = (s32[1,48,32]{1,2,0:T(8,128)S(1)}, s32[1,48,32]{1,2,0:T(8,128)}, u32[]{:S(2)}) copy-start(s32[1,48,32]{1,2,0:T(8,128)} %param.13) | copy-start | bytes 18436
  25.9 0.7 %copy-start.2 = (s32[1,1,48]{2,1,0:T(1,128)S(1)}, s32[1,1,48]{2,1,0:T(1,128)}, u32[]{:S(2)}) copy-start(s32[1,1,48]{2,1,0:T(1,128)} %param.10) | copy-start | bytes 580
  38.1 9.4 %collective-permute-start.7 = (f32[3,48,128]{2,1,0:T(8,128)S(1)}, f32[3,48,128]{2,1,0:T(8,128)S(1)}, u32[]{:S(2)}, u32[]{:S(2)}) collective-permute-start(f32[3,48,128]{2,1,0:T(8,128)S(1)} %get-tuple-element.25), channel_id=1, source_target_pairs={{0,24},{1,25},{2,26},{3,27},{4,28},{5,29},{6,30},{7,31},{8,0},{9,1... | collective-permute-start | bytes 221192 | tf_op jit(solution)/shard_map/ppermute | solution.py:399
  38.2 9.4 %collective-permute-start.8 = (f32[3,48,128]{2,1,0:T(8,128)S(1)}, f32[3,48,128]{2,1,0:T(8,128)S(1)}, u32[]{:S(2)}, u32[]{:S(2)}) collective-permute-start(f32[3,48,128]{2,1,0:T(8,128)S(1)} %get-tuple-element.26), channel_id=1, source_target_pairs={{0,8},{1,9},{2,10},{3,11},{4,12},{5,13},{6,14},{7,15},{8,16},{9,17... | collective-permute-start | bytes 221192 | tf_op jit(solution)/shard_map/ppermute | solution.py:399
  40.2 7.4 %collective-permute-start.9 = (f32[3,48,128]{2,1,0:T(8,128)S(1)}, f32[3,48,128]{2,1,0:T(8,128)S(1)}, u32[]{:S(2)}, u32[]{:S(2)}) collective-permute-start(f32[3,48,128]{2,1,0:T(8,128)S(1)} %get-tuple-element.27), channel_id=1, source_target_pairs={{0,16},{1,17},{2,18},{3,19},{4,20},{5,21},{6,22},{7,23},{8,24},{9,... | collective-permute-start | bytes 221192 | tf_op jit(solution)/shard_map/ppermute | solution.py:399

commit v10 on v9

--- a/solution.py
+++ b/solution.py
@@ -16,7 +16,8 @@
 NX = 4
 SOFT = 0.01
 UNROLL = (18, 16)
-UNROLL_OWN = (18, 6)
+UNROLL_OWN = (12, 8)
+FULL_SLOTS = 54
 MIB = 1 << 20
 TILES = 36
 F32 = jnp.float32
@@ -183,7 +184,7 @@
     half = jnp.where((count > 0.5) & (count < 2.5), 1.0, 0.0)
     group = lane >> 6
     mine = group == 0
-    lists = [jnp.where(mine, 0.0, v) for v in (full, half)] + [jnp.where(mine, v, 0.0) for v in (full, half)]
+    lists = [jnp.where(m, v, 0.0) for v in (full, half) for m in (~mine, mine)]
     marks = jnp.concatenate(lists + [jnp.zeros((12, wide), F32)], axis=0).astype(BF16)
     a = lax.broadcasted_iota(I32, (wide, wide), 0)
     b = lax.broadcasted_iota(I32, (wide, wide), 1)
@@ -195,7 +196,7 @@
         begin = begin + sizes[i]
     moved = jnp.where(a == place.astype(I32), 1.0, 0.0).astype(BF16)
     bucket = lane & 63
-    home = jnp.where(mine, bucket, (group - 1) * NB + bucket)
+    home = ((group - 1) & (NY - 1)) * NB + bucket
     slot, ins, outs = [], jnp.zeros((1, wide), F32), jnp.zeros((1, wide), F32)
     for k in range(K):
         slot.append(jnp.where(flag[k] > 0.5, ins, count + outs))
@@ -216,14 +217,17 @@
     tab[...] = jnp.concatenate([out, sizes], axis=0).astype(I32)
 
 
-def near_kernel(first, table, tall, src_ref, *refs):
+def near_kernel(first, *refs):
+    (table, tall, src_ref), refs = refs[:3], refs[3:]
     outs, (out_ref, hold, spots, tab, sem) = refs[:-5], refs[-5:]
+    if not first:
+        kept, outs = outs[0], outs[1:]
     copies = [pltpu.make_async_copy(table, tab, sem.at[0]), pltpu.make_async_copy(hold, spots, sem.at[1])]
     copies[0].start()
     for z in range(NZ):
         hold[z : z + 1, :] = src_ref[z * (TILES + 1) + TILES][0:1].astype(I32)
     copies[1].start()
-    out_ref[...] = jnp.zeros(out_ref.shape, F32)
+    out_ref[...] = jnp.zeros(out_ref.shape, F32) if first else kept[...]
     for copy in copies:
         copy.wait()
     lane1 = lax.broadcasted_iota(I32, (1, PL), 1)
@@ -242,6 +246,8 @@
 
     def stack(*v):
         return jnp.concatenate(v, axis=0).astype(BF16)
+
+    row_base = 0 if first else (NY - 1) * NB
 
     def job(e, width):
         n = tab[6, e]
@@ -274,7 +280,7 @@
         o = jnp.dot(g, jnp.concatenate([high, low], axis=1), preferred_element_type=F32)
         o = o[:, :PL] + o[:, PL:]
         a = o[0:4] + o[4:8] + o[8:12]
-        out_ref[tab[5, e]] = jnp.where(lane4 < tab[4, e], a - t * a[3:4], 0.0)
+        out_ref[tab[5, e] - row_base] = jnp.where(lane4 < tab[4, e], a - t * a[3:4], 0.0)
 
     sizes = [tab[8 + i, 0] for i in range(4)]
 
@@ -285,11 +291,21 @@
 
         lax.fori_loop(0, (size + step - 1) // step, body, None)
 
-    begin = jnp.int32(0) if first else sizes[0] + sizes[1]
-    n_full, n_half = (sizes[0], sizes[1]) if first else (sizes[2], sizes[3])
-    steps = UNROLL if first else UNROLL_OWN
-    run(begin, n_full, 4, steps[0])
-    run(begin + n_full, n_half, 2, steps[1])
+    def whole_steps(size, step):
+        return (size + step - 1) // step * step
+
+    n_full, n_half = sizes[0] + sizes[1], sizes[2] + sizes[3]
+    early_full = jnp.minimum(n_full, jnp.maximum(whole_steps(sizes[0], UNROLL[0]), FULL_SLOTS))
+    early_half = jnp.minimum(n_half, whole_steps(sizes[2], UNROLL[1]))
+    if first:
+        run(jnp.int32(0), early_full, 4, UNROLL[0])
+        run(n_full, early_half, 2, UNROLL[1])
+    else:
+        run(early_full, n_full - early_full, 4, UNROLL_OWN[0])
+        run(n_full + early_half, n_half - early_half, 2, UNROLL_OWN[1])
+    if first:
+        outs[-1][...] = out_ref[(NY - 1) * NB : NY * NB]
+        outs = outs[:-1]
     for i, o in enumerate(outs):
         for c in range(3):
             o[c] = out_ref[i * NB : (i + 1) * NB, c, :]
@@ -377,28 +393,29 @@
     tall, tab, far = lax.optimization_barrier((tall, tab, far))
     window = window.reshape(NZ * (TILES + 1), 4, PL)
 
-    def near(first, tab):
-        count = NY - 1 if first else 1
+    def near(first, *arrays):
+        partial = ((3, NB, PL), F32)
+        kept = ((NB, 4, PL), F32)
+        outs = (partial,) * (NY - 1) + (kept,) if first else (partial,)
         return call(
             functools.partial(near_kernel, first),
-            (((3, NB, PL), F32),) * count,
-            [vspec()] * 3,
-            [vspec()] * count,
+            outs,
+            [vspec()] * len(arrays),
+            [vspec()] * len(outs),
             "near",
-            24,
+            32,
             [
-                pltpu.VMEM((count * NB, 4, PL), F32),
+                pltpu.VMEM(((NY if first else 1) * NB, 4, PL), F32),
                 pltpu.VMEM((NZ, PL), I32),
                 pltpu.SMEM((NZ, PL), I32),
                 pltpu.SMEM((16, 2 * PL), I32),
                 pltpu.SemaphoreType.DMA((2,)),
             ],
-        )(tab, tall, window)
-
-    sent = near(True, tab)
+        )(*arrays)
+
+    *sent, kept = near(True, tab, tall, window)
     back = [lax.ppermute(v, "space", along_y(-k)) for v, k in zip(sent, (1, -1, 2))]
-    tab, sent = lax.optimization_barrier((tab, sent))
-    (own,) = near(False, tab)
+    (own,) = near(False, tab, tall, window, kept)
     (out,) = call(
         final_kernel,
         (((3, NB, PL), F32),),

time: 48.9 us -> 49.6 us (1.014)
  the two profiles are of different devices: /device:TPU:8 before, /device:TPU:6 now
where the time goes in v10:
time: 49.6 us; the launch traced here: 48.7 us
  starting transfers between devices  25.7 us (52%)
  Pallas kernels  11.9 us (24%)
  waiting for transfers between devices  10.3 us (21%)
  local copies, waits for them, and re-layouts  0.65 us (1%)
    all_to_all x1, starting transfers between devices, per_device(): lax.all_to_all(src, 'space', 0, 0, axis_index_groups=z_rows, tiled=True)  8.48 us
    ppermute x3, starting transfers between devices, per_device(): lax.ppermute(v, 'space', along_y(-k))  7.32 us
    pallas_call x2, Pallas kernels, near(): call(functools.partial(near_kernel, first), outs, [vspec()] * len(arrays)...  7.24 us
    ppermute x3, starting transfers between devices, per_device(): tgts = [tgt] + [lax.ppermute(tgt, 'space', along_y(k)) for k in (1, -1, 2)]  5.22 us
    ppermute x3, starting transfers between devices, per_device(): lax.ppermute(pair, 'slab', along_x(k))  4.73 us
    ppermute x3, waiting for transfers between devices, per_device(): lax.ppermute(v, 'space', along_y(-k))  3.51 us
    all_to_all x1, waiting for transfers between devices, per_device(): lax.all_to_all(src, 'space', 0, 0, axis_index_groups=z_rows, tiled=True)  3.34 us
    ppermute x3, waiting for transfers between devices, per_device(): lax.ppermute(pair, 'slab', along_x(k))  2.24 us
  transfers between devices with their start and end apart: 11, of which 4 were waited for; matrix products, arithmetic and copies ran while one was open for 0% of the time, Pallas kernels for 6%

profile of v10, /device:TPU:6, one launch (start us, length us, event | category | flops | bytes accessed | tf_op | source)
XLA Modules:
  0.0 48.7 jit_solution(3718229365575463714)
XLA Ops:
  0.0 2.1 %pack.1 = (f32[8,37,4,128]{3,2,1,0:T(4,128)}, f32[49,4,128]{2,1,0:T(4,128)S(1)}, f32[16,4,128]{2,1,0:T(4,128)S(1)}) custom-call(f32[3,48,128]{2,1,0:T(8,128)} %bitcast.22, f32[48,128]{1,0:T(8,128)} %bitcast.30, s32[1,48]{1,0:T(1,128)} %bitcast.26, s32[1,48]{1,0:T(1,128)} %refs_3_.1, s32[4,48]{1,0:T(4,128)} %bitcast.32, f32[3,2048]{1,0:T(4,128)} %refs_5_.1, ...), custom_call_target="tpu_custom_call" | custom-call | tf_op jit(solution)/shard_map/pack/pallas_call | solution.py:344
  2.1 8.5 %all-to-all-start = ((f32[8,37,4,128]{3,2,1,0:T(4,128)}), f32[8,37,4,128]{3,2,1,0:T(4,128)S(1)}, u32[]{:S(2)}, u32[]{:S(2)}) async-start(f32[8,37,4,128]{3,2,1,0:T(4,128)} %get-tuple-element.24), calls=%async_computation | async-start | bytes 1212416 | tf_op jit(solution)/shard_map/all_to_all | solution.py:370
  10.6 0.0 collective-permute-start.3
  10.6 1.2 %collective-permute-done.3 = f32[16,4,128]{2,1,0:T(4,128)S(1)} collective-permute-done((f32[16,4,128]{2,1,0:T(4,128)S(1)}, f32[16,4,128]{2,1,0:T(4,128)S(1)}, u32[]{:S(2)}, u32[]{:S(2)}) %collective-permute-start.3) | collective-permute-done | bytes 32800 | tf_op jit(solution)/shard_map/ppermute | solution.py:372
  11.8 1.5 %collective-permute-start.6 = (f32[2,16,4,128]{3,2,1,0:T(4,128)S(1)}, f32[2,16,4,128]{3,2,1,0:T(4,128)S(1)}, u32[]{:S(2)}, u32[]{:S(2)}) collective-permute-start(f32[2,16,4,128]{3,2,1,0:T(4,128)S(1)} %pad_maximum_fusion.c0), channel_id=1, source_target_pairs={{0,128},{32,160},{64,192},{96,224},{128,0},{160,32},{192,64},{224,... | collective-permute-start | bytes 196616 | tf_op jit(solution)/shard_map/ppermute | solution.py:373
  13.3 3.2 %collective-permute-start.2 = (f32[49,4,128]{2,1,0:T(4,128)S(1)}, f32[49,4,128]{2,1,0:T(4,128)S(1)}, u32[]{:S(2)}, u32[]{:S(2)}) collective-permute-start(f32[49,4,128]{2,1,0:T(4,128)S(1)} %get-tuple-element.17.t0), channel_id=1, source_target_pairs={{0,16},{1,17},{2,18},{3,19},{4,20},{5,21},{6,22},{7,23},{8,24},{9,... | collective-permute-start | bytes 301064 | tf_op jit(solution)/shard_map/ppermute | solution.py:371
  16.5 1.1 %collective-permute-start.1 = (f32[49,4,128]{2,1,0:T(4,128)S(1)}, f32[49,4,128]{2,1,0:T(4,128)S(1)}, u32[]{:S(2)}, u32[]{:S(2)}) collective-permute-start(f32[49,4,128]{2,1,0:T(4,128)S(1)} %get-tuple-element.17.t0), channel_id=1, source_target_pairs={{0,24},{1,25},{2,26},{3,27},{4,28},{5,29},{6,30},{7,31},{8,0},{9,1... | collective-permute-start | bytes 301064 | tf_op jit(solution)/shard_map/ppermute | solution.py:371
  17.6 1.0 %collective-permute-start = (f32[49,4,128]{2,1,0:T(4,128)S(1)}, f32[49,4,128]{2,1,0:T(4,128)S(1)}, u32[]{:S(2)}, u32[]{:S(2)}) collective-permute-start(f32[49,4,128]{2,1,0:T(4,128)S(1)} %get-tuple-element.17.t0), channel_id=1, source_target_pairs={{0,8},{1,9},{2,10},{3,11},{4,12},{5,13},{6,14},{7,15},{8,16},{9,17... | collective-permute-start | bytes 301064 | tf_op jit(solution)/shard_map/ppermute | solution.py:371
  18.6 0.0 collective-permute-start.5
  18.6 0.0 collective-permute-done.6.c3
  18.6 3.2 %collective-permute-start.4 = (f32[2,16,4,128]{3,2,1,0:T(4,128)S(1)}, f32[2,16,4,128]{3,2,1,0:T(4,128)S(1)}, u32[]{:S(2)}, u32[]{:S(2)}) collective-permute-start(f32[2,16,4,128]{3,2,1,0:T(4,128)S(1)} %pad_maximum_fusion.c0), channel_id=1, source_target_pairs={{0,64},{32,96},{64,128},{96,160},{128,192},{160,224},{192,0},{224,... | collective-permute-start | bytes 196616 | tf_op jit(solution)/shard_map/ppermute | solution.py:373
  21.8 2.2 %collective-permute-done.5.c2 = f32[2,16,4,128]{3,2,1,0:T(4,128)S(1)} collective-permute-done((f32[2,16,4,128]{3,2,1,0:T(4,128)S(1)}, f32[2,16,4,128]{3,2,1,0:T(4,128)S(1)}, u32[]{:S(2)}, u32[]{:S(2)}) %collective-permute-start.5) | collective-permute-done | bytes 65568 | tf_op jit(solution)/shard_map/ppermute | solution.py:373
  24.0 0.0 collective-permute-done.4.c1
  24.1 0.6 %copy-done.2 = s32[1,1,48]{2,1,0:T(1,128)S(1)} copy-done((s32[1,1,48]{2,1,0:T(1,128)S(1)}, s32[1,1,48]{2,1,0:T(1,128)}, u32[]{:S(2)}) %copy-start.2) | copy-done | bytes 216
  24.7 1.4 %far.1.far_ref = f32[3,48,128]{2,1,0:T(8,128)S(1)} custom-call(s32[1]{0:T(128)} %bitcast.8.place_ref, f32[3,48,128]{2,1,0:T(8,128)S(1)} %bitcast.23, s32[1,48]{1,0:T(1,128)S(1)} %bitcast.27, s32[32,48]{1,0:T(8,128)S(1)} %bitcast.25, f32[2,16,4,128]{3,2,1,0:T(4,128)S(1)} %pad_maximum_fusion.c0, f32[2,16,4,128]{3,2,1,0:T(4,128)S(1)} %collective-permute-done.4.c1, ...), custom_call_target="tpu_custom_call" | custom-call | tf_op jit(solution)/shard_map/far/pallas_call | solution.py:384
  26.1 0.0 collective-permute-done.2.t3
  26.1 0.4 prep.1
  26.5 3.3 %all-to-all-done = f32[8,37,4,128]{3,2,1,0:T(4,128)S(1)} async-done(((f32[8,37,4,128]{3,2,1,0:T(4,128)}), f32[8,37,4,128]{3,2,1,0:T(4,128)S(1)}, u32[]{:S(2)}, u32[]{:S(2)}) %all-to-all-start) | async-done | bytes 606240 | tf_op jit(solution)/shard_map/all_to_all | solution.py:370
  29.9 6.3 %near.2 = (f32[3,48,128]{2,1,0:T(8,128)S(1)}, f32[3,48,128]{2,1,0:T(8,128)S(1)}, f32[3,48,128]{2,1,0:T(8,128)S(1)}, f32[48,4,128]{2,1,0:T(4,128)S(1)}) custom-call(s32[16,256]{1,0:T(8,128)S(1)} %get-tuple-element.22.refs_0_, f32[192,4,128]{2,1,0:T(4,128)S(1)} %get-tuple-element.23.refs_1_, f32[296,4,128]{2,1,0:T(4,128)S(1)} %bitcast.20), custom_call_target="tpu_custom_call" | custom-call | tf_op jit(solution)/shard_map/near/pallas_call | solution.py:400
  36.1 5.1 %collective-permute-start.7 = (f32[3,48,128]{2,1,0:T(8,128)S(1)}, f32[3,48,128]{2,1,0:T(8,128)S(1)}, u32[]{:S(2)}, u32[]{:S(2)}) collective-permute-start(f32[3,48,128]{2,1,0:T(8,128)S(1)} %get-tuple-element.26), channel_id=1, source_target_pairs={{0,24},{1,25},{2,26},{3,27},{4,28},{5,29},{6,30},{7,31},{8,0},{9,1... | collective-permute-start | bytes 221192 | tf_op jit(solution)/shard_map/ppermute | solution.py:417
  41.3 2.2 %collective-permute-start.9 = (f32[3,48,128]{2,1,0:T(8,128)S(1)}, f32[3,48,128]{2,1,0:T(8,128)S(1)}, u32[]{:S(2)}, u32[]{:S(2)}) collective-permute-start(f32[3,48,128]{2,1,0:T(8,128)S(1)} %get-tuple-element.28), channel_id=1, source_target_pairs={{0,16},{1,17},{2,18},{3,19},{4,20},{5,21},{6,22},{7,23},{8,24},{9,... | collective-permute-start | bytes 221192 | tf_op jit(solution)/shard_map/ppermute | solution.py:417
  43.5 1.0 %near.3.p0 = f32[3,48,128]{2,1,0:T(8,128)S(1)} custom-call(s32[16,256]{1,0:T(8,128)S(1)} %get-tuple-element.22.refs_0_, f32[192,4,128]{2,1,0:T(4,128)S(1)} %get-tuple-element.23.refs_1_, f32[296,4,128]{2,1,0:T(4,128)S(1)} %bitcast.21, f32[48,4,128]{2,1,0:T(4,128)S(1)} %get-tuple-element.25.refs_3_), custom_call_target="tpu_custom_call" | custom-call | tf_op jit(solution)/shard_map/near/pallas_call | solution.py:400
  44.4 3.5 %collective-permute-done.8.p2 = f32[3,48,128]{2,1,0:T(8,128)S(1)} collective-permute-done((f32[3,48,128]{2,1,0:T(8,128)S(1)}, f32[3,48,128]{2,1,0:T(8,128)S(1)}, u32[]{:S(2)}, u32[]{:S(2)}) %collective-permute-start.8) | collective-permute-done | bytes 73760 | tf_op jit(solution)/shard_map/ppermute | solution.py:417
  48.0 0.7 %final.1 = f32[3,48,128]{2,1,0:T(8,128)} custom-call(s32[1,48]{1,0:T(1,128)S(1)} %bitcast.28, f32[3,48,128]{2,1,0:T(8,128)S(1)} %far.1.far_ref, f32[3,48,128]{2,1,0:T(8,128)S(1)} %near.3.p0, f32[3,48,128]{2,1,0:T(8,128)S(1)} %collective-permute-done.7.p1, f32[3,48,128]{2,1,0:T(8,128)S(1)} %collective-permute-done.8.p2, ...), custom_call_target="tpu_custom_call" | custom-call | tf_op jit(solution)/shard_map/final/pallas_call | solution.py:419
  (11 shorter events, 0.0 us)
Async XLA Ops:
  2.1 27.7 %all-to-all-start = ((f32[8,37,4,128]{3,2,1,0:T(4,128)}), f32[8,37,4,128]{3,2,1,0:T(4,128)S(1)}, u32[]{:S(2)}, u32[]{:S(2)}) async-start(f32[8,37,4,128]{3,2,1,0:T(4,128)} %get-tuple-element.24), calls=%async_computation | async-start | bytes 1212416 | tf_op jit(solution)/shard_map/all_to_all | solution.py:370
  10.6 1.2 %collective-permute-start.3 = (f32[16,4,128]{2,1,0:T(4,128)S(1)}, f32[16,4,128]{2,1,0:T(4,128)S(1)}, u32[]{:S(2)}, u32[]{:S(2)}) collective-permute-start(f32[16,4,128]{2,1,0:T(4,128)S(1)} %get-tuple-element.20), channel_id=1, source_target_pairs={{0,32},{32,0},{64,96},{96,64},{128,160},{160,128},{192,224},{224,1... | collective-permute-start | bytes 98312 | tf_op jit(solution)/shard_map/ppermute | solution.py:372
  11.8 12.2 %copy-start = (f32[1,48,3,128]{3,1,2,0:T(8,128)S(1)}, f32[1,48,3,128]{3,1,2,0:T(8,128)}, u32[]{:S(2)}) copy-start(f32[1,48,3,128]{3,1,2,0:T(8,128)} %param.8) | copy-start | bytes 221188
  11.8 6.7 %collective-permute-start.6 = (f32[2,16,4,128]{3,2,1,0:T(4,128)S(1)}, f32[2,16,4,128]{3,2,1,0:T(4,128)S(1)}, u32[]{:S(2)}, u32[]{:S(2)}) collective-permute-start(f32[2,16,4,128]{3,2,1,0:T(4,128)S(1)} %pad_maximum_fusion.c0), channel_id=1, source_target_pairs={{0,128},{32,160},{64,192},{96,224},{128,0},{160,32},{192,64},{224,... | collective-permute-start | bytes 196616 | tf_op jit(solution)/shard_map/ppermute | solution.py:373
  13.3 12.8 %collective-permute-start.2 = (f32[49,4,128]{2,1,0:T(4,128)S(1)}, f32[49,4,128]{2,1,0:T(4,128)S(1)}, u32[]{:S(2)}, u32[]{:S(2)}) collective-permute-start(f32[49,4,128]{2,1,0:T(4,128)S(1)} %get-tuple-element.17.t0), channel_id=1, source_target_pairs={{0,16},{1,17},{2,18},{3,19},{4,20},{5,21},{6,22},{7,23},{8,24},{9,... | collective-permute-start | bytes 301064 | tf_op jit(solution)/shard_map/ppermute | solution.py:371
  16.5 9.6 %collective-permute-start.1 = (f32[49,4,128]{2,1,0:T(4,128)S(1)}, f32[49,4,128]{2,1,0:T(4,128)S(1)}, u32[]{:S(2)}, u32[]{:S(2)}) collective-permute-start(f32[49,4,128]{2,1,0:T(4,128)S(1)} %get-tuple-element.17.t0), channel_id=1, source_target_pairs={{0,24},{1,25},{2,26},{3,27},{4,28},{5,29},{6,30},{7,31},{8,0},{9,1... | collective-permute-start | bytes 301064 | tf_op jit(solution)/shard_map/ppermute | solution.py:371
  17.6 8.6 %collective-permute-start = (f32[49,4,128]{2,1,0:T(4,128)S(1)}, f32[49,4,128]{2,1,0:T(4,128)S(1)}, u32[]{:S(2)}, u32[]{:S(2)}) collective-permute-start(f32[49,4,128]{2,1,0:T(4,128)S(1)} %get-tuple-element.17.t0), channel_id=1, source_target_pairs={{0,8},{1,9},{2,10},{3,11},{4,12},{5,13},{6,14},{7,15},{8,16},{9,17... | collective-permute-start | bytes 301064 | tf_op jit(solution)/shard_map/ppermute | solution.py:371
  18.6 5.5 %collective-permute-start.5 = (f32[2,16,4,128]{3,2,1,0:T(4,128)S(1)}, f32[2,16,4,128]{3,2,1,0:T(4,128)S(1)}, u32[]{:S(2)}, u32[]{:S(2)}) collective-permute-start(f32[2,16,4,128]{3,2,1,0:T(4,128)S(1)} %pad_maximum_fusion.c0), channel_id=1, source_target_pairs={{0,192},{32,224},{64,0},{96,32},{128,64},{160,96},{192,128},{224,1... | collective-permute-start | bytes 196616 | tf_op jit(solution)/shard_map/ppermute | solution.py:373
  18.6 5.5 %collective-permute-start.4 = (f32[2,16,4,128]{3,2,1,0:T(4,128)S(1)}, f32[2,16,4,128]{3,2,1,0:T(4,128)S(1)}, u32[]{:S(2)}, u32[]{:S(2)}) collective-permute-start(f32[2,16,4,128]{3,2,1,0:T(4,128)S(1)} %pad_maximum_fusion.c0), channel_id=1, source_target_pairs={{0,64},{32,96},{64,128},{96,160},{128,192},{160,224},{192,0},{224,... | collective-permute-start | bytes 196616 | tf_op jit(solution)/shard_map/ppermute | solution.py:373
  21.8 2.2 %copy-start.1 = (s32[1,48,32]{1,2,0:T(8,128)S(1)}, s32[1,48,32]{1,2,0:T(8,128)}, u32[]{:S(2)}) copy-start(s32[1,48,32]{1,2,0:T(8,128)} %param.13) | copy-start | bytes 18436
  24.0 0.7 %copy-start.2 = (s32[1,1,48]{2,1,0:T(1,128)S(1)}, s32[1,1,48]{2,1,0:T(1,128)}, u32[]{:S(2)}) copy-start(s32[1,1,48]{2,1,0:T(1,128)} %param.10) | copy-start | bytes 580
  36.1 8.3 %collective-permute-start.7 = (f32[3,48,128]{2,1,0:T(8,128)S(1)}, f32[3,48,128]{2,1,0:T(8,128)S(1)}, u32[]{:S(2)}, u32[]{:S(2)}) collective-permute-start(f32[3,48,128]{2,1,0:T(8,128)S(1)} %get-tuple-element.26), channel_id=1, source_target_pairs={{0,24},{1,25},{2,26},{3,27},{4,28},{5,29},{6,30},{7,31},{8,0},{9,1... | collective-permute-start | bytes 221192 | tf_op jit(solution)/shard_map/ppermute | solution.py:417
  41.3 6.7 %collective-permute-start.8 = (f32[3,48,128]{2,1,0:T(8,128)S(1)}, f32[3,48,128]{2,1,0:T(8,128)S(1)}, u32[]{:S(2)}, u32[]{:S(2)}) collective-permute-start(f32[3,48,128]{2,1,0:T(8,128)S(1)} %get-tuple-element.27), channel_id=1, source_target_pairs={{0,8},{1,9},{2,10},{3,11},{4,12},{5,13},{6,14},{7,15},{8,16},{9,17... | collective-permute-start | bytes 221192 | tf_op jit(solution)/shard_map/ppermute | solution.py:417
  41.3 6.7 %collective-permute-start.9 = (f32[3,48,128]{2,1,0:T(8,128)S(1)}, f32[3,48,128]{2,1,0:T(8,128)S(1)}, u32[]{:S(2)}, u32[]{:S(2)}) collective-permute-start(f32[3,48,128]{2,1,0:T(8,128)S(1)} %get-tuple-element.28), channel_id=1, source_target_pairs={{0,16},{1,17},{2,18},{3,19},{4,20},{5,21},{6,22},{7,23},{8,24},{9,... | collective-permute-start | bytes 221192 | tf_op jit(solution)/shard_map/ppermute | solution.py:417

commit v11 on v10

--- a/solution.py
+++ b/solution.py
@@ -17,7 +17,6 @@
 SOFT = 0.01
 UNROLL = (18, 16)
 UNROLL_OWN = (12, 8)
-FULL_SLOTS = 54
 MIB = 1 << 20
 TILES = 36
 F32 = jnp.float32
@@ -196,7 +195,8 @@
         begin = begin + sizes[i]
     moved = jnp.where(a == place.astype(I32), 1.0, 0.0).astype(BF16)
     bucket = lane & 63
-    home = ((group - 1) & (NY - 1)) * NB + bucket
+    step = jnp.where(group == 2, -1, jnp.where(group == 3, 2, group))
+    home = ((me - step) & (NY - 1)) * NB + bucket
     slot, ins, outs = [], jnp.zeros((1, wide), F32), jnp.zeros((1, wide), F32)
     for k in range(K):
         slot.append(jnp.where(flag[k] > 0.5, ins, count + outs))
@@ -219,15 +219,13 @@
 
 def near_kernel(first, *refs):
     (table, tall, src_ref), refs = refs[:3], refs[3:]
-    outs, (out_ref, hold, spots, tab, sem) = refs[:-5], refs[-5:]
-    if not first:
-        kept, outs = outs[0], outs[1:]
+    sums, out_ref, hold, spots, tab, sem = refs
     copies = [pltpu.make_async_copy(table, tab, sem.at[0]), pltpu.make_async_copy(hold, spots, sem.at[1])]
     copies[0].start()
     for z in range(NZ):
         hold[z : z + 1, :] = src_ref[z * (TILES + 1) + TILES][0:1].astype(I32)
     copies[1].start()
-    out_ref[...] = jnp.zeros(out_ref.shape, F32) if first else kept[...]
+    out_ref[...] = jnp.zeros(out_ref.shape, F32)
     for copy in copies:
         copy.wait()
     lane1 = lax.broadcasted_iota(I32, (1, PL), 1)
@@ -247,7 +245,7 @@
     def stack(*v):
         return jnp.concatenate(v, axis=0).astype(BF16)
 
-    row_base = 0 if first else (NY - 1) * NB
+    row_field = 5 if first else 7
 
     def job(e, width):
         n = tab[6, e]
@@ -280,7 +278,7 @@
         o = jnp.dot(g, jnp.concatenate([high, low], axis=1), preferred_element_type=F32)
         o = o[:, :PL] + o[:, PL:]
         a = o[0:4] + o[4:8] + o[8:12]
-        out_ref[tab[5, e] - row_base] = jnp.where(lane4 < tab[4, e], a - t * a[3:4], 0.0)
+        out_ref[tab[row_field, e]] = jnp.where(lane4 < tab[4, e], a - t * a[3:4], 0.0)
 
     sizes = [tab[8 + i, 0] for i in range(4)]
 
@@ -295,7 +293,7 @@
         return (size + step - 1) // step * step
 
     n_full, n_half = sizes[0] + sizes[1], sizes[2] + sizes[3]
-    early_full = jnp.minimum(n_full, jnp.maximum(whole_steps(sizes[0], UNROLL[0]), FULL_SLOTS))
+    early_full = jnp.minimum(n_full, whole_steps(sizes[0], UNROLL[0]))
     early_half = jnp.minimum(n_half, whole_steps(sizes[2], UNROLL[1]))
     if first:
         run(jnp.int32(0), early_full, 4, UNROLL[0])
@@ -303,19 +301,16 @@
     else:
         run(early_full, n_full - early_full, 4, UNROLL_OWN[0])
         run(n_full + early_half, n_half - early_half, 2, UNROLL_OWN[1])
-    if first:
-        outs[-1][...] = out_ref[(NY - 1) * NB : NY * NB]
-        outs = outs[:-1]
-    for i, o in enumerate(outs):
+    for i in range(sums.shape[0]):
         for c in range(3):
-            o[c] = out_ref[i * NB : (i + 1) * NB, c, :]
-
-
-def final_kernel(cnt_ref, far_ref, p0, p1, p2, p3, out_ref):
+            sums[i, c] = out_ref[i * NB : (i + 1) * NB, c, :]
+
+
+def final_kernel(cnt_ref, far_ref, own_ref, back_ref, out_ref):
     live = lax.broadcasted_iota(I32, (NB, PL), 1) < column_of(cnt_ref[...], NB)
     for c in range(3):
-        near = (p0[c] + p1[c]) + (p2[c] + p3[c])
-        out_ref[c] = jnp.where(live, far_ref[c] + near, 0.0)
+        near = (back_ref[0, c] + back_ref[1, c]) + (back_ref[2, c] + back_ref[3, c])
+        out_ref[c] = jnp.where(live, far_ref[c] + (near + own_ref[0, c]), 0.0)
 
 
 def along_y(k):
@@ -393,37 +388,37 @@
     tall, tab, far = lax.optimization_barrier((tall, tab, far))
     window = window.reshape(NZ * (TILES + 1), 4, PL)
 
-    def near(first, *arrays):
-        partial = ((3, NB, PL), F32)
-        kept = ((NB, 4, PL), F32)
-        outs = (partial,) * (NY - 1) + (kept,) if first else (partial,)
+    def near(first, tab):
+        count = NY if first else 1
         return call(
             functools.partial(near_kernel, first),
-            outs,
-            [vspec()] * len(arrays),
-            [vspec()] * len(outs),
+            (((count, 3, NB, PL), F32),),
+            [vspec()] * 3,
+            [vspec()],
             "near",
             32,
             [
-                pltpu.VMEM(((NY if first else 1) * NB, 4, PL), F32),
+                pltpu.VMEM((count * NB, 4, PL), F32),
                 pltpu.VMEM((NZ, PL), I32),
                 pltpu.SMEM((NZ, PL), I32),
                 pltpu.SMEM((16, 2 * PL), I32),
                 pltpu.SemaphoreType.DMA((2,)),
             ],
-        )(*arrays)
-
-    *sent, kept = near(True, tab, tall, window)
-    back = [lax.ppermute(v, "space", along_y(-k)) for v, k in zip(sent, (1, -1, 2))]
-    (own,) = near(False, tab, tall, window, kept)
+        )(tab, tall, window)[0]
+
+    sums = near(True, tab)
+    y_rows = [[NZ * y + z for y in range(NY)] for z in range(NZ)]
+    back = lax.all_to_all(sums, "space", 0, 0, axis_index_groups=y_rows, tiled=True)
+    tab, sums = lax.optimization_barrier((tab, sums))
+    own = near(False, tab)
     (out,) = call(
         final_kernel,
         (((3, NB, PL), F32),),
-        [vspec()] * 6,
+        [vspec()] * 4,
         [vspec()],
         "final",
         8,
-    )(cnt, far, own, *back)
+    )(cnt, far, own, back)
     return jnp.transpose(out, (1, 0, 2))[None]
 
 

time: 49.6 us -> 52.9 us (1.067)
  the two profiles are of different devices: /device:TPU:6 before, /device:TPU:1 now
where the time goes in v11:
time: 52.9 us; the launch traced here: 51.9 us
  starting transfers between devices  23.5 us (44%)
  Pallas kernels  15.2 us (29%)
  waiting for transfers between devices  12.4 us (23%)
  local copies, waits for them, and re-layouts  0.66 us (1%)
    pallas_call x2, Pallas kernels, near(): call(functools.partial(near_kernel, first), (((count, 3, NB, PL), F32),),...  10.6 us
    all_to_all x1, starting transfers between devices, per_device(): lax.all_to_all(src, 'space', 0, 0, axis_index_groups=z_rows, tiled=True)  9.03 us
    all_to_all x1, starting transfers between devices, per_device(): lax.all_to_all(sums, 'space', 0, 0, axis_index_groups=y_rows, tiled=True)  4.89 us
    all_to_all x1, waiting for transfers between devices, per_device(): lax.all_to_all(sums, 'space', 0, 0, axis_index_groups=y_rows, tiled=True)  4.82 us
    ppermute x3, starting transfers between devices, per_device(): tgts = [tgt] + [lax.ppermute(tgt, 'space', along_y(k)) for k in (1, -1, 2)]  4.38 us
    ppermute x3, starting transfers between devices, per_device(): lax.ppermute(pair, 'slab', along_x(k))  4.3 us
    ppermute x3, waiting for transfers between devices, per_device(): lax.ppermute(pair, 'slab', along_x(k))  4.02 us
    all_to_all x1, waiting for transfers between devices, per_device(): lax.all_to_all(src, 'space', 0, 0, axis_index_groups=z_rows, tiled=True)  2.69 us
  transfers between devices with their start and end apart: 9, of which 5 were waited for; matrix products, arithmetic and copies ran while one was open for 0% of the time, Pallas kernels for 8%

profile of v11, /device:TPU:1, one launch (start us, length us, event | category | flops | bytes accessed | tf_op | source)
XLA Modules:
  0.0 51.9 jit_solution(12651698406801029146)
XLA Ops:
  0.0 2.1 %pack.1 = (f32[8,37,4,128]{3,2,1,0:T(4,128)}, f32[49,4,128]{2,1,0:T(4,128)S(1)}, f32[16,4,128]{2,1,0:T(4,128)S(1)}) custom-call(f32[3,48,128]{2,1,0:T(8,128)} %bitcast.22, f32[48,128]{1,0:T(8,128)} %bitcast.30, s32[1,48]{1,0:T(1,128)} %bitcast.26, s32[1,48]{1,0:T(1,128)} %refs_3_.1, s32[4,48]{1,0:T(4,128)} %bitcast.32, f32[3,2048]{1,0:T(4,128)} %refs_5_.1, ...), custom_call_target="tpu_custom_call" | custom-call | tf_op jit(solution)/shard_map/pack/pallas_call | solution.py:339
  2.1 9.0 %all-to-all-start = ((f32[8,37,4,128]{3,2,1,0:T(4,128)}), f32[8,37,4,128]{3,2,1,0:T(4,128)S(1)}, u32[]{:S(2)}, u32[]{:S(2)}) async-start(f32[8,37,4,128]{3,2,1,0:T(4,128)} %get-tuple-element.21), calls=%async_computation | async-start | bytes 1212416 | tf_op jit(solution)/shard_map/all_to_all | solution.py:365
  11.1 1.0 %collective-permute-start.3 = (f32[16,4,128]{2,1,0:T(4,128)S(1)}, f32[16,4,128]{2,1,0:T(4,128)S(1)}, u32[]{:S(2)}, u32[]{:S(2)}) collective-permute-start(f32[16,4,128]{2,1,0:T(4,128)S(1)} %get-tuple-element.17), channel_id=1, source_target_pairs={{0,32},{32,0},{64,96},{96,64},{128,160},{160,128},{192,224},{224,1... | collective-permute-start | bytes 98312 | tf_op jit(solution)/shard_map/ppermute | solution.py:367
  12.1 0.9 %collective-permute-done.3 = f32[16,4,128]{2,1,0:T(4,128)S(1)} collective-permute-done((f32[16,4,128]{2,1,0:T(4,128)S(1)}, f32[16,4,128]{2,1,0:T(4,128)S(1)}, u32[]{:S(2)}, u32[]{:S(2)}) %collective-permute-start.3) | collective-permute-done | bytes 32800 | tf_op jit(solution)/shard_map/ppermute | solution.py:367
  13.0 2.8 %collective-permute-start.6 = (f32[2,16,4,128]{3,2,1,0:T(4,128)S(1)}, f32[2,16,4,128]{3,2,1,0:T(4,128)S(1)}, u32[]{:S(2)}, u32[]{:S(2)}) collective-permute-start(f32[2,16,4,128]{3,2,1,0:T(4,128)S(1)} %pad_maximum_fusion.c0), channel_id=1, source_target_pairs={{0,128},{32,160},{64,192},{96,224},{128,0},{160,32},{192,64},{224,... | collective-permute-start | bytes 196616 | tf_op jit(solution)/shard_map/ppermute | solution.py:368
  15.8 2.9 %collective-permute-start.2 = (f32[49,4,128]{2,1,0:T(4,128)S(1)}, f32[49,4,128]{2,1,0:T(4,128)S(1)}, u32[]{:S(2)}, u32[]{:S(2)}) collective-permute-start(f32[49,4,128]{2,1,0:T(4,128)S(1)} %get-tuple-element.14.t0), channel_id=1, source_target_pairs={{0,16},{1,17},{2,18},{3,19},{4,20},{5,21},{6,22},{7,23},{8,24},{9,... | collective-permute-start | bytes 301064 | tf_op jit(solution)/shard_map/ppermute | solution.py:366
  18.7 0.8 %collective-permute-start.1 = (f32[49,4,128]{2,1,0:T(4,128)S(1)}, f32[49,4,128]{2,1,0:T(4,128)S(1)}, u32[]{:S(2)}, u32[]{:S(2)}) collective-permute-start(f32[49,4,128]{2,1,0:T(4,128)S(1)} %get-tuple-element.14.t0), channel_id=1, source_target_pairs={{0,24},{1,25},{2,26},{3,27},{4,28},{5,29},{6,30},{7,31},{8,0},{9,1... | collective-permute-start | bytes 301064 | tf_op jit(solution)/shard_map/ppermute | solution.py:366
  19.5 0.7 %collective-permute-start = (f32[49,4,128]{2,1,0:T(4,128)S(1)}, f32[49,4,128]{2,1,0:T(4,128)S(1)}, u32[]{:S(2)}, u32[]{:S(2)}) collective-permute-start(f32[49,4,128]{2,1,0:T(4,128)S(1)} %get-tuple-element.14.t0), channel_id=1, source_target_pairs={{0,8},{1,9},{2,10},{3,11},{4,12},{5,13},{6,14},{7,15},{8,16},{9,17... | collective-permute-start | bytes 301064 | tf_op jit(solution)/shard_map/ppermute | solution.py:366
  20.2 0.9 %collective-permute-start.5 = (f32[2,16,4,128]{3,2,1,0:T(4,128)S(1)}, f32[2,16,4,128]{3,2,1,0:T(4,128)S(1)}, u32[]{:S(2)}, u32[]{:S(2)}) collective-permute-start(f32[2,16,4,128]{3,2,1,0:T(4,128)S(1)} %pad_maximum_fusion.c0), channel_id=1, source_target_pairs={{0,192},{32,224},{64,0},{96,32},{128,64},{160,96},{192,128},{224,1... | collective-permute-start | bytes 196616 | tf_op jit(solution)/shard_map/ppermute | solution.py:368
  21.1 0.0 collective-permute-done.6.c3
  21.1 0.6 %collective-permute-start.4 = (f32[2,16,4,128]{3,2,1,0:T(4,128)S(1)}, f32[2,16,4,128]{3,2,1,0:T(4,128)S(1)}, u32[]{:S(2)}, u32[]{:S(2)}) collective-permute-start(f32[2,16,4,128]{3,2,1,0:T(4,128)S(1)} %pad_maximum_fusion.c0), channel_id=1, source_target_pairs={{0,64},{32,96},{64,128},{96,160},{128,192},{160,224},{192,0},{224,... | collective-permute-start | bytes 196616 | tf_op jit(solution)/shard_map/ppermute | solution.py:368
  21.7 1.9 %collective-permute-done.5.c2 = f32[2,16,4,128]{3,2,1,0:T(4,128)S(1)} collective-permute-done((f32[2,16,4,128]{3,2,1,0:T(4,128)S(1)}, f32[2,16,4,128]{3,2,1,0:T(4,128)S(1)}, u32[]{:S(2)}, u32[]{:S(2)}) %collective-permute-start.5) | collective-permute-done | bytes 65568 | tf_op jit(solution)/shard_map/ppermute | solution.py:368
  23.6 2.1 %collective-permute-done.4.c1 = f32[2,16,4,128]{3,2,1,0:T(4,128)S(1)} collective-permute-done((f32[2,16,4,128]{3,2,1,0:T(4,128)S(1)}, f32[2,16,4,128]{3,2,1,0:T(4,128)S(1)}, u32[]{:S(2)}, u32[]{:S(2)}) %collective-permute-start.4) | collective-permute-done | bytes 65568 | tf_op jit(solution)/shard_map/ppermute | solution.py:368
  25.7 0.6 %copy-done.2 = s32[1,1,48]{2,1,0:T(1,128)S(1)} copy-done((s32[1,1,48]{2,1,0:T(1,128)S(1)}, s32[1,1,48]{2,1,0:T(1,128)}, u32[]{:S(2)}) %copy-start.2) | copy-done | bytes 216
  26.3 1.4 %far.1.far_ref = f32[3,48,128]{2,1,0:T(8,128)S(1)} custom-call(s32[1]{0:T(128)} %bitcast.8.place_ref, f32[3,48,128]{2,1,0:T(8,128)S(1)} %bitcast.23, s32[1,48]{1,0:T(1,128)S(1)} %bitcast.27, s32[32,48]{1,0:T(8,128)S(1)} %bitcast.25, f32[2,16,4,128]{3,2,1,0:T(4,128)S(1)} %pad_maximum_fusion.c0, f32[2,16,4,128]{3,2,1,0:T(4,128)S(1)} %collective-permute-done.4.c1, ...), custom_call_target="tpu_custom_call" | custom-call | tf_op jit(solution)/shard_map/far/pallas_call | solution.py:379
  27.8 0.0 collective-permute-done.2.t3
  27.8 0.0 collective-permute-done.t1
  27.8 0.4 prep.1
  28.2 2.7 %all-to-all-done = f32[8,37,4,128]{3,2,1,0:T(4,128)S(1)} async-done(((f32[8,37,4,128]{3,2,1,0:T(4,128)}), f32[8,37,4,128]{3,2,1,0:T(4,128)S(1)}, u32[]{:S(2)}, u32[]{:S(2)}) %all-to-all-start) | async-done | bytes 606240 | tf_op jit(solution)/shard_map/all_to_all | solution.py:365
  30.9 8.1 %near.2 = f32[4,3,48,128]{3,2,1,0:T(8,128)} custom-call(s32[16,256]{1,0:T(8,128)S(1)} %get-tuple-element.22.refs_0_, f32[192,4,128]{2,1,0:T(4,128)S(1)} %get-tuple-element.20.refs_1_, f32[296,4,128]{2,1,0:T(4,128)S(1)} %bitcast.20), custom_call_target="tpu_custom_call" | custom-call | tf_op jit(solution)/shard_map/near/pallas_call | solution.py:393
  39.0 4.9 %all-to-all-start.1 = ((f32[4,3,48,128]{3,2,1,0:T(8,128)}), f32[4,3,48,128]{3,2,1,0:T(8,128)S(1)}, u32[]{:S(2)}, u32[]{:S(2)}) async-start(f32[4,3,48,128]{3,2,1,0:T(8,128)} %near.2), calls=%async_computation.1 | async-start | bytes 589824 | tf_op jit(solution)/shard_map/all_to_all | solution.py:411
  43.9 2.5 %near.3.own_ref = f32[1,3,48,128]{3,2,1,0:T(8,128)S(1)} custom-call(s32[16,256]{1,0:T(8,128)S(1)} %get-tuple-element.22.refs_0_, f32[192,4,128]{2,1,0:T(4,128)S(1)} %get-tuple-element.20.refs_1_, f32[296,4,128]{2,1,0:T(4,128)S(1)} %bitcast.21), custom_call_target="tpu_custom_call" | custom-call | tf_op jit(solution)/shard_map/near/pallas_call | solution.py:393
  46.4 4.8 %all-to-all-done.1.back_ref = f32[4,3,48,128]{3,2,1,0:T(8,128)S(1)} async-done(((f32[4,3,48,128]{3,2,1,0:T(8,128)}), f32[4,3,48,128]{3,2,1,0:T(8,128)S(1)}, u32[]{:S(2)}, u32[]{:S(2)}) %all-to-all-start.1) | async-done | bytes 294944 | tf_op jit(solution)/shard_map/all_to_all | solution.py:411
  51.2 0.7 %final.1 = f32[3,48,128]{2,1,0:T(8,128)} custom-call(s32[1,48]{1,0:T(1,128)S(1)} %bitcast.28, f32[3,48,128]{2,1,0:T(8,128)S(1)} %far.1.far_ref, f32[1,3,48,128]{3,2,1,0:T(8,128)S(1)} %near.3.own_ref, f32[4,3,48,128]{3,2,1,0:T(8,128)S(1)} %all-to-all-done.1.back_ref), custom_call_target="tpu_custom_call" | custom-call | tf_op jit(solution)/shard_map/final/pallas_call | solution.py:414
  (7 shorter events, 0.0 us)
Async XLA Ops:
  2.1 28.7 %all-to-all-start = ((f32[8,37,4,128]{3,2,1,0:T(4,128)}), f32[8,37,4,128]{3,2,1,0:T(4,128)S(1)}, u32[]{:S(2)}, u32[]{:S(2)}) async-start(f32[8,37,4,128]{3,2,1,0:T(4,128)} %get-tuple-element.21), calls=%async_computation | async-start | bytes 1212416 | tf_op jit(solution)/shard_map/all_to_all | solution.py:365
  11.1 1.8 %collective-permute-start.3 = (f32[16,4,128]{2,1,0:T(4,128)S(1)}, f32[16,4,128]{2,1,0:T(4,128)S(1)}, u32[]{:S(2)}, u32[]{:S(2)}) collective-permute-start(f32[16,4,128]{2,1,0:T(4,128)S(1)} %get-tuple-element.17), channel_id=1, source_target_pairs={{0,32},{32,0},{64,96},{96,64},{128,160},{160,128},{192,224},{224,1... | collective-permute-start | bytes 98312 | tf_op jit(solution)/shard_map/ppermute | solution.py:367
  13.0 12.7 %copy-start = (f32[1,48,3,128]{3,1,2,0:T(8,128)S(1)}, f32[1,48,3,128]{3,1,2,0:T(8,128)}, u32[]{:S(2)}) copy-start(f32[1,48,3,128]{3,1,2,0:T(8,128)} %param.8) | copy-start | bytes 221188
  13.0 8.1 %collective-permute-start.6 = (f32[2,16,4,128]{3,2,1,0:T(4,128)S(1)}, f32[2,16,4,128]{3,2,1,0:T(4,128)S(1)}, u32[]{:S(2)}, u32[]{:S(2)}) collective-permute-start(f32[2,16,4,128]{3,2,1,0:T(4,128)S(1)} %pad_maximum_fusion.c0), channel_id=1, source_target_pairs={{0,128},{32,160},{64,192},{96,224},{128,0},{160,32},{192,64},{224,... | collective-permute-start | bytes 196616 | tf_op jit(solution)/shard_map/ppermute | solution.py:368
  15.8 11.9 %collective-permute-start.2 = (f32[49,4,128]{2,1,0:T(4,128)S(1)}, f32[49,4,128]{2,1,0:T(4,128)S(1)}, u32[]{:S(2)}, u32[]{:S(2)}) collective-permute-start(f32[49,4,128]{2,1,0:T(4,128)S(1)} %get-tuple-element.14.t0), channel_id=1, source_target_pairs={{0,16},{1,17},{2,18},{3,19},{4,20},{5,21},{6,22},{7,23},{8,24},{9,... | collective-permute-start | bytes 301064 | tf_op jit(solution)/shard_map/ppermute | solution.py:366
  18.7 9.0 %collective-permute-start.1 = (f32[49,4,128]{2,1,0:T(4,128)S(1)}, f32[49,4,128]{2,1,0:T(4,128)S(1)}, u32[]{:S(2)}, u32[]{:S(2)}) collective-permute-start(f32[49,4,128]{2,1,0:T(4,128)S(1)} %get-tuple-element.14.t0), channel_id=1, source_target_pairs={{0,24},{1,25},{2,26},{3,27},{4,28},{5,29},{6,30},{7,31},{8,0},{9,1... | collective-permute-start | bytes 301064 | tf_op jit(solution)/shard_map/ppermute | solution.py:366
  19.5 8.3 %collective-permute-start = (f32[49,4,128]{2,1,0:T(4,128)S(1)}, f32[49,4,128]{2,1,0:T(4,128)S(1)}, u32[]{:S(2)}, u32[]{:S(2)}) collective-permute-start(f32[49,4,128]{2,1,0:T(4,128)S(1)} %get-tuple-element.14.t0), channel_id=1, source_target_pairs={{0,8},{1,9},{2,10},{3,11},{4,12},{5,13},{6,14},{7,15},{8,16},{9,17... | collective-permute-start | bytes 301064 | tf_op jit(solution)/shard_map/ppermute | solution.py:366
  20.2 3.4 %collective-permute-start.5 = (f32[2,16,4,128]{3,2,1,0:T(4,128)S(1)}, f32[2,16,4,128]{3,2,1,0:T(4,128)S(1)}, u32[]{:S(2)}, u32[]{:S(2)}) collective-permute-start(f32[2,16,4,128]{3,2,1,0:T(4,128)S(1)} %pad_maximum_fusion.c0), channel_id=1, source_target_pairs={{0,192},{32,224},{64,0},{96,32},{128,64},{160,96},{192,128},{224,1... | collective-permute-start | bytes 196616 | tf_op jit(solution)/shard_map/ppermute | solution.py:368
  21.1 4.6 %collective-permute-start.4 = (f32[2,16,4,128]{3,2,1,0:T(4,128)S(1)}, f32[2,16,4,128]{3,2,1,0:T(4,128)S(1)}, u32[]{:S(2)}, u32[]{:S(2)}) collective-permute-start(f32[2,16,4,128]{3,2,1,0:T(4,128)S(1)} %pad_maximum_fusion.c0), channel_id=1, source_target_pairs={{0,64},{32,96},{64,128},{96,160},{128,192},{160,224},{192,0},{224,... | collective-permute-start | bytes 196616 | tf_op jit(solution)/shard_map/ppermute | solution.py:368
  21.7 4.0 %copy-start.1 = (s32[1,48,32]{1,2,0:T(8,128)S(1)}, s32[1,48,32]{1,2,0:T(8,128)}, u32[]{:S(2)}) copy-start(s32[1,48,32]{1,2,0:T(8,128)} %param.13) | copy-start | bytes 18436
  25.7 0.7 %copy-start.2 = (s32[1,1,48]{2,1,0:T(1,128)S(1)}, s32[1,1,48]{2,1,0:T(1,128)}, u32[]{:S(2)}) copy-start(s32[1,1,48]{2,1,0:T(1,128)} %param.10) | copy-start | bytes 580
  39.0 12.2 %all-to-all-start.1 = ((f32[4,3,48,128]{3,2,1,0:T(8,128)}), f32[4,3,48,128]{3,2,1,0:T(8,128)S(1)}, u32[]{:S(2)}, u32[]{:S(2)}) async-start(f32[4,3,48,128]{3,2,1,0:T(8,128)} %near.2), calls=%async_computation.1 | async-start | bytes 589824 | tf_op jit(solution)/shard_map/all_to_all | solution.py:411

commit v12 on v10

--- a/solution.py
+++ b/solution.py
@@ -15,9 +15,8 @@
 NZ = 8
 NX = 4
 SOFT = 0.01
-UNROLL = (18, 16)
+UNROLL = (18, 20)
 UNROLL_OWN = (12, 8)
-FULL_SLOTS = 54
 MIB = 1 << 20
 TILES = 36
 F32 = jnp.float32
@@ -295,7 +294,7 @@
         return (size + step - 1) // step * step
 
     n_full, n_half = sizes[0] + sizes[1], sizes[2] + sizes[3]
-    early_full = jnp.minimum(n_full, jnp.maximum(whole_steps(sizes[0], UNROLL[0]), FULL_SLOTS))
+    early_full = jnp.minimum(n_full, whole_steps(sizes[0], UNROLL[0]))
     early_half = jnp.minimum(n_half, whole_steps(sizes[2], UNROLL[1]))
     if first:
         run(jnp.int32(0), early_full, 4, UNROLL[0])
@@ -414,7 +413,7 @@
         )(*arrays)
 
     *sent, kept = near(True, tab, tall, window)
-    back = [lax.ppermute(v, "space", along_y(-k)) for v, k in zip(sent, (1, -1, 2))]
+    back = [lax.ppermute(sent[i], "space", along_y(-k)) for i, k in ((2, 2), (0, 1), (1, -1))]
     (own,) = near(False, tab, tall, window, kept)
     (out,) = call(
         final_kernel,

time: 49.6 us -> 48.8 us (0.984)
  the two profiles are of different devices: /device:TPU:6 before, /device:TPU:1 now
where the time goes in v12:
time: 48.8 us; the launch traced here: 48.3 us
  starting transfers between devices  25.2 us (52%)
  Pallas kernels  12.1 us (25%)
  waiting for transfers between devices  10.3 us (21%)
  local copies, waits for them, and re-layouts  0.66 us (1%)
    all_to_all x1, starting transfers between devices, per_device(): lax.all_to_all(src, 'space', 0, 0, axis_index_groups=z_rows, tiled=True)  9.03 us
    pallas_call x2, Pallas kernels, near(): call(functools.partial(near_kernel, first), outs, [vspec()] * len(arrays)...  7.4 us
    ppermute x3, starting transfers between devices, per_device(): lax.ppermute(sent[i], 'space', along_y(-k))  6.49 us
    ppermute x3, starting transfers between devices, per_device(): tgts = [tgt] + [lax.ppermute(tgt, 'space', along_y(k)) for k in (1, -1, 2)]  4.38 us
    ppermute x3, starting transfers between devices, per_device(): lax.ppermute(pair, 'slab', along_x(k))  4.3 us
    ppermute x3, waiting for transfers between devices, per_device(): lax.ppermute(pair, 'slab', along_x(k))  4.02 us
    ppermute x3, waiting for transfers between devices, per_device(): lax.ppermute(sent[i], 'space', along_y(-k))  2.74 us
    all_to_all x1, waiting for transfers between devices, per_device(): lax.all_to_all(src, 'space', 0, 0, axis_index_groups=z_rows, tiled=True)  2.69 us
  transfers between devices with their start and end apart: 11, of which 6 were waited for; matrix products, arithmetic and copies ran while one was open for 0% of the time, Pallas kernels for 6%

profile of v12, /device:TPU:1, one launch (start us, length us, event | category | flops | bytes accessed | tf_op | source)
XLA Modules:
  0.0 48.3 jit_solution(4924218466757096817)
XLA Ops:
  0.0 2.1 %pack.1 = (f32[8,37,4,128]{3,2,1,0:T(4,128)}, f32[49,4,128]{2,1,0:T(4,128)S(1)}, f32[16,4,128]{2,1,0:T(4,128)S(1)}) custom-call(f32[3,48,128]{2,1,0:T(8,128)} %bitcast.22, f32[48,128]{1,0:T(8,128)} %bitcast.30, s32[1,48]{1,0:T(1,128)} %bitcast.26, s32[1,48]{1,0:T(1,128)} %refs_3_.1, s32[4,48]{1,0:T(4,128)} %bitcast.32, f32[3,2048]{1,0:T(4,128)} %refs_5_.1, ...), custom_call_target="tpu_custom_call" | custom-call | tf_op jit(solution)/shard_map/pack/pallas_call | solution.py:343
  2.1 9.0 %all-to-all-start = ((f32[8,37,4,128]{3,2,1,0:T(4,128)}), f32[8,37,4,128]{3,2,1,0:T(4,128)S(1)}, u32[]{:S(2)}, u32[]{:S(2)}) async-start(f32[8,37,4,128]{3,2,1,0:T(4,128)} %get-tuple-element.24), calls=%async_computation | async-start | bytes 1212416 | tf_op jit(solution)/shard_map/all_to_all | solution.py:369
  11.2 1.0 %collective-permute-start.3 = (f32[16,4,128]{2,1,0:T(4,128)S(1)}, f32[16,4,128]{2,1,0:T(4,128)S(1)}, u32[]{:S(2)}, u32[]{:S(2)}) collective-permute-start(f32[16,4,128]{2,1,0:T(4,128)S(1)} %get-tuple-element.20), channel_id=1, source_target_pairs={{0,32},{32,0},{64,96},{96,64},{128,160},{160,128},{192,224},{224,1... | collective-permute-start | bytes 98312 | tf_op jit(solution)/shard_map/ppermute | solution.py:371
  12.1 0.9 %collective-permute-done.3 = f32[16,4,128]{2,1,0:T(4,128)S(1)} collective-permute-done((f32[16,4,128]{2,1,0:T(4,128)S(1)}, f32[16,4,128]{2,1,0:T(4,128)S(1)}, u32[]{:S(2)}, u32[]{:S(2)}) %collective-permute-start.3) | collective-permute-done | bytes 32800 | tf_op jit(solution)/shard_map/ppermute | solution.py:371
  13.0 2.8 %collective-permute-start.6 = (f32[2,16,4,128]{3,2,1,0:T(4,128)S(1)}, f32[2,16,4,128]{3,2,1,0:T(4,128)S(1)}, u32[]{:S(2)}, u32[]{:S(2)}) collective-permute-start(f32[2,16,4,128]{3,2,1,0:T(4,128)S(1)} %pad_maximum_fusion.c0), channel_id=1, source_target_pairs={{0,128},{32,160},{64,192},{96,224},{128,0},{160,32},{192,64},{224,... | collective-permute-start | bytes 196616 | tf_op jit(solution)/shard_map/ppermute | solution.py:372
  15.8 2.9 %collective-permute-start.2 = (f32[49,4,128]{2,1,0:T(4,128)S(1)}, f32[49,4,128]{2,1,0:T(4,128)S(1)}, u32[]{:S(2)}, u32[]{:S(2)}) collective-permute-start(f32[49,4,128]{2,1,0:T(4,128)S(1)} %get-tuple-element.17.t0), channel_id=1, source_target_pairs={{0,16},{1,17},{2,18},{3,19},{4,20},{5,21},{6,22},{7,23},{8,24},{9,... | collective-permute-start | bytes 301064 | tf_op jit(solution)/shard_map/ppermute | solution.py:370
  18.7 0.8 %collective-permute-start.1 = (f32[49,4,128]{2,1,0:T(4,128)S(1)}, f32[49,4,128]{2,1,0:T(4,128)S(1)}, u32[]{:S(2)}, u32[]{:S(2)}) collective-permute-start(f32[49,4,128]{2,1,0:T(4,128)S(1)} %get-tuple-element.17.t0), channel_id=1, source_target_pairs={{0,24},{1,25},{2,26},{3,27},{4,28},{5,29},{6,30},{7,31},{8,0},{9,1... | collective-permute-start | bytes 301064 | tf_op jit(solution)/shard_map/ppermute | solution.py:370
  19.5 0.7 %collective-permute-start = (f32[49,4,128]{2,1,0:T(4,128)S(1)}, f32[49,4,128]{2,1,0:T(4,128)S(1)}, u32[]{:S(2)}, u32[]{:S(2)}) collective-permute-start(f32[49,4,128]{2,1,0:T(4,128)S(1)} %get-tuple-element.17.t0), channel_id=1, source_target_pairs={{0,8},{1,9},{2,10},{3,11},{4,12},{5,13},{6,14},{7,15},{8,16},{9,17... | collective-permute-start | bytes 301064 | tf_op jit(solution)/shard_map/ppermute | solution.py:370
  20.2 0.9 %collective-permute-start.5 = (f32[2,16,4,128]{3,2,1,0:T(4,128)S(1)}, f32[2,16,4,128]{3,2,1,0:T(4,128)S(1)}, u32[]{:S(2)}, u32[]{:S(2)}) collective-permute-start(f32[2,16,4,128]{3,2,1,0:T(4,128)S(1)} %pad_maximum_fusion.c0), channel_id=1, source_target_pairs={{0,192},{32,224},{64,0},{96,32},{128,64},{160,96},{192,128},{224,1... | collective-permute-start | bytes 196616 | tf_op jit(solution)/shard_map/ppermute | solution.py:372
  21.1 0.6 %collective-permute-start.4 = (f32[2,16,4,128]{3,2,1,0:T(4,128)S(1)}, f32[2,16,4,128]{3,2,1,0:T(4,128)S(1)}, u32[]{:S(2)}, u32[]{:S(2)}) collective-permute-start(f32[2,16,4,128]{3,2,1,0:T(4,128)S(1)} %pad_maximum_fusion.c0), channel_id=1, source_target_pairs={{0,64},{32,96},{64,128},{96,160},{128,192},{160,224},{192,0},{224,... | collective-permute-start | bytes 196616 | tf_op jit(solution)/shard_map/ppermute | solution.py:372
  21.7 1.9 %collective-permute-done.5.c2 = f32[2,16,4,128]{3,2,1,0:T(4,128)S(1)} collective-permute-done((f32[2,16,4,128]{3,2,1,0:T(4,128)S(1)}, f32[2,16,4,128]{3,2,1,0:T(4,128)S(1)}, u32[]{:S(2)}, u32[]{:S(2)}) %collective-permute-start.5) | collective-permute-done | bytes 65568 | tf_op jit(solution)/shard_map/ppermute | solution.py:372
  23.6 2.1 %collective-permute-done.4.c1 = f32[2,16,4,128]{3,2,1,0:T(4,128)S(1)} collective-permute-done((f32[2,16,4,128]{3,2,1,0:T(4,128)S(1)}, f32[2,16,4,128]{3,2,1,0:T(4,128)S(1)}, u32[]{:S(2)}, u32[]{:S(2)}) %collective-permute-start.4) | collective-permute-done | bytes 65568 | tf_op jit(solution)/shard_map/ppermute | solution.py:372
  25.7 0.6 %copy-done.2 = s32[1,1,48]{2,1,0:T(1,128)S(1)} copy-done((s32[1,1,48]{2,1,0:T(1,128)S(1)}, s32[1,1,48]{2,1,0:T(1,128)}, u32[]{:S(2)}) %copy-start.2) | copy-done | bytes 216
  26.4 1.4 %far.1.far_ref = f32[3,48,128]{2,1,0:T(8,128)S(1)} custom-call(s32[1]{0:T(128)} %bitcast.8.place_ref, f32[3,48,128]{2,1,0:T(8,128)S(1)} %bitcast.23, s32[1,48]{1,0:T(1,128)S(1)} %bitcast.27, s32[32,48]{1,0:T(8,128)S(1)} %bitcast.25, f32[2,16,4,128]{3,2,1,0:T(4,128)S(1)} %pad_maximum_fusion.c0, f32[2,16,4,128]{3,2,1,0:T(4,128)S(1)} %collective-permute-done.4.c1, ...), custom_call_target="tpu_custom_call" | custom-call | tf_op jit(solution)/shard_map/far/pallas_call | solution.py:383
  27.8 0.4 prep.1
  28.2 2.7 %all-to-all-done = f32[8,37,4,128]{3,2,1,0:T(4,128)S(1)} async-done(((f32[8,37,4,128]{3,2,1,0:T(4,128)}), f32[8,37,4,128]{3,2,1,0:T(4,128)S(1)}, u32[]{:S(2)}, u32[]{:S(2)}) %all-to-all-start) | async-done | bytes 606240 | tf_op jit(solution)/shard_map/all_to_all | solution.py:369
  30.9 6.4 %near.2 = (f32[3,48,128]{2,1,0:T(8,128)S(1)}, f32[3,48,128]{2,1,0:T(8,128)S(1)}, f32[3,48,128]{2,1,0:T(8,128)S(1)}, f32[48,4,128]{2,1,0:T(4,128)S(1)}) custom-call(s32[16,256]{1,0:T(8,128)S(1)} %get-tuple-element.22.refs_0_, f32[192,4,128]{2,1,0:T(4,128)S(1)} %get-tuple-element.23.refs_1_, f32[296,4,128]{2,1,0:T(4,128)S(1)} %bitcast.20), custom_call_target="tpu_custom_call" | custom-call | tf_op jit(solution)/shard_map/near/pallas_call | solution.py:399
  37.3 5.0 %collective-permute-start.7 = (f32[3,48,128]{2,1,0:T(8,128)S(1)}, f32[3,48,128]{2,1,0:T(8,128)S(1)}, u32[]{:S(2)}, u32[]{:S(2)}) collective-permute-start(f32[3,48,128]{2,1,0:T(8,128)S(1)} %get-tuple-element.26), channel_id=1, source_target_pairs={{0,16},{1,17},{2,18},{3,19},{4,20},{5,21},{6,22},{7,23},{8,24},{9,... | collective-permute-start | bytes 221192 | tf_op jit(solution)/shard_map/ppermute | solution.py:416
  42.3 0.8 %collective-permute-start.8 = (f32[3,48,128]{2,1,0:T(8,128)S(1)}, f32[3,48,128]{2,1,0:T(8,128)S(1)}, u32[]{:S(2)}, u32[]{:S(2)}) collective-permute-start(f32[3,48,128]{2,1,0:T(8,128)S(1)} %get-tuple-element.27), channel_id=1, source_target_pairs={{0,24},{1,25},{2,26},{3,27},{4,28},{5,29},{6,30},{7,31},{8,0},{9,1... | collective-permute-start | bytes 221192 | tf_op jit(solution)/shard_map/ppermute | solution.py:416
  43.1 0.7 %collective-permute-start.9 = (f32[3,48,128]{2,1,0:T(8,128)S(1)}, f32[3,48,128]{2,1,0:T(8,128)S(1)}, u32[]{:S(2)}, u32[]{:S(2)}) collective-permute-start(f32[3,48,128]{2,1,0:T(8,128)S(1)} %get-tuple-element.28), channel_id=1, source_target_pairs={{0,8},{1,9},{2,10},{3,11},{4,12},{5,13},{6,14},{7,15},{8,16},{9,17... | collective-permute-start | bytes 221192 | tf_op jit(solution)/shard_map/ppermute | solution.py:416
  43.8 1.0 %near.3.p0 = f32[3,48,128]{2,1,0:T(8,128)S(1)} custom-call(s32[16,256]{1,0:T(8,128)S(1)} %get-tuple-element.22.refs_0_, f32[192,4,128]{2,1,0:T(4,128)S(1)} %get-tuple-element.23.refs_1_, f32[296,4,128]{2,1,0:T(4,128)S(1)} %bitcast.21, f32[48,4,128]{2,1,0:T(4,128)S(1)} %get-tuple-element.25.refs_3_), custom_call_target="tpu_custom_call" | custom-call | tf_op jit(solution)/shard_map/near/pallas_call | solution.py:399
  44.8 1.3 %collective-permute-done.8.p2 = f32[3,48,128]{2,1,0:T(8,128)S(1)} collective-permute-done((f32[3,48,128]{2,1,0:T(8,128)S(1)}, f32[3,48,128]{2,1,0:T(8,128)S(1)}, u32[]{:S(2)}, u32[]{:S(2)}) %collective-permute-start.8) | collective-permute-done | bytes 73760 | tf_op jit(solution)/shard_map/ppermute | solution.py:416
  46.1 1.5 %collective-permute-done.9.p3 = f32[3,48,128]{2,1,0:T(8,128)S(1)} collective-permute-done((f32[3,48,128]{2,1,0:T(8,128)S(1)}, f32[3,48,128]{2,1,0:T(8,128)S(1)}, u32[]{:S(2)}, u32[]{:S(2)}) %collective-permute-start.9) | collective-permute-done | bytes 73760 | tf_op jit(solution)/shard_map/ppermute | solution.py:416
  47.5 0.7 %final.1 = f32[3,48,128]{2,1,0:T(8,128)} custom-call(s32[1,48]{1,0:T(1,128)S(1)} %bitcast.28, f32[3,48,128]{2,1,0:T(8,128)S(1)} %far.1.far_ref, f32[3,48,128]{2,1,0:T(8,128)S(1)} %near.3.p0, f32[3,48,128]{2,1,0:T(8,128)S(1)} %collective-permute-done.7.p1, f32[3,48,128]{2,1,0:T(8,128)S(1)} %collective-permute-done.8.p2, ...), custom_call_target="tpu_custom_call" | custom-call | tf_op jit(solution)/shard_map/final/pallas_call | solution.py:418
  (11 shorter events, 0.0 us)
Async XLA Ops:
  2.1 28.7 %all-to-all-start = ((f32[8,37,4,128]{3,2,1,0:T(4,128)}), f32[8,37,4,128]{3,2,1,0:T(4,128)S(1)}, u32[]{:S(2)}, u32[]{:S(2)}) async-start(f32[8,37,4,128]{3,2,1,0:T(4,128)} %get-tuple-element.24), calls=%async_computation | async-start | bytes 1212416 | tf_op jit(solution)/shard_map/all_to_all | solution.py:369
  11.2 1.8 %collective-permute-start.3 = (f32[16,4,128]{2,1,0:T(4,128)S(1)}, f32[16,4,128]{2,1,0:T(4,128)S(1)}, u32[]{:S(2)}, u32[]{:S(2)}) collective-permute-start(f32[16,4,128]{2,1,0:T(4,128)S(1)} %get-tuple-element.20), channel_id=1, source_target_pairs={{0,32},{32,0},{64,96},{96,64},{128,160},{160,128},{192,224},{224,1... | collective-permute-start | bytes 98312 | tf_op jit(solution)/shard_map/ppermute | solution.py:371
  13.0 12.7 %copy-start = (f32[1,48,3,128]{3,1,2,0:T(8,128)S(1)}, f32[1,48,3,128]{3,1,2,0:T(8,128)}, u32[]{:S(2)}) copy-start(f32[1,48,3,128]{3,1,2,0:T(8,128)} %param.8) | copy-start | bytes 221188
  13.0 8.1 %collective-permute-start.6 = (f32[2,16,4,128]{3,2,1,0:T(4,128)S(1)}, f32[2,16,4,128]{3,2,1,0:T(4,128)S(1)}, u32[]{:S(2)}, u32[]{:S(2)}) collective-permute-start(f32[2,16,4,128]{3,2,1,0:T(4,128)S(1)} %pad_maximum_fusion.c0), channel_id=1, source_target_pairs={{0,128},{32,160},{64,192},{96,224},{128,0},{160,32},{192,64},{224,... | collective-permute-start | bytes 196616 | tf_op jit(solution)/shard_map/ppermute | solution.py:372
  15.8 12.0 %collective-permute-start.2 = (f32[49,4,128]{2,1,0:T(4,128)S(1)}, f32[49,4,128]{2,1,0:T(4,128)S(1)}, u32[]{:S(2)}, u32[]{:S(2)}) collective-permute-start(f32[49,4,128]{2,1,0:T(4,128)S(1)} %get-tuple-element.17.t0), channel_id=1, source_target_pairs={{0,16},{1,17},{2,18},{3,19},{4,20},{5,21},{6,22},{7,23},{8,24},{9,... | collective-permute-start | bytes 301064 | tf_op jit(solution)/shard_map/ppermute | solution.py:370
  18.7 9.0 %collective-permute-start.1 = (f32[49,4,128]{2,1,0:T(4,128)S(1)}, f32[49,4,128]{2,1,0:T(4,128)S(1)}, u32[]{:S(2)}, u32[]{:S(2)}) collective-permute-start(f32[49,4,128]{2,1,0:T(4,128)S(1)} %get-tuple-element.17.t0), channel_id=1, source_target_pairs={{0,24},{1,25},{2,26},{3,27},{4,28},{5,29},{6,30},{7,31},{8,0},{9,1... | collective-permute-start | bytes 301064 | tf_op jit(solution)/shard_map/ppermute | solution.py:370
  19.5 8.3 %collective-permute-start = (f32[49,4,128]{2,1,0:T(4,128)S(1)}, f32[49,4,128]{2,1,0:T(4,128)S(1)}, u32[]{:S(2)}, u32[]{:S(2)}) collective-permute-start(f32[49,4,128]{2,1,0:T(4,128)S(1)} %get-tuple-element.17.t0), channel_id=1, source_target_pairs={{0,8},{1,9},{2,10},{3,11},{4,12},{5,13},{6,14},{7,15},{8,16},{9,17... | collective-permute-start | bytes 301064 | tf_op jit(solution)/shard_map/ppermute | solution.py:370
  20.2 3.4 %collective-permute-start.5 = (f32[2,16,4,128]{3,2,1,0:T(4,128)S(1)}, f32[2,16,4,128]{3,2,1,0:T(4,128)S(1)}, u32[]{:S(2)}, u32[]{:S(2)}) collective-permute-start(f32[2,16,4,128]{3,2,1,0:T(4,128)S(1)} %pad_maximum_fusion.c0), channel_id=1, source_target_pairs={{0,192},{32,224},{64,0},{96,32},{128,64},{160,96},{192,128},{224,1... | collective-permute-start | bytes 196616 | tf_op jit(solution)/shard_map/ppermute | solution.py:372
  21.1 4.6 %collective-permute-start.4 = (f32[2,16,4,128]{3,2,1,0:T(4,128)S(1)}, f32[2,16,4,128]{3,2,1,0:T(4,128)S(1)}, u32[]{:S(2)}, u32[]{:S(2)}) collective-permute-start(f32[2,16,4,128]{3,2,1,0:T(4,128)S(1)} %pad_maximum_fusion.c0), channel_id=1, source_target_pairs={{0,64},{32,96},{64,128},{96,160},{128,192},{160,224},{192,0},{224,... | collective-permute-start | bytes 196616 | tf_op jit(solution)/shard_map/ppermute | solution.py:372
  21.7 4.0 %copy-start.1 = (s32[1,48,32]{1,2,0:T(8,128)S(1)}, s32[1,48,32]{1,2,0:T(8,128)}, u32[]{:S(2)}) copy-start(s32[1,48,32]{1,2,0:T(8,128)} %param.13) | copy-start | bytes 18436
  25.7 0.7 %copy-start.2 = (s32[1,1,48]{2,1,0:T(1,128)S(1)}, s32[1,1,48]{2,1,0:T(1,128)}, u32[]{:S(2)}) copy-start(s32[1,1,48]{2,1,0:T(1,128)} %param.10) | copy-start | bytes 580
  37.3 7.5 %collective-permute-start.7 = (f32[3,48,128]{2,1,0:T(8,128)S(1)}, f32[3,48,128]{2,1,0:T(8,128)S(1)}, u32[]{:S(2)}, u32[]{:S(2)}) collective-permute-start(f32[3,48,128]{2,1,0:T(8,128)S(1)} %get-tuple-element.26), channel_id=1, source_target_pairs={{0,16},{1,17},{2,18},{3,19},{4,20},{5,21},{6,22},{7,23},{8,24},{9,... | collective-permute-start | bytes 221192 | tf_op jit(solution)/shard_map/ppermute | solution.py:416
  42.3 3.7 %collective-permute-start.8 = (f32[3,48,128]{2,1,0:T(8,128)S(1)}, f32[3,48,128]{2,1,0:T(8,128)S(1)}, u32[]{:S(2)}, u32[]{:S(2)}) collective-permute-start(f32[3,48,128]{2,1,0:T(8,128)S(1)} %get-tuple-element.27), channel_id=1, source_target_pairs={{0,24},{1,25},{2,26},{3,27},{4,28},{5,29},{6,30},{7,31},{8,0},{9,1... | collective-permute-start | bytes 221192 | tf_op jit(solution)/shard_map/ppermute | solution.py:416
  43.1 4.4 %collective-permute-start.9 = (f32[3,48,128]{2,1,0:T(8,128)S(1)}, f32[3,48,128]{2,1,0:T(8,128)S(1)}, u32[]{:S(2)}, u32[]{:S(2)}) collective-permute-start(f32[3,48,128]{2,1,0:T(8,128)S(1)} %get-tuple-element.28), channel_id=1, source_target_pairs={{0,8},{1,9},{2,10},{3,11},{4,12},{5,13},{6,14},{7,15},{8,16},{9,17... | collective-permute-start | bytes 221192 | tf_op jit(solution)/shard_map/ppermute | solution.py:416

commit v13 on v12

--- a/solution.py
+++ b/solution.py
@@ -55,7 +55,7 @@
     near = near_ref[...]
     off = (near >= NB).astype(I32) + (near >= 2 * NB).astype(I32)
     dev = (dest_ref[...] + off - 1) & (NY * NZ - 1)
-    code = (dev >> 3) * 512 + (dev & (NZ - 1)) * 64 + (near - off * NB)
+    code = (dev >> 3) * 512 + ((NZ - 1) - (dev & (NZ - 1))) * 64 + (near - off * NB)
     gap = jnp.zeros((4, 64 - NB), I32)
     info = jnp.concatenate([code, gap, jnp.broadcast_to(counts, (4, NB)), gap], axis=1)
     lane = lax.broadcasted_iota(I32, (NB, PL), 1)
@@ -365,7 +365,7 @@
             for v in (pos, masses[0], cnt, dest_ids, near_list[0].T, cell_centers, cell_mass[None])
         ]
     )
-    z_rows = [[NZ * y + z for z in range(NZ)] for y in range(NY)]
+    z_rows = [[NZ * y + NZ - 1 - z for z in range(NZ)] for y in range(NY)]
     window = lax.all_to_all(src, "space", 0, 0, axis_index_groups=z_rows, tiled=True)
     tgts = [tgt] + [lax.ppermute(tgt, "space", along_y(k)) for k in (1, -1, 2)]
     pair = jnp.stack([cells, lax.ppermute(cells, "slab", [(i, i ^ 1) for i in range(2 * NX)])])

time: 48.8 us -> 46.6 us (0.955)
  the two profiles are of different devices: /device:TPU:1 before, /device:TPU:32 now
where the time goes in v13:
time: 46.6 us; the launch traced here: 45.9 us
  starting transfers between devices  24.1 us (52%)
  Pallas kernels  13.6 us (29%)
  waiting for transfers between devices  7.46 us (16%)
  local copies, waits for them, and re-layouts  0.66 us (1%)
    pallas_call x2, Pallas kernels, near(): call(functools.partial(near_kernel, first), outs, [vspec()] * len(arrays)...  8.92 us
    all_to_all x1, starting transfers between devices, per_device(): lax.all_to_all(src, 'space', 0, 0, axis_index_groups=z_rows, tiled=True)  8.89 us
    ppermute x3, starting transfers between devices, per_device(): tgts = [tgt] + [lax.ppermute(tgt, 'space', along_y(k)) for k in (1, -1, 2)]  5.22 us
    ppermute x3, starting transfers between devices, per_device(): lax.ppermute(pair, 'slab', along_x(k))  5.14 us
    ppermute x3, starting transfers between devices, per_device(): lax.ppermute(sent[i], 'space', along_y(-k))  4.86 us
    ppermute x3, waiting for transfers between devices, per_device(): lax.ppermute(pair, 'slab', along_x(k))  4.59 us
    pallas_call x1, Pallas kernels, per_device(): call(pack_kernel, (((NZ, TILES + 1, 4, PL), F32), ((NB + 1, 4, PL), F32),...  2.12 us
    ppermute x3, waiting for transfers between devices, per_device(): lax.ppermute(sent[i], 'space', along_y(-k))  1.66 us
  transfers between devices with their start and end apart: 11, of which 4 were waited for; matrix products, arithmetic and copies ran while one was open for 0% of the time, Pallas kernels for 9%

profile of v13, /device:TPU:32, one launch (start us, length us, event | category | flops | bytes accessed | tf_op | source)
XLA Modules:
  0.0 45.9 jit_solution(14196827840214993606)
XLA Ops:
  0.0 2.1 %pack.1 = (f32[8,37,4,128]{3,2,1,0:T(4,128)}, f32[49,4,128]{2,1,0:T(4,128)S(1)}, f32[16,4,128]{2,1,0:T(4,128)S(1)}) custom-call(f32[3,48,128]{2,1,0:T(8,128)} %bitcast.22, f32[48,128]{1,0:T(8,128)} %bitcast.30, s32[1,48]{1,0:T(1,128)} %bitcast.26, s32[1,48]{1,0:T(1,128)} %refs_3_.1, s32[4,48]{1,0:T(4,128)} %bitcast.32, f32[3,2048]{1,0:T(4,128)} %refs_5_.1, ...), custom_call_target="tpu_custom_call" | custom-call | tf_op jit(solution)/shard_map/pack/pallas_call | solution.py:343
  2.1 8.9 %all-to-all-start = ((f32[8,37,4,128]{3,2,1,0:T(4,128)}), f32[8,37,4,128]{3,2,1,0:T(4,128)S(1)}, u32[]{:S(2)}, u32[]{:S(2)}) async-start(f32[8,37,4,128]{3,2,1,0:T(4,128)} %get-tuple-element.24), calls=%async_computation | async-start | bytes 1212416 | tf_op jit(solution)/shard_map/all_to_all | solution.py:369
  11.0 0.0 collective-permute-start.3
  11.0 1.2 %collective-permute-done.3 = f32[16,4,128]{2,1,0:T(4,128)S(1)} collective-permute-done((f32[16,4,128]{2,1,0:T(4,128)S(1)}, f32[16,4,128]{2,1,0:T(4,128)S(1)}, u32[]{:S(2)}, u32[]{:S(2)}) %collective-permute-start.3) | collective-permute-done | bytes 32800 | tf_op jit(solution)/shard_map/ppermute | solution.py:371
  12.2 3.1 %collective-permute-start.6 = (f32[2,16,4,128]{3,2,1,0:T(4,128)S(1)}, f32[2,16,4,128]{3,2,1,0:T(4,128)S(1)}, u32[]{:S(2)}, u32[]{:S(2)}) collective-permute-start(f32[2,16,4,128]{3,2,1,0:T(4,128)S(1)} %pad_maximum_fusion.c0), channel_id=1, source_target_pairs={{0,128},{32,160},{64,192},{96,224},{128,0},{160,32},{192,64},{224,... | collective-permute-start | bytes 196616 | tf_op jit(solution)/shard_map/ppermute | solution.py:372
  15.4 3.2 %collective-permute-start.2 = (f32[49,4,128]{2,1,0:T(4,128)S(1)}, f32[49,4,128]{2,1,0:T(4,128)S(1)}, u32[]{:S(2)}, u32[]{:S(2)}) collective-permute-start(f32[49,4,128]{2,1,0:T(4,128)S(1)} %get-tuple-element.17.t0), channel_id=1, source_target_pairs={{0,16},{1,17},{2,18},{3,19},{4,20},{5,21},{6,22},{7,23},{8,24},{9,... | collective-permute-start | bytes 301064 | tf_op jit(solution)/shard_map/ppermute | solution.py:370
  18.6 1.1 %collective-permute-start.1 = (f32[49,4,128]{2,1,0:T(4,128)S(1)}, f32[49,4,128]{2,1,0:T(4,128)S(1)}, u32[]{:S(2)}, u32[]{:S(2)}) collective-permute-start(f32[49,4,128]{2,1,0:T(4,128)S(1)} %get-tuple-element.17.t0), channel_id=1, source_target_pairs={{0,24},{1,25},{2,26},{3,27},{4,28},{5,29},{6,30},{7,31},{8,0},{9,1... | collective-permute-start | bytes 301064 | tf_op jit(solution)/shard_map/ppermute | solution.py:370
  19.6 1.0 %collective-permute-start = (f32[49,4,128]{2,1,0:T(4,128)S(1)}, f32[49,4,128]{2,1,0:T(4,128)S(1)}, u32[]{:S(2)}, u32[]{:S(2)}) collective-permute-start(f32[49,4,128]{2,1,0:T(4,128)S(1)} %get-tuple-element.17.t0), channel_id=1, source_target_pairs={{0,8},{1,9},{2,10},{3,11},{4,12},{5,13},{6,14},{7,15},{8,16},{9,17... | collective-permute-start | bytes 301064 | tf_op jit(solution)/shard_map/ppermute | solution.py:370
  20.6 1.1 %collective-permute-start.5 = (f32[2,16,4,128]{3,2,1,0:T(4,128)S(1)}, f32[2,16,4,128]{3,2,1,0:T(4,128)S(1)}, u32[]{:S(2)}, u32[]{:S(2)}) collective-permute-start(f32[2,16,4,128]{3,2,1,0:T(4,128)S(1)} %pad_maximum_fusion.c0), channel_id=1, source_target_pairs={{0,192},{32,224},{64,0},{96,32},{128,64},{160,96},{192,128},{224,1... | collective-permute-start | bytes 196616 | tf_op jit(solution)/shard_map/ppermute | solution.py:372
  21.7 0.9 %collective-permute-start.4 = (f32[2,16,4,128]{3,2,1,0:T(4,128)S(1)}, f32[2,16,4,128]{3,2,1,0:T(4,128)S(1)}, u32[]{:S(2)}, u32[]{:S(2)}) collective-permute-start(f32[2,16,4,128]{3,2,1,0:T(4,128)S(1)} %pad_maximum_fusion.c0), channel_id=1, source_target_pairs={{0,64},{32,96},{64,128},{96,160},{128,192},{160,224},{192,0},{224,... | collective-permute-start | bytes 196616 | tf_op jit(solution)/shard_map/ppermute | solution.py:372
  22.6 2.2 %collective-permute-done.5.c2 = f32[2,16,4,128]{3,2,1,0:T(4,128)S(1)} collective-permute-done((f32[2,16,4,128]{3,2,1,0:T(4,128)S(1)}, f32[2,16,4,128]{3,2,1,0:T(4,128)S(1)}, u32[]{:S(2)}, u32[]{:S(2)}) %collective-permute-start.5) | collective-permute-done | bytes 65568 | tf_op jit(solution)/shard_map/ppermute | solution.py:372
  24.8 2.4 %collective-permute-done.4.c1 = f32[2,16,4,128]{3,2,1,0:T(4,128)S(1)} collective-permute-done((f32[2,16,4,128]{3,2,1,0:T(4,128)S(1)}, f32[2,16,4,128]{3,2,1,0:T(4,128)S(1)}, u32[]{:S(2)}, u32[]{:S(2)}) %collective-permute-start.4) | collective-permute-done | bytes 65568 | tf_op jit(solution)/shard_map/ppermute | solution.py:372
  27.2 0.6 %copy-done.2 = s32[1,1,48]{2,1,0:T(1,128)S(1)} copy-done((s32[1,1,48]{2,1,0:T(1,128)S(1)}, s32[1,1,48]{2,1,0:T(1,128)}, u32[]{:S(2)}) %copy-start.2) | copy-done | bytes 216
  27.9 1.4 %far.1.far_ref = f32[3,48,128]{2,1,0:T(8,128)S(1)} custom-call(s32[1]{0:T(128)} %bitcast.8.place_ref, f32[3,48,128]{2,1,0:T(8,128)S(1)} %bitcast.23, s32[1,48]{1,0:T(1,128)S(1)} %bitcast.27, s32[32,48]{1,0:T(8,128)S(1)} %bitcast.25, f32[2,16,4,128]{3,2,1,0:T(4,128)S(1)} %pad_maximum_fusion.c0, f32[2,16,4,128]{3,2,1,0:T(4,128)S(1)} %collective-permute-done.4.c1, ...), custom_call_target="tpu_custom_call" | custom-call | tf_op jit(solution)/shard_map/far/pallas_call | solution.py:383
  29.3 0.0 collective-permute-done.1.t2
  29.3 0.0 collective-permute-done.t1
  29.3 0.4 prep.1
  29.7 6.5 %near.2 = (f32[3,48,128]{2,1,0:T(8,128)S(1)}, f32[3,48,128]{2,1,0:T(8,128)S(1)}, f32[3,48,128]{2,1,0:T(8,128)S(1)}, f32[48,4,128]{2,1,0:T(4,128)S(1)}) custom-call(s32[16,256]{1,0:T(8,128)S(1)} %get-tuple-element.22.refs_0_, f32[192,4,128]{2,1,0:T(4,128)S(1)} %get-tuple-element.23.refs_1_, f32[296,4,128]{2,1,0:T(4,128)S(1)} %bitcast.20), custom_call_target="tpu_custom_call" | custom-call | tf_op jit(solution)/shard_map/near/pallas_call | solution.py:399
  36.2 2.8 %collective-permute-start.7 = (f32[3,48,128]{2,1,0:T(8,128)S(1)}, f32[3,48,128]{2,1,0:T(8,128)S(1)}, u32[]{:S(2)}, u32[]{:S(2)}) collective-permute-start(f32[3,48,128]{2,1,0:T(8,128)S(1)} %get-tuple-element.26), channel_id=1, source_target_pairs={{0,16},{1,17},{2,18},{3,19},{4,20},{5,21},{6,22},{7,23},{8,24},{9,... | collective-permute-start | bytes 221192 | tf_op jit(solution)/shard_map/ppermute | solution.py:416
  39.0 0.6 %collective-permute-start.8 = (f32[3,48,128]{2,1,0:T(8,128)S(1)}, f32[3,48,128]{2,1,0:T(8,128)S(1)}, u32[]{:S(2)}, u32[]{:S(2)}) collective-permute-start(f32[3,48,128]{2,1,0:T(8,128)S(1)} %get-tuple-element.27), channel_id=1, source_target_pairs={{0,24},{1,25},{2,26},{3,27},{4,28},{5,29},{6,30},{7,31},{8,0},{9,1... | collective-permute-start | bytes 221192 | tf_op jit(solution)/shard_map/ppermute | solution.py:416
  39.6 1.4 %collective-permute-start.9 = (f32[3,48,128]{2,1,0:T(8,128)S(1)}, f32[3,48,128]{2,1,0:T(8,128)S(1)}, u32[]{:S(2)}, u32[]{:S(2)}) collective-permute-start(f32[3,48,128]{2,1,0:T(8,128)S(1)} %get-tuple-element.28), channel_id=1, source_target_pairs={{0,8},{1,9},{2,10},{3,11},{4,12},{5,13},{6,14},{7,15},{8,16},{9,17... | collective-permute-start | bytes 221192 | tf_op jit(solution)/shard_map/ppermute | solution.py:416
  41.0 2.5 %near.3.p0 = f32[3,48,128]{2,1,0:T(8,128)S(1)} custom-call(s32[16,256]{1,0:T(8,128)S(1)} %get-tuple-element.22.refs_0_, f32[192,4,128]{2,1,0:T(4,128)S(1)} %get-tuple-element.23.refs_1_, f32[296,4,128]{2,1,0:T(4,128)S(1)} %bitcast.21, f32[48,4,128]{2,1,0:T(4,128)S(1)} %get-tuple-element.25.refs_3_), custom_call_target="tpu_custom_call" | custom-call | tf_op jit(solution)/shard_map/near/pallas_call | solution.py:399
  43.5 1.7 %collective-permute-done.9.p3 = f32[3,48,128]{2,1,0:T(8,128)S(1)} collective-permute-done((f32[3,48,128]{2,1,0:T(8,128)S(1)}, f32[3,48,128]{2,1,0:T(8,128)S(1)}, u32[]{:S(2)}, u32[]{:S(2)}) %collective-permute-start.9) | collective-permute-done | bytes 73760 | tf_op jit(solution)/shard_map/ppermute | solution.py:416
  45.2 0.7 %final.1 = f32[3,48,128]{2,1,0:T(8,128)} custom-call(s32[1,48]{1,0:T(1,128)S(1)} %bitcast.28, f32[3,48,128]{2,1,0:T(8,128)S(1)} %far.1.far_ref, f32[3,48,128]{2,1,0:T(8,128)S(1)} %near.3.p0, f32[3,48,128]{2,1,0:T(8,128)S(1)} %collective-permute-done.7.p1, f32[3,48,128]{2,1,0:T(8,128)S(1)} %collective-permute-done.8.p2, ...), custom_call_target="tpu_custom_call" | custom-call | tf_op jit(solution)/shard_map/final/pallas_call | solution.py:418
  (11 shorter events, 0.0 us)
Async XLA Ops:
  2.1 27.6 %all-to-all-start = ((f32[8,37,4,128]{3,2,1,0:T(4,128)}), f32[8,37,4,128]{3,2,1,0:T(4,128)S(1)}, u32[]{:S(2)}, u32[]{:S(2)}) async-start(f32[8,37,4,128]{3,2,1,0:T(4,128)} %get-tuple-element.24), calls=%async_computation | async-start | bytes 1212416 | tf_op jit(solution)/shard_map/all_to_all | solution.py:369
  11.0 1.2 %collective-permute-start.3 = (f32[16,4,128]{2,1,0:T(4,128)S(1)}, f32[16,4,128]{2,1,0:T(4,128)S(1)}, u32[]{:S(2)}, u32[]{:S(2)}) collective-permute-start(f32[16,4,128]{2,1,0:T(4,128)S(1)} %get-tuple-element.20), channel_id=1, source_target_pairs={{0,32},{32,0},{64,96},{96,64},{128,160},{160,128},{192,224},{224,1... | collective-permute-start | bytes 98312 | tf_op jit(solution)/shard_map/ppermute | solution.py:371
  12.2 15.0 %copy-start = (f32[1,48,3,128]{3,1,2,0:T(8,128)S(1)}, f32[1,48,3,128]{3,1,2,0:T(8,128)}, u32[]{:S(2)}) copy-start(f32[1,48,3,128]{3,1,2,0:T(8,128)} %param.8) | copy-start | bytes 221188
  12.2 9.5 %collective-permute-start.6 = (f32[2,16,4,128]{3,2,1,0:T(4,128)S(1)}, f32[2,16,4,128]{3,2,1,0:T(4,128)S(1)}, u32[]{:S(2)}, u32[]{:S(2)}) collective-permute-start(f32[2,16,4,128]{3,2,1,0:T(4,128)S(1)} %pad_maximum_fusion.c0), channel_id=1, source_target_pairs={{0,128},{32,160},{64,192},{96,224},{128,0},{160,32},{192,64},{224,... | collective-permute-start | bytes 196616 | tf_op jit(solution)/shard_map/ppermute | solution.py:372
  15.4 13.9 %collective-permute-start.2 = (f32[49,4,128]{2,1,0:T(4,128)S(1)}, f32[49,4,128]{2,1,0:T(4,128)S(1)}, u32[]{:S(2)}, u32[]{:S(2)}) collective-permute-start(f32[49,4,128]{2,1,0:T(4,128)S(1)} %get-tuple-element.17.t0), channel_id=1, source_target_pairs={{0,16},{1,17},{2,18},{3,19},{4,20},{5,21},{6,22},{7,23},{8,24},{9,... | collective-permute-start | bytes 301064 | tf_op jit(solution)/shard_map/ppermute | solution.py:370
  18.6 10.7 %collective-permute-start.1 = (f32[49,4,128]{2,1,0:T(4,128)S(1)}, f32[49,4,128]{2,1,0:T(4,128)S(1)}, u32[]{:S(2)}, u32[]{:S(2)}) collective-permute-start(f32[49,4,128]{2,1,0:T(4,128)S(1)} %get-tuple-element.17.t0), channel_id=1, source_target_pairs={{0,24},{1,25},{2,26},{3,27},{4,28},{5,29},{6,30},{7,31},{8,0},{9,1... | collective-permute-start | bytes 301064 | tf_op jit(solution)/shard_map/ppermute | solution.py:370
  19.6 9.7 %collective-permute-start = (f32[49,4,128]{2,1,0:T(4,128)S(1)}, f32[49,4,128]{2,1,0:T(4,128)S(1)}, u32[]{:S(2)}, u32[]{:S(2)}) collective-permute-start(f32[49,4,128]{2,1,0:T(4,128)S(1)} %get-tuple-element.17.t0), channel_id=1, source_target_pairs={{0,8},{1,9},{2,10},{3,11},{4,12},{5,13},{6,14},{7,15},{8,16},{9,17... | collective-permute-start | bytes 301064 | tf_op jit(solution)/shard_map/ppermute | solution.py:370
  20.6 4.3 %collective-permute-start.5 = (f32[2,16,4,128]{3,2,1,0:T(4,128)S(1)}, f32[2,16,4,128]{3,2,1,0:T(4,128)S(1)}, u32[]{:S(2)}, u32[]{:S(2)}) collective-permute-start(f32[2,16,4,128]{3,2,1,0:T(4,128)S(1)} %pad_maximum_fusion.c0), channel_id=1, source_target_pairs={{0,192},{32,224},{64,0},{96,32},{128,64},{160,96},{192,128},{224,1... | collective-permute-start | bytes 196616 | tf_op jit(solution)/shard_map/ppermute | solution.py:372
  21.7 5.5 %collective-permute-start.4 = (f32[2,16,4,128]{3,2,1,0:T(4,128)S(1)}, f32[2,16,4,128]{3,2,1,0:T(4,128)S(1)}, u32[]{:S(2)}, u32[]{:S(2)}) collective-permute-start(f32[2,16,4,128]{3,2,1,0:T(4,128)S(1)} %pad_maximum_fusion.c0), channel_id=1, source_target_pairs={{0,64},{32,96},{64,128},{96,160},{128,192},{160,224},{192,0},{224,... | collective-permute-start | bytes 196616 | tf_op jit(solution)/shard_map/ppermute | solution.py:372
  22.6 4.6 %copy-start.1 = (s32[1,48,32]{1,2,0:T(8,128)S(1)}, s32[1,48,32]{1,2,0:T(8,128)}, u32[]{:S(2)}) copy-start(s32[1,48,32]{1,2,0:T(8,128)} %param.13) | copy-start | bytes 18436
  27.2 0.7 %copy-start.2 = (s32[1,1,48]{2,1,0:T(1,128)S(1)}, s32[1,1,48]{2,1,0:T(1,128)}, u32[]{:S(2)}) copy-start(s32[1,1,48]{2,1,0:T(1,128)} %param.10) | copy-start | bytes 580
  36.2 7.3 %collective-permute-start.7 = (f32[3,48,128]{2,1,0:T(8,128)S(1)}, f32[3,48,128]{2,1,0:T(8,128)S(1)}, u32[]{:S(2)}, u32[]{:S(2)}) collective-permute-start(f32[3,48,128]{2,1,0:T(8,128)S(1)} %get-tuple-element.26), channel_id=1, source_target_pairs={{0,16},{1,17},{2,18},{3,19},{4,20},{5,21},{6,22},{7,23},{8,24},{9,... | collective-permute-start | bytes 221192 | tf_op jit(solution)/shard_map/ppermute | solution.py:416
  39.0 4.5 %collective-permute-start.8 = (f32[3,48,128]{2,1,0:T(8,128)S(1)}, f32[3,48,128]{2,1,0:T(8,128)S(1)}, u32[]{:S(2)}, u32[]{:S(2)}) collective-permute-start(f32[3,48,128]{2,1,0:T(8,128)S(1)} %get-tuple-element.27), channel_id=1, source_target_pairs={{0,24},{1,25},{2,26},{3,27},{4,28},{5,29},{6,30},{7,31},{8,0},{9,1... | collective-permute-start | bytes 221192 | tf_op jit(solution)/shard_map/ppermute | solution.py:416
  39.6 5.6 %collective-permute-start.9 = (f32[3,48,128]{2,1,0:T(8,128)S(1)}, f32[3,48,128]{2,1,0:T(8,128)S(1)}, u32[]{:S(2)}, u32[]{:S(2)}) collective-permute-start(f32[3,48,128]{2,1,0:T(8,128)S(1)} %get-tuple-element.28), channel_id=1, source_target_pairs={{0,8},{1,9},{2,10},{3,11},{4,12},{5,13},{6,14},{7,15},{8,16},{9,17... | collective-permute-start | bytes 221192 | tf_op jit(solution)/shard_map/ppermute | solution.py:416

commit v14 on v13

--- a/solution.py
+++ b/solution.py
@@ -367,9 +367,11 @@
     )
     z_rows = [[NZ * y + NZ - 1 - z for z in range(NZ)] for y in range(NY)]
     window = lax.all_to_all(src, "space", 0, 0, axis_index_groups=z_rows, tiled=True)
-    tgts = [tgt] + [lax.ppermute(tgt, "space", along_y(k)) for k in (1, -1, 2)]
+    tgts = [tgt] + [lax.ppermute(tgt, "space", along_y(k)) for k in (1, -1)]
+    tgts.append(lax.ppermute(tgts[1], "space", along_y(1)))
     pair = jnp.stack([cells, lax.ppermute(cells, "slab", [(i, i ^ 1) for i in range(2 * NX)])])
-    pairs = [pair] + [lax.ppermute(pair, "slab", along_x(k)) for k in (1, -1, 2)]
+    pairs = [pair] + [lax.ppermute(pair, "slab", along_x(k)) for k in (1, -1)]
+    pairs.append(lax.ppermute(pairs[1], "slab", along_x(1)))
     me = (lax.axis_index("space") // NZ).astype(I32).reshape(1)
     place = lax.axis_index("slab").astype(I32).reshape(1)
     tall, tab = call(
@@ -380,16 +382,7 @@
         "prep",
         8,
     )(me, *tgts)
-    (far,) = call(
-        far_kernel,
-        (((3, NB, PL), F32),),
-        [sspec()] + [vspec()] * 7,
-        [vspec()],
-        "far",
-        16,
-        [pltpu.VMEM((PL, PL), F32)],
-    )(place, pos, cnt, cell_list[0].T, *pairs)
-    tall, tab, far = lax.optimization_barrier((tall, tab, far))
+    tall, tab, *pairs = lax.optimization_barrier((tall, tab, *pairs))
     window = window.reshape(NZ * (TILES + 1), 4, PL)
 
     def near(first, *arrays):
@@ -414,6 +407,16 @@
 
     *sent, kept = near(True, tab, tall, window)
     back = [lax.ppermute(sent[i], "space", along_y(-k)) for i, k in ((2, 2), (0, 1), (1, -1))]
+    *pairs, kept, sent[0] = lax.optimization_barrier((*pairs, kept, sent[0]))
+    (far,) = call(
+        far_kernel,
+        (((3, NB, PL), F32),),
+        [sspec()] + [vspec()] * 7,
+        [vspec()],
+        "far",
+        16,
+        [pltpu.VMEM((PL, PL), F32)],
+    )(place, pos, cnt, cell_list[0].T, *pairs)
     (own,) = near(False, tab, tall, window, kept)
     (out,) = call(
         final_kernel,

time: 46.6 us -> 47.8 us (1.026)
  the two profiles are of different devices: /device:TPU:32 before, /device:TPU:38 now
where the time goes in v14:
time: 47.8 us; the launch traced here: 47.3 us
  starting transfers between devices  25.7 us (54%)
  Pallas kernels  13.7 us (29%)
  waiting for transfers between devices  7.06 us (15%)
  local copies, waits for them, and re-layouts  0.64 us (1%)
    pallas_call x2, Pallas kernels, near(): call(functools.partial(near_kernel, first), outs, [vspec()] * len(arrays)...  9.07 us
    all_to_all x1, starting transfers between devices, per_device(): lax.all_to_all(src, 'space', 0, 0, axis_index_groups=z_rows, tiled=True)  8.89 us
    ppermute x3, starting transfers between devices, per_device(): lax.ppermute(sent[i], 'space', along_y(-k))  8.54 us
    ppermute x2, starting transfers between devices, per_device(): tgts = [tgt] + [lax.ppermute(tgt, 'space', along_y(k)) for k in (1, -1)]  4.21 us
    all_to_all x1, waiting for transfers between devices, per_device(): lax.all_to_all(src, 'space', 0, 0, axis_index_groups=z_rows, tiled=True)  2.99 us
    ppermute x1, starting transfers between devices, per_device(): pairs.append(lax.ppermute(pairs[1], 'slab', along_x(1)))  2.41 us
    ppermute x1, waiting for transfers between devices, per_device(): tgts.append(lax.ppermute(tgts[1], 'space', along_y(1)))  2.3 us
    pallas_call x1, Pallas kernels, per_device(): call(pack_kernel, (((NZ, TILES + 1, 4, PL), F32), ((NB + 1, 4, PL), F32),...  2.12 us
  transfers between devices with their start and end apart: 11, of which 3 were waited for; matrix products, arithmetic and copies ran while one was open for 0% of the time, Pallas kernels for 9%

profile of v14, /device:TPU:38, one launch (start us, length us, event | category | flops | bytes accessed | tf_op | source)
XLA Modules:
  0.0 47.3 jit_solution(10672628434087307025)
XLA Ops:
  0.0 2.1 %pack.1 = (f32[8,37,4,128]{3,2,1,0:T(4,128)}, f32[49,4,128]{2,1,0:T(4,128)S(1)}, f32[16,4,128]{2,1,0:T(4,128)S(1)}) custom-call(f32[3,48,128]{2,1,0:T(8,128)} %bitcast.22, f32[48,128]{1,0:T(8,128)} %bitcast.30, s32[1,48]{1,0:T(1,128)} %bitcast.26, s32[1,48]{1,0:T(1,128)} %refs_3_.1, s32[4,48]{1,0:T(4,128)} %bitcast.32, f32[3,2048]{1,0:T(4,128)} %refs_5_.1, ...), custom_call_target="tpu_custom_call" | custom-call | tf_op jit(solution)/shard_map/pack/pallas_call | solution.py:343
  2.1 8.9 %all-to-all-start = ((f32[8,37,4,128]{3,2,1,0:T(4,128)}), f32[8,37,4,128]{3,2,1,0:T(4,128)S(1)}, u32[]{:S(2)}, u32[]{:S(2)}) async-start(f32[8,37,4,128]{3,2,1,0:T(4,128)} %get-tuple-element.35), calls=%async_computation | async-start | bytes 1212416 | tf_op jit(solution)/shard_map/all_to_all | solution.py:369
  11.0 0.0 collective-permute-start.3
  11.0 1.6 %collective-permute-start = (f32[49,4,128]{2,1,0:T(4,128)S(1)}, f32[49,4,128]{2,1,0:T(4,128)S(1)}, u32[]{:S(2)}, u32[]{:S(2)}) collective-permute-start(f32[49,4,128]{2,1,0:T(4,128)S(1)} %get-tuple-element.25.t0), channel_id=1, source_target_pairs={{0,8},{1,9},{2,10},{3,11},{4,12},{5,13},{6,14},{7,15},{8,16},{9,17... | collective-permute-start | bytes 301064 | tf_op jit(solution)/shard_map/ppermute | solution.py:370
  12.6 0.0 collective-permute-done.3
  12.6 0.6 %collective-permute-start.4 = (f32[2,16,4,128]{3,2,1,0:T(4,128)S(1)}, f32[2,16,4,128]{3,2,1,0:T(4,128)S(1)}, u32[]{:S(2)}, u32[]{:S(2)}) collective-permute-start(f32[2,16,4,128]{3,2,1,0:T(4,128)S(1)} %pad_maximum_fusion.c0), channel_id=1, source_target_pairs={{0,64},{32,96},{64,128},{96,160},{128,192},{160,224},{192,0},{224,... | collective-permute-start | bytes 196616 | tf_op jit(solution)/shard_map/ppermute | solution.py:373
  13.2 2.6 %collective-permute-start.1 = (f32[49,4,128]{2,1,0:T(4,128)S(1)}, f32[49,4,128]{2,1,0:T(4,128)S(1)}, u32[]{:S(2)}, u32[]{:S(2)}) collective-permute-start(f32[49,4,128]{2,1,0:T(4,128)S(1)} %get-tuple-element.25.t0), channel_id=1, source_target_pairs={{0,24},{1,25},{2,26},{3,27},{4,28},{5,29},{6,30},{7,31},{8,0},{9,1... | collective-permute-start | bytes 301064 | tf_op jit(solution)/shard_map/ppermute | solution.py:370
  15.8 1.7 %collective-permute-done.t1 = f32[49,4,128]{2,1,0:T(4,128)S(1)} collective-permute-done((f32[49,4,128]{2,1,0:T(4,128)S(1)}, f32[49,4,128]{2,1,0:T(4,128)S(1)}, u32[]{:S(2)}, u32[]{:S(2)}) %collective-permute-start) | collective-permute-done | bytes 100384 | tf_op jit(solution)/shard_map/ppermute | solution.py:370
  17.5 0.3 collective-permute-start.2
  17.9 0.8 %collective-permute-start.5 = (f32[2,16,4,128]{3,2,1,0:T(4,128)S(1)}, f32[2,16,4,128]{3,2,1,0:T(4,128)S(1)}, u32[]{:S(2)}, u32[]{:S(2)}) collective-permute-start(f32[2,16,4,128]{3,2,1,0:T(4,128)S(1)} %pad_maximum_fusion.c0), channel_id=1, source_target_pairs={{0,192},{32,224},{64,0},{96,32},{128,64},{160,96},{192,128},{224,1... | collective-permute-start | bytes 196616 | tf_op jit(solution)/shard_map/ppermute | solution.py:373
  18.7 2.4 %collective-permute-start.6 = (f32[2,16,4,128]{3,2,1,0:T(4,128)S(1)}, f32[2,16,4,128]{3,2,1,0:T(4,128)S(1)}, u32[]{:S(2)}, u32[]{:S(2)}) collective-permute-start(f32[2,16,4,128]{3,2,1,0:T(4,128)S(1)} %collective-permute-done.4.c1), channel_id=1, source_target_pairs={{0,64},{32,96},{64,128},{96,160},{128,192},{160,224},{192,0},{224,... | collective-permute-start | bytes 196616 | tf_op jit(solution)/shard_map/ppermute | solution.py:374
  21.1 0.0 collective-permute-done.1.t2
  21.1 2.3 %collective-permute-done.2.t3 = f32[49,4,128]{2,1,0:T(4,128)S(1)} collective-permute-done((f32[49,4,128]{2,1,0:T(4,128)S(1)}, f32[49,4,128]{2,1,0:T(4,128)S(1)}, u32[]{:S(2)}, u32[]{:S(2)}) %collective-permute-start.2) | collective-permute-done | bytes 100384 | tf_op jit(solution)/shard_map/ppermute | solution.py:371
  23.4 0.4 prep.1
  23.8 0.0 collective-permute-done.6.c3
  23.8 3.0 %all-to-all-done = f32[8,37,4,128]{3,2,1,0:T(4,128)S(1)} async-done(((f32[8,37,4,128]{3,2,1,0:T(4,128)}), f32[8,37,4,128]{3,2,1,0:T(4,128)S(1)}, u32[]{:S(2)}, u32[]{:S(2)}) %all-to-all-start) | async-done | bytes 606240 | tf_op jit(solution)/shard_map/all_to_all | solution.py:369
  26.8 6.4 %near.2 = (f32[3,48,128]{2,1,0:T(8,128)S(1)}, f32[3,48,128]{2,1,0:T(8,128)S(1)}, f32[3,48,128]{2,1,0:T(8,128)S(1)}, f32[48,4,128]{2,1,0:T(4,128)S(1)}) custom-call(s32[16,256]{1,0:T(8,128)S(1)} %get-tuple-element.33.refs_0_, f32[192,4,128]{2,1,0:T(4,128)S(1)} %get-tuple-element.34.refs_1_, f32[296,4,128]{2,1,0:T(4,128)S(1)} %bitcast.20), custom_call_target="tpu_custom_call" | custom-call | tf_op jit(solution)/shard_map/near/pallas_call | solution.py:392
  33.2 5.3 %collective-permute-start.7 = (f32[3,48,128]{2,1,0:T(8,128)S(1)}, f32[3,48,128]{2,1,0:T(8,128)S(1)}, u32[]{:S(2)}, u32[]{:S(2)}) collective-permute-start(f32[3,48,128]{2,1,0:T(8,128)S(1)} %get-tuple-element.43), channel_id=1, source_target_pairs={{0,16},{1,17},{2,18},{3,19},{4,20},{5,21},{6,22},{7,23},{8,24},{9,... | collective-permute-start | bytes 221192 | tf_op jit(solution)/shard_map/ppermute | solution.py:409
  38.5 3.2 %collective-permute-start.8 = (f32[3,48,128]{2,1,0:T(8,128)S(1)}, f32[3,48,128]{2,1,0:T(8,128)S(1)}, u32[]{:S(2)}, u32[]{:S(2)}) collective-permute-start(f32[3,48,128]{2,1,0:T(8,128)S(1)} %get-tuple-element.37), channel_id=1, source_target_pairs={{0,24},{1,25},{2,26},{3,27},{4,28},{5,29},{6,30},{7,31},{8,0},{9,1... | collective-permute-start | bytes 221192 | tf_op jit(solution)/shard_map/ppermute | solution.py:409
  41.8 2.6 %near.3.p0 = f32[3,48,128]{2,1,0:T(8,128)S(1)} custom-call(s32[16,256]{1,0:T(8,128)S(1)} %get-tuple-element.33.refs_0_, f32[192,4,128]{2,1,0:T(4,128)S(1)} %get-tuple-element.34.refs_1_, f32[296,4,128]{2,1,0:T(4,128)S(1)} %bitcast.21, f32[48,4,128]{2,1,0:T(4,128)S(1)} %get-tuple-element.42.refs_3_), custom_call_target="tpu_custom_call" | custom-call | tf_op jit(solution)/shard_map/near/pallas_call | solution.py:392
  44.4 0.0 copy-start.2
  44.5 0.6 %copy-done.2 = s32[1,1,48]{2,1,0:T(1,128)S(1)} copy-done((s32[1,1,48]{2,1,0:T(1,128)S(1)}, s32[1,1,48]{2,1,0:T(1,128)}, u32[]{:S(2)}) %copy-start.2) | copy-done | bytes 216
  45.1 1.4 %far.1.far_ref = f32[3,48,128]{2,1,0:T(8,128)S(1)} custom-call(s32[1]{0:T(128)} %bitcast.1.place_ref, f32[3,48,128]{2,1,0:T(8,128)S(1)} %bitcast.23, s32[1,48]{1,0:T(1,128)S(1)} %bitcast.27, s32[32,48]{1,0:T(8,128)S(1)} %bitcast.25, f32[2,16,4,128]{3,2,1,0:T(4,128)S(1)} %pad_maximum_fusion.c0, f32[2,16,4,128]{3,2,1,0:T(4,128)S(1)} %collective-permute-done.4.c1, ...), custom_call_target="tpu_custom_call" | custom-call | tf_op jit(solution)/shard_map/far/pallas_call | solution.py:411
  46.5 0.7 %final.1 = f32[3,48,128]{2,1,0:T(8,128)} custom-call(s32[1,48]{1,0:T(1,128)S(1)} %bitcast.28, f32[3,48,128]{2,1,0:T(8,128)S(1)} %far.1.far_ref, f32[3,48,128]{2,1,0:T(8,128)S(1)} %near.3.p0, f32[3,48,128]{2,1,0:T(8,128)S(1)} %collective-permute-done.7.p1, f32[3,48,128]{2,1,0:T(8,128)S(1)} %collective-permute-done.8.p2, ...), custom_call_target="tpu_custom_call" | custom-call | tf_op jit(solution)/shard_map/final/pallas_call | solution.py:421
  (11 shorter events, 0.0 us)
Async XLA Ops:
  2.1 24.7 %all-to-all-start = ((f32[8,37,4,128]{3,2,1,0:T(4,128)}), f32[8,37,4,128]{3,2,1,0:T(4,128)S(1)}, u32[]{:S(2)}, u32[]{:S(2)}) async-start(f32[8,37,4,128]{3,2,1,0:T(4,128)} %get-tuple-element.35), calls=%async_computation | async-start | bytes 1212416 | tf_op jit(solution)/shard_map/all_to_all | solution.py:369
  11.0 1.6 %collective-permute-start.3 = (f32[16,4,128]{2,1,0:T(4,128)S(1)}, f32[16,4,128]{2,1,0:T(4,128)S(1)}, u32[]{:S(2)}, u32[]{:S(2)}) collective-permute-start(f32[16,4,128]{2,1,0:T(4,128)S(1)} %get-tuple-element.28), channel_id=1, source_target_pairs={{0,32},{32,0},{64,96},{96,64},{128,160},{160,128},{192,224},{224,1... | collective-permute-start | bytes 98312 | tf_op jit(solution)/shard_map/ppermute | solution.py:372
  11.0 6.5 %collective-permute-start = (f32[49,4,128]{2,1,0:T(4,128)S(1)}, f32[49,4,128]{2,1,0:T(4,128)S(1)}, u32[]{:S(2)}, u32[]{:S(2)}) collective-permute-start(f32[49,4,128]{2,1,0:T(4,128)S(1)} %get-tuple-element.25.t0), channel_id=1, source_target_pairs={{0,8},{1,9},{2,10},{3,11},{4,12},{5,13},{6,14},{7,15},{8,16},{9,17... | collective-permute-start | bytes 301064 | tf_op jit(solution)/shard_map/ppermute | solution.py:370
  12.6 6.1 %collective-permute-start.4 = (f32[2,16,4,128]{3,2,1,0:T(4,128)S(1)}, f32[2,16,4,128]{3,2,1,0:T(4,128)S(1)}, u32[]{:S(2)}, u32[]{:S(2)}) collective-permute-start(f32[2,16,4,128]{3,2,1,0:T(4,128)S(1)} %pad_maximum_fusion.c0), channel_id=1, source_target_pairs={{0,64},{32,96},{64,128},{96,160},{128,192},{160,224},{192,0},{224,... | collective-permute-start | bytes 196616 | tf_op jit(solution)/shard_map/ppermute | solution.py:373
  13.2 7.9 %collective-permute-start.1 = (f32[49,4,128]{2,1,0:T(4,128)S(1)}, f32[49,4,128]{2,1,0:T(4,128)S(1)}, u32[]{:S(2)}, u32[]{:S(2)}) collective-permute-start(f32[49,4,128]{2,1,0:T(4,128)S(1)} %get-tuple-element.25.t0), channel_id=1, source_target_pairs={{0,24},{1,25},{2,26},{3,27},{4,28},{5,29},{6,30},{7,31},{8,0},{9,1... | collective-permute-start | bytes 301064 | tf_op jit(solution)/shard_map/ppermute | solution.py:370
  17.5 5.8 %collective-permute-start.2 = (f32[49,4,128]{2,1,0:T(4,128)S(1)}, f32[49,4,128]{2,1,0:T(4,128)S(1)}, u32[]{:S(2)}, u32[]{:S(2)}) collective-permute-start(f32[49,4,128]{2,1,0:T(4,128)S(1)} %collective-permute-done.t1), channel_id=1, source_target_pairs={{0,8},{1,9},{2,10},{3,11},{4,12},{5,13},{6,14},{7,15},{8,16},{9,17... | collective-permute-start | bytes 301064 | tf_op jit(solution)/shard_map/ppermute | solution.py:371
  17.9 5.9 %collective-permute-start.5 = (f32[2,16,4,128]{3,2,1,0:T(4,128)S(1)}, f32[2,16,4,128]{3,2,1,0:T(4,128)S(1)}, u32[]{:S(2)}, u32[]{:S(2)}) collective-permute-start(f32[2,16,4,128]{3,2,1,0:T(4,128)S(1)} %pad_maximum_fusion.c0), channel_id=1, source_target_pairs={{0,192},{32,224},{64,0},{96,32},{128,64},{160,96},{192,128},{224,1... | collective-permute-start | bytes 196616 | tf_op jit(solution)/shard_map/ppermute | solution.py:373
  18.7 5.1 %collective-permute-start.6 = (f32[2,16,4,128]{3,2,1,0:T(4,128)S(1)}, f32[2,16,4,128]{3,2,1,0:T(4,128)S(1)}, u32[]{:S(2)}, u32[]{:S(2)}) collective-permute-start(f32[2,16,4,128]{3,2,1,0:T(4,128)S(1)} %collective-permute-done.4.c1), channel_id=1, source_target_pairs={{0,64},{32,96},{64,128},{96,160},{128,192},{160,224},{192,0},{224,... | collective-permute-start | bytes 196616 | tf_op jit(solution)/shard_map/ppermute | solution.py:374
  33.2 13.3 %collective-permute-start.7 = (f32[3,48,128]{2,1,0:T(8,128)S(1)}, f32[3,48,128]{2,1,0:T(8,128)S(1)}, u32[]{:S(2)}, u32[]{:S(2)}) collective-permute-start(f32[3,48,128]{2,1,0:T(8,128)S(1)} %get-tuple-element.43), channel_id=1, source_target_pairs={{0,16},{1,17},{2,18},{3,19},{4,20},{5,21},{6,22},{7,23},{8,24},{9,... | collective-permute-start | bytes 221192 | tf_op jit(solution)/shard_map/ppermute | solution.py:409
  38.5 8.0 %collective-permute-start.9 = (f32[3,48,128]{2,1,0:T(8,128)S(1)}, f32[3,48,128]{2,1,0:T(8,128)S(1)}, u32[]{:S(2)}, u32[]{:S(2)}) collective-permute-start(f32[3,48,128]{2,1,0:T(8,128)S(1)} %get-tuple-element.44), channel_id=1, source_target_pairs={{0,8},{1,9},{2,10},{3,11},{4,12},{5,13},{6,14},{7,15},{8,16},{9,17... | collective-permute-start | bytes 221192 | tf_op jit(solution)/shard_map/ppermute | solution.py:409
  38.5 8.0 %collective-permute-start.8 = (f32[3,48,128]{2,1,0:T(8,128)S(1)}, f32[3,48,128]{2,1,0:T(8,128)S(1)}, u32[]{:S(2)}, u32[]{:S(2)}) collective-permute-start(f32[3,48,128]{2,1,0:T(8,128)S(1)} %get-tuple-element.37), channel_id=1, source_target_pairs={{0,24},{1,25},{2,26},{3,27},{4,28},{5,29},{6,30},{7,31},{8,0},{9,1... | collective-permute-start | bytes 221192 | tf_op jit(solution)/shard_map/ppermute | solution.py:409
  41.8 2.7 %copy-start = (f32[1,48,3,128]{3,1,2,0:T(8,128)S(1)}, f32[1,48,3,128]{3,1,2,0:T(8,128)}, u32[]{:S(2)}) copy-start(f32[1,48,3,128]{3,1,2,0:T(8,128)} %param.8) | copy-start | bytes 221188
  41.8 2.7 %copy-start.1 = (s32[1,48,32]{1,2,0:T(8,128)S(1)}, s32[1,48,32]{1,2,0:T(8,128)}, u32[]{:S(2)}) copy-start(s32[1,48,32]{1,2,0:T(8,128)} %param.13) | copy-start | bytes 18436
  44.4 0.7 %copy-start.2 = (s32[1,1,48]{2,1,0:T(1,128)S(1)}, s32[1,1,48]{2,1,0:T(1,128)}, u32[]{:S(2)}) copy-start(s32[1,1,48]{2,1,0:T(1,128)} %param.10) | copy-start | bytes 580

commit v15 on v13

--- a/solution.py
+++ b/solution.py
@@ -367,9 +367,11 @@
     )
     z_rows = [[NZ * y + NZ - 1 - z for z in range(NZ)] for y in range(NY)]
     window = lax.all_to_all(src, "space", 0, 0, axis_index_groups=z_rows, tiled=True)
-    tgts = [tgt] + [lax.ppermute(tgt, "space", along_y(k)) for k in (1, -1, 2)]
+    tgts = [tgt] + [lax.ppermute(tgt, "space", along_y(k)) for k in (1, -1)]
+    tgts.append(lax.ppermute(tgts[1], "space", along_y(1)))
     pair = jnp.stack([cells, lax.ppermute(cells, "slab", [(i, i ^ 1) for i in range(2 * NX)])])
-    pairs = [pair] + [lax.ppermute(pair, "slab", along_x(k)) for k in (1, -1, 2)]
+    pairs = [pair] + [lax.ppermute(pair, "slab", along_x(k)) for k in (1, -1)]
+    pairs.append(lax.ppermute(pairs[1], "slab", along_x(1)))
     me = (lax.axis_index("space") // NZ).astype(I32).reshape(1)
     place = lax.axis_index("slab").astype(I32).reshape(1)
     tall, tab = call(

time: 46.6 us -> 47.3 us (1.015)
  Pallas kernels: 13.6 us -> 14.3 us
  starting transfers between devices: 24.1 us -> 23.6 us
    ppermute x6, waiting for transfers between devices: 4.6 us -> 6.18 us  [the longest x1 3.57 us: per_device(): pairs.append(lax.ppermute(pairs[1], 'slab', along_x(1)))]
    ppermute x6, starting transfers between devices: 10.4 us -> 8.85 us  [the longest x2 4.33 us: per_device(): pairs = [pair] + [lax.ppermute(pair, 'slab', along_x(k)) for k in (1, -1)]]
    ppermute x1, waiting for transfers between devices: 1.2 us -> 0.01 us  [per_device(): lax.ppermute(cells, 'slab', [(i, i ^ 1) for i in range(2 * NX)])]
    ppermute x3, starting transfers between devices: 4.86 us -> 5.91 us  [per_device(): lax.ppermute(sent[i], 'space', along_y(-k))]
    pallas_call x2, Pallas kernels: 8.92 us -> 9.67 us  [near(): call(functools.partial(near_kernel, first), outs, [vspec()] * len(arrays)...]
  transfers between devices with their start and end apart: 11 -> 11, of which waited for: 4 -> 4; matrix products, arithmetic and copies ran while one was open for 0% -> 0% of each run, Pallas kernels for 9% -> 11%
where the time goes in v15:
time: 47.3 us; the launch traced here: 46.5 us
  starting transfers between devices  23.6 us (50%)
  Pallas kernels  14.3 us (30%)
  waiting for transfers between devices  7.74 us (16%)
  local copies, waits for them, and re-layouts  0.66 us (1%)
    pallas_call x2, Pallas kernels, near(): call(functools.partial(near_kernel, first), outs, [vspec()] * len(arrays)...  9.67 us
    all_to_all x1, starting transfers between devices, per_device(): lax.all_to_all(src, 'space', 0, 0, axis_index_groups=z_rows, tiled=True)  8.89 us
    ppermute x3, starting transfers between devices, per_device(): lax.ppermute(sent[i], 'space', along_y(-k))  5.91 us
    ppermute x2, starting transfers between devices, per_device(): pairs = [pair] + [lax.ppermute(pair, 'slab', along_x(k)) for k in (1, -1)]  4.33 us
    ppermute x2, starting transfers between devices, per_device(): tgts = [tgt] + [lax.ppermute(tgt, 'space', along_y(k)) for k in (1, -1)]  4.21 us
    ppermute x1, waiting for transfers between devices, per_device(): pairs.append(lax.ppermute(pairs[1], 'slab', along_x(1)))  3.57 us
    pallas_call x1, Pallas kernels, per_device(): call(pack_kernel, (((NZ, TILES + 1, 4, PL), F32), ((NB + 1, 4, PL), F32),...  2.12 us
    ppermute x2, waiting for transfers between devices, per_device(): pairs = [pair] + [lax.ppermute(pair, 'slab', along_x(k)) for k in (1, -1)]  1.89 us
  transfers between devices with their start and end apart: 11, of which 4 were waited for; matrix products, arithmetic and copies ran while one was open for 0% of the time, Pallas kernels for 11%

profile of v15, /device:TPU:32, one launch (start us, length us, event | category | flops | bytes accessed | tf_op | source)
XLA Modules:
  0.0 46.5 jit_solution(7747523385017119047)
XLA Ops:
  0.0 2.1 %pack.1 = (f32[8,37,4,128]{3,2,1,0:T(4,128)}, f32[49,4,128]{2,1,0:T(4,128)S(1)}, f32[16,4,128]{2,1,0:T(4,128)S(1)}) custom-call(f32[3,48,128]{2,1,0:T(8,128)} %bitcast.22, f32[48,128]{1,0:T(8,128)} %bitcast.30, s32[1,48]{1,0:T(1,128)} %bitcast.26, s32[1,48]{1,0:T(1,128)} %refs_3_.1, s32[4,48]{1,0:T(4,128)} %bitcast.32, f32[3,2048]{1,0:T(4,128)} %refs_5_.1, ...), custom_call_target="tpu_custom_call" | custom-call | tf_op jit(solution)/shard_map/pack/pallas_call | solution.py:343
  2.1 8.9 %all-to-all-start = ((f32[8,37,4,128]{3,2,1,0:T(4,128)}), f32[8,37,4,128]{3,2,1,0:T(4,128)S(1)}, u32[]{:S(2)}, u32[]{:S(2)}) async-start(f32[8,37,4,128]{3,2,1,0:T(4,128)} %get-tuple-element.24), calls=%async_computation | async-start | bytes 1212416 | tf_op jit(solution)/shard_map/all_to_all | solution.py:369
  11.0 0.0 collective-permute-start.3
  11.0 1.6 %collective-permute-start = (f32[49,4,128]{2,1,0:T(4,128)S(1)}, f32[49,4,128]{2,1,0:T(4,128)S(1)}, u32[]{:S(2)}, u32[]{:S(2)}) collective-permute-start(f32[49,4,128]{2,1,0:T(4,128)S(1)} %get-tuple-element.17.t0), channel_id=1, source_target_pairs={{0,8},{1,9},{2,10},{3,11},{4,12},{5,13},{6,14},{7,15},{8,16},{9,17... | collective-permute-start | bytes 301064 | tf_op jit(solution)/shard_map/ppermute | solution.py:370
  12.6 0.0 collective-permute-done.3
  12.6 1.6 %collective-permute-start.4 = (f32[2,16,4,128]{3,2,1,0:T(4,128)S(1)}, f32[2,16,4,128]{3,2,1,0:T(4,128)S(1)}, u32[]{:S(2)}, u32[]{:S(2)}) collective-permute-start(f32[2,16,4,128]{3,2,1,0:T(4,128)S(1)} %pad_maximum_fusion.c0), channel_id=1, source_target_pairs={{0,64},{32,96},{64,128},{96,160},{128,192},{160,224},{192,0},{224,... | collective-permute-start | bytes 196616 | tf_op jit(solution)/shard_map/ppermute | solution.py:373
  14.2 2.6 %collective-permute-start.1 = (f32[49,4,128]{2,1,0:T(4,128)S(1)}, f32[49,4,128]{2,1,0:T(4,128)S(1)}, u32[]{:S(2)}, u32[]{:S(2)}) collective-permute-start(f32[49,4,128]{2,1,0:T(4,128)S(1)} %get-tuple-element.17.t0), channel_id=1, source_target_pairs={{0,24},{1,25},{2,26},{3,27},{4,28},{5,29},{6,30},{7,31},{8,0},{9,1... | collective-permute-start | bytes 301064 | tf_op jit(solution)/shard_map/ppermute | solution.py:370
  16.8 0.7 %collective-permute-done.t1 = f32[49,4,128]{2,1,0:T(4,128)S(1)} collective-permute-done((f32[49,4,128]{2,1,0:T(4,128)S(1)}, f32[49,4,128]{2,1,0:T(4,128)S(1)}, u32[]{:S(2)}, u32[]{:S(2)}) %collective-permute-start) | collective-permute-done | bytes 100384 | tf_op jit(solution)/shard_map/ppermute | solution.py:370
  17.5 0.3 collective-permute-start.2
  17.9 2.8 %collective-permute-start.5 = (f32[2,16,4,128]{3,2,1,0:T(4,128)S(1)}, f32[2,16,4,128]{3,2,1,0:T(4,128)S(1)}, u32[]{:S(2)}, u32[]{:S(2)}) collective-permute-start(f32[2,16,4,128]{3,2,1,0:T(4,128)S(1)} %pad_maximum_fusion.c0), channel_id=1, source_target_pairs={{0,192},{32,224},{64,0},{96,32},{128,64},{160,96},{192,128},{224,1... | collective-permute-start | bytes 196616 | tf_op jit(solution)/shard_map/ppermute | solution.py:373
  20.6 0.0 collective-permute-done.4.c1
  20.6 0.0 collective-permute-start.6
  20.6 1.9 %collective-permute-done.5.c2 = f32[2,16,4,128]{3,2,1,0:T(4,128)S(1)} collective-permute-done((f32[2,16,4,128]{3,2,1,0:T(4,128)S(1)}, f32[2,16,4,128]{3,2,1,0:T(4,128)S(1)}, u32[]{:S(2)}, u32[]{:S(2)}) %collective-permute-start.5) | collective-permute-done | bytes 65568 | tf_op jit(solution)/shard_map/ppermute | solution.py:373
  22.5 3.6 %collective-permute-done.6.c3 = f32[2,16,4,128]{3,2,1,0:T(4,128)S(1)} collective-permute-done((f32[2,16,4,128]{3,2,1,0:T(4,128)S(1)}, f32[2,16,4,128]{3,2,1,0:T(4,128)S(1)}, u32[]{:S(2)}, u32[]{:S(2)}) %collective-permute-start.6) | collective-permute-done | bytes 65568 | tf_op jit(solution)/shard_map/ppermute | solution.py:374
  26.1 0.6 %copy-done.2 = s32[1,1,48]{2,1,0:T(1,128)S(1)} copy-done((s32[1,1,48]{2,1,0:T(1,128)S(1)}, s32[1,1,48]{2,1,0:T(1,128)}, u32[]{:S(2)}) %copy-start.2) | copy-done | bytes 216
  26.7 1.4 %far.1.far_ref = f32[3,48,128]{2,1,0:T(8,128)S(1)} custom-call(s32[1]{0:T(128)} %bitcast.8.place_ref, f32[3,48,128]{2,1,0:T(8,128)S(1)} %bitcast.23, s32[1,48]{1,0:T(1,128)S(1)} %bitcast.27, s32[32,48]{1,0:T(8,128)S(1)} %bitcast.25, f32[2,16,4,128]{3,2,1,0:T(4,128)S(1)} %pad_maximum_fusion.c0, f32[2,16,4,128]{3,2,1,0:T(4,128)S(1)} %collective-permute-done.4.c1, ...), custom_call_target="tpu_custom_call" | custom-call | tf_op jit(solution)/shard_map/far/pallas_call | solution.py:385
  28.2 0.4 prep.1
  28.6 6.5 %near.2 = (f32[3,48,128]{2,1,0:T(8,128)S(1)}, f32[3,48,128]{2,1,0:T(8,128)S(1)}, f32[3,48,128]{2,1,0:T(8,128)S(1)}, f32[48,4,128]{2,1,0:T(4,128)S(1)}) custom-call(s32[16,256]{1,0:T(8,128)S(1)} %get-tuple-element.22.refs_0_, f32[192,4,128]{2,1,0:T(4,128)S(1)} %get-tuple-element.23.refs_1_, f32[296,4,128]{2,1,0:T(4,128)S(1)} %bitcast.20), custom_call_target="tpu_custom_call" | custom-call | tf_op jit(solution)/shard_map/near/pallas_call | solution.py:401
  35.0 3.0 %collective-permute-start.7 = (f32[3,48,128]{2,1,0:T(8,128)S(1)}, f32[3,48,128]{2,1,0:T(8,128)S(1)}, u32[]{:S(2)}, u32[]{:S(2)}) collective-permute-start(f32[3,48,128]{2,1,0:T(8,128)S(1)} %get-tuple-element.26), channel_id=1, source_target_pairs={{0,16},{1,17},{2,18},{3,19},{4,20},{5,21},{6,22},{7,23},{8,24},{9,... | collective-permute-start | bytes 221192 | tf_op jit(solution)/shard_map/ppermute | solution.py:418
  38.0 2.1 %collective-permute-start.8 = (f32[3,48,128]{2,1,0:T(8,128)S(1)}, f32[3,48,128]{2,1,0:T(8,128)S(1)}, u32[]{:S(2)}, u32[]{:S(2)}) collective-permute-start(f32[3,48,128]{2,1,0:T(8,128)S(1)} %get-tuple-element.27), channel_id=1, source_target_pairs={{0,24},{1,25},{2,26},{3,27},{4,28},{5,29},{6,30},{7,31},{8,0},{9,1... | collective-permute-start | bytes 221192 | tf_op jit(solution)/shard_map/ppermute | solution.py:418
  40.2 0.8 %collective-permute-start.9 = (f32[3,48,128]{2,1,0:T(8,128)S(1)}, f32[3,48,128]{2,1,0:T(8,128)S(1)}, u32[]{:S(2)}, u32[]{:S(2)}) collective-permute-start(f32[3,48,128]{2,1,0:T(8,128)S(1)} %get-tuple-element.28), channel_id=1, source_target_pairs={{0,8},{1,9},{2,10},{3,11},{4,12},{5,13},{6,14},{7,15},{8,16},{9,17... | collective-permute-start | bytes 221192 | tf_op jit(solution)/shard_map/ppermute | solution.py:418
  40.9 3.2 %near.3.p0 = f32[3,48,128]{2,1,0:T(8,128)S(1)} custom-call(s32[16,256]{1,0:T(8,128)S(1)} %get-tuple-element.22.refs_0_, f32[192,4,128]{2,1,0:T(4,128)S(1)} %get-tuple-element.23.refs_1_, f32[296,4,128]{2,1,0:T(4,128)S(1)} %bitcast.21, f32[48,4,128]{2,1,0:T(4,128)S(1)} %get-tuple-element.25.refs_3_), custom_call_target="tpu_custom_call" | custom-call | tf_op jit(solution)/shard_map/near/pallas_call | solution.py:401
  44.2 1.6 %collective-permute-done.9.p3 = f32[3,48,128]{2,1,0:T(8,128)S(1)} collective-permute-done((f32[3,48,128]{2,1,0:T(8,128)S(1)}, f32[3,48,128]{2,1,0:T(8,128)S(1)}, u32[]{:S(2)}, u32[]{:S(2)}) %collective-permute-start.9) | collective-permute-done | bytes 73760 | tf_op jit(solution)/shard_map/ppermute | solution.py:418
  45.7 0.7 %final.1 = f32[3,48,128]{2,1,0:T(8,128)} custom-call(s32[1,48]{1,0:T(1,128)S(1)} %bitcast.28, f32[3,48,128]{2,1,0:T(8,128)S(1)} %far.1.far_ref, f32[3,48,128]{2,1,0:T(8,128)S(1)} %near.3.p0, f32[3,48,128]{2,1,0:T(8,128)S(1)} %collective-permute-done.7.p1, f32[3,48,128]{2,1,0:T(8,128)S(1)} %collective-permute-done.8.p2, ...), custom_call_target="tpu_custom_call" | custom-call | tf_op jit(solution)/shard_map/final/pallas_call | solution.py:420
  (11 shorter events, 0.0 us)
Async XLA Ops:
  2.1 26.4 %all-to-all-start = ((f32[8,37,4,128]{3,2,1,0:T(4,128)}), f32[8,37,4,128]{3,2,1,0:T(4,128)S(1)}, u32[]{:S(2)}, u32[]{:S(2)}) async-start(f32[8,37,4,128]{3,2,1,0:T(4,128)} %get-tuple-element.24), calls=%async_computation | async-start | bytes 1212416 | tf_op jit(solution)/shard_map/all_to_all | solution.py:369
  11.0 1.6 %collective-permute-start.3 = (f32[16,4,128]{2,1,0:T(4,128)S(1)}, f32[16,4,128]{2,1,0:T(4,128)S(1)}, u32[]{:S(2)}, u32[]{:S(2)}) collective-permute-start(f32[16,4,128]{2,1,0:T(4,128)S(1)} %get-tuple-element.20), channel_id=1, source_target_pairs={{0,32},{32,0},{64,96},{96,64},{128,160},{160,128},{192,224},{224,1... | collective-permute-start | bytes 98312 | tf_op jit(solution)/shard_map/ppermute | solution.py:372
  11.0 6.5 %collective-permute-start = (f32[49,4,128]{2,1,0:T(4,128)S(1)}, f32[49,4,128]{2,1,0:T(4,128)S(1)}, u32[]{:S(2)}, u32[]{:S(2)}) collective-permute-start(f32[49,4,128]{2,1,0:T(4,128)S(1)} %get-tuple-element.17.t0), channel_id=1, source_target_pairs={{0,8},{1,9},{2,10},{3,11},{4,12},{5,13},{6,14},{7,15},{8,16},{9,17... | collective-permute-start | bytes 301064 | tf_op jit(solution)/shard_map/ppermute | solution.py:370
  12.6 13.5 %copy-start = (f32[1,48,3,128]{3,1,2,0:T(8,128)S(1)}, f32[1,48,3,128]{3,1,2,0:T(8,128)}, u32[]{:S(2)}) copy-start(f32[1,48,3,128]{3,1,2,0:T(8,128)} %param.8) | copy-start | bytes 221188
  12.6 8.0 %collective-permute-start.4 = (f32[2,16,4,128]{3,2,1,0:T(4,128)S(1)}, f32[2,16,4,128]{3,2,1,0:T(4,128)S(1)}, u32[]{:S(2)}, u32[]{:S(2)}) collective-permute-start(f32[2,16,4,128]{3,2,1,0:T(4,128)S(1)} %pad_maximum_fusion.c0), channel_id=1, source_target_pairs={{0,64},{32,96},{64,128},{96,160},{128,192},{160,224},{192,0},{224,... | collective-permute-start | bytes 196616 | tf_op jit(solution)/shard_map/ppermute | solution.py:373
  14.2 14.0 %collective-permute-start.1 = (f32[49,4,128]{2,1,0:T(4,128)S(1)}, f32[49,4,128]{2,1,0:T(4,128)S(1)}, u32[]{:S(2)}, u32[]{:S(2)}) collective-permute-start(f32[49,4,128]{2,1,0:T(4,128)S(1)} %get-tuple-element.17.t0), channel_id=1, source_target_pairs={{0,24},{1,25},{2,26},{3,27},{4,28},{5,29},{6,30},{7,31},{8,0},{9,1... | collective-permute-start | bytes 301064 | tf_op jit(solution)/shard_map/ppermute | solution.py:370
  17.5 10.6 %collective-permute-start.2 = (f32[49,4,128]{2,1,0:T(4,128)S(1)}, f32[49,4,128]{2,1,0:T(4,128)S(1)}, u32[]{:S(2)}, u32[]{:S(2)}) collective-permute-start(f32[49,4,128]{2,1,0:T(4,128)S(1)} %collective-permute-done.t1), channel_id=1, source_target_pairs={{0,8},{1,9},{2,10},{3,11},{4,12},{5,13},{6,14},{7,15},{8,16},{9,17... | collective-permute-start | bytes 301064 | tf_op jit(solution)/shard_map/ppermute | solution.py:371
  17.9 4.7 %collective-permute-start.5 = (f32[2,16,4,128]{3,2,1,0:T(4,128)S(1)}, f32[2,16,4,128]{3,2,1,0:T(4,128)S(1)}, u32[]{:S(2)}, u32[]{:S(2)}) collective-permute-start(f32[2,16,4,128]{3,2,1,0:T(4,128)S(1)} %pad_maximum_fusion.c0), channel_id=1, source_target_pairs={{0,192},{32,224},{64,0},{96,32},{128,64},{160,96},{192,128},{224,1... | collective-permute-start | bytes 196616 | tf_op jit(solution)/shard_map/ppermute | solution.py:373
  20.6 5.5 %collective-permute-start.6 = (f32[2,16,4,128]{3,2,1,0:T(4,128)S(1)}, f32[2,16,4,128]{3,2,1,0:T(4,128)S(1)}, u32[]{:S(2)}, u32[]{:S(2)}) collective-permute-start(f32[2,16,4,128]{3,2,1,0:T(4,128)S(1)} %collective-permute-done.4.c1), channel_id=1, source_target_pairs={{0,64},{32,96},{64,128},{96,160},{128,192},{160,224},{192,0},{224,... | collective-permute-start | bytes 196616 | tf_op jit(solution)/shard_map/ppermute | solution.py:374
  20.6 5.5 %copy-start.1 = (s32[1,48,32]{1,2,0:T(8,128)S(1)}, s32[1,48,32]{1,2,0:T(8,128)}, u32[]{:S(2)}) copy-start(s32[1,48,32]{1,2,0:T(8,128)} %param.13) | copy-start | bytes 18436
  26.1 0.7 %copy-start.2 = (s32[1,1,48]{2,1,0:T(1,128)S(1)}, s32[1,1,48]{2,1,0:T(1,128)}, u32[]{:S(2)}) copy-start(s32[1,1,48]{2,1,0:T(1,128)} %param.10) | copy-start | bytes 580
  35.0 9.1 %collective-permute-start.7 = (f32[3,48,128]{2,1,0:T(8,128)S(1)}, f32[3,48,128]{2,1,0:T(8,128)S(1)}, u32[]{:S(2)}, u32[]{:S(2)}) collective-permute-start(f32[3,48,128]{2,1,0:T(8,128)S(1)} %get-tuple-element.26), channel_id=1, source_target_pairs={{0,16},{1,17},{2,18},{3,19},{4,20},{5,21},{6,22},{7,23},{8,24},{9,... | collective-permute-start | bytes 221192 | tf_op jit(solution)/shard_map/ppermute | solution.py:418
  38.0 6.2 %collective-permute-start.8 = (f32[3,48,128]{2,1,0:T(8,128)S(1)}, f32[3,48,128]{2,1,0:T(8,128)S(1)}, u32[]{:S(2)}, u32[]{:S(2)}) collective-permute-start(f32[3,48,128]{2,1,0:T(8,128)S(1)} %get-tuple-element.27), channel_id=1, source_target_pairs={{0,24},{1,25},{2,26},{3,27},{4,28},{5,29},{6,30},{7,31},{8,0},{9,1... | collective-permute-start | bytes 221192 | tf_op jit(solution)/shard_map/ppermute | solution.py:418
  40.2 5.6 %collective-permute-start.9 = (f32[3,48,128]{2,1,0:T(8,128)S(1)}, f32[3,48,128]{2,1,0:T(8,128)S(1)}, u32[]{:S(2)}, u32[]{:S(2)}) collective-permute-start(f32[3,48,128]{2,1,0:T(8,128)S(1)} %get-tuple-element.28), channel_id=1, source_target_pairs={{0,8},{1,9},{2,10},{3,11},{4,12},{5,13},{6,14},{7,15},{8,16},{9,17... | collective-permute-start | bytes 221192 | tf_op jit(solution)/shard_map/ppermute | solution.py:418

commit v16 on v14

--- a/solution.py
+++ b/solution.py
@@ -17,6 +17,7 @@
 SOFT = 0.01
 UNROLL = (18, 20)
 UNROLL_OWN = (12, 8)
+FULL_SLOTS = 54
 MIB = 1 << 20
 TILES = 36
 F32 = jnp.float32
@@ -294,7 +295,7 @@
         return (size + step - 1) // step * step
 
     n_full, n_half = sizes[0] + sizes[1], sizes[2] + sizes[3]
-    early_full = jnp.minimum(n_full, whole_steps(sizes[0], UNROLL[0]))
+    early_full = jnp.minimum(n_full, jnp.maximum(whole_steps(sizes[0], UNROLL[0]), FULL_SLOTS))
     early_half = jnp.minimum(n_half, whole_steps(sizes[2], UNROLL[1]))
     if first:
         run(jnp.int32(0), early_full, 4, UNROLL[0])

time: 47.8 us -> 47 us (0.983)
  the two profiles are of different devices: /device:TPU:38 before, /device:TPU:4 now
where the time goes in v16:
time: 47 us
  starting transfers between devices  23.7 us (50%)
  Pallas kernels  15.8 us (34%)
  waiting for transfers between devices  6.78 us (14%)
  local copies, waits for them, and re-layouts  0.64 us (1%)
    pallas_call x2, Pallas kernels, near(): call(functools.partial(near_kernel, first), outs, [vspec()] * len(arrays)...  11.1 us
    all_to_all x1, starting transfers between devices, per_device(): lax.all_to_all(src, 'space', 0, 0, axis_index_groups=z_rows, tiled=True)  9.35 us
    ppermute x3, starting transfers between devices, per_device(): lax.ppermute(sent[i], 'space', along_y(-k))  6.52 us
    ppermute x2, starting transfers between devices, per_device(): tgts = [tgt] + [lax.ppermute(tgt, 'space', along_y(k)) for k in (1, -1)]  4.22 us
    ppermute x1, waiting for transfers between devices, per_device(): tgts.append(lax.ppermute(tgts[1], 'space', along_y(1)))  3.51 us
    all_to_all x1, waiting for transfers between devices, per_device(): lax.all_to_all(src, 'space', 0, 0, axis_index_groups=z_rows, tiled=True)  2.22 us
    pallas_call x1, Pallas kernels, per_device(): call(pack_kernel, (((NZ, TILES + 1, 4, PL), F32), ((NB + 1, 4, PL), F32),...  2.12 us
    ppermute x2, starting transfers between devices, per_device(): pairs = [pair] + [lax.ppermute(pair, 'slab', along_x(k)) for k in (1, -1)]  1.81 us
  transfers between devices with their start and end apart: 11, of which 3 were waited for; matrix products, arithmetic and copies ran while one was open for 0% of the time, Pallas kernels for 9%

profile of v16, /device:TPU:4, one launch (start us, length us, event | category | flops | bytes accessed | tf_op | source)
XLA Modules:
  0.0 47.0 jit_solution(2631862671012650441)
XLA Ops:
  0.0 2.1 %pack.1 = (f32[8,37,4,128]{3,2,1,0:T(4,128)}, f32[49,4,128]{2,1,0:T(4,128)S(1)}, f32[16,4,128]{2,1,0:T(4,128)S(1)}) custom-call(f32[3,48,128]{2,1,0:T(8,128)} %bitcast.22, f32[48,128]{1,0:T(8,128)} %bitcast.30, s32[1,48]{1,0:T(1,128)} %bitcast.26, s32[1,48]{1,0:T(1,128)} %refs_3_.1, s32[4,48]{1,0:T(4,128)} %bitcast.32, f32[3,2048]{1,0:T(4,128)} %refs_5_.1, ...), custom_call_target="tpu_custom_call" | custom-call | tf_op jit(solution)/shard_map/pack/pallas_call | solution.py:344
  2.1 9.3 %all-to-all-start = ((f32[8,37,4,128]{3,2,1,0:T(4,128)}), f32[8,37,4,128]{3,2,1,0:T(4,128)S(1)}, u32[]{:S(2)}, u32[]{:S(2)}) async-start(f32[8,37,4,128]{3,2,1,0:T(4,128)} %get-tuple-element.35), calls=%async_computation | async-start | bytes 1212416 | tf_op jit(solution)/shard_map/all_to_all | solution.py:370
  11.5 0.0 collective-permute-start.3
  11.5 1.6 %collective-permute-start = (f32[49,4,128]{2,1,0:T(4,128)S(1)}, f32[49,4,128]{2,1,0:T(4,128)S(1)}, u32[]{:S(2)}, u32[]{:S(2)}) collective-permute-start(f32[49,4,128]{2,1,0:T(4,128)S(1)} %get-tuple-element.25.t0), channel_id=1, source_target_pairs={{0,8},{1,9},{2,10},{3,11},{4,12},{5,13},{6,14},{7,15},{8,16},{9,17... | collective-permute-start | bytes 301064 | tf_op jit(solution)/shard_map/ppermute | solution.py:371
  13.1 0.0 collective-permute-done.3
  13.1 1.3 %collective-permute-start.4 = (f32[2,16,4,128]{3,2,1,0:T(4,128)S(1)}, f32[2,16,4,128]{3,2,1,0:T(4,128)S(1)}, u32[]{:S(2)}, u32[]{:S(2)}) collective-permute-start(f32[2,16,4,128]{3,2,1,0:T(4,128)S(1)} %pad_maximum_fusion.c0), channel_id=1, source_target_pairs={{0,64},{32,96},{64,128},{96,160},{128,192},{160,224},{192,0},{224,... | collective-permute-start | bytes 196616 | tf_op jit(solution)/shard_map/ppermute | solution.py:374
  14.4 2.6 %collective-permute-start.1 = (f32[49,4,128]{2,1,0:T(4,128)S(1)}, f32[49,4,128]{2,1,0:T(4,128)S(1)}, u32[]{:S(2)}, u32[]{:S(2)}) collective-permute-start(f32[49,4,128]{2,1,0:T(4,128)S(1)} %get-tuple-element.25.t0), channel_id=1, source_target_pairs={{0,24},{1,25},{2,26},{3,27},{4,28},{5,29},{6,30},{7,31},{8,0},{9,1... | collective-permute-start | bytes 301064 | tf_op jit(solution)/shard_map/ppermute | solution.py:371
  17.0 1.0 %collective-permute-done.t1 = f32[49,4,128]{2,1,0:T(4,128)S(1)} collective-permute-done((f32[49,4,128]{2,1,0:T(4,128)S(1)}, f32[49,4,128]{2,1,0:T(4,128)S(1)}, u32[]{:S(2)}, u32[]{:S(2)}) %collective-permute-start) | collective-permute-done | bytes 100384 | tf_op jit(solution)/shard_map/ppermute | solution.py:371
  18.0 0.3 collective-permute-start.2
  18.3 0.5 %collective-permute-start.5 = (f32[2,16,4,128]{3,2,1,0:T(4,128)S(1)}, f32[2,16,4,128]{3,2,1,0:T(4,128)S(1)}, u32[]{:S(2)}, u32[]{:S(2)}) collective-permute-start(f32[2,16,4,128]{3,2,1,0:T(4,128)S(1)} %pad_maximum_fusion.c0), channel_id=1, source_target_pairs={{0,192},{32,224},{64,0},{96,32},{128,64},{160,96},{192,128},{224,1... | collective-permute-start | bytes 196616 | tf_op jit(solution)/shard_map/ppermute | solution.py:374
  18.8 0.0 collective-permute-done.4.c1
  18.9 1.5 %collective-permute-start.6 = (f32[2,16,4,128]{3,2,1,0:T(4,128)S(1)}, f32[2,16,4,128]{3,2,1,0:T(4,128)S(1)}, u32[]{:S(2)}, u32[]{:S(2)}) collective-permute-start(f32[2,16,4,128]{3,2,1,0:T(4,128)S(1)} %collective-permute-done.4.c1), channel_id=1, source_target_pairs={{0,64},{32,96},{64,128},{96,160},{128,192},{160,224},{192,0},{224,... | collective-permute-start | bytes 196616 | tf_op jit(solution)/shard_map/ppermute | solution.py:375
  20.3 3.5 %collective-permute-done.2.t3 = f32[49,4,128]{2,1,0:T(4,128)S(1)} collective-permute-done((f32[49,4,128]{2,1,0:T(4,128)S(1)}, f32[49,4,128]{2,1,0:T(4,128)S(1)}, u32[]{:S(2)}, u32[]{:S(2)}) %collective-permute-start.2) | collective-permute-done | bytes 100384 | tf_op jit(solution)/shard_map/ppermute | solution.py:372
  23.9 0.4 prep.1
  24.2 0.0 collective-permute-done.6.c3
  24.3 2.2 %all-to-all-done = f32[8,37,4,128]{3,2,1,0:T(4,128)S(1)} async-done(((f32[8,37,4,128]{3,2,1,0:T(4,128)}), f32[8,37,4,128]{3,2,1,0:T(4,128)S(1)}, u32[]{:S(2)}, u32[]{:S(2)}) %all-to-all-start) | async-done | bytes 606240 | tf_op jit(solution)/shard_map/all_to_all | solution.py:370
  26.5 8.5 %near.2 = (f32[3,48,128]{2,1,0:T(8,128)S(1)}, f32[3,48,128]{2,1,0:T(8,128)S(1)}, f32[3,48,128]{2,1,0:T(8,128)S(1)}, f32[48,4,128]{2,1,0:T(4,128)S(1)}) custom-call(s32[16,256]{1,0:T(8,128)S(1)} %get-tuple-element.33.refs_0_, f32[192,4,128]{2,1,0:T(4,128)S(1)} %get-tuple-element.34.refs_1_, f32[296,4,128]{2,1,0:T(4,128)S(1)} %bitcast.20), custom_call_target="tpu_custom_call" | custom-call | tf_op jit(solution)/shard_map/near/pallas_call | solution.py:393
  35.0 3.3 %collective-permute-start.7 = (f32[3,48,128]{2,1,0:T(8,128)S(1)}, f32[3,48,128]{2,1,0:T(8,128)S(1)}, u32[]{:S(2)}, u32[]{:S(2)}) collective-permute-start(f32[3,48,128]{2,1,0:T(8,128)S(1)} %get-tuple-element.43), channel_id=1, source_target_pairs={{0,16},{1,17},{2,18},{3,19},{4,20},{5,21},{6,22},{7,23},{8,24},{9,... | collective-permute-start | bytes 221192 | tf_op jit(solution)/shard_map/ppermute | solution.py:410
  38.2 3.2 %collective-permute-start.8 = (f32[3,48,128]{2,1,0:T(8,128)S(1)}, f32[3,48,128]{2,1,0:T(8,128)S(1)}, u32[]{:S(2)}, u32[]{:S(2)}) collective-permute-start(f32[3,48,128]{2,1,0:T(8,128)S(1)} %get-tuple-element.37), channel_id=1, source_target_pairs={{0,24},{1,25},{2,26},{3,27},{4,28},{5,29},{6,30},{7,31},{8,0},{9,1... | collective-permute-start | bytes 221192 | tf_op jit(solution)/shard_map/ppermute | solution.py:410
  41.5 2.6 %near.3.p0 = f32[3,48,128]{2,1,0:T(8,128)S(1)} custom-call(s32[16,256]{1,0:T(8,128)S(1)} %get-tuple-element.33.refs_0_, f32[192,4,128]{2,1,0:T(4,128)S(1)} %get-tuple-element.34.refs_1_, f32[296,4,128]{2,1,0:T(4,128)S(1)} %bitcast.21, f32[48,4,128]{2,1,0:T(4,128)S(1)} %get-tuple-element.42.refs_3_), custom_call_target="tpu_custom_call" | custom-call | tf_op jit(solution)/shard_map/near/pallas_call | solution.py:393
  44.1 0.0 copy-start.2
  44.2 0.6 %copy-done.2 = s32[1,1,48]{2,1,0:T(1,128)S(1)} copy-done((s32[1,1,48]{2,1,0:T(1,128)S(1)}, s32[1,1,48]{2,1,0:T(1,128)}, u32[]{:S(2)}) %copy-start.2) | copy-done | bytes 216
  44.8 1.4 %far.1.far_ref = f32[3,48,128]{2,1,0:T(8,128)S(1)} custom-call(s32[1]{0:T(128)} %bitcast.1.place_ref, f32[3,48,128]{2,1,0:T(8,128)S(1)} %bitcast.23, s32[1,48]{1,0:T(1,128)S(1)} %bitcast.27, s32[32,48]{1,0:T(8,128)S(1)} %bitcast.25, f32[2,16,4,128]{3,2,1,0:T(4,128)S(1)} %pad_maximum_fusion.c0, f32[2,16,4,128]{3,2,1,0:T(4,128)S(1)} %collective-permute-done.4.c1, ...), custom_call_target="tpu_custom_call" | custom-call | tf_op jit(solution)/shard_map/far/pallas_call | solution.py:412
  46.2 0.7 %final.1 = f32[3,48,128]{2,1,0:T(8,128)} custom-call(s32[1,48]{1,0:T(1,128)S(1)} %bitcast.28, f32[3,48,128]{2,1,0:T(8,128)S(1)} %far.1.far_ref, f32[3,48,128]{2,1,0:T(8,128)S(1)} %near.3.p0, f32[3,48,128]{2,1,0:T(8,128)S(1)} %collective-permute-done.7.p1, f32[3,48,128]{2,1,0:T(8,128)S(1)} %collective-permute-done.8.p2, ...), custom_call_target="tpu_custom_call" | custom-call | tf_op jit(solution)/shard_map/final/pallas_call | solution.py:422
  (11 shorter events, 0.0 us)
Async XLA Ops:
  2.1 24.4 %all-to-all-start = ((f32[8,37,4,128]{3,2,1,0:T(4,128)}), f32[8,37,4,128]{3,2,1,0:T(4,128)S(1)}, u32[]{:S(2)}, u32[]{:S(2)}) async-start(f32[8,37,4,128]{3,2,1,0:T(4,128)} %get-tuple-element.35), calls=%async_computation | async-start | bytes 1212416 | tf_op jit(solution)/shard_map/all_to_all | solution.py:370
  11.5 1.6 %collective-permute-start.3 = (f32[16,4,128]{2,1,0:T(4,128)S(1)}, f32[16,4,128]{2,1,0:T(4,128)S(1)}, u32[]{:S(2)}, u32[]{:S(2)}) collective-permute-start(f32[16,4,128]{2,1,0:T(4,128)S(1)} %get-tuple-element.28), channel_id=1, source_target_pairs={{0,32},{32,0},{64,96},{96,64},{128,160},{160,128},{192,224},{224,1... | collective-permute-start | bytes 98312 | tf_op jit(solution)/shard_map/ppermute | solution.py:373
  11.5 6.5 %collective-permute-start = (f32[49,4,128]{2,1,0:T(4,128)S(1)}, f32[49,4,128]{2,1,0:T(4,128)S(1)}, u32[]{:S(2)}, u32[]{:S(2)}) collective-permute-start(f32[49,4,128]{2,1,0:T(4,128)S(1)} %get-tuple-element.25.t0), channel_id=1, source_target_pairs={{0,8},{1,9},{2,10},{3,11},{4,12},{5,13},{6,14},{7,15},{8,16},{9,17... | collective-permute-start | bytes 301064 | tf_op jit(solution)/shard_map/ppermute | solution.py:371
  13.1 5.8 %collective-permute-start.4 = (f32[2,16,4,128]{3,2,1,0:T(4,128)S(1)}, f32[2,16,4,128]{3,2,1,0:T(4,128)S(1)}, u32[]{:S(2)}, u32[]{:S(2)}) collective-permute-start(f32[2,16,4,128]{3,2,1,0:T(4,128)S(1)} %pad_maximum_fusion.c0), channel_id=1, source_target_pairs={{0,64},{32,96},{64,128},{96,160},{128,192},{160,224},{192,0},{224,... | collective-permute-start | bytes 196616 | tf_op jit(solution)/shard_map/ppermute | solution.py:374
  14.4 6.0 %collective-permute-start.1 = (f32[49,4,128]{2,1,0:T(4,128)S(1)}, f32[49,4,128]{2,1,0:T(4,128)S(1)}, u32[]{:S(2)}, u32[]{:S(2)}) collective-permute-start(f32[49,4,128]{2,1,0:T(4,128)S(1)} %get-tuple-element.25.t0), channel_id=1, source_target_pairs={{0,24},{1,25},{2,26},{3,27},{4,28},{5,29},{6,30},{7,31},{8,0},{9,1... | collective-permute-start | bytes 301064 | tf_op jit(solution)/shard_map/ppermute | solution.py:371
  18.0 5.8 %collective-permute-start.2 = (f32[49,4,128]{2,1,0:T(4,128)S(1)}, f32[49,4,128]{2,1,0:T(4,128)S(1)}, u32[]{:S(2)}, u32[]{:S(2)}) collective-permute-start(f32[49,4,128]{2,1,0:T(4,128)S(1)} %collective-permute-done.t1), channel_id=1, source_target_pairs={{0,8},{1,9},{2,10},{3,11},{4,12},{5,13},{6,14},{7,15},{8,16},{9,17... | collective-permute-start | bytes 301064 | tf_op jit(solution)/shard_map/ppermute | solution.py:372
  18.3 5.9 %collective-permute-start.5 = (f32[2,16,4,128]{3,2,1,0:T(4,128)S(1)}, f32[2,16,4,128]{3,2,1,0:T(4,128)S(1)}, u32[]{:S(2)}, u32[]{:S(2)}) collective-permute-start(f32[2,16,4,128]{3,2,1,0:T(4,128)S(1)} %pad_maximum_fusion.c0), channel_id=1, source_target_pairs={{0,192},{32,224},{64,0},{96,32},{128,64},{160,96},{192,128},{224,1... | collective-permute-start | bytes 196616 | tf_op jit(solution)/shard_map/ppermute | solution.py:374
  18.9 5.4 %collective-permute-start.6 = (f32[2,16,4,128]{3,2,1,0:T(4,128)S(1)}, f32[2,16,4,128]{3,2,1,0:T(4,128)S(1)}, u32[]{:S(2)}, u32[]{:S(2)}) collective-permute-start(f32[2,16,4,128]{3,2,1,0:T(4,128)S(1)} %collective-permute-done.4.c1), channel_id=1, source_target_pairs={{0,64},{32,96},{64,128},{96,160},{128,192},{160,224},{192,0},{224,... | collective-permute-start | bytes 196616 | tf_op jit(solution)/shard_map/ppermute | solution.py:375
  35.0 11.3 %collective-permute-start.7 = (f32[3,48,128]{2,1,0:T(8,128)S(1)}, f32[3,48,128]{2,1,0:T(8,128)S(1)}, u32[]{:S(2)}, u32[]{:S(2)}) collective-permute-start(f32[3,48,128]{2,1,0:T(8,128)S(1)} %get-tuple-element.43), channel_id=1, source_target_pairs={{0,16},{1,17},{2,18},{3,19},{4,20},{5,21},{6,22},{7,23},{8,24},{9,... | collective-permute-start | bytes 221192 | tf_op jit(solution)/shard_map/ppermute | solution.py:410
  38.2 8.0 %collective-permute-start.9 = (f32[3,48,128]{2,1,0:T(8,128)S(1)}, f32[3,48,128]{2,1,0:T(8,128)S(1)}, u32[]{:S(2)}, u32[]{:S(2)}) collective-permute-start(f32[3,48,128]{2,1,0:T(8,128)S(1)} %get-tuple-element.44), channel_id=1, source_target_pairs={{0,8},{1,9},{2,10},{3,11},{4,12},{5,13},{6,14},{7,15},{8,16},{9,17... | collective-permute-start | bytes 221192 | tf_op jit(solution)/shard_map/ppermute | solution.py:410
  38.2 8.0 %collective-permute-start.8 = (f32[3,48,128]{2,1,0:T(8,128)S(1)}, f32[3,48,128]{2,1,0:T(8,128)S(1)}, u32[]{:S(2)}, u32[]{:S(2)}) collective-permute-start(f32[3,48,128]{2,1,0:T(8,128)S(1)} %get-tuple-element.37), channel_id=1, source_target_pairs={{0,24},{1,25},{2,26},{3,27},{4,28},{5,29},{6,30},{7,31},{8,0},{9,1... | collective-permute-start | bytes 221192 | tf_op jit(solution)/shard_map/ppermute | solution.py:410
  41.5 2.7 %copy-start = (f32[1,48,3,128]{3,1,2,0:T(8,128)S(1)}, f32[1,48,3,128]{3,1,2,0:T(8,128)}, u32[]{:S(2)}) copy-start(f32[1,48,3,128]{3,1,2,0:T(8,128)} %param.8) | copy-start | bytes 221188
  41.5 2.7 %copy-start.1 = (s32[1,48,32]{1,2,0:T(8,128)S(1)}, s32[1,48,32]{1,2,0:T(8,128)}, u32[]{:S(2)}) copy-start(s32[1,48,32]{1,2,0:T(8,128)} %param.13) | copy-start | bytes 18436
  44.1 0.7 %copy-start.2 = (s32[1,1,48]{2,1,0:T(1,128)S(1)}, s32[1,1,48]{2,1,0:T(1,128)}, u32[]{:S(2)}) copy-start(s32[1,1,48]{2,1,0:T(1,128)} %param.10) | copy-start | bytes 580

commit v17 on v15

--- a/solution.py
+++ b/solution.py
@@ -89,8 +89,22 @@
         cell_ref[j, 3:4, :] = cm_ref[0:1, part]
 
 
-def far_kernel(place_ref, pos_ref, cnt_ref, list_ref, c0, c1, c2, c3, out_ref, pad):
+def far_kernel(place_ref, pos_hbm, cnt_hbm, list_hbm, c0, c1, c2, c3, out_ref, pad, pos_ref, cnt_ref, list_ref, sem):
     xs, cs = place_ref[0] >> 1, place_ref[0] & 1
+    moves = ((pos_hbm, pos_ref), (cnt_hbm, cnt_ref), (list_hbm, list_ref))
+    copies = [pltpu.make_async_copy(a, b, sem.at[i]) for i, (a, b) in enumerate(moves)]
+    for copy in copies:
+        copy.start()
+    tables = []
+    for c in range(4):
+        whole = jnp.concatenate([ref[i, :, c, :] for ref in (c0, c1, c2, c3) for i in range(2)], axis=0)
+        whole = whole.T
+        high = whole.astype(BF16)
+        low = (whole - high.astype(F32)).astype(BF16)
+        tables.append(jnp.concatenate([high, low], axis=1))
+    tables = jnp.concatenate(tables, axis=0)
+    for copy in copies:
+        copy.wait()
     lane = lax.broadcasted_iota(I32, (NB, PL), 1)
     cnt = column_of(cnt_ref[...], NB)
     live = lane < cnt
@@ -109,14 +123,6 @@
     order = jnp.where(dx == 3, 1, jnp.where(dx == 0, 0, dx + 1))
     rows = (order * 2 + ((slab & 1) ^ cs)) * 16 + ((ids >> 7) & 15)
     lanes = ids & (PL - 1)
-    tables = []
-    for c in range(4):
-        whole = jnp.concatenate([ref[i, :, c, :] for ref in (c0, c1, c2, c3) for i in range(2)], axis=0)
-        whole = whole.T
-        high = whole.astype(BF16)
-        low = (whole - high.astype(F32)).astype(BF16)
-        tables.append(jnp.concatenate([high, low], axis=1))
-    tables = jnp.concatenate(tables, axis=0)
     sub = lax.broadcasted_iota(I32, (PL, 2 * PL), 0)
     got = [[] for _ in range(4)]
     for j in range(0, LC // 2, 2):
@@ -385,12 +391,18 @@
     (far,) = call(
         far_kernel,
         (((3, NB, PL), F32),),
-        [sspec()] + [vspec()] * 7,
+        [sspec()] + [pl.BlockSpec(memory_space=pltpu.HBM)] * 3 + [vspec()] * 4,
         [vspec()],
         "far",
         16,
-        [pltpu.VMEM((PL, PL), F32)],
-    )(place, pos, cnt, cell_list[0].T, *pairs)
+        [
+            pltpu.VMEM((PL, PL), F32),
+            pltpu.VMEM((3, NB, PL), F32),
+            pltpu.VMEM((1, NB), I32),
+            pltpu.VMEM((LC, NB), I32),
+            pltpu.SemaphoreType.DMA((3,)),
+        ],
+    )(place, *[pltpu.with_memory_space_constraint(v, pltpu.HBM) for v in (pos, cnt, cell_list[0].T)], *pairs)
     tall, tab, far = lax.optimization_barrier((tall, tab, far))
     window = window.reshape(NZ * (TILES + 1), 4, PL)
 

time: 47.3 us -> 46.8 us (0.989)
  the two profiles are of different devices: /device:TPU:32 before, /device:TPU:0 now
where the time goes in v17:
time: 46.8 us; the launch traced here: 45.8 us
  starting transfers between devices  23.5 us (50%)
  Pallas kernels  16 us (34%)
  waiting for transfers between devices  6.21 us (13%)
    pallas_call x2, Pallas kernels, near(): call(functools.partial(near_kernel, first), outs, [vspec()] * len(arrays)...  10.4 us
    all_to_all x1, starting transfers between devices, per_device(): lax.all_to_all(src, 'space', 0, 0, axis_index_groups=z_rows, tiled=True)  7.61 us
    ppermute x3, starting transfers between devices, per_device(): lax.ppermute(sent[i], 'space', along_y(-k))  7.03 us
    ppermute x2, starting transfers between devices, per_device(): pairs = [pair] + [lax.ppermute(pair, 'slab', along_x(k)) for k in (1, -1)]  4.33 us
    ppermute x2, starting transfers between devices, per_device(): tgts = [tgt] + [lax.ppermute(tgt, 'space', along_y(k)) for k in (1, -1)]  4.22 us
    ppermute x1, waiting for transfers between devices, per_device(): pairs.append(lax.ppermute(pairs[1], 'slab', along_x(1)))  3.57 us
    pallas_call x1, Pallas kernels, per_device(): call(far_kernel, (((3, NB, PL), F32),), [sspec()] + [pl.BlockSpec(memory_...  2.39 us
    pallas_call x1, Pallas kernels, per_device(): call(pack_kernel, (((NZ, TILES + 1, 4, PL), F32), ((NB + 1, 4, PL), F32),...  2.11 us
  transfers between devices with their start and end apart: 11, of which 3 were waited for; matrix products, arithmetic and copies ran while one was open for 0% of the time, Pallas kernels for 15%

profile of v17, /device:TPU:0, one launch (start us, length us, event | category | flops | bytes accessed | tf_op | source)
XLA Modules:
  0.0 45.8 jit_solution(13495733500326680642)
XLA Ops:
  0.0 2.1 %pack.1 = (f32[8,37,4,128]{3,2,1,0:T(4,128)}, f32[49,4,128]{2,1,0:T(4,128)S(1)}, f32[16,4,128]{2,1,0:T(4,128)S(1)}) custom-call(f32[3,48,128]{2,1,0:T(8,128)} %bitcast.26, f32[48,128]{1,0:T(8,128)} %bitcast.29, s32[1,48]{1,0:T(1,128)} %bitcast.23, s32[1,48]{1,0:T(1,128)} %refs_3_.1, s32[4,48]{1,0:T(4,128)} %bitcast.32, f32[3,2048]{1,0:T(4,128)} %refs_5_.1, ...), custom_call_target="tpu_custom_call" | custom-call | tf_op jit(solution)/shard_map/pack/pallas_call | solution.py:349
  2.1 7.6 %all-to-all-start = ((f32[8,37,4,128]{3,2,1,0:T(4,128)}), f32[8,37,4,128]{3,2,1,0:T(4,128)S(1)}, u32[]{:S(2)}, u32[]{:S(2)}) async-start(f32[8,37,4,128]{3,2,1,0:T(4,128)} %get-tuple-element.24), calls=%async_computation | async-start | bytes 1212416 | tf_op jit(solution)/shard_map/all_to_all | solution.py:375
  9.7 0.0 collective-permute-start.3
  9.7 1.6 %collective-permute-start = (f32[49,4,128]{2,1,0:T(4,128)S(1)}, f32[49,4,128]{2,1,0:T(4,128)S(1)}, u32[]{:S(2)}, u32[]{:S(2)}) collective-permute-start(f32[49,4,128]{2,1,0:T(4,128)S(1)} %get-tuple-element.17.t0), channel_id=1, source_target_pairs={{0,8},{1,9},{2,10},{3,11},{4,12},{5,13},{6,14},{7,15},{8,16},{9,17... | collective-permute-start | bytes 301064 | tf_op jit(solution)/shard_map/ppermute | solution.py:376
  11.3 0.0 collective-permute-done.3
  11.3 1.6 %collective-permute-start.4 = (f32[2,16,4,128]{3,2,1,0:T(4,128)S(1)}, f32[2,16,4,128]{3,2,1,0:T(4,128)S(1)}, u32[]{:S(2)}, u32[]{:S(2)}) collective-permute-start(f32[2,16,4,128]{3,2,1,0:T(4,128)S(1)} %pad_maximum_fusion.c0), channel_id=1, source_target_pairs={{0,64},{32,96},{64,128},{96,160},{128,192},{160,224},{192,0},{224,... | collective-permute-start | bytes 196616 | tf_op jit(solution)/shard_map/ppermute | solution.py:379
  12.9 2.6 %collective-permute-start.1 = (f32[49,4,128]{2,1,0:T(4,128)S(1)}, f32[49,4,128]{2,1,0:T(4,128)S(1)}, u32[]{:S(2)}, u32[]{:S(2)}) collective-permute-start(f32[49,4,128]{2,1,0:T(4,128)S(1)} %get-tuple-element.17.t0), channel_id=1, source_target_pairs={{0,24},{1,25},{2,26},{3,27},{4,28},{5,29},{6,30},{7,31},{8,0},{9,1... | collective-permute-start | bytes 301064 | tf_op jit(solution)/shard_map/ppermute | solution.py:376
  15.5 0.7 %collective-permute-done.t1 = f32[49,4,128]{2,1,0:T(4,128)S(1)} collective-permute-done((f32[49,4,128]{2,1,0:T(4,128)S(1)}, f32[49,4,128]{2,1,0:T(4,128)S(1)}, u32[]{:S(2)}, u32[]{:S(2)}) %collective-permute-start) | collective-permute-done | bytes 100384 | tf_op jit(solution)/shard_map/ppermute | solution.py:376
  16.3 0.3 collective-permute-start.2
  16.6 2.8 %collective-permute-start.5 = (f32[2,16,4,128]{3,2,1,0:T(4,128)S(1)}, f32[2,16,4,128]{3,2,1,0:T(4,128)S(1)}, u32[]{:S(2)}, u32[]{:S(2)}) collective-permute-start(f32[2,16,4,128]{3,2,1,0:T(4,128)S(1)} %pad_maximum_fusion.c0), channel_id=1, source_target_pairs={{0,192},{32,224},{64,0},{96,32},{128,64},{160,96},{192,128},{224,1... | collective-permute-start | bytes 196616 | tf_op jit(solution)/shard_map/ppermute | solution.py:379
  19.3 0.0 collective-permute-done.4.c1
  19.3 1.9 %collective-permute-done.5.c2 = f32[2,16,4,128]{3,2,1,0:T(4,128)S(1)} collective-permute-done((f32[2,16,4,128]{3,2,1,0:T(4,128)S(1)}, f32[2,16,4,128]{3,2,1,0:T(4,128)S(1)}, u32[]{:S(2)}, u32[]{:S(2)}) %collective-permute-start.5) | collective-permute-done | bytes 65568 | tf_op jit(solution)/shard_map/ppermute | solution.py:379
  21.2 3.6 %collective-permute-done.6.c3 = f32[2,16,4,128]{3,2,1,0:T(4,128)S(1)} collective-permute-done((f32[2,16,4,128]{3,2,1,0:T(4,128)S(1)}, f32[2,16,4,128]{3,2,1,0:T(4,128)S(1)}, u32[]{:S(2)}, u32[]{:S(2)}) %collective-permute-start.6) | collective-permute-done | bytes 65568 | tf_op jit(solution)/shard_map/ppermute | solution.py:380
  24.8 2.4 %far.1.far_ref = f32[3,48,128]{2,1,0:T(8,128)S(1)} custom-call(s32[1]{0:T(128)} %bitcast.8.place_ref, f32[3,48,128]{2,1,0:T(8,128)} %bitcast.27, s32[1,48]{1,0:T(1,128)} %bitcast.24, s32[32,48]{1,0:T(8,128)} %bitcast.30, f32[2,16,4,128]{3,2,1,0:T(4,128)S(1)} %pad_maximum_fusion.c0, f32[2,16,4,128]{3,2,1,0:T(4,128)S(1)} %collective-permute-done.4.c1, ...), custom_call_target="tpu_custom_call" | custom-call | tf_op jit(solution)/shard_map/far/pallas_call | solution.py:391
  27.2 0.0 collective-permute-done.2.t3
  27.2 0.4 prep.1
  27.6 0.0 all-to-all-done
  27.6 6.5 %near.2 = (f32[3,48,128]{2,1,0:T(8,128)S(1)}, f32[3,48,128]{2,1,0:T(8,128)S(1)}, f32[3,48,128]{2,1,0:T(8,128)S(1)}, f32[48,4,128]{2,1,0:T(4,128)S(1)}) custom-call(s32[16,256]{1,0:T(8,128)S(1)} %get-tuple-element.22.refs_0_, f32[192,4,128]{2,1,0:T(4,128)S(1)} %get-tuple-element.23.refs_1_, f32[296,4,128]{2,1,0:T(4,128)S(1)} %bitcast.20), custom_call_target="tpu_custom_call" | custom-call | tf_op jit(solution)/shard_map/near/pallas_call | solution.py:413
  34.1 5.0 %collective-permute-start.7 = (f32[3,48,128]{2,1,0:T(8,128)S(1)}, f32[3,48,128]{2,1,0:T(8,128)S(1)}, u32[]{:S(2)}, u32[]{:S(2)}) collective-permute-start(f32[3,48,128]{2,1,0:T(8,128)S(1)} %get-tuple-element.26), channel_id=1, source_target_pairs={{0,16},{1,17},{2,18},{3,19},{4,20},{5,21},{6,22},{7,23},{8,24},{9,... | collective-permute-start | bytes 221192 | tf_op jit(solution)/shard_map/ppermute | solution.py:430
  39.1 2.0 %collective-permute-start.9 = (f32[3,48,128]{2,1,0:T(8,128)S(1)}, f32[3,48,128]{2,1,0:T(8,128)S(1)}, u32[]{:S(2)}, u32[]{:S(2)}) collective-permute-start(f32[3,48,128]{2,1,0:T(8,128)S(1)} %get-tuple-element.28), channel_id=1, source_target_pairs={{0,8},{1,9},{2,10},{3,11},{4,12},{5,13},{6,14},{7,15},{8,16},{9,17... | collective-permute-start | bytes 221192 | tf_op jit(solution)/shard_map/ppermute | solution.py:430
  41.1 4.0 %near.3.p0 = f32[3,48,128]{2,1,0:T(8,128)S(1)} custom-call(s32[16,256]{1,0:T(8,128)S(1)} %get-tuple-element.22.refs_0_, f32[192,4,128]{2,1,0:T(4,128)S(1)} %get-tuple-element.23.refs_1_, f32[296,4,128]{2,1,0:T(4,128)S(1)} %bitcast.21, f32[48,4,128]{2,1,0:T(4,128)S(1)} %get-tuple-element.25.refs_3_), custom_call_target="tpu_custom_call" | custom-call | tf_op jit(solution)/shard_map/near/pallas_call | solution.py:413
  45.1 0.0 collective-permute-done.8.p2
  45.1 0.0 collective-permute-done.9.p3
  45.1 0.7 %final.1 = f32[3,48,128]{2,1,0:T(8,128)} custom-call(s32[1,48]{1,0:T(1,128)S(1)} %bitcast.25, f32[3,48,128]{2,1,0:T(8,128)S(1)} %far.1.far_ref, f32[3,48,128]{2,1,0:T(8,128)S(1)} %near.3.p0, f32[3,48,128]{2,1,0:T(8,128)S(1)} %collective-permute-done.7.p1, f32[3,48,128]{2,1,0:T(8,128)S(1)} %collective-permute-done.8.p2, ...), custom_call_target="tpu_custom_call" | custom-call | tf_op jit(solution)/shard_map/final/pallas_call | solution.py:432
  (7 shorter events, 0.0 us)
Async XLA Ops:
  2.1 25.5 %all-to-all-start = ((f32[8,37,4,128]{3,2,1,0:T(4,128)}), f32[8,37,4,128]{3,2,1,0:T(4,128)S(1)}, u32[]{:S(2)}, u32[]{:S(2)}) async-start(f32[8,37,4,128]{3,2,1,0:T(4,128)} %get-tuple-element.24), calls=%async_computation | async-start | bytes 1212416 | tf_op jit(solution)/shard_map/all_to_all | solution.py:375
  9.7 1.6 %collective-permute-start.3 = (f32[16,4,128]{2,1,0:T(4,128)S(1)}, f32[16,4,128]{2,1,0:T(4,128)S(1)}, u32[]{:S(2)}, u32[]{:S(2)}) collective-permute-start(f32[16,4,128]{2,1,0:T(4,128)S(1)} %get-tuple-element.20), channel_id=1, source_target_pairs={{0,32},{32,0},{64,96},{96,64},{128,160},{160,128},{192,224},{224,1... | collective-permute-start | bytes 98312 | tf_op jit(solution)/shard_map/ppermute | solution.py:378
  9.7 6.5 %collective-permute-start = (f32[49,4,128]{2,1,0:T(4,128)S(1)}, f32[49,4,128]{2,1,0:T(4,128)S(1)}, u32[]{:S(2)}, u32[]{:S(2)}) collective-permute-start(f32[49,4,128]{2,1,0:T(4,128)S(1)} %get-tuple-element.17.t0), channel_id=1, source_target_pairs={{0,8},{1,9},{2,10},{3,11},{4,12},{5,13},{6,14},{7,15},{8,16},{9,17... | collective-permute-start | bytes 301064 | tf_op jit(solution)/shard_map/ppermute | solution.py:376
  11.3 8.0 %collective-permute-start.4 = (f32[2,16,4,128]{3,2,1,0:T(4,128)S(1)}, f32[2,16,4,128]{3,2,1,0:T(4,128)S(1)}, u32[]{:S(2)}, u32[]{:S(2)}) collective-permute-start(f32[2,16,4,128]{3,2,1,0:T(4,128)S(1)} %pad_maximum_fusion.c0), channel_id=1, source_target_pairs={{0,64},{32,96},{64,128},{96,160},{128,192},{160,224},{192,0},{224,... | collective-permute-start | bytes 196616 | tf_op jit(solution)/shard_map/ppermute | solution.py:379
  12.9 14.3 %collective-permute-start.1 = (f32[49,4,128]{2,1,0:T(4,128)S(1)}, f32[49,4,128]{2,1,0:T(4,128)S(1)}, u32[]{:S(2)}, u32[]{:S(2)}) collective-permute-start(f32[49,4,128]{2,1,0:T(4,128)S(1)} %get-tuple-element.17.t0), channel_id=1, source_target_pairs={{0,24},{1,25},{2,26},{3,27},{4,28},{5,29},{6,30},{7,31},{8,0},{9,1... | collective-permute-start | bytes 301064 | tf_op jit(solution)/shard_map/ppermute | solution.py:376
  16.3 11.0 %collective-permute-start.2 = (f32[49,4,128]{2,1,0:T(4,128)S(1)}, f32[49,4,128]{2,1,0:T(4,128)S(1)}, u32[]{:S(2)}, u32[]{:S(2)}) collective-permute-start(f32[49,4,128]{2,1,0:T(4,128)S(1)} %collective-permute-done.t1), channel_id=1, source_target_pairs={{0,8},{1,9},{2,10},{3,11},{4,12},{5,13},{6,14},{7,15},{8,16},{9,17... | collective-permute-start | bytes 301064 | tf_op jit(solution)/shard_map/ppermute | solution.py:377
  16.6 4.7 %collective-permute-start.5 = (f32[2,16,4,128]{3,2,1,0:T(4,128)S(1)}, f32[2,16,4,128]{3,2,1,0:T(4,128)S(1)}, u32[]{:S(2)}, u32[]{:S(2)}) collective-permute-start(f32[2,16,4,128]{3,2,1,0:T(4,128)S(1)} %pad_maximum_fusion.c0), channel_id=1, source_target_pairs={{0,192},{32,224},{64,0},{96,32},{128,64},{160,96},{192,128},{224,1... | collective-permute-start | bytes 196616 | tf_op jit(solution)/shard_map/ppermute | solution.py:379
  19.3 5.5 %collective-permute-start.6 = (f32[2,16,4,128]{3,2,1,0:T(4,128)S(1)}, f32[2,16,4,128]{3,2,1,0:T(4,128)S(1)}, u32[]{:S(2)}, u32[]{:S(2)}) collective-permute-start(f32[2,16,4,128]{3,2,1,0:T(4,128)S(1)} %collective-permute-done.4.c1), channel_id=1, source_target_pairs={{0,64},{32,96},{64,128},{96,160},{128,192},{160,224},{192,0},{224,... | collective-permute-start | bytes 196616 | tf_op jit(solution)/shard_map/ppermute | solution.py:380
  34.1 11.0 %collective-permute-start.7 = (f32[3,48,128]{2,1,0:T(8,128)S(1)}, f32[3,48,128]{2,1,0:T(8,128)S(1)}, u32[]{:S(2)}, u32[]{:S(2)}) collective-permute-start(f32[3,48,128]{2,1,0:T(8,128)S(1)} %get-tuple-element.26), channel_id=1, source_target_pairs={{0,16},{1,17},{2,18},{3,19},{4,20},{5,21},{6,22},{7,23},{8,24},{9,... | collective-permute-start | bytes 221192 | tf_op jit(solution)/shard_map/ppermute | solution.py:430
  39.1 6.0 %collective-permute-start.8 = (f32[3,48,128]{2,1,0:T(8,128)S(1)}, f32[3,48,128]{2,1,0:T(8,128)S(1)}, u32[]{:S(2)}, u32[]{:S(2)}) collective-permute-start(f32[3,48,128]{2,1,0:T(8,128)S(1)} %get-tuple-element.27), channel_id=1, source_target_pairs={{0,24},{1,25},{2,26},{3,27},{4,28},{5,29},{6,30},{7,31},{8,0},{9,1... | collective-permute-start | bytes 221192 | tf_op jit(solution)/shard_map/ppermute | solution.py:430
  39.1 6.0 %collective-permute-start.9 = (f32[3,48,128]{2,1,0:T(8,128)S(1)}, f32[3,48,128]{2,1,0:T(8,128)S(1)}, u32[]{:S(2)}, u32[]{:S(2)}) collective-permute-start(f32[3,48,128]{2,1,0:T(8,128)S(1)} %get-tuple-element.28), channel_id=1, source_target_pairs={{0,8},{1,9},{2,10},{3,11},{4,12},{5,13},{6,14},{7,15},{8,16},{9,17... | collective-permute-start | bytes 221192 | tf_op jit(solution)/shard_map/ppermute | solution.py:430
  41.1 4.0 %copy-start = (s32[1,1,48]{2,1,0:T(1,128)S(1)}, s32[1,1,48]{2,1,0:T(1,128)}, u32[]{:S(2)}) copy-start(s32[1,1,48]{2,1,0:T(1,128)} %param.10) | copy-start | bytes 580

commit v18 on v15

--- a/solution.py
+++ b/solution.py
@@ -370,8 +370,10 @@
     tgts = [tgt] + [lax.ppermute(tgt, "space", along_y(k)) for k in (1, -1)]
     tgts.append(lax.ppermute(tgts[1], "space", along_y(1)))
     pair = jnp.stack([cells, lax.ppermute(cells, "slab", [(i, i ^ 1) for i in range(2 * NX)])])
-    pairs = [pair] + [lax.ppermute(pair, "slab", along_x(k)) for k in (1, -1)]
-    pairs.append(lax.ppermute(pairs[1], "slab", along_x(1)))
+    first = lax.ppermute(pair, "slab", along_x(1))
+    pair, first = lax.optimization_barrier((pair, first))
+    third = lax.ppermute(first, "slab", along_x(1))
+    pairs = [pair, first, lax.ppermute(pair, "slab", along_x(-1)), third]
     me = (lax.axis_index("space") // NZ).astype(I32).reshape(1)
     place = lax.axis_index("slab").astype(I32).reshape(1)
     tall, tab = call(

time: 47.3 us -> 46.5 us (0.983)
  the two profiles are of different devices: /device:TPU:32 before, /device:TPU:1 now
where the time goes in v18:
time: 46.5 us; the launch traced here: 45.8 us
  starting transfers between devices  21.7 us (47%)
  Pallas kernels  15.6 us (34%)
  waiting for transfers between devices  7.75 us (17%)
  local copies, waits for them, and re-layouts  0.66 us (1%)
    pallas_call x2, Pallas kernels, near(): call(functools.partial(near_kernel, first), outs, [vspec()] * len(arrays)...  10.9 us
    all_to_all x1, starting transfers between devices, per_device(): lax.all_to_all(src, 'space', 0, 0, axis_index_groups=z_rows, tiled=True)  9.9 us
    ppermute x3, starting transfers between devices, per_device(): lax.ppermute(sent[i], 'space', along_y(-k))  3.73 us
    ppermute x2, starting transfers between devices, per_device(): tgts = [tgt] + [lax.ppermute(tgt, 'space', along_y(k)) for k in (1, -1)]  3.59 us
    ppermute x1, waiting for transfers between devices, per_device(): third = lax.ppermute(first, 'slab', along_x(1))  3.29 us
    ppermute x1, starting transfers between devices, per_device(): pairs = [pair, first, lax.ppermute(pair, 'slab', along_x(-1)), third]  2.28 us
    pallas_call x1, Pallas kernels, per_device(): call(pack_kernel, (((NZ, TILES + 1, 4, PL), F32), ((NB + 1, 4, PL), F32),...  2.12 us
    ppermute x3, waiting for transfers between devices, per_device(): lax.ppermute(sent[i], 'space', along_y(-k))  2.01 us
  transfers between devices with their start and end apart: 11, of which 5 were waited for; matrix products, arithmetic and copies ran while one was open for 0% of the time, Pallas kernels for 9%

profile of v18, /device:TPU:1, one launch (start us, length us, event | category | flops | bytes accessed | tf_op | source)
XLA Modules:
  0.0 45.8 jit_solution(1912975741233613910)
XLA Ops:
  0.0 2.1 %pack.1 = (f32[8,37,4,128]{3,2,1,0:T(4,128)}, f32[49,4,128]{2,1,0:T(4,128)S(1)}, f32[16,4,128]{2,1,0:T(4,128)S(1)}) custom-call(f32[3,48,128]{2,1,0:T(8,128)} %bitcast.22, f32[48,128]{1,0:T(8,128)} %bitcast.30, s32[1,48]{1,0:T(1,128)} %bitcast.26, s32[1,48]{1,0:T(1,128)} %refs_3_.1, s32[4,48]{1,0:T(4,128)} %bitcast.32, f32[3,2048]{1,0:T(4,128)} %refs_5_.1, ...), custom_call_target="tpu_custom_call" | custom-call | tf_op jit(solution)/shard_map/pack/pallas_call | solution.py:343
  2.1 9.9 %all-to-all-start = ((f32[8,37,4,128]{3,2,1,0:T(4,128)}), f32[8,37,4,128]{3,2,1,0:T(4,128)S(1)}, u32[]{:S(2)}, u32[]{:S(2)}) async-start(f32[8,37,4,128]{3,2,1,0:T(4,128)} %get-tuple-element.28), calls=%async_computation | async-start | bytes 1212416 | tf_op jit(solution)/shard_map/all_to_all | solution.py:369
  12.0 1.0 %collective-permute-start.3 = (f32[16,4,128]{2,1,0:T(4,128)S(1)}, f32[16,4,128]{2,1,0:T(4,128)S(1)}, u32[]{:S(2)}, u32[]{:S(2)}) collective-permute-start(f32[16,4,128]{2,1,0:T(4,128)S(1)} %get-tuple-element.22), channel_id=1, source_target_pairs={{0,32},{32,0},{64,96},{96,64},{128,160},{160,128},{192,224},{224,1... | collective-permute-start | bytes 98312 | tf_op jit(solution)/shard_map/ppermute | solution.py:372
  13.0 1.3 %collective-permute-start = (f32[49,4,128]{2,1,0:T(4,128)S(1)}, f32[49,4,128]{2,1,0:T(4,128)S(1)}, u32[]{:S(2)}, u32[]{:S(2)}) collective-permute-start(f32[49,4,128]{2,1,0:T(4,128)S(1)} %get-tuple-element.19.t0), channel_id=1, source_target_pairs={{0,8},{1,9},{2,10},{3,11},{4,12},{5,13},{6,14},{7,15},{8,16},{9,17... | collective-permute-start | bytes 301064 | tf_op jit(solution)/shard_map/ppermute | solution.py:370
  14.3 1.3 %collective-permute-start.4 = (f32[2,16,4,128]{3,2,1,0:T(4,128)S(1)}, f32[2,16,4,128]{3,2,1,0:T(4,128)S(1)}, u32[]{:S(2)}, u32[]{:S(2)}) collective-permute-start(f32[2,16,4,128]{3,2,1,0:T(4,128)S(1)} %pad_maximum_fusion.c0), channel_id=1, source_target_pairs={{0,64},{32,96},{64,128},{96,160},{128,192},{160,224},{192,0},{224,... | collective-permute-start | bytes 196616 | tf_op jit(solution)/shard_map/ppermute | solution.py:373
  15.6 2.3 %collective-permute-start.1 = (f32[49,4,128]{2,1,0:T(4,128)S(1)}, f32[49,4,128]{2,1,0:T(4,128)S(1)}, u32[]{:S(2)}, u32[]{:S(2)}) collective-permute-start(f32[49,4,128]{2,1,0:T(4,128)S(1)} %get-tuple-element.19.t0), channel_id=1, source_target_pairs={{0,24},{1,25},{2,26},{3,27},{4,28},{5,29},{6,30},{7,31},{8,0},{9,1... | collective-permute-start | bytes 301064 | tf_op jit(solution)/shard_map/ppermute | solution.py:370
  17.9 0.9 %collective-permute-done.t1 = f32[49,4,128]{2,1,0:T(4,128)S(1)} collective-permute-done((f32[49,4,128]{2,1,0:T(4,128)S(1)}, f32[49,4,128]{2,1,0:T(4,128)S(1)}, u32[]{:S(2)}, u32[]{:S(2)}) %collective-permute-start) | collective-permute-done | bytes 100384 | tf_op jit(solution)/shard_map/ppermute | solution.py:370
  18.8 0.0 collective-permute-start.2
  18.8 0.2 collective-permute-done.4.c1
  19.0 2.3 %collective-permute-start.5 = (f32[2,16,4,128]{3,2,1,0:T(4,128)S(1)}, f32[2,16,4,128]{3,2,1,0:T(4,128)S(1)}, u32[]{:S(2)}, u32[]{:S(2)}) collective-permute-start(f32[2,16,4,128]{3,2,1,0:T(4,128)S(1)} %pad_maximum_fusion.c0), channel_id=1, source_target_pairs={{0,192},{32,224},{64,0},{96,32},{128,64},{160,96},{192,128},{224,1... | collective-permute-start | bytes 196616 | tf_op jit(solution)/shard_map/ppermute | solution.py:376
  21.3 0.0 collective-permute-start.6
  21.3 1.3 %collective-permute-done.5.c2 = f32[2,16,4,128]{3,2,1,0:T(4,128)S(1)} collective-permute-done((f32[2,16,4,128]{3,2,1,0:T(4,128)S(1)}, f32[2,16,4,128]{3,2,1,0:T(4,128)S(1)}, u32[]{:S(2)}, u32[]{:S(2)}) %collective-permute-start.5) | collective-permute-done | bytes 65568 | tf_op jit(solution)/shard_map/ppermute | solution.py:376
  22.6 3.3 %collective-permute-done.6.c3 = f32[2,16,4,128]{3,2,1,0:T(4,128)S(1)} collective-permute-done((f32[2,16,4,128]{3,2,1,0:T(4,128)S(1)}, f32[2,16,4,128]{3,2,1,0:T(4,128)S(1)}, u32[]{:S(2)}, u32[]{:S(2)}) %collective-permute-start.6) | collective-permute-done | bytes 65568 | tf_op jit(solution)/shard_map/ppermute | solution.py:375
  25.9 0.6 %copy-done.2 = s32[1,1,48]{2,1,0:T(1,128)S(1)} copy-done((s32[1,1,48]{2,1,0:T(1,128)S(1)}, s32[1,1,48]{2,1,0:T(1,128)}, u32[]{:S(2)}) %copy-start.2) | copy-done | bytes 216
  26.6 1.4 %far.1.far_ref = f32[3,48,128]{2,1,0:T(8,128)S(1)} custom-call(s32[1]{0:T(128)} %bitcast.8.place_ref, f32[3,48,128]{2,1,0:T(8,128)S(1)} %bitcast.23, s32[1,48]{1,0:T(1,128)S(1)} %bitcast.27, s32[32,48]{1,0:T(8,128)S(1)} %bitcast.25, f32[2,16,4,128]{3,2,1,0:T(4,128)S(1)} %pad_maximum_fusion.c0, f32[2,16,4,128]{3,2,1,0:T(4,128)S(1)} %collective-permute-done.4.c1, ...), custom_call_target="tpu_custom_call" | custom-call | tf_op jit(solution)/shard_map/far/pallas_call | solution.py:387
  28.0 0.4 prep.1
  28.4 8.5 %near.2 = (f32[3,48,128]{2,1,0:T(8,128)S(1)}, f32[3,48,128]{2,1,0:T(8,128)S(1)}, f32[3,48,128]{2,1,0:T(8,128)S(1)}, f32[48,4,128]{2,1,0:T(4,128)S(1)}) custom-call(s32[16,256]{1,0:T(8,128)S(1)} %get-tuple-element.26.refs_0_, f32[192,4,128]{2,1,0:T(4,128)S(1)} %get-tuple-element.27.refs_1_, f32[296,4,128]{2,1,0:T(4,128)S(1)} %bitcast.20), custom_call_target="tpu_custom_call" | custom-call | tf_op jit(solution)/shard_map/near/pallas_call | solution.py:403
  36.9 0.6 %collective-permute-start.7 = (f32[3,48,128]{2,1,0:T(8,128)S(1)}, f32[3,48,128]{2,1,0:T(8,128)S(1)}, u32[]{:S(2)}, u32[]{:S(2)}) collective-permute-start(f32[3,48,128]{2,1,0:T(8,128)S(1)} %get-tuple-element.30), channel_id=1, source_target_pairs={{0,16},{1,17},{2,18},{3,19},{4,20},{5,21},{6,22},{7,23},{8,24},{9,... | collective-permute-start | bytes 221192 | tf_op jit(solution)/shard_map/ppermute | solution.py:420
  37.5 3.1 %collective-permute-start.8 = (f32[3,48,128]{2,1,0:T(8,128)S(1)}, f32[3,48,128]{2,1,0:T(8,128)S(1)}, u32[]{:S(2)}, u32[]{:S(2)}) collective-permute-start(f32[3,48,128]{2,1,0:T(8,128)S(1)} %get-tuple-element.31), channel_id=1, source_target_pairs={{0,24},{1,25},{2,26},{3,27},{4,28},{5,29},{6,30},{7,31},{8,0},{9,1... | collective-permute-start | bytes 221192 | tf_op jit(solution)/shard_map/ppermute | solution.py:420
  40.6 0.0 collective-permute-start.9
  40.6 2.5 %near.3.p0 = f32[3,48,128]{2,1,0:T(8,128)S(1)} custom-call(s32[16,256]{1,0:T(8,128)S(1)} %get-tuple-element.26.refs_0_, f32[192,4,128]{2,1,0:T(4,128)S(1)} %get-tuple-element.27.refs_1_, f32[296,4,128]{2,1,0:T(4,128)S(1)} %bitcast.21, f32[48,4,128]{2,1,0:T(4,128)S(1)} %get-tuple-element.29.refs_3_), custom_call_target="tpu_custom_call" | custom-call | tf_op jit(solution)/shard_map/near/pallas_call | solution.py:403
  43.1 0.0 collective-permute-done.7.p1
  43.1 2.0 %collective-permute-done.9.p3 = f32[3,48,128]{2,1,0:T(8,128)S(1)} collective-permute-done((f32[3,48,128]{2,1,0:T(8,128)S(1)}, f32[3,48,128]{2,1,0:T(8,128)S(1)}, u32[]{:S(2)}, u32[]{:S(2)}) %collective-permute-start.9) | collective-permute-done | bytes 73760 | tf_op jit(solution)/shard_map/ppermute | solution.py:420
  45.1 0.7 %final.1 = f32[3,48,128]{2,1,0:T(8,128)} custom-call(s32[1,48]{1,0:T(1,128)S(1)} %bitcast.28, f32[3,48,128]{2,1,0:T(8,128)S(1)} %far.1.far_ref, f32[3,48,128]{2,1,0:T(8,128)S(1)} %near.3.p0, f32[3,48,128]{2,1,0:T(8,128)S(1)} %collective-permute-done.7.p1, f32[3,48,128]{2,1,0:T(8,128)S(1)} %collective-permute-done.8.p2, ...), custom_call_target="tpu_custom_call" | custom-call | tf_op jit(solution)/shard_map/final/pallas_call | solution.py:422
  (11 shorter events, 0.0 us)
Async XLA Ops:
  2.1 26.2 %all-to-all-start = ((f32[8,37,4,128]{3,2,1,0:T(4,128)}), f32[8,37,4,128]{3,2,1,0:T(4,128)S(1)}, u32[]{:S(2)}, u32[]{:S(2)}) async-start(f32[8,37,4,128]{3,2,1,0:T(4,128)} %get-tuple-element.28), calls=%async_computation | async-start | bytes 1212416 | tf_op jit(solution)/shard_map/all_to_all | solution.py:369
  12.0 2.3 %collective-permute-start.3 = (f32[16,4,128]{2,1,0:T(4,128)S(1)}, f32[16,4,128]{2,1,0:T(4,128)S(1)}, u32[]{:S(2)}, u32[]{:S(2)}) collective-permute-start(f32[16,4,128]{2,1,0:T(4,128)S(1)} %get-tuple-element.22), channel_id=1, source_target_pairs={{0,32},{32,0},{64,96},{96,64},{128,160},{160,128},{192,224},{224,1... | collective-permute-start | bytes 98312 | tf_op jit(solution)/shard_map/ppermute | solution.py:372
  13.0 5.8 %collective-permute-start = (f32[49,4,128]{2,1,0:T(4,128)S(1)}, f32[49,4,128]{2,1,0:T(4,128)S(1)}, u32[]{:S(2)}, u32[]{:S(2)}) collective-permute-start(f32[49,4,128]{2,1,0:T(4,128)S(1)} %get-tuple-element.19.t0), channel_id=1, source_target_pairs={{0,8},{1,9},{2,10},{3,11},{4,12},{5,13},{6,14},{7,15},{8,16},{9,17... | collective-permute-start | bytes 301064 | tf_op jit(solution)/shard_map/ppermute | solution.py:370
  14.3 11.6 %copy-start = (f32[1,48,3,128]{3,1,2,0:T(8,128)S(1)}, f32[1,48,3,128]{3,1,2,0:T(8,128)}, u32[]{:S(2)}) copy-start(f32[1,48,3,128]{3,1,2,0:T(8,128)} %param.8) | copy-start | bytes 221188
  14.3 4.7 %collective-permute-start.4 = (f32[2,16,4,128]{3,2,1,0:T(4,128)S(1)}, f32[2,16,4,128]{3,2,1,0:T(4,128)S(1)}, u32[]{:S(2)}, u32[]{:S(2)}) collective-permute-start(f32[2,16,4,128]{3,2,1,0:T(4,128)S(1)} %pad_maximum_fusion.c0), channel_id=1, source_target_pairs={{0,64},{32,96},{64,128},{96,160},{128,192},{160,224},{192,0},{224,... | collective-permute-start | bytes 196616 | tf_op jit(solution)/shard_map/ppermute | solution.py:373
  15.6 12.4 %collective-permute-start.1 = (f32[49,4,128]{2,1,0:T(4,128)S(1)}, f32[49,4,128]{2,1,0:T(4,128)S(1)}, u32[]{:S(2)}, u32[]{:S(2)}) collective-permute-start(f32[49,4,128]{2,1,0:T(4,128)S(1)} %get-tuple-element.19.t0), channel_id=1, source_target_pairs={{0,24},{1,25},{2,26},{3,27},{4,28},{5,29},{6,30},{7,31},{8,0},{9,1... | collective-permute-start | bytes 301064 | tf_op jit(solution)/shard_map/ppermute | solution.py:370
  18.8 9.2 %collective-permute-start.2 = (f32[49,4,128]{2,1,0:T(4,128)S(1)}, f32[49,4,128]{2,1,0:T(4,128)S(1)}, u32[]{:S(2)}, u32[]{:S(2)}) collective-permute-start(f32[49,4,128]{2,1,0:T(4,128)S(1)} %collective-permute-done.t1), channel_id=1, source_target_pairs={{0,8},{1,9},{2,10},{3,11},{4,12},{5,13},{6,14},{7,15},{8,16},{9,17... | collective-permute-start | bytes 301064 | tf_op jit(solution)/shard_map/ppermute | solution.py:371
  19.0 3.6 %collective-permute-start.5 = (f32[2,16,4,128]{3,2,1,0:T(4,128)S(1)}, f32[2,16,4,128]{3,2,1,0:T(4,128)S(1)}, u32[]{:S(2)}, u32[]{:S(2)}) collective-permute-start(f32[2,16,4,128]{3,2,1,0:T(4,128)S(1)} %pad_maximum_fusion.c0), channel_id=1, source_target_pairs={{0,192},{32,224},{64,0},{96,32},{128,64},{160,96},{192,128},{224,1... | collective-permute-start | bytes 196616 | tf_op jit(solution)/shard_map/ppermute | solution.py:376
  21.3 4.6 %collective-permute-start.6 = (f32[2,16,4,128]{3,2,1,0:T(4,128)S(1)}, f32[2,16,4,128]{3,2,1,0:T(4,128)S(1)}, u32[]{:S(2)}, u32[]{:S(2)}) collective-permute-start(f32[2,16,4,128]{3,2,1,0:T(4,128)S(1)} %collective-permute-done.4.c1), channel_id=1, source_target_pairs={{0,64},{32,96},{64,128},{96,160},{128,192},{160,224},{192,0},{224,... | collective-permute-start | bytes 196616 | tf_op jit(solution)/shard_map/ppermute | solution.py:375
  21.3 4.6 %copy-start.1 = (s32[1,48,32]{1,2,0:T(8,128)S(1)}, s32[1,48,32]{1,2,0:T(8,128)}, u32[]{:S(2)}) copy-start(s32[1,48,32]{1,2,0:T(8,128)} %param.13) | copy-start | bytes 18436
  25.9 0.7 %copy-start.2 = (s32[1,1,48]{2,1,0:T(1,128)S(1)}, s32[1,1,48]{2,1,0:T(1,128)}, u32[]{:S(2)}) copy-start(s32[1,1,48]{2,1,0:T(1,128)} %param.10) | copy-start | bytes 580
  36.9 6.2 %collective-permute-start.7 = (f32[3,48,128]{2,1,0:T(8,128)S(1)}, f32[3,48,128]{2,1,0:T(8,128)S(1)}, u32[]{:S(2)}, u32[]{:S(2)}) collective-permute-start(f32[3,48,128]{2,1,0:T(8,128)S(1)} %get-tuple-element.30), channel_id=1, source_target_pairs={{0,16},{1,17},{2,18},{3,19},{4,20},{5,21},{6,22},{7,23},{8,24},{9,... | collective-permute-start | bytes 221192 | tf_op jit(solution)/shard_map/ppermute | solution.py:420
  37.5 5.6 %collective-permute-start.8 = (f32[3,48,128]{2,1,0:T(8,128)S(1)}, f32[3,48,128]{2,1,0:T(8,128)S(1)}, u32[]{:S(2)}, u32[]{:S(2)}) collective-permute-start(f32[3,48,128]{2,1,0:T(8,128)S(1)} %get-tuple-element.31), channel_id=1, source_target_pairs={{0,24},{1,25},{2,26},{3,27},{4,28},{5,29},{6,30},{7,31},{8,0},{9,1... | collective-permute-start | bytes 221192 | tf_op jit(solution)/shard_map/ppermute | solution.py:420
  40.6 4.5 %collective-permute-start.9 = (f32[3,48,128]{2,1,0:T(8,128)S(1)}, f32[3,48,128]{2,1,0:T(8,128)S(1)}, u32[]{:S(2)}, u32[]{:S(2)}) collective-permute-start(f32[3,48,128]{2,1,0:T(8,128)S(1)} %get-tuple-element.32), channel_id=1, source_target_pairs={{0,8},{1,9},{2,10},{3,11},{4,12},{5,13},{6,14},{7,15},{8,16},{9,17... | collective-permute-start | bytes 221192 | tf_op jit(solution)/shard_map/ppermute | solution.py:420

commit v19 on v18

--- a/solution.py
+++ b/solution.py
@@ -371,8 +371,8 @@
     tgts.append(lax.ppermute(tgts[1], "space", along_y(1)))
     pair = jnp.stack([cells, lax.ppermute(cells, "slab", [(i, i ^ 1) for i in range(2 * NX)])])
     first = lax.ppermute(pair, "slab", along_x(1))
-    pair, first = lax.optimization_barrier((pair, first))
     third = lax.ppermute(first, "slab", along_x(1))
+    pair, tgts[2] = lax.optimization_barrier((pair, tgts[2]))
     pairs = [pair, first, lax.ppermute(pair, "slab", along_x(-1)), third]
     me = (lax.axis_index("space") // NZ).astype(I32).reshape(1)
     place = lax.axis_index("slab").astype(I32).reshape(1)

time: 46.5 us -> 47.5 us (1.022)
  the two profiles are of different devices: /device:TPU:1 before, /device:TPU:6 now
where the time goes in v19:
time: 47.5 us; the launch traced here: 47.3 us
  starting transfers between devices  21.2 us (45%)
  Pallas kernels  13.6 us (29%)
  waiting for transfers between devices  11.8 us (25%)
  local copies, waits for them, and re-layouts  0.66 us (1%)
    all_to_all x1, starting transfers between devices, per_device(): lax.all_to_all(src, 'space', 0, 0, axis_index_groups=z_rows, tiled=True)  9.35 us
    pallas_call x2, Pallas kernels, near(): call(functools.partial(near_kernel, first), outs, [vspec()] * len(arrays)...  8.92 us
    ppermute x3, starting transfers between devices, per_device(): lax.ppermute(sent[i], 'space', along_y(-k))  6.22 us
    ppermute x2, waiting for transfers between devices, per_device(): tgts = [tgt] + [lax.ppermute(tgt, 'space', along_y(k)) for k in (1, -1)]  5.59 us
    ppermute x2, starting transfers between devices, per_device(): tgts = [tgt] + [lax.ppermute(tgt, 'space', along_y(k)) for k in (1, -1)]  3.02 us
    ppermute x3, waiting for transfers between devices, per_device(): lax.ppermute(sent[i], 'space', along_y(-k))  2.32 us
    ppermute x1, waiting for transfers between devices, per_device(): third = lax.ppermute(first, 'slab', along_x(1))  2.23 us
    pallas_call x1, Pallas kernels, per_device(): call(pack_kernel, (((NZ, TILES + 1, 4, PL), F32), ((NB + 1, 4, PL), F32),...  2.12 us
  transfers between devices with their start and end apart: 11, of which 5 were waited for; matrix products, arithmetic and copies ran while one was open for 0% of the time, Pallas kernels for 9%

profile of v19, /device:TPU:6, one launch (start us, length us, event | category | flops | bytes accessed | tf_op | source)
XLA Modules:
  0.0 47.3 jit_solution(1101847069820421087)
XLA Ops:
  0.0 2.1 %pack.1 = (f32[8,37,4,128]{3,2,1,0:T(4,128)}, f32[49,4,128]{2,1,0:T(4,128)S(1)}, f32[16,4,128]{2,1,0:T(4,128)S(1)}) custom-call(f32[3,48,128]{2,1,0:T(8,128)} %bitcast.22, f32[48,128]{1,0:T(8,128)} %bitcast.30, s32[1,48]{1,0:T(1,128)} %bitcast.26, s32[1,48]{1,0:T(1,128)} %refs_3_.1, s32[4,48]{1,0:T(4,128)} %bitcast.32, f32[3,2048]{1,0:T(4,128)} %refs_5_.1, ...), custom_call_target="tpu_custom_call" | custom-call | tf_op jit(solution)/shard_map/pack/pallas_call | solution.py:343
  2.1 9.3 %all-to-all-start = ((f32[8,37,4,128]{3,2,1,0:T(4,128)}), f32[8,37,4,128]{3,2,1,0:T(4,128)S(1)}, u32[]{:S(2)}, u32[]{:S(2)}) async-start(f32[8,37,4,128]{3,2,1,0:T(4,128)} %get-tuple-element.28), calls=%async_computation | async-start | bytes 1212416 | tf_op jit(solution)/shard_map/all_to_all | solution.py:369
  11.5 0.0 collective-permute-start.1
  11.5 3.0 %collective-permute-start.2 = (f32[49,4,128]{2,1,0:T(4,128)S(1)}, f32[49,4,128]{2,1,0:T(4,128)S(1)}, u32[]{:S(2)}, u32[]{:S(2)}) collective-permute-start(f32[49,4,128]{2,1,0:T(4,128)S(1)} %get-tuple-element.19.t0), channel_id=1, source_target_pairs={{0,24},{1,25},{2,26},{3,27},{4,28},{5,29},{6,30},{7,31},{8,0},{9,1... | collective-permute-start | bytes 301064 | tf_op jit(solution)/shard_map/ppermute | solution.py:370
  14.5 0.0 collective-permute-start
  14.5 0.6 %collective-permute-start.4 = (f32[2,16,4,128]{3,2,1,0:T(4,128)S(1)}, f32[2,16,4,128]{3,2,1,0:T(4,128)S(1)}, u32[]{:S(2)}, u32[]{:S(2)}) collective-permute-start(f32[2,16,4,128]{3,2,1,0:T(4,128)S(1)} %pad_maximum_fusion.c0), channel_id=1, source_target_pairs={{0,64},{32,96},{64,128},{96,160},{128,192},{160,224},{192,0},{224,... | collective-permute-start | bytes 196616 | tf_op jit(solution)/shard_map/ppermute | solution.py:373
  15.1 5.6 %collective-permute-done.t1 = f32[49,4,128]{2,1,0:T(4,128)S(1)} collective-permute-done((f32[49,4,128]{2,1,0:T(4,128)S(1)}, f32[49,4,128]{2,1,0:T(4,128)S(1)}, u32[]{:S(2)}, u32[]{:S(2)}) %collective-permute-start) | collective-permute-done | bytes 100384 | tf_op jit(solution)/shard_map/ppermute | solution.py:370
  20.7 0.0 collective-permute-start.3
  20.7 0.0 collective-permute-done.4.c1
  20.7 0.5 %collective-permute-start.6 = (f32[2,16,4,128]{3,2,1,0:T(4,128)S(1)}, f32[2,16,4,128]{3,2,1,0:T(4,128)S(1)}, u32[]{:S(2)}, u32[]{:S(2)}) collective-permute-start(f32[2,16,4,128]{3,2,1,0:T(4,128)S(1)} %collective-permute-done.4.c1), channel_id=1, source_target_pairs={{0,64},{32,96},{64,128},{96,160},{128,192},{160,224},{192,0},{224,... | collective-permute-start | bytes 196616 | tf_op jit(solution)/shard_map/ppermute | solution.py:374
  21.2 1.5 %collective-permute-start.5 = (f32[2,16,4,128]{3,2,1,0:T(4,128)S(1)}, f32[2,16,4,128]{3,2,1,0:T(4,128)S(1)}, u32[]{:S(2)}, u32[]{:S(2)}) collective-permute-start(f32[2,16,4,128]{3,2,1,0:T(4,128)S(1)} %pad_maximum_fusion.c0), channel_id=1, source_target_pairs={{0,192},{32,224},{64,0},{96,32},{128,64},{160,96},{192,128},{224,1... | collective-permute-start | bytes 196616 | tf_op jit(solution)/shard_map/ppermute | solution.py:376
  22.7 2.2 %collective-permute-done.6.c3 = f32[2,16,4,128]{3,2,1,0:T(4,128)S(1)} collective-permute-done((f32[2,16,4,128]{3,2,1,0:T(4,128)S(1)}, f32[2,16,4,128]{3,2,1,0:T(4,128)S(1)}, u32[]{:S(2)}, u32[]{:S(2)}) %collective-permute-start.6) | collective-permute-done | bytes 65568 | tf_op jit(solution)/shard_map/ppermute | solution.py:374
  25.0 1.7 %collective-permute-done.5.c2 = f32[2,16,4,128]{3,2,1,0:T(4,128)S(1)} collective-permute-done((f32[2,16,4,128]{3,2,1,0:T(4,128)S(1)}, f32[2,16,4,128]{3,2,1,0:T(4,128)S(1)}, u32[]{:S(2)}, u32[]{:S(2)}) %collective-permute-start.5) | collective-permute-done | bytes 65568 | tf_op jit(solution)/shard_map/ppermute | solution.py:376
  26.7 0.6 %copy-done.2 = s32[1,1,48]{2,1,0:T(1,128)S(1)} copy-done((s32[1,1,48]{2,1,0:T(1,128)S(1)}, s32[1,1,48]{2,1,0:T(1,128)}, u32[]{:S(2)}) %copy-start.2) | copy-done | bytes 216
  27.3 1.4 %far.1.far_ref = f32[3,48,128]{2,1,0:T(8,128)S(1)} custom-call(s32[1]{0:T(128)} %bitcast.10.place_ref, f32[3,48,128]{2,1,0:T(8,128)S(1)} %bitcast.23, s32[1,48]{1,0:T(1,128)S(1)} %bitcast.27, s32[32,48]{1,0:T(8,128)S(1)} %bitcast.25, f32[2,16,4,128]{3,2,1,0:T(4,128)S(1)} %pad_maximum_fusion.c0, f32[2,16,4,128]{3,2,1,0:T(4,128)S(1)} %collective-permute-done.4.c1, ...), custom_call_target="tpu_custom_call" | custom-call | tf_op jit(solution)/shard_map/far/pallas_call | solution.py:387
  28.7 0.4 prep.1
  29.1 6.5 %near.2 = (f32[3,48,128]{2,1,0:T(8,128)S(1)}, f32[3,48,128]{2,1,0:T(8,128)S(1)}, f32[3,48,128]{2,1,0:T(8,128)S(1)}, f32[48,4,128]{2,1,0:T(4,128)S(1)}) custom-call(s32[16,256]{1,0:T(8,128)S(1)} %get-tuple-element.26.refs_0_, f32[192,4,128]{2,1,0:T(4,128)S(1)} %get-tuple-element.27.refs_1_, f32[296,4,128]{2,1,0:T(4,128)S(1)} %bitcast.20), custom_call_target="tpu_custom_call" | custom-call | tf_op jit(solution)/shard_map/near/pallas_call | solution.py:403
  35.6 1.7 %collective-permute-start.7 = (f32[3,48,128]{2,1,0:T(8,128)S(1)}, f32[3,48,128]{2,1,0:T(8,128)S(1)}, u32[]{:S(2)}, u32[]{:S(2)}) collective-permute-start(f32[3,48,128]{2,1,0:T(8,128)S(1)} %get-tuple-element.30), channel_id=1, source_target_pairs={{0,16},{1,17},{2,18},{3,19},{4,20},{5,21},{6,22},{7,23},{8,24},{9,... | collective-permute-start | bytes 221192 | tf_op jit(solution)/shard_map/ppermute | solution.py:420
  37.3 3.8 %collective-permute-start.8 = (f32[3,48,128]{2,1,0:T(8,128)S(1)}, f32[3,48,128]{2,1,0:T(8,128)S(1)}, u32[]{:S(2)}, u32[]{:S(2)}) collective-permute-start(f32[3,48,128]{2,1,0:T(8,128)S(1)} %get-tuple-element.31), channel_id=1, source_target_pairs={{0,24},{1,25},{2,26},{3,27},{4,28},{5,29},{6,30},{7,31},{8,0},{9,1... | collective-permute-start | bytes 221192 | tf_op jit(solution)/shard_map/ppermute | solution.py:420
  41.0 0.8 %collective-permute-start.9 = (f32[3,48,128]{2,1,0:T(8,128)S(1)}, f32[3,48,128]{2,1,0:T(8,128)S(1)}, u32[]{:S(2)}, u32[]{:S(2)}) collective-permute-start(f32[3,48,128]{2,1,0:T(8,128)S(1)} %get-tuple-element.32), channel_id=1, source_target_pairs={{0,8},{1,9},{2,10},{3,11},{4,12},{5,13},{6,14},{7,15},{8,16},{9,17... | collective-permute-start | bytes 221192 | tf_op jit(solution)/shard_map/ppermute | solution.py:420
  41.8 2.5 %near.3.p0 = f32[3,48,128]{2,1,0:T(8,128)S(1)} custom-call(s32[16,256]{1,0:T(8,128)S(1)} %get-tuple-element.26.refs_0_, f32[192,4,128]{2,1,0:T(4,128)S(1)} %get-tuple-element.27.refs_1_, f32[296,4,128]{2,1,0:T(4,128)S(1)} %bitcast.21, f32[48,4,128]{2,1,0:T(4,128)S(1)} %get-tuple-element.29.refs_3_), custom_call_target="tpu_custom_call" | custom-call | tf_op jit(solution)/shard_map/near/pallas_call | solution.py:403
  44.3 0.6 %collective-permute-done.8.p2 = f32[3,48,128]{2,1,0:T(8,128)S(1)} collective-permute-done((f32[3,48,128]{2,1,0:T(8,128)S(1)}, f32[3,48,128]{2,1,0:T(8,128)S(1)}, u32[]{:S(2)}, u32[]{:S(2)}) %collective-permute-start.8) | collective-permute-done | bytes 73760 | tf_op jit(solution)/shard_map/ppermute | solution.py:420
  44.9 1.7 %collective-permute-done.9.p3 = f32[3,48,128]{2,1,0:T(8,128)S(1)} collective-permute-done((f32[3,48,128]{2,1,0:T(8,128)S(1)}, f32[3,48,128]{2,1,0:T(8,128)S(1)}, u32[]{:S(2)}, u32[]{:S(2)}) %collective-permute-start.9) | collective-permute-done | bytes 73760 | tf_op jit(solution)/shard_map/ppermute | solution.py:420
  46.6 0.7 %final.1 = f32[3,48,128]{2,1,0:T(8,128)} custom-call(s32[1,48]{1,0:T(1,128)S(1)} %bitcast.28, f32[3,48,128]{2,1,0:T(8,128)S(1)} %far.1.far_ref, f32[3,48,128]{2,1,0:T(8,128)S(1)} %near.3.p0, f32[3,48,128]{2,1,0:T(8,128)S(1)} %collective-permute-done.7.p1, f32[3,48,128]{2,1,0:T(8,128)S(1)} %collective-permute-done.8.p2, ...), custom_call_target="tpu_custom_call" | custom-call | tf_op jit(solution)/shard_map/final/pallas_call | solution.py:422
  (11 shorter events, 0.0 us)
Async XLA Ops:
  2.1 27.0 %all-to-all-start = ((f32[8,37,4,128]{3,2,1,0:T(4,128)}), f32[8,37,4,128]{3,2,1,0:T(4,128)S(1)}, u32[]{:S(2)}, u32[]{:S(2)}) async-start(f32[8,37,4,128]{3,2,1,0:T(4,128)} %get-tuple-element.28), calls=%async_computation | async-start | bytes 1212416 | tf_op jit(solution)/shard_map/all_to_all | solution.py:369
  11.5 3.0 %collective-permute-start.1 = (f32[16,4,128]{2,1,0:T(4,128)S(1)}, f32[16,4,128]{2,1,0:T(4,128)S(1)}, u32[]{:S(2)}, u32[]{:S(2)}) collective-permute-start(f32[16,4,128]{2,1,0:T(4,128)S(1)} %get-tuple-element.20), channel_id=1, source_target_pairs={{0,32},{32,0},{64,96},{96,64},{128,160},{160,128},{192,224},{224,1... | collective-permute-start | bytes 98312 | tf_op jit(solution)/shard_map/ppermute | solution.py:372
  11.5 9.7 %collective-permute-start.2 = (f32[49,4,128]{2,1,0:T(4,128)S(1)}, f32[49,4,128]{2,1,0:T(4,128)S(1)}, u32[]{:S(2)}, u32[]{:S(2)}) collective-permute-start(f32[49,4,128]{2,1,0:T(4,128)S(1)} %get-tuple-element.19.t0), channel_id=1, source_target_pairs={{0,24},{1,25},{2,26},{3,27},{4,28},{5,29},{6,30},{7,31},{8,0},{9,1... | collective-permute-start | bytes 301064 | tf_op jit(solution)/shard_map/ppermute | solution.py:370
  14.5 6.2 %collective-permute-start = (f32[49,4,128]{2,1,0:T(4,128)S(1)}, f32[49,4,128]{2,1,0:T(4,128)S(1)}, u32[]{:S(2)}, u32[]{:S(2)}) collective-permute-start(f32[49,4,128]{2,1,0:T(4,128)S(1)} %get-tuple-element.19.t0), channel_id=1, source_target_pairs={{0,8},{1,9},{2,10},{3,11},{4,12},{5,13},{6,14},{7,15},{8,16},{9,17... | collective-permute-start | bytes 301064 | tf_op jit(solution)/shard_map/ppermute | solution.py:370
  14.5 12.1 %copy-start = (f32[1,48,3,128]{3,1,2,0:T(8,128)S(1)}, f32[1,48,3,128]{3,1,2,0:T(8,128)}, u32[]{:S(2)}) copy-start(f32[1,48,3,128]{3,1,2,0:T(8,128)} %param.8) | copy-start | bytes 221188
  14.5 6.2 %collective-permute-start.4 = (f32[2,16,4,128]{3,2,1,0:T(4,128)S(1)}, f32[2,16,4,128]{3,2,1,0:T(4,128)S(1)}, u32[]{:S(2)}, u32[]{:S(2)}) collective-permute-start(f32[2,16,4,128]{3,2,1,0:T(4,128)S(1)} %pad_maximum_fusion.c0), channel_id=1, source_target_pairs={{0,64},{32,96},{64,128},{96,160},{128,192},{160,224},{192,0},{224,... | collective-permute-start | bytes 196616 | tf_op jit(solution)/shard_map/ppermute | solution.py:373
  20.7 8.0 %collective-permute-start.3 = (f32[49,4,128]{2,1,0:T(4,128)S(1)}, f32[49,4,128]{2,1,0:T(4,128)S(1)}, u32[]{:S(2)}, u32[]{:S(2)}) collective-permute-start(f32[49,4,128]{2,1,0:T(4,128)S(1)} %collective-permute-done.t1), channel_id=1, source_target_pairs={{0,8},{1,9},{2,10},{3,11},{4,12},{5,13},{6,14},{7,15},{8,16},{9,17... | collective-permute-start | bytes 301064 | tf_op jit(solution)/shard_map/ppermute | solution.py:371
  20.7 4.3 %collective-permute-start.6 = (f32[2,16,4,128]{3,2,1,0:T(4,128)S(1)}, f32[2,16,4,128]{3,2,1,0:T(4,128)S(1)}, u32[]{:S(2)}, u32[]{:S(2)}) collective-permute-start(f32[2,16,4,128]{3,2,1,0:T(4,128)S(1)} %collective-permute-done.4.c1), channel_id=1, source_target_pairs={{0,64},{32,96},{64,128},{96,160},{128,192},{160,224},{192,0},{224,... | collective-permute-start | bytes 196616 | tf_op jit(solution)/shard_map/ppermute | solution.py:374
  21.2 5.5 %collective-permute-start.5 = (f32[2,16,4,128]{3,2,1,0:T(4,128)S(1)}, f32[2,16,4,128]{3,2,1,0:T(4,128)S(1)}, u32[]{:S(2)}, u32[]{:S(2)}) collective-permute-start(f32[2,16,4,128]{3,2,1,0:T(4,128)S(1)} %pad_maximum_fusion.c0), channel_id=1, source_target_pairs={{0,192},{32,224},{64,0},{96,32},{128,64},{160,96},{192,128},{224,1... | collective-permute-start | bytes 196616 | tf_op jit(solution)/shard_map/ppermute | solution.py:376
  22.7 3.9 %copy-start.1 = (s32[1,48,32]{1,2,0:T(8,128)S(1)}, s32[1,48,32]{1,2,0:T(8,128)}, u32[]{:S(2)}) copy-start(s32[1,48,32]{1,2,0:T(8,128)} %param.13) | copy-start | bytes 18436
  26.6 0.7 %copy-start.2 = (s32[1,1,48]{2,1,0:T(1,128)S(1)}, s32[1,1,48]{2,1,0:T(1,128)}, u32[]{:S(2)}) copy-start(s32[1,1,48]{2,1,0:T(1,128)} %param.10) | copy-start | bytes 580
  35.6 8.7 %collective-permute-start.7 = (f32[3,48,128]{2,1,0:T(8,128)S(1)}, f32[3,48,128]{2,1,0:T(8,128)S(1)}, u32[]{:S(2)}, u32[]{:S(2)}) collective-permute-start(f32[3,48,128]{2,1,0:T(8,128)S(1)} %get-tuple-element.30), channel_id=1, source_target_pairs={{0,16},{1,17},{2,18},{3,19},{4,20},{5,21},{6,22},{7,23},{8,24},{9,... | collective-permute-start | bytes 221192 | tf_op jit(solution)/shard_map/ppermute | solution.py:420
  37.3 7.7 %collective-permute-start.8 = (f32[3,48,128]{2,1,0:T(8,128)S(1)}, f32[3,48,128]{2,1,0:T(8,128)S(1)}, u32[]{:S(2)}, u32[]{:S(2)}) collective-permute-start(f32[3,48,128]{2,1,0:T(8,128)S(1)} %get-tuple-element.31), channel_id=1, source_target_pairs={{0,24},{1,25},{2,26},{3,27},{4,28},{5,29},{6,30},{7,31},{8,0},{9,1... | collective-permute-start | bytes 221192 | tf_op jit(solution)/shard_map/ppermute | solution.py:420
  41.0 5.6 %collective-permute-start.9 = (f32[3,48,128]{2,1,0:T(8,128)S(1)}, f32[3,48,128]{2,1,0:T(8,128)S(1)}, u32[]{:S(2)}, u32[]{:S(2)}) collective-permute-start(f32[3,48,128]{2,1,0:T(8,128)S(1)} %get-tuple-element.32), channel_id=1, source_target_pairs={{0,8},{1,9},{2,10},{3,11},{4,12},{5,13},{6,14},{7,15},{8,16},{9,17... | collective-permute-start | bytes 221192 | tf_op jit(solution)/shard_map/ppermute | solution.py:420
